TPU v7x, 32 devices: a whole 2x2x4 slice. The times are simulated.
32 devices in a mesh: groups: 2 (over x), fsdp: 16 (over z, y, core).
Axes of the slice: x: 2, y: 2, z: 4, core: 2. Of those that a mesh axis runs over, the one named last changes fastest.
Arguments:
- activations: bfloat16 [8192, 8192], P(('groups', 'fsdp')), parts along dimension 0, may hold values from -6 to 6
- quant_codes: bfloat16 [8192, 512], P('fsdp'), may hold values from -120 to 120, as said below
- block_scales: float32 [64, 4], P('fsdp'), may hold values from 0.00012 to 0.0012
- lowrank_down_factor: bfloat16 [16384, 64], P('groups'), parts along dimension 0, may hold values from -0.0625 to 0.0625
- lowrank_up_factor: bfloat16 [128, 512], P('groups'), parts along dimension 0, may hold values from -0.75 to 0.75
- cotangent: bfloat16 [8192, 512], P(('groups', 'fsdp')), parts along dimension 0, may hold values from -6 to 6
Outputs:
- projected: bfloat16 [8192, 512], P(('groups', 'fsdp')), parts along dimension 0
- input_gradient: bfloat16 [8192, 8192], P(('groups', 'fsdp')), parts along dimension 0
- grad_down: float32 [16384, 64], P(('groups', 'fsdp')), parts along dimension 0
- grad_up: float32 [128, 512], P('groups'), parts along dimension 0
There are 2 independent parts, one for each index of `groups`. A program takes and returns all parts, laid end to end along the dimension named above; an argument that names none is the same for every part. Nothing has to cross between parts.
Inputs may be any that keep to these rules, and one draw needn't show every extreme that they name: `quant_codes`: every entry is a value of the FP8 E4M3 grid.
All inputs are finite; a program needn't handle non-finite values.
Results may differ from a plain program's by a relative error of at most 0.0051.
Values may be sent and summed in bfloat16 or wider, within the bound.
No kernel may reach another device: no remote copies, remote signals or barrier semaphores. Data moves between devices by JAX's collectives and lax.ppermute only.
A program may use at most 64 MiB of HBM per device.

v0:
```python
import math

import jax
import jax.numpy as jnp
from jax import lax
from jax.sharding import PartitionSpec as P

BLOCK = 128


lowrank_scale = 0.5


def weight_transpose(left, right):
    return lax.dot_general(
        left, right, (((1,), (1,)), ((), ())), preferred_element_type=jnp.float32
    )


def leading(left, right):
    return lax.dot_general(
        left, right, (((0,), (0,)), ((), ())), preferred_element_type=jnp.float32
    )


def dequantize(quant_codes, block_scales):
    spread_scales = jnp.repeat(jnp.repeat(block_scales, BLOCK, axis=0), BLOCK, axis=1)
    return (quant_codes.astype(jnp.float32) * spread_scales).astype(jnp.bfloat16)


def per_device(
    activations, quant_codes, block_scales, lowrank_down_factor, lowrank_up_factor, cotangent
):
    value_weight = dequantize(quant_codes, block_scales)
    lowrank_hidden = jnp.dot(
        activations, lowrank_down_factor, preferred_element_type=jnp.float32
    ).astype(jnp.bfloat16)
    lowrank_update = lowrank_scale * jnp.dot(
        lowrank_hidden, lowrank_up_factor, preferred_element_type=jnp.float32
    )
    hidden_gradient = weight_transpose(cotangent, lowrank_up_factor).astype(jnp.bfloat16)
    columns = activations
    projected = (
        lowrank_update
        + jnp.dot(
            columns,
            lax.all_gather(value_weight, "fsdp", axis=0, tiled=True),
            preferred_element_type=jnp.float32,
        )
    ).astype(jnp.bfloat16)
    input_gradient = (
        weight_transpose(cotangent, lax.all_gather(value_weight, "fsdp", axis=0, tiled=True))
        + lowrank_scale * weight_transpose(hidden_gradient, lowrank_down_factor)
    ).astype(jnp.bfloat16)
    scaling_factor = lowrank_scale / math.sqrt(activations.shape[0] * lax.axis_size("fsdp"))
    columns = activations
    grad_down = lax.psum_scatter(
        scaling_factor * leading(columns, hidden_gradient), "fsdp", scatter_dimension=0, tiled=True
    )
    grad_up = lax.psum(scaling_factor * leading(lowrank_hidden, cotangent), "fsdp")
    return (projected, input_gradient, grad_down, grad_up)


def solution(mesh):
    in_specs = (
        P(("groups", "fsdp"), None),
        P("fsdp", None),
        P("fsdp", None),
        P("groups", None),
        P("groups", None),
        P(("groups", "fsdp"), None),
    )
    out_specs = (
        P(("groups", "fsdp"), None),
        P(("groups", "fsdp"), None),
        P(("groups", "fsdp"), None),
        P("groups", None),
    )
    return jax.shard_map(
        per_device, mesh=mesh, in_specs=in_specs, out_specs=out_specs, check_vma=False
    )
```

profile of v0, /device:TPU:0, one launch (start us, length us, event | category | flops | bytes accessed | tf_op | source)
XLA Modules:
  0.0 253.3 jit_solution(8080913003574166532)
XLA Ops:
  7.2 0.0 copy-start
  7.2 0.0 all-gather.2.cloned.1.call-start
  7.2 0.8 broadcast_in_dim.6
  8.0 0.6 broadcast_in_dim.7
  8.6 0.0 copy-start.1
  8.6 0.0 copy-start.2
  8.6 2.1 fusion.5
  10.7 0.0 all-gather.2.cloned.1.call-update
  10.7 0.0 all-reduce.2.cloned.1.call-start
  10.8 0.0 copy-done
  10.8 3.6 %convolution_convert_fusion.1 = bf16[256,64]{0,1:T(8,128)(2,1)S(1)} fusion(bf16[256,8192]{1,0:T(8,128)(2,1)} %param.6, bf16[8192,64]{0,1:T(8,128)(2,1)S(1)} %copy-done), kind=kOutput, calls=%fused_computation.12 | convolution fusion | flops 268451840 | bytes 5275648 | tf_op jit(solution)/shard_map/dot_general | solution.py:35
  14.4 0.0 copy-done.1
  14.4 0.8 convolution_multiply_fusion.3
  15.2 0.0 all-reduce.2.cloned.1.call-update
  15.2 0.0 reduce-scatter.2.cloned.1.call-start
  15.3 0.0 copy-done.2
  15.3 0.2 convolution_convert_fusion
  15.5 4.4 %fusion.2 = f32[8192,64]{0,1:T(8,128)} fusion(bf16[256,64]{0,1:T(8,128)(2,1)S(1)} %convolution_convert_fusion, bf16[256,8192]{1,0:T(8,128)(2,1)} %param.6), kind=kOutput, calls=%fused_computation.5 | convolution fusion | flops 268959744 | bytes 6324224 | tf_op jit(solution)/shard_map/dot_general | solution.py:21
  19.9 0.0 reduce-scatter.2.cloned.1.call-update
  19.9 68.6 %all-gather.2.cloned.1.call-done = bf16[8192,512]{1,0:T(8,128)(2,1)} async-done(((bf16[512,512]{1,0:T(8,128)(2,1)}), bf16[8192,512]{1,0:T(8,128)(2,1)}) %all-gather.2.cloned.1.call-update) | async-done | bytes 8388624 | tf_op jit(solution)/shard_map/all_gather | solution.py:47
  88.5 5.8 %convolution_bitcast_fusion = f32[256,8192]{0,1:T(8,128)S(1)} fusion(bf16[8192,512]{1,0:T(8,128)(2,1)} %all-gather.2.cloned.1.call-done, bf16[256,512]{1,0:T(8,128)(2,1)S(1)} %copy-done.1), kind=kOutput, calls=%fused_computation.2 | convolution fusion | flops 2147483648 | bytes 17039360 | tf_op jit(solution)/shard_map/dot_general | solution.py:15
  94.2 3.3 %fusion.1 = bf16[256,8192]{0,1:T(8,128)(2,1)} fusion(f32[256,8192]{0,1:T(8,128)S(1)} %convolution_bitcast_fusion, bf16[256,64]{0,1:T(8,128)(2,1)S(1)} %convolution_convert_fusion, bf16[8192,64]{0,1:T(8,128)(2,1)S(1)} %copy-done), kind=kOutput, calls=%fused_computation.3 | convolution fusion | flops 274726912 | bytes 13664256 | tf_op jit(solution)/shard_map/dot_general | solution.py:15
  97.6 6.3 %copy.12 = bf16[256,8192]{1,0:T(8,128)(2,1)} copy(bf16[256,8192]{0,1:T(8,128)(2,1)} %fusion.1) | data formatting | bytes 8388608
  103.9 7.0 %convolution_bitcast_fusion.1 = f32[256,512]{1,0:T(8,128)S(1)} fusion(bf16[256,8192]{1,0:T(8,128)(2,1)} %param.6, bf16[8192,512]{1,0:T(8,128)(2,1)} %all-gather.2.cloned.1.call-done), kind=kOutput, calls=%fused_computation.8 | convolution fusion | flops 2147483648 | bytes 13107200 | tf_op jit(solution)/shard_map/dot_general | solution.py:45
  110.9 1.0 fusion.4
  111.9 65.8 %all-reduce.2.cloned.1.call-done = f32[64,512]{1,0:T(8,128)} async-done(((f32[64,512]{1,0:T(8,128)}), f32[64,512]{1,0:T(8,128)}) %all-reduce.2.cloned.1.call-update) | async-done | bytes 131088 | tf_op jit(solution)/shard_map/psum | solution.py:60
  177.7 67.5 %reduce-scatter.2.cloned.1.call-done = f32[512,64]{0,1:T(8,128)} async-done(((f32[8192,64]{0,1:T(8,128)}), f32[512,64]{0,1:T(8,128)}) %reduce-scatter.2.cloned.1.call-update) | async-done | bytes 131088 | tf_op jit(solution)/shard_map/reduce_scatter | solution.py:57
  245.2 1.6 copy.18
Async XLA Ops:
  7.2 3.6 %copy-start = (bf16[8192,64]{0,1:T(8,128)(2,1)S(1)}, bf16[8192,64]{0,1:T(8,128)(2,1)}, u32[]{:S(2)}) copy-start(bf16[8192,64]{0,1:T(8,128)(2,1)} %param.9) | copy-start | bytes 3145732
  7.2 81.3 %all-gather.2.cloned.1.call-start = ((), (), s32[]{:S(2)}) async-start(), calls=%async_computation.1 | async-start | bytes 8912896 | tf_op jit(solution)/shard_map/all_gather | solution.py:47
  8.6 5.8 %copy-start.1 = (bf16[256,512]{1,0:T(8,128)(2,1)S(1)}, bf16[256,512]{1,0:T(8,128)(2,1)}, u32[]{:S(2)}) copy-start(bf16[256,512]{1,0:T(8,128)(2,1)} %param.11) | copy-start | bytes 786436
  8.6 6.7 %copy-start.2 = (bf16[64,512]{1,0:T(8,128)(2,1)S(1)}, bf16[64,512]{1,0:T(8,128)(2,1)}, u32[]{:S(2)}) copy-start(bf16[64,512]{1,0:T(8,128)(2,1)} %param.10) | copy-start | bytes 196612
  10.7 166.9 %all-reduce.2.cloned.1.call-start = ((), (), s32[]{:S(2)}) async-start(), calls=%async_computation.3 | async-start | bytes 262144 | tf_op jit(solution)/shard_map/psum | solution.py:60
  15.2 230.0 %reduce-scatter.2.cloned.1.call-start = ((), (), s32[]{:S(2)}) async-start(), calls=%async_computation.2 | async-start | bytes 2228224 | tf_op jit(solution)/shard_map/reduce_scatter | solution.py:57
Sparse Core Ops, SparseCore 0:
  10.8 77.5 all-gather.1
  92.5 85.1 all-reduce.1
  182.0 63.1 reduce-scatter.1
where the time goes:
time: 254 us; the launch traced here: 253 us
  waiting for transfers between devices  202 us (80%)
  matrix products  26 us (10%)
  between operations  13.8 us (5%)
  local copies, waits for them, and re-layouts  9.29 us (4%)
    all_gather x1, waiting for transfers between devices, per_device(): lax.all_gather(value_weight, 'fsdp', axis=0, tiled=True)  68.6 us
    reduce_scatter x1, waiting for transfers between devices, per_device(): lax.psum_scatter(scaling_factor * leading(columns, hidden_gradient), 'fsd...  67.5 us
    psum x1, waiting for transfers between devices, per_device(): lax.psum(scaling_factor * leading(lowrank_hidden, cotangent), 'fsdp')  65.8 us
    dot_general x3, matrix products, weight_transpose(): lax.dot_general(left, right, (((1,), (1,)), ((), ())), preferred_element_...  9.26 us
    unnamed x8, local copies, waits for them, and re-layouts  7.92 us
    dot_general x1, matrix products, per_device(): jnp.dot(columns, lax.all_gather(value_weight, 'fsdp', axis=0, tiled=True)...  7.01 us
    dot_general x2, matrix products, leading(): lax.dot_general(left, right, (((0,), (0,)), ((), ())), preferred_element_...  5.2 us
  transfers between devices with their start and end apart: 3, of which 3 were waited for; matrix products, arithmetic and copies ran while one was open for 13% of the time, Pallas kernels for 0%

commit v1 on v0

v1 whole, which is shorter than its diff:
```python
import math

import jax
import jax.numpy as jnp
from jax import lax
from jax.experimental import pallas as pl
from jax.experimental.pallas import tpu as pltpu
from jax.sharding import PartitionSpec as P

BLOCK = 128
AXES = ("groups", "fsdp")

lowrank_scale = 0.5


def weight_transpose(left, right):
    return lax.dot_general(
        left, right, (((1,), (1,)), ((), ())), preferred_element_type=jnp.float32
    )


def leading(left, right):
    return lax.dot_general(
        left, right, (((0,), (0,)), ((), ())), preferred_element_type=jnp.float32
    )


def dequantize(quant_codes, block_scales):
    spread_scales = jnp.repeat(jnp.repeat(block_scales, BLOCK, axis=0), BLOCK, axis=1)
    return (quant_codes.astype(jnp.float32) * spread_scales).astype(jnp.bfloat16)


def per_device_general(
    activations, quant_codes, block_scales, lowrank_down_factor, lowrank_up_factor, cotangent
):
    value_weight = dequantize(quant_codes, block_scales)
    lowrank_hidden = jnp.dot(
        activations, lowrank_down_factor, preferred_element_type=jnp.float32
    ).astype(jnp.bfloat16)
    lowrank_update = lowrank_scale * jnp.dot(
        lowrank_hidden, lowrank_up_factor, preferred_element_type=jnp.float32
    )
    hidden_gradient = weight_transpose(cotangent, lowrank_up_factor).astype(jnp.bfloat16)
    gathered = lax.all_gather(value_weight, "fsdp", axis=0, tiled=True)
    projected = (
        lowrank_update + jnp.dot(activations, gathered, preferred_element_type=jnp.float32)
    ).astype(jnp.bfloat16)
    input_gradient = (
        weight_transpose(cotangent, gathered)
        + lowrank_scale * weight_transpose(hidden_gradient, lowrank_down_factor)
    ).astype(jnp.bfloat16)
    scaling_factor = lowrank_scale / math.sqrt(activations.shape[0] * lax.axis_size("fsdp"))
    grad_down = lax.psum_scatter(
        scaling_factor * leading(activations, hidden_gradient),
        "fsdp",
        scatter_dimension=0,
        tiled=True,
    )
    grad_up = lax.psum(scaling_factor * leading(lowrank_hidden, cotangent), "fsdp")
    return (projected, input_gradient, grad_down, grad_up)


NZ = 4
VMEM_LIMIT = 40 * 1024 * 1024


def pairs_of(move):
    found = []
    for g in range(2):
        for z in range(NZ):
            for y in range(2):
                for c in range(2):
                    to = move(g, z, y, c)
                    found.append((index_of(g, z, y, c), index_of(*to)))
    return found


def index_of(g, z, y, c):
    return ((g * NZ + z) * 2 + y) * 2 + c


OVER_CORE = pairs_of(lambda g, z, y, c: (g, z, y, 1 - c))
OVER_Y = pairs_of(lambda g, z, y, c: (g, z, 1 - y, c))
OVER_X = pairs_of(lambda g, z, y, c: (1 - g, z, y, c))
Z_UP = pairs_of(lambda g, z, y, c: (g, (z + 1) % NZ, y, c))
Z_DOWN = pairs_of(lambda g, z, y, c: (g, (z - 1) % NZ, y, c))
Z_FAR = pairs_of(lambda g, z, y, c: (g, (z + 2) % NZ, y, c))


def send(array, pairs):
    return lax.ppermute(array, AXES, pairs)


def whole():
    return pl.BlockSpec(memory_space=pltpu.VMEM)


def scalars():
    return pl.BlockSpec(memory_space=pltpu.SMEM)


def anywhere():
    return pl.BlockSpec(memory_space=pl.ANY)


def params():
    return pltpu.CompilerParams(vmem_limit_bytes=VMEM_LIMIT)


LITTLE = pl.CostEstimate(flops=1, bytes_accessed=1, transcendentals=0)


def dequantize_halves(place, quant_codes, block_scales):
    rows, columns = quant_codes.shape
    half = rows // 2

    def kernel(place_ref, codes_ref, scales_ref, first_ref, other_ref):
        g = place_ref[0]
        for which, out_ref in ((g, first_ref), (1 - g, other_ref)):
            for i in range(half // BLOCK):
                start = pl.multiple_of(which * half + i * BLOCK, BLOCK)
                for j in range(columns // BLOCK):
                    block = codes_ref[pl.ds(start, BLOCK), j * BLOCK : (j + 1) * BLOCK]
                    scale = scales_ref[which * (half // BLOCK) + i, j]
                    out_ref[i * BLOCK : (i + 1) * BLOCK, j * BLOCK : (j + 1) * BLOCK] = (
                        block.astype(jnp.float32) * scale
                    ).astype(jnp.bfloat16)

    return pl.pallas_call(
        kernel,
        out_shape=[jax.ShapeDtypeStruct((half, columns), jnp.bfloat16)] * 2,
        in_specs=[scalars(), whole(), scalars()],
        out_specs=[whole()] * 2,
        compiler_params=params(),
        cost_estimate=LITTLE,
        name="dequantize",
    )(place, quant_codes, block_scales)


def local_gradients(place, activations, down_t, up, cotangent):
    tokens, width = activations.shape
    rank, features = up.shape
    chips = NZ * 2
    chunk = width // chips
    part = chunk // 2
    up_part = features // 2
    packed = chips * part + up_part

    def kernel(
        place_ref, act_ref, down_ref, up_ref, cot_ref, latent_ref, lgrad_ref, own_ref, away_ref,
        total, lgrad_t,
    ):
        step = pl.program_id(0)
        y, c = place_ref[2], place_ref[3]

        @pl.when(step == 0)
        def _():
            total[...] = jnp.zeros_like(total)
            held = weight_transpose(cot_ref[...], up_ref[...]).astype(jnp.bfloat16)
            lgrad_ref[...] = held
            lgrad_t[...] = weight_transpose(up_ref[...], cot_ref[...]).astype(jnp.bfloat16)

        block = act_ref[...]
        total[...] += weight_transpose(block, down_ref[...])
        term = jnp.dot(lgrad_t[...], block, preferred_element_type=jnp.float32)
        z_of, y_of = step // 2, step % 2
        here = jnp.where(y_of == y, NZ, 0) + z_of
        at = pl.ds(pl.multiple_of(here * part, part), part)

        @pl.when(c == 0)
        def _():
            own_ref[:, at] = term[:, :part]
            away_ref[:, at] = term[:, part:]

        @pl.when(c == 1)
        def _():
            own_ref[:, at] = term[:, part:]
            away_ref[:, at] = term[:, :part]

        @pl.when(step == chips - 1)
        def _():
            latent = total[...].astype(jnp.bfloat16)
            latent_ref[...] = latent
            both = leading(latent, cot_ref[...])

            @pl.when(c == 0)
            def _():
                own_ref[:, chips * part :] = both[:, :up_part]
                away_ref[:, chips * part :] = both[:, up_part:]

            @pl.when(c == 1)
            def _():
                own_ref[:, chips * part :] = both[:, up_part:]
                away_ref[:, chips * part :] = both[:, :up_part]

    fixed = lambda shape: pl.BlockSpec(shape, lambda i: (0,) * len(shape))
    return pl.pallas_call(
        kernel,
        grid=(chips,),
        out_shape=[
            jax.ShapeDtypeStruct((tokens, rank), jnp.bfloat16),
            jax.ShapeDtypeStruct((tokens, rank), jnp.bfloat16),
            jax.ShapeDtypeStruct((rank, packed), jnp.float32),
            jax.ShapeDtypeStruct((rank, packed), jnp.float32),
        ],
        in_specs=[
            scalars(),
            pl.BlockSpec((tokens, chunk), lambda i: (0, i)),
            pl.BlockSpec((rank, chunk), lambda i: (0, i)),
            fixed((rank, features)),
            fixed((tokens, features)),
        ],
        out_specs=[
            fixed((tokens, rank)),
            fixed((tokens, rank)),
            fixed((rank, packed)),
            fixed((rank, packed)),
        ],
        scratch_shapes=[
            pltpu.VMEM((tokens, rank), jnp.float32),
            pltpu.VMEM((rank, tokens), jnp.bfloat16),
        ],
        compiler_params=params(),
        cost_estimate=LITTLE,
        name="local_gradients",
    )(place, activations, down_t, up, cotangent)


def add_cores(own, came, up_part):
    rank, packed = own.shape
    half = (packed - up_part) // 2

    def kernel(own_ref, came_ref, message_ref, kept_ref):
        message_ref[:, :half] = (own_ref[:, :half] + came_ref[:, :half]).astype(jnp.bfloat16)
        kept_ref[...] = own_ref[:, half : 2 * half] + came_ref[:, half : 2 * half]
        message_ref[:, half:] = (own_ref[:, 2 * half :] + came_ref[:, 2 * half :]).astype(
            jnp.bfloat16
        )

    return pl.pallas_call(
        kernel,
        out_shape=[
            jax.ShapeDtypeStruct((rank, half + up_part), jnp.bfloat16),
            jax.ShapeDtypeStruct((rank, half), jnp.float32),
        ],
        in_specs=[whole()] * 2,
        out_specs=[whole()] * 2,
        compiler_params=params(),
        cost_estimate=LITTLE,
        name="add_cores",
    )(own, came)


def add_y(place, kept, sent, came, up_part):
    rank, half = kept.shape
    part = half // NZ

    def kernel(place_ref, kept_ref, sent_ref, came_ref, up_ref, far_ref, down_ref, own_ref):
        z = place_ref[1]
        tail = sent_ref[:, half:].astype(jnp.float32) + came_ref[:, half:].astype(jnp.float32)
        tail = tail.astype(jnp.bfloat16)
        for shift, out_ref in ((0, own_ref), (1, up_ref), (2, far_ref), (3, down_ref)):
            at = pl.ds(pl.multiple_of(lax.rem(z + shift, NZ) * part, part), part)
            summed = kept_ref[:, at] + came_ref[:, at].astype(jnp.float32)
            out_ref[:, :part] = summed.astype(out_ref.dtype)
            out_ref[:, part:] = tail.astype(out_ref.dtype)

    shape = (rank, part + up_part)
    return pl.pallas_call(
        kernel,
        out_shape=[jax.ShapeDtypeStruct(shape, jnp.bfloat16)] * 3
        + [jax.ShapeDtypeStruct(shape, jnp.float32)],
        in_specs=[scalars()] + [whole()] * 3,
        out_specs=[whole()] * 4,
        compiler_params=params(),
        cost_estimate=LITTLE,
        name="add_y",
    )(place, kept, sent, came)


def add_z(own, from_down, from_far, from_up, up_part, factor):
    rank, wide = own.shape
    part = wide - up_part

    def kernel(own_ref, a_ref, b_ref, c_ref, gd_ref, gu_ref):
        f32 = jnp.float32
        summed = (own_ref[...] + b_ref[...].astype(f32)) + (
            a_ref[...].astype(f32) + c_ref[...].astype(f32)
        )
        summed = summed * factor
        gd_ref[...] = summed[:, :part]
        gu_ref[...] = summed[:, part:]

    return pl.pallas_call(
        kernel,
        out_shape=[
            jax.ShapeDtypeStruct((rank, part), jnp.float32),
            jax.ShapeDtypeStruct((rank, up_part), jnp.float32),
        ],
        in_specs=[whole()] * 4,
        out_specs=[whole()] * 2,
        compiler_params=params(),
        cost_estimate=LITTLE,
        name="add_z",
    )(own, from_down, from_far, from_up)


def join_cores(place, own, came):
    rank, up_part = own.shape

    def kernel(place_ref, own_ref, came_ref, out_ref):
        c = place_ref[3]
        out_ref[:, pl.ds(pl.multiple_of(c * up_part, up_part), up_part)] = own_ref[...]
        out_ref[:, pl.ds(pl.multiple_of((1 - c) * up_part, up_part), up_part)] = came_ref[...]

    return pl.pallas_call(
        kernel,
        out_shape=jax.ShapeDtypeStruct((rank, 2 * up_part), jnp.float32),
        in_specs=[scalars(), whole(), whole()],
        out_specs=whole(),
        compiler_params=params(),
        cost_estimate=LITTLE,
        name="join_cores",
    )(place, own, came)


def multiply(
    place, keys, pieces, activations, down_t, cotangent, lgrad, total, gradient, finish=None
):
    count = len(pieces)
    tokens, width = activations.shape
    rank = down_t.shape[0]
    rows, features = pieces[0].shape
    started = total is not None

    def kernel(*refs):
        refs = list(refs)
        place_ref, act_ref, down_ref, cot_ref, lgrad_ref = refs[:5]
        del refs[:5]
        if started:
            total_ref = refs.pop(0)
            refs.pop(0)
        if finish is not None:
            latent_ref, up_ref = refs.pop(0), refs.pop(0)
        piece_refs = refs[:count]
        del refs[:count]
        out_ref, grad_ref, weights, acts, downs, grads, in_sems, out_sems = refs
        g, z, y, c = (place_ref[i] for i in range(4))
        columns = []
        for dz, dy, dc, dh in keys:
            chip = lax.rem(z + (NZ - dz), NZ) * 2 + (1 - y if dy else y)
            device = chip * 2 + (1 - c if dc else c)
            start = (device * 2 + (1 - g if dh else g)) * rows
            columns.append(pl.ds(pl.multiple_of(start, rows), rows))
        coming, going = [], []
        for p in range(count):
            at = columns[p]
            trio = [
                pltpu.make_async_copy(piece_refs[p], weights.at[p], in_sems.at[3 * p]),
                pltpu.make_async_copy(act_ref.at[:, at], acts.at[p], in_sems.at[3 * p + 1]),
                pltpu.make_async_copy(down_ref.at[:, at], downs.at[p], in_sems.at[3 * p + 2]),
            ]
            for copy in trio:
                copy.start()
            coming.append(trio)
        if finish is not None:
            sum_so_far = total_ref[...] + lowrank_scale * jnp.dot(
                latent_ref[...], up_ref[...], preferred_element_type=jnp.float32
            )
        elif started:
            sum_so_far = total_ref[...]
        else:
            sum_so_far = None
        for p in range(count):
            for copy in coming[p]:
                copy.wait()
            weight = weights[p]
            term = jnp.dot(acts[p], weight, preferred_element_type=jnp.float32)
            sum_so_far = term if sum_so_far is None else sum_so_far + term
            grads[p] = (
                weight_transpose(cot_ref[...], weight)
                + lowrank_scale
                * jnp.dot(lgrad_ref[...], downs[p], preferred_element_type=jnp.float32)
            ).astype(jnp.bfloat16)
            copy = pltpu.make_async_copy(grads.at[p], grad_ref.at[:, columns[p]], out_sems.at[p])
            copy.start()
            going.append(copy)
        out_ref[...] = sum_so_far.astype(out_ref.dtype)
        for copy in going:
            copy.wait()

    operands = [place, activations, down_t, cotangent, lgrad]
    specs = [scalars(), anywhere(), anywhere(), whole(), whole()]
    aliases = {}
    if started:
        operands += [total, gradient]
        specs += [whole(), anywhere()]
        aliases = {6: 1}
    if finish is not None:
        operands += list(finish)
        specs += [whole(), whole()]
    operands += list(pieces)
    specs += [anywhere()] * count
    out_type = jnp.float32 if finish is None else jnp.bfloat16
    return pl.pallas_call(
        kernel,
        out_shape=[
            jax.ShapeDtypeStruct((tokens, features), out_type),
            jax.ShapeDtypeStruct((tokens, width), jnp.bfloat16),
        ],
        in_specs=specs,
        out_specs=[whole(), anywhere()],
        scratch_shapes=[
            pltpu.VMEM((count, rows, features), jnp.bfloat16),
            pltpu.VMEM((count, tokens, rows), jnp.bfloat16),
            pltpu.VMEM((count, rank, rows), jnp.bfloat16),
            pltpu.VMEM((count, tokens, rows), jnp.bfloat16),
            pltpu.SemaphoreType.DMA((3 * count,)),
            pltpu.SemaphoreType.DMA((count,)),
        ],
        input_output_aliases=aliases,
        compiler_params=params(),
        cost_estimate=LITTLE,
        name="multiply",
    )(*operands)


def per_device(
    activations, quant_codes, block_scales, lowrank_down_factor, lowrank_up_factor, cotangent
):
    g = lax.axis_index("groups")
    f = lax.axis_index("fsdp")
    c, y, z = f & 1, (f >> 1) & 1, f >> 2
    place = jnp.stack([g, z, y, c]).astype(jnp.int32)
    shard = quant_codes.shape[0]
    half = shard // 2
    up_part = lowrank_up_factor.shape[1] // 2
    down_t = lowrank_down_factor.T
    factor = lowrank_scale / math.sqrt(activations.shape[0] * lax.axis_size("fsdp"))

    def both_cores(keys):
        return [(a, b, 0, h) for a, b, h in keys] + [(a, b, 1, h) for a, b, h in keys]

    barrier = lax.optimization_barrier
    held = {}

    held[0, 0, 0], held[0, 0, 1] = dequantize_halves(place, quant_codes, block_scales)
    own_keys = [(0, 0, 0), (0, 0, 1)]

    r1 = {
        (1, 0, 0): send(held[0, 0, 0], Z_UP),
        (3, 0, 0): send(held[0, 0, 0], Z_DOWN),
        (0, 1, 0): send(held[0, 0, 0], OVER_Y),
        (0, 1, 1): send(held[0, 0, 1], OVER_Y),
    }
    swapped = [send(held[k], OVER_CORE) for k in own_keys]
    latent, lgrad, own_terms, away_terms = local_gradients(
        place, activations, down_t, lowrank_up_factor, cotangent
    )
    came = send(away_terms, OVER_CORE)
    total, gradient = multiply(
        place, both_cores(own_keys),
        [held[k] for k in own_keys] + swapped,
        activations, down_t, cotangent, lgrad, None, None,
    )
    message_y, kept = add_cores(own_terms, came, up_part)
    r1, message_y, kept, total, gradient = barrier((r1, message_y, kept, total, gradient))
    held.update(r1)

    r2 = {
        (1, 1, 0): send(held[1, 0, 0], OVER_Y),
        (1, 0, 1): send(held[1, 0, 0], OVER_X),
        (3, 0, 1): send(held[3, 0, 0], OVER_X),
        (2, 0, 0): send(held[1, 0, 0], Z_UP),
        (3, 1, 1): send(held[0, 1, 1], Z_DOWN),
    }
    came_y = send(message_y, OVER_Y)
    keys = list(r1)
    swapped = [send(held[k], OVER_CORE) for k in keys]
    total, gradient = multiply(
        place, both_cores(keys),
        [held[k] for k in keys] + swapped,
        activations, down_t, cotangent, lgrad, total, gradient,
    )
    r2, came_y, total, gradient = barrier((r2, came_y, total, gradient))
    held.update(r2)

    to_up, to_far, to_down, own_part = add_y(place, kept, message_y, came_y, up_part)
    r3 = {
        (3, 1, 0): send(held[3, 0, 0], OVER_Y),
        (2, 1, 0): send(held[2, 0, 0], OVER_Y),
        (2, 0, 1): send(held[2, 0, 0], OVER_X),
        (1, 1, 1): send(held[1, 1, 0], OVER_X),
        (2, 1, 1): send(held[3, 1, 1], Z_DOWN),
    }
    from_down, from_far, from_up = send(to_up, Z_UP), send(to_far, Z_FAR), send(to_down, Z_DOWN)
    keys = list(r2)
    swapped = [send(held[k], OVER_CORE) for k in keys]
    total, gradient = multiply(
        place, both_cores(keys),
        [held[k] for k in keys] + swapped,
        activations, down_t, cotangent, lgrad, total, gradient,
    )
    r3, from_down, from_far, from_up, total, gradient = barrier(
        (r3, from_down, from_far, from_up, total, gradient)
    )
    held.update(r3)

    keys = list(r3)
    swapped = [send(held[k], OVER_CORE) for k in keys]
    grad_down_t, up_own = add_z(own_part, from_down, from_far, from_up, up_part, factor)
    up_came = send(up_own, OVER_CORE)
    total, gradient = multiply(
        place, both_cores(keys)[: len(keys)], [held[k] for k in keys],
        activations, down_t, cotangent, lgrad, total, gradient,
    )
    projected, gradient = multiply(
        place, both_cores(keys)[len(keys) :], swapped,
        activations, down_t, cotangent, lgrad, total, gradient,
        finish=(latent, lowrank_up_factor),
    )
    grad_up = join_cores(place, up_own, up_came)
    return (projected, gradient, grad_down_t.T, grad_up)


def solution(mesh):
    in_specs = (
        P(("groups", "fsdp"), None),
        P("fsdp", None),
        P("fsdp", None),
        P("groups", None),
        P("groups", None),
        P(("groups", "fsdp"), None),
    )
    out_specs = (
        P(("groups", "fsdp"), None),
        P(("groups", "fsdp"), None),
        P(("groups", "fsdp"), None),
        P("groups", None),
    )
    small = mesh.shape["groups"] == 2 and mesh.shape["fsdp"] == NZ * 4
    return jax.shard_map(
        per_device if small else per_device_general,
        mesh=mesh,
        in_specs=in_specs,
        out_specs=out_specs,
        check_vma=False,
    )
```

time: 254 us -> 89.5 us (0.35)
  waiting for transfers between devices: 202 us -> 25.3 us
  Pallas kernels: 0 us -> 30.7 us
  starting transfers between devices: 0.12 us -> 27 us
  matrix products: 26 us -> 0 us
  between operations: 13.8 us -> 0.98 us
  local copies, waits for them, and re-layouts: 9.29 us -> 5.22 us
    all_gather x1 -> x0, waiting for transfers between devices: 68.6 us -> none  [per_device(): lax.all_gather(value_weight, 'fsdp', axis=0, tiled=True)]
    reduce_scatter x1 -> x0, waiting for transfers between devices: 67.5 us -> none  [per_device(): lax.psum_scatter(scaling_factor * leading(columns, hidden_gradient), 'fsd...]
    psum x1 -> x0, waiting for transfers between devices: 65.8 us -> none  [per_device(): lax.psum(scaling_factor * leading(lowrank_hidden, cotangent), 'fsdp')]
    pallas_call x0 -> x11, Pallas kernels: none -> 30.7 us  [the longest x5 23.2 us: multiply(): pl.pallas_call(kernel, out_shape=[jax.ShapeDtypeStruct((tokens, features)...]
    ppermute x0 -> x36, starting transfers between devices: none -> 27 us  [send(): return lax.ppermute(array, AXES, pairs)]
    dot_general x8 -> x0, matrix products: 26 us -> none  [the longest x3 9.26 us: weight_transpose(): lax.dot_general(left, right, (((1,), (1,)), ((), ())), preferred_element_...]
    ppermute x0 -> x36, waiting for transfers between devices: none -> 25.3 us  [send(): return lax.ppermute(array, AXES, pairs)]
    unnamed x8 -> x16, local copies, waits for them, and re-layouts: 7.92 us -> 5.22 us
  transfers between devices with their start and end apart: 3 -> 36, of which waited for: 3 -> 10; matrix products, arithmetic and copies ran while one was open for 13% -> 0% of each run, Pallas kernels for 0% -> 24%
where the time goes in v1:
time: 89.5 us; the launch traced here: 89.2 us
  Pallas kernels  30.7 us (34%)
  starting transfers between devices  27 us (30%)
  waiting for transfers between devices  25.3 us (28%)
  local copies, waits for them, and re-layouts  5.22 us (6%)
  between operations  0.98 us (1%)
    ppermute x36, starting transfers between devices, send(): return lax.ppermute(array, AXES, pairs)  27 us
    ppermute x36, waiting for transfers between devices, send(): return lax.ppermute(array, AXES, pairs)  25.3 us
    pallas_call x5, Pallas kernels, multiply(): pl.pallas_call(kernel, out_shape=[jax.ShapeDtypeStruct((tokens, features)...  23.2 us
    unnamed x16, local copies, waits for them, and re-layouts  5.22 us
    pallas_call x1, Pallas kernels, local_gradients(): pl.pallas_call(kernel, grid=(chips,), out_shape=[jax.ShapeDtypeStruct((to...  4.19 us
  transfers between devices with their start and end apart: 36, of which 10 were waited for; matrix products, arithmetic and copies ran while one was open for 0% of the time, Pallas kernels for 24%

profile of v1, /device:TPU:0, one launch (start us, length us, event | category | flops | bytes accessed | tf_op | source)
XLA Modules:
  0.0 89.2 jit_solution(8079228085114570738)
XLA Ops:
  0.7 2.2 %copy-done = bf16[256,8192]{1,0:T(8,128)(2,1)S(1)} copy-done((bf16[256,8192]{1,0:T(8,128)(2,1)S(1)}, bf16[256,8192]{1,0:T(8,128)(2,1)}, u32[]{:S(2)}) %copy-start) | copy-done | bytes 4194328
  2.9 1.2 %copy-done.2 = bf16[8192,64]{0,1:T(8,128)(2,1)S(1)} copy-done((bf16[8192,64]{0,1:T(8,128)(2,1)S(1)}, bf16[8192,64]{0,1:T(8,128)(2,1)}, u32[]{:S(2)}) %copy-start.2) | copy-done | bytes 1048600
  4.1 0.9 %copy-done.3 = bf16[256,512]{1,0:T(8,128)(2,1)S(1)} copy-done((bf16[256,512]{1,0:T(8,128)(2,1)S(1)}, bf16[256,512]{1,0:T(8,128)(2,1)}, u32[]{:S(2)}) %copy-start.3) | copy-done | bytes 262168
  5.1 0.8 copy-done.6
  5.9 4.2 %local_gradients.1 = (bf16[256,64]{1,0:T(8,128)(2,1)S(1)}, bf16[256,64]{1,0:T(8,128)(2,1)S(1)}, f32[64,4352]{1,0:T(8,128)S(1)}, f32[64,4352]{1,0:T(8,128)S(1)}) custom-call(s32[4]{0:T(128)S(1)} %pad_add_fusion.place_ref.refs_0_, bf16[256,8192]{1,0:T(8,128)(2,1)S(1)} %copy-done, bf16[64,8192]{1,0:T(8,128)(2,1)S(1)} %bitcast.6, bf16[64,512]{1,0:T(8,128)(2,1)S(1)} %copy-done.6, ...), custom_call_target="tpu_custom_call" | custom-call | flops 1 | bytes 1 | tf_op jit(solution)/shard_map/local_gradients/pallas_call | solution.py:197
  10.1 0.7 collective-permute-start.4
  10.8 0.7 dequantize.1
  11.6 0.5 collective-permute-start.5
  12.1 2.4 %collective-permute-start.1 = (bf16[256,512]{1,0:T(8,128)(2,1)S(1)}, bf16[256,512]{1,0:T(8,128)(2,1)S(1)}, u32[]{:S(2)}, u32[]{:S(2)}) collective-permute-start(bf16[256,512]{1,0:T(8,128)(2,1)S(1)} %get-tuple-element.56.refs_6_), channel_id=1, source_target_pairs={{0,2},{1,3},{2,0},{3,1},{4,6},{5,7},{6,4},{7,5},{8,10},{9,11},{10,... | collective-permute-start | bytes 786440 | tf_op jit(solution)/shard_map/ppermute | solution.py:91
  14.5 3.6 %collective-permute-start.3 = (bf16[256,512]{1,0:T(8,128)(2,1)S(1)}, bf16[256,512]{1,0:T(8,128)(2,1)S(1)}, u32[]{:S(2)}, u32[]{:S(2)}) collective-permute-start(bf16[256,512]{1,0:T(8,128)(2,1)S(1)} %get-tuple-element.55.refs_5_), channel_id=1, source_target_pairs={{0,12},{1,13},{2,14},{3,15},{4,0},{5,1},{6,2},{7,3},{8,4},{9,5},{1... | collective-permute-start | bytes 786440 | tf_op jit(solution)/shard_map/ppermute | solution.py:91
  18.1 0.6 collective-permute-start
  18.7 3.0 %multiply.5 = (f32[256,512]{1,0:T(8,128)S(1)}, bf16[256,8192]{1,0:T(8,128)(2,1)}) custom-call(s32[4]{0:T(128)S(1)} %pad_add_fusion.place_ref.refs_0_, bf16[256,8192]{1,0:T(8,128)(2,1)S(1)} %copy-done.1, bf16[64,8192]{1,0:T(8,128)(2,1)S(1)} %bitcast.7, bf16[256,512]{1,0:T(8,128)(2,1)S(1)} %copy-done.4, bf16[256,64]{1,0:T(8,128)(2,1)S(1)} %get-tuple-element.54.refs_4_, ...), custom_call_target="tpu_custom_call" | custom-call | flops 1 | bytes 1 | tf_op jit(solution)/shard_map/multiply/pallas_call | solution.py:405
  21.9 2.9 %collective-permute-done.3.refs_10_ = bf16[256,512]{1,0:T(8,128)(2,1)S(1)} collective-permute-done((bf16[256,512]{1,0:T(8,128)(2,1)S(1)}, bf16[256,512]{1,0:T(8,128)(2,1)S(1)}, u32[]{:S(2)}, u32[]{:S(2)}) %collective-permute-start.3) | collective-permute-done | bytes 262176 | tf_op jit(solution)/shard_map/ppermute | solution.py:91
  24.8 5.7 %collective-permute-done.2.refs_9_ = bf16[256,512]{1,0:T(8,128)(2,1)S(1)} collective-permute-done((bf16[256,512]{1,0:T(8,128)(2,1)S(1)}, bf16[256,512]{1,0:T(8,128)(2,1)S(1)}, u32[]{:S(2)}, u32[]{:S(2)}) %collective-permute-start.2) | collective-permute-done | bytes 262176 | tf_op jit(solution)/shard_map/ppermute | solution.py:91
  30.5 0.5 collective-permute-start.14
  31.1 1.8 %collective-permute-start.11 = (bf16[256,512]{1,0:T(8,128)(2,1)S(1)}, bf16[256,512]{1,0:T(8,128)(2,1)S(1)}, u32[]{:S(2)}, u32[]{:S(2)}) collective-permute-start(bf16[256,512]{1,0:T(8,128)(2,1)S(1)} %collective-permute-done.1.refs_8_), channel_id=1, source_target_pairs={{0,12},{1,13},{2,14},{3,15},{4,0},{5,1},{6,2},{7,3},{8,4},{9,5},{1... | collective-permute-start | bytes 786440 | tf_op jit(solution)/shard_map/ppermute | solution.py:91
  32.9 1.5 %collective-permute-start.10 = (bf16[256,512]{1,0:T(8,128)(2,1)S(1)}, bf16[256,512]{1,0:T(8,128)(2,1)S(1)}, u32[]{:S(2)}, u32[]{:S(2)}) collective-permute-start(bf16[256,512]{1,0:T(8,128)(2,1)S(1)} %collective-permute-done.3.refs_10_), channel_id=1, source_target_pairs={{0,16},{1,17},{2,18},{3,19},{4,20},{5,21},{6,22},{7,23},{8,24},{9,... | collective-permute-start | bytes 786440 | tf_op jit(solution)/shard_map/ppermute | solution.py:91
  34.4 0.2 collective-permute-start.15
  34.6 1.5 %collective-permute-start.12 = (bf16[64,2304]{1,0:T(8,128)(2,1)S(1)}, bf16[64,2304]{1,0:T(8,128)(2,1)S(1)}, u32[]{:S(2)}, u32[]{:S(2)}) collective-permute-start(bf16[64,2304]{1,0:T(8,128)(2,1)S(1)} %get-tuple-element.66.sent_ref), channel_id=1, source_target_pairs={{0,2},{1,3},{2,0},{3,1},{4,6},{5,7},{6,4},{7,5},{8,10},{9,11},{10,... | collective-permute-start | bytes 884744 | tf_op jit(solution)/shard_map/ppermute | solution.py:91
  36.1 3.2 %collective-permute-done.11.refs_11_ = bf16[256,512]{1,0:T(8,128)(2,1)S(1)} collective-permute-done((bf16[256,512]{1,0:T(8,128)(2,1)S(1)}, bf16[256,512]{1,0:T(8,128)(2,1)S(1)}, u32[]{:S(2)}, u32[]{:S(2)}) %collective-permute-start.11) | collective-permute-done | bytes 262176 | tf_op jit(solution)/shard_map/ppermute | solution.py:91
  39.3 1.6 %collective-permute-start.9 = (bf16[256,512]{1,0:T(8,128)(2,1)S(1)}, bf16[256,512]{1,0:T(8,128)(2,1)S(1)}, u32[]{:S(2)}, u32[]{:S(2)}) collective-permute-start(bf16[256,512]{1,0:T(8,128)(2,1)S(1)} %collective-permute-done.2.refs_9_), channel_id=1, source_target_pairs={{0,4},{1,5},{2,6},{3,7},{4,8},{5,9},{6,10},{7,11},{8,12},{9,13},{1... | collective-permute-start | bytes 786440 | tf_op jit(solution)/shard_map/ppermute | solution.py:91
  40.9 0.5 collective-permute-start.8
  41.4 0.2 collective-permute-done.10.refs_10_
  41.6 1.5 %collective-permute-start.7 = (bf16[256,512]{1,0:T(8,128)(2,1)S(1)}, bf16[256,512]{1,0:T(8,128)(2,1)S(1)}, u32[]{:S(2)}, u32[]{:S(2)}) collective-permute-start(bf16[256,512]{1,0:T(8,128)(2,1)S(1)} %collective-permute-done.2.refs_9_), channel_id=1, source_target_pairs={{0,16},{1,17},{2,18},{3,19},{4,20},{5,21},{6,22},{7,23},{8,24},{9,... | collective-permute-start | bytes 786440 | tf_op jit(solution)/shard_map/ppermute | solution.py:91
  43.1 1.5 %collective-permute-start.21 = (bf16[256,512]{1,0:T(8,128)(2,1)S(1)}, bf16[256,512]{1,0:T(8,128)(2,1)S(1)}, u32[]{:S(2)}, u32[]{:S(2)}) collective-permute-start(bf16[256,512]{1,0:T(8,128)(2,1)S(1)} %collective-permute-done.3.refs_10_), channel_id=1, source_target_pairs={{0,2},{1,3},{2,0},{3,1},{4,6},{5,7},{6,4},{7,5},{8,10},{9,11},{10,... | collective-permute-start | bytes 786440 | tf_op jit(solution)/shard_map/ppermute | solution.py:91
  44.6 5.4 %multiply.6 = (f32[256,512]{1,0:T(8,128)S(1)}, bf16[256,8192]{1,0:T(8,128)(2,1)}) custom-call(s32[4]{0:T(128)S(1)} %pad_add_fusion.place_ref.refs_0_, bf16[256,8192]{1,0:T(8,128)(2,1)S(1)} %copy-done.1, bf16[64,8192]{1,0:T(8,128)(2,1)S(1)} %bitcast.8, bf16[256,512]{1,0:T(8,128)(2,1)S(1)} %copy-done.4, ...), custom_call_target="tpu_custom_call", output_to_operand_aliasing={{1}: (6, {})} | custom-call | flops 1 | bytes 1 | tf_op jit(solution)/shard_map/multiply/pallas_call | solution.py:405
  50.0 0.2 collective-permute-done.8.refs_8_
  50.2 0.6 add_y.1
  50.9 0.5 collective-permute-start.28
  51.5 3.5 %collective-permute-done.21.refs_11_ = bf16[256,512]{1,0:T(8,128)(2,1)S(1)} collective-permute-done((bf16[256,512]{1,0:T(8,128)(2,1)S(1)}, bf16[256,512]{1,0:T(8,128)(2,1)S(1)}, u32[]{:S(2)}, u32[]{:S(2)}) %collective-permute-start.21) | collective-permute-done | bytes 262176 | tf_op jit(solution)/shard_map/ppermute | solution.py:91
  55.0 2.2 %collective-permute-done.22.a_ref = bf16[64,768]{1,0:T(8,128)(2,1)S(1)} collective-permute-done((bf16[64,768]{1,0:T(8,128)(2,1)S(1)}, bf16[64,768]{1,0:T(8,128)(2,1)S(1)}, u32[]{:S(2)}, u32[]{:S(2)}) %collective-permute-start.22) | collective-permute-done | bytes 98336 | tf_op jit(solution)/shard_map/ppermute | solution.py:91
  57.2 0.7 collective-permute-start.23
  58.0 4.9 %collective-permute-done.23.b_ref = bf16[64,768]{1,0:T(8,128)(2,1)S(1)} collective-permute-done((bf16[64,768]{1,0:T(8,128)(2,1)S(1)}, bf16[64,768]{1,0:T(8,128)(2,1)S(1)}, u32[]{:S(2)}, u32[]{:S(2)}) %collective-permute-start.23) | collective-permute-done | bytes 98336 | tf_op jit(solution)/shard_map/ppermute | solution.py:91
  62.9 1.3 %collective-permute-start.17 = (bf16[256,512]{1,0:T(8,128)(2,1)S(1)}, bf16[256,512]{1,0:T(8,128)(2,1)S(1)}, u32[]{:S(2)}, u32[]{:S(2)}) collective-permute-start(bf16[256,512]{1,0:T(8,128)(2,1)S(1)} %collective-permute-done.8.refs_8_), channel_id=1, source_target_pairs={{0,16},{1,17},{2,18},{3,19},{4,20},{5,21},{6,22},{7,23},{8,24},{9,... | collective-permute-start | bytes 786440 | tf_op jit(solution)/shard_map/ppermute | solution.py:91
  64.2 0.4 collective-permute-start.20
  64.7 1.5 %collective-permute-start.19 = (bf16[256,512]{1,0:T(8,128)(2,1)S(1)}, bf16[256,512]{1,0:T(8,128)(2,1)S(1)}, u32[]{:S(2)}, u32[]{:S(2)}) collective-permute-start(bf16[256,512]{1,0:T(8,128)(2,1)S(1)} %collective-permute-done.9.refs_9_), channel_id=1, source_target_pairs={{0,2},{1,3},{2,0},{3,1},{4,6},{5,7},{6,4},{7,5},{8,10},{9,11},{10,... | collective-permute-start | bytes 786440 | tf_op jit(solution)/shard_map/ppermute | solution.py:91
  66.2 0.5 collective-permute-start.18
  66.7 1.8 %collective-permute-start.24 = (bf16[64,768]{1,0:T(8,128)(2,1)S(1)}, bf16[64,768]{1,0:T(8,128)(2,1)S(1)}, u32[]{:S(2)}, u32[]{:S(2)}) collective-permute-start(bf16[64,768]{1,0:T(8,128)(2,1)S(1)} %get-tuple-element.79), channel_id=1, source_target_pairs={{0,12},{1,13},{2,14},{3,15},{4,0},{5,1},{6,2},{7,3},{8,4},{9,5},{1... | collective-permute-start | bytes 294920 | tf_op jit(solution)/shard_map/ppermute | solution.py:91
  68.6 6.4 %multiply.7 = (f32[256,512]{1,0:T(8,128)S(1)}, bf16[256,8192]{1,0:T(8,128)(2,1)}) custom-call(s32[4]{0:T(128)S(1)} %pad_add_fusion.place_ref.refs_0_, bf16[256,8192]{1,0:T(8,128)(2,1)S(1)} %copy-done.1, bf16[64,8192]{1,0:T(8,128)(2,1)S(1)} %bitcast.9, bf16[256,512]{1,0:T(8,128)(2,1)S(1)} %copy-done.4, ...), custom_call_target="tpu_custom_call", output_to_operand_aliasing={{1}: (6, {})} | custom-call | flops 1 | bytes 1 | tf_op jit(solution)/shard_map/multiply/pallas_call | solution.py:405
  75.0 2.2 %collective-permute-done.18.refs_8_ = bf16[256,512]{1,0:T(8,128)(2,1)S(1)} collective-permute-done((bf16[256,512]{1,0:T(8,128)(2,1)S(1)}, bf16[256,512]{1,0:T(8,128)(2,1)S(1)}, u32[]{:S(2)}, u32[]{:S(2)}) %collective-permute-start.18) | collective-permute-done | bytes 262176 | tf_op jit(solution)/shard_map/ppermute | solution.py:91
  77.2 0.7 add_z.1
  77.9 0.5 collective-permute-start.30
  78.4 0.5 collective-permute-start.32
  79.0 0.2 collective-permute-done.35.came_ref
  79.2 0.3 collective-permute-start.34
  79.5 3.7 %multiply.8 = (f32[256,512]{1,0:T(8,128)S(1)}, bf16[256,8192]{1,0:T(8,128)(2,1)}) custom-call(s32[4]{0:T(128)S(1)} %pad_add_fusion.place_ref.refs_0_, bf16[256,8192]{1,0:T(8,128)(2,1)S(1)} %copy-done.1, bf16[64,8192]{1,0:T(8,128)(2,1)S(1)} %bitcast.10, bf16[256,512]{1,0:T(8,128)(2,1)S(1)} %copy-done.4, ...), custom_call_target="tpu_custom_call", output_to_operand_aliasing={{1}: (6, {})} | custom-call | flops 1 | bytes 1 | tf_op jit(solution)/shard_map/multiply/pallas_call | solution.py:405
  83.2 1.2 %join_cores.1 = f32[64,512]{1,0:T(8,128)} custom-call(s32[4]{0:T(128)S(1)} %pad_add_fusion.place_ref.refs_0_, f32[64,256]{1,0:T(8,128)S(1)} %get-tuple-element.103.own_ref, f32[64,256]{1,0:T(8,128)S(1)} %collective-permute-done.35.came_ref), custom_call_target="tpu_custom_call" | custom-call | flops 1 | bytes 1 | tf_op jit(solution)/shard_map/join_cores/pallas_call | solution.py:316
  84.4 4.7 %multiply.9 = (bf16[256,512]{1,0:T(8,128)(2,1)}, bf16[256,8192]{1,0:T(8,128)(2,1)}) custom-call(s32[4]{0:T(128)S(1)} %pad_add_fusion.place_ref.refs_0_, bf16[256,8192]{1,0:T(8,128)(2,1)S(1)} %copy-done.1, bf16[64,8192]{1,0:T(8,128)(2,1)S(1)} %bitcast.11, bf16[256,512]{1,0:T(8,128)(2,1)S(1)} %copy-done.4, ...), custom_call_target="tpu_custom_call", output_to_operand_aliasing={{1}: (6, {})} | custom-call | flops 1 | bytes 1 | tf_op jit(solution)/shard_map/multiply/pallas_call | solution.py:405
  (52 shorter events, 0.6 us)
Async XLA Ops:
  0.6 10.2 %copy-start.7 = (f32[4,4]{1,0:T(4,128)S(1)}, f32[4,4]{1,0:T(4,128)}, u32[]{:S(2)}) copy-start(f32[4,4]{1,0:T(4,128)} %scales_ref.1) | copy-start | bytes 196
  0.7 2.2 %copy-start = (bf16[256,8192]{1,0:T(8,128)(2,1)S(1)}, bf16[256,8192]{1,0:T(8,128)(2,1)}, u32[]{:S(2)}) copy-start(bf16[256,8192]{1,0:T(8,128)(2,1)} %refs_1_.9) | copy-start | bytes 12582916
  2.9 1.2 %copy-start.2 = (bf16[8192,64]{0,1:T(8,128)(2,1)S(1)}, bf16[8192,64]{0,1:T(8,128)(2,1)}, u32[]{:S(2)}) copy-start(bf16[8192,64]{0,1:T(8,128)(2,1)} %param.9) | copy-start | bytes 3145732
  4.1 0.9 %copy-start.3 = (bf16[256,512]{1,0:T(8,128)(2,1)S(1)}, bf16[256,512]{1,0:T(8,128)(2,1)}, u32[]{:S(2)}) copy-start(bf16[256,512]{1,0:T(8,128)(2,1)} %refs_3_.9) | copy-start | bytes 786436
  5.1 0.8 copy-start.6
  5.9 4.9 %copy-start.5 = (bf16[512,512]{1,0:T(8,128)(2,1)S(1)}, bf16[512,512]{1,0:T(8,128)(2,1)}, u32[]{:S(2)}) copy-start(bf16[512,512]{1,0:T(8,128)(2,1)} %codes_ref.1) | copy-start | bytes 1572868
  5.9 12.8 %copy-start.1 = (bf16[256,8192]{1,0:T(8,128)(2,1)S(1)}, bf16[256,8192]{1,0:T(8,128)(2,1)}, u32[]{:S(2)}) copy-start(bf16[256,8192]{1,0:T(8,128)(2,1)} %refs_1_.9) | copy-start | bytes 12582916
  5.9 12.8 %copy-start.4 = (bf16[256,512]{1,0:T(8,128)(2,1)S(1)}, bf16[256,512]{1,0:T(8,128)(2,1)}, u32[]{:S(2)}) copy-start(bf16[256,512]{1,0:T(8,128)(2,1)} %refs_3_.9) | copy-start | bytes 786436
  10.1 11.6 %collective-permute-start.4 = (f32[64,4352]{1,0:T(8,128)S(1)}, f32[64,4352]{1,0:T(8,128)S(1)}, u32[]{:S(2)}, u32[]{:S(2)}) collective-permute-start(f32[64,4352]{1,0:T(8,128)S(1)} %get-tuple-element.58), channel_id=1, source_target_pairs={{0,1},{1,0},{2,3},{3,2},{4,5},{5,4},{6,7},{7,6},{8,9},{9,8},{10,11... | collective-permute-start | bytes 3342344 | tf_op jit(solution)/shard_map/ppermute | solution.py:91
  11.5 6.6 %collective-permute-start.6 = (bf16[256,512]{1,0:T(8,128)(2,1)S(1)}, bf16[256,512]{1,0:T(8,128)(2,1)S(1)}, u32[]{:S(2)}, u32[]{:S(2)}) collective-permute-start(bf16[256,512]{1,0:T(8,128)(2,1)S(1)} %get-tuple-element.56.refs_6_), channel_id=1, source_target_pairs={{0,1},{1,0},{2,3},{3,2},{4,5},{5,4},{6,7},{7,6},{8,9},{9,8},{10,11... | collective-permute-start | bytes 786440 | tf_op jit(solution)/shard_map/ppermute | solution.py:91
  11.6 6.6 %collective-permute-start.5 = (bf16[256,512]{1,0:T(8,128)(2,1)S(1)}, bf16[256,512]{1,0:T(8,128)(2,1)S(1)}, u32[]{:S(2)}, u32[]{:S(2)}) collective-permute-start(bf16[256,512]{1,0:T(8,128)(2,1)S(1)} %get-tuple-element.55.refs_5_), channel_id=1, source_target_pairs={{0,1},{1,0},{2,3},{3,2},{4,5},{5,4},{6,7},{7,6},{8,9},{9,8},{10,11... | collective-permute-start | bytes 786440 | tf_op jit(solution)/shard_map/ppermute | solution.py:91
  12.1 9.8 %collective-permute-start.1 = (bf16[256,512]{1,0:T(8,128)(2,1)S(1)}, bf16[256,512]{1,0:T(8,128)(2,1)S(1)}, u32[]{:S(2)}, u32[]{:S(2)}) collective-permute-start(bf16[256,512]{1,0:T(8,128)(2,1)S(1)} %get-tuple-element.56.refs_6_), channel_id=1, source_target_pairs={{0,2},{1,3},{2,0},{3,1},{4,6},{5,7},{6,4},{7,5},{8,10},{9,11},{10,... | collective-permute-start | bytes 786440 | tf_op jit(solution)/shard_map/ppermute | solution.py:91
  14.5 10.3 %collective-permute-start.3 = (bf16[256,512]{1,0:T(8,128)(2,1)S(1)}, bf16[256,512]{1,0:T(8,128)(2,1)S(1)}, u32[]{:S(2)}, u32[]{:S(2)}) collective-permute-start(bf16[256,512]{1,0:T(8,128)(2,1)S(1)} %get-tuple-element.55.refs_5_), channel_id=1, source_target_pairs={{0,12},{1,13},{2,14},{3,15},{4,0},{5,1},{6,2},{7,3},{8,4},{9,5},{1... | collective-permute-start | bytes 786440 | tf_op jit(solution)/shard_map/ppermute | solution.py:91
  18.1 12.4 %collective-permute-start.2 = (bf16[256,512]{1,0:T(8,128)(2,1)S(1)}, bf16[256,512]{1,0:T(8,128)(2,1)S(1)}, u32[]{:S(2)}, u32[]{:S(2)}) collective-permute-start(bf16[256,512]{1,0:T(8,128)(2,1)S(1)} %get-tuple-element.55.refs_5_), channel_id=1, source_target_pairs={{0,4},{1,5},{2,6},{3,7},{4,8},{5,9},{6,10},{7,11},{8,12},{9,13},{1... | collective-permute-start | bytes 786440 | tf_op jit(solution)/shard_map/ppermute | solution.py:91
  18.1 12.4 %collective-permute-start = (bf16[256,512]{1,0:T(8,128)(2,1)S(1)}, bf16[256,512]{1,0:T(8,128)(2,1)S(1)}, u32[]{:S(2)}, u32[]{:S(2)}) collective-permute-start(bf16[256,512]{1,0:T(8,128)(2,1)S(1)} %get-tuple-element.55.refs_5_), channel_id=1, source_target_pairs={{0,2},{1,3},{2,0},{3,1},{4,6},{5,7},{6,4},{7,5},{8,10},{9,11},{10,... | collective-permute-start | bytes 786440 | tf_op jit(solution)/shard_map/ppermute | solution.py:91
  30.5 3.8 %collective-permute-start.13 = (bf16[256,512]{1,0:T(8,128)(2,1)S(1)}, bf16[256,512]{1,0:T(8,128)(2,1)S(1)}, u32[]{:S(2)}, u32[]{:S(2)}) collective-permute-start(bf16[256,512]{1,0:T(8,128)(2,1)S(1)} %collective-permute-done.refs_7_), channel_id=1, source_target_pairs={{0,1},{1,0},{2,3},{3,2},{4,5},{5,4},{6,7},{7,6},{8,9},{9,8},{10,11... | collective-permute-start | bytes 786440 | tf_op jit(solution)/shard_map/ppermute | solution.py:91
  30.5 4.0 %collective-permute-start.14 = (bf16[256,512]{1,0:T(8,128)(2,1)S(1)}, bf16[256,512]{1,0:T(8,128)(2,1)S(1)}, u32[]{:S(2)}, u32[]{:S(2)}) collective-permute-start(bf16[256,512]{1,0:T(8,128)(2,1)S(1)} %collective-permute-done.1.refs_8_), channel_id=1, source_target_pairs={{0,1},{1,0},{2,3},{3,2},{4,5},{5,4},{6,7},{7,6},{8,9},{9,8},{10,11... | collective-permute-start | bytes 786440 | tf_op jit(solution)/shard_map/ppermute | solution.py:91
  31.1 8.2 %collective-permute-start.11 = (bf16[256,512]{1,0:T(8,128)(2,1)S(1)}, bf16[256,512]{1,0:T(8,128)(2,1)S(1)}, u32[]{:S(2)}, u32[]{:S(2)}) collective-permute-start(bf16[256,512]{1,0:T(8,128)(2,1)S(1)} %collective-permute-done.1.refs_8_), channel_id=1, source_target_pairs={{0,12},{1,13},{2,14},{3,15},{4,0},{5,1},{6,2},{7,3},{8,4},{9,5},{1... | collective-permute-start | bytes 786440 | tf_op jit(solution)/shard_map/ppermute | solution.py:91
  32.9 8.0 %collective-permute-start.16 = (bf16[256,512]{1,0:T(8,128)(2,1)S(1)}, bf16[256,512]{1,0:T(8,128)(2,1)S(1)}, u32[]{:S(2)}, u32[]{:S(2)}) collective-permute-start(bf16[256,512]{1,0:T(8,128)(2,1)S(1)} %collective-permute-done.3.refs_10_), channel_id=1, source_target_pairs={{0,1},{1,0},{2,3},{3,2},{4,5},{5,4},{6,7},{7,6},{8,9},{9,8},{10,11... | collective-permute-start | bytes 786440 | tf_op jit(solution)/shard_map/ppermute | solution.py:91
  32.9 8.7 %collective-permute-start.10 = (bf16[256,512]{1,0:T(8,128)(2,1)S(1)}, bf16[256,512]{1,0:T(8,128)(2,1)S(1)}, u32[]{:S(2)}, u32[]{:S(2)}) collective-permute-start(bf16[256,512]{1,0:T(8,128)(2,1)S(1)} %collective-permute-done.3.refs_10_), channel_id=1, source_target_pairs={{0,16},{1,17},{2,18},{3,19},{4,20},{5,21},{6,22},{7,23},{8,24},{9,... | collective-permute-start | bytes 786440 | tf_op jit(solution)/shard_map/ppermute | solution.py:91
  34.4 8.7 %collective-permute-start.15 = (bf16[256,512]{1,0:T(8,128)(2,1)S(1)}, bf16[256,512]{1,0:T(8,128)(2,1)S(1)}, u32[]{:S(2)}, u32[]{:S(2)}) collective-permute-start(bf16[256,512]{1,0:T(8,128)(2,1)S(1)} %collective-permute-done.2.refs_9_), channel_id=1, source_target_pairs={{0,1},{1,0},{2,3},{3,2},{4,5},{5,4},{6,7},{7,6},{8,9},{9,8},{10,11... | collective-permute-start | bytes 786440 | tf_op jit(solution)/shard_map/ppermute | solution.py:91
  34.6 15.6 %collective-permute-start.12 = (bf16[64,2304]{1,0:T(8,128)(2,1)S(1)}, bf16[64,2304]{1,0:T(8,128)(2,1)S(1)}, u32[]{:S(2)}, u32[]{:S(2)}) collective-permute-start(bf16[64,2304]{1,0:T(8,128)(2,1)S(1)} %get-tuple-element.66.sent_ref), channel_id=1, source_target_pairs={{0,2},{1,3},{2,0},{3,1},{4,6},{5,7},{6,4},{7,5},{8,10},{9,11},{10,... | collective-permute-start | bytes 884744 | tf_op jit(solution)/shard_map/ppermute | solution.py:91
  39.3 10.7 %collective-permute-start.9 = (bf16[256,512]{1,0:T(8,128)(2,1)S(1)}, bf16[256,512]{1,0:T(8,128)(2,1)S(1)}, u32[]{:S(2)}, u32[]{:S(2)}) collective-permute-start(bf16[256,512]{1,0:T(8,128)(2,1)S(1)} %collective-permute-done.2.refs_9_), channel_id=1, source_target_pairs={{0,4},{1,5},{2,6},{3,7},{4,8},{5,9},{6,10},{7,11},{8,12},{9,13},{1... | collective-permute-start | bytes 786440 | tf_op jit(solution)/shard_map/ppermute | solution.py:91
  40.9 9.2 %collective-permute-start.8 = (bf16[256,512]{1,0:T(8,128)(2,1)S(1)}, bf16[256,512]{1,0:T(8,128)(2,1)S(1)}, u32[]{:S(2)}, u32[]{:S(2)}) collective-permute-start(bf16[256,512]{1,0:T(8,128)(2,1)S(1)} %collective-permute-done.2.refs_9_), channel_id=1, source_target_pairs={{0,2},{1,3},{2,0},{3,1},{4,6},{5,7},{6,4},{7,5},{8,10},{9,11},{10,... | collective-permute-start | bytes 786440 | tf_op jit(solution)/shard_map/ppermute | solution.py:91
  41.6 8.6 %collective-permute-start.7 = (bf16[256,512]{1,0:T(8,128)(2,1)S(1)}, bf16[256,512]{1,0:T(8,128)(2,1)S(1)}, u32[]{:S(2)}, u32[]{:S(2)}) collective-permute-start(bf16[256,512]{1,0:T(8,128)(2,1)S(1)} %collective-permute-done.2.refs_9_), channel_id=1, source_target_pairs={{0,16},{1,17},{2,18},{3,19},{4,20},{5,21},{6,22},{7,23},{8,24},{9,... | collective-permute-start | bytes 786440 | tf_op jit(solution)/shard_map/ppermute | solution.py:91
  43.1 11.9 %collective-permute-start.21 = (bf16[256,512]{1,0:T(8,128)(2,1)S(1)}, bf16[256,512]{1,0:T(8,128)(2,1)S(1)}, u32[]{:S(2)}, u32[]{:S(2)}) collective-permute-start(bf16[256,512]{1,0:T(8,128)(2,1)S(1)} %collective-permute-done.3.refs_10_), channel_id=1, source_target_pairs={{0,2},{1,3},{2,0},{3,1},{4,6},{5,7},{6,4},{7,5},{8,10},{9,11},{10,... | collective-permute-start | bytes 786440 | tf_op jit(solution)/shard_map/ppermute | solution.py:91
  50.8 6.5 %collective-permute-start.22 = (bf16[64,768]{1,0:T(8,128)(2,1)S(1)}, bf16[64,768]{1,0:T(8,128)(2,1)S(1)}, u32[]{:S(2)}, u32[]{:S(2)}) collective-permute-start(bf16[64,768]{1,0:T(8,128)(2,1)S(1)} %get-tuple-element.77), channel_id=1, source_target_pairs={{0,4},{1,5},{2,6},{3,7},{4,8},{5,9},{6,10},{7,11},{8,12},{9,13},{1... | collective-permute-start | bytes 294920 | tf_op jit(solution)/shard_map/ppermute | solution.py:91
  50.9 12.0 %collective-permute-start.25 = (bf16[256,512]{1,0:T(8,128)(2,1)S(1)}, bf16[256,512]{1,0:T(8,128)(2,1)S(1)}, u32[]{:S(2)}, u32[]{:S(2)}) collective-permute-start(bf16[256,512]{1,0:T(8,128)(2,1)S(1)} %collective-permute-done.7.refs_7_), channel_id=1, source_target_pairs={{0,1},{1,0},{2,3},{3,2},{4,5},{5,4},{6,7},{7,6},{8,9},{9,8},{10,11... | collective-permute-start | bytes 786440 | tf_op jit(solution)/shard_map/ppermute | solution.py:91
  50.9 13.3 %collective-permute-start.28 = (bf16[256,512]{1,0:T(8,128)(2,1)S(1)}, bf16[256,512]{1,0:T(8,128)(2,1)S(1)}, u32[]{:S(2)}, u32[]{:S(2)}) collective-permute-start(bf16[256,512]{1,0:T(8,128)(2,1)S(1)} %collective-permute-done.10.refs_10_), channel_id=1, source_target_pairs={{0,1},{1,0},{2,3},{3,2},{4,5},{5,4},{6,7},{7,6},{8,9},{9,8},{10,11... | collective-permute-start | bytes 786440 | tf_op jit(solution)/shard_map/ppermute | solution.py:91
  51.4 13.2 %collective-permute-start.26 = (bf16[256,512]{1,0:T(8,128)(2,1)S(1)}, bf16[256,512]{1,0:T(8,128)(2,1)S(1)}, u32[]{:S(2)}, u32[]{:S(2)}) collective-permute-start(bf16[256,512]{1,0:T(8,128)(2,1)S(1)} %collective-permute-done.8.refs_8_), channel_id=1, source_target_pairs={{0,1},{1,0},{2,3},{3,2},{4,5},{5,4},{6,7},{7,6},{8,9},{9,8},{10,11... | collective-permute-start | bytes 786440 | tf_op jit(solution)/shard_map/ppermute | solution.py:91
  55.0 11.2 %collective-permute-start.29 = (bf16[256,512]{1,0:T(8,128)(2,1)S(1)}, bf16[256,512]{1,0:T(8,128)(2,1)S(1)}, u32[]{:S(2)}, u32[]{:S(2)}) collective-permute-start(bf16[256,512]{1,0:T(8,128)(2,1)S(1)} %collective-permute-done.11.refs_11_), channel_id=1, source_target_pairs={{0,1},{1,0},{2,3},{3,2},{4,5},{5,4},{6,7},{7,6},{8,9},{9,8},{10,11... | collective-permute-start | bytes 786440 | tf_op jit(solution)/shard_map/ppermute | solution.py:91
  57.2 5.7 %collective-permute-start.23 = (bf16[64,768]{1,0:T(8,128)(2,1)S(1)}, bf16[64,768]{1,0:T(8,128)(2,1)S(1)}, u32[]{:S(2)}, u32[]{:S(2)}) collective-permute-start(bf16[64,768]{1,0:T(8,128)(2,1)S(1)} %get-tuple-element.78), channel_id=1, source_target_pairs={{0,8},{1,9},{2,10},{3,11},{4,12},{5,13},{6,14},{7,15},{8,0},{9,1},... | collective-permute-start | bytes 294920 | tf_op jit(solution)/shard_map/ppermute | solution.py:91
  62.9 3.8 %collective-permute-start.27 = (bf16[256,512]{1,0:T(8,128)(2,1)S(1)}, bf16[256,512]{1,0:T(8,128)(2,1)S(1)}, u32[]{:S(2)}, u32[]{:S(2)}) collective-permute-start(bf16[256,512]{1,0:T(8,128)(2,1)S(1)} %collective-permute-done.9.refs_9_), channel_id=1, source_target_pairs={{0,1},{1,0},{2,3},{3,2},{4,5},{5,4},{6,7},{7,6},{8,9},{9,8},{10,11... | collective-permute-start | bytes 786440 | tf_op jit(solution)/shard_map/ppermute | solution.py:91
  62.9 12.1 %collective-permute-start.17 = (bf16[256,512]{1,0:T(8,128)(2,1)S(1)}, bf16[256,512]{1,0:T(8,128)(2,1)S(1)}, u32[]{:S(2)}, u32[]{:S(2)}) collective-permute-start(bf16[256,512]{1,0:T(8,128)(2,1)S(1)} %collective-permute-done.8.refs_8_), channel_id=1, source_target_pairs={{0,16},{1,17},{2,18},{3,19},{4,20},{5,21},{6,22},{7,23},{8,24},{9,... | collective-permute-start | bytes 786440 | tf_op jit(solution)/shard_map/ppermute | solution.py:91
  64.2 10.8 %collective-permute-start.20 = (bf16[256,512]{1,0:T(8,128)(2,1)S(1)}, bf16[256,512]{1,0:T(8,128)(2,1)S(1)}, u32[]{:S(2)}, u32[]{:S(2)}) collective-permute-start(bf16[256,512]{1,0:T(8,128)(2,1)S(1)} %collective-permute-done.11.refs_11_), channel_id=1, source_target_pairs={{0,12},{1,13},{2,14},{3,15},{4,0},{5,1},{6,2},{7,3},{8,4},{9,5},{1... | collective-permute-start | bytes 786440 | tf_op jit(solution)/shard_map/ppermute | solution.py:91
  64.7 10.4 %collective-permute-start.19 = (bf16[256,512]{1,0:T(8,128)(2,1)S(1)}, bf16[256,512]{1,0:T(8,128)(2,1)S(1)}, u32[]{:S(2)}, u32[]{:S(2)}) collective-permute-start(bf16[256,512]{1,0:T(8,128)(2,1)S(1)} %collective-permute-done.9.refs_9_), channel_id=1, source_target_pairs={{0,2},{1,3},{2,0},{3,1},{4,6},{5,7},{6,4},{7,5},{8,10},{9,11},{10,... | collective-permute-start | bytes 786440 | tf_op jit(solution)/shard_map/ppermute | solution.py:91
  66.2 11.1 %collective-permute-start.18 = (bf16[256,512]{1,0:T(8,128)(2,1)S(1)}, bf16[256,512]{1,0:T(8,128)(2,1)S(1)}, u32[]{:S(2)}, u32[]{:S(2)}) collective-permute-start(bf16[256,512]{1,0:T(8,128)(2,1)S(1)} %collective-permute-done.9.refs_9_), channel_id=1, source_target_pairs={{0,16},{1,17},{2,18},{3,19},{4,20},{5,21},{6,22},{7,23},{8,24},{9,... | collective-permute-start | bytes 786440 | tf_op jit(solution)/shard_map/ppermute | solution.py:91
  66.7 8.3 %collective-permute-start.24 = (bf16[64,768]{1,0:T(8,128)(2,1)S(1)}, bf16[64,768]{1,0:T(8,128)(2,1)S(1)}, u32[]{:S(2)}, u32[]{:S(2)}) collective-permute-start(bf16[64,768]{1,0:T(8,128)(2,1)S(1)} %get-tuple-element.79), channel_id=1, source_target_pairs={{0,12},{1,13},{2,14},{3,15},{4,0},{5,1},{6,2},{7,3},{8,4},{9,5},{1... | collective-permute-start | bytes 294920 | tf_op jit(solution)/shard_map/ppermute | solution.py:91
  77.9 1.3 %collective-permute-start.35 = (f32[64,256]{1,0:T(8,128)S(1)}, f32[64,256]{1,0:T(8,128)S(1)}, u32[]{:S(2)}, u32[]{:S(2)}) collective-permute-start(f32[64,256]{1,0:T(8,128)S(1)} %get-tuple-element.103.own_ref), channel_id=1, source_target_pairs={{0,1},{1,0},{2,3},{3,2},{4,5},{5,4},{6,7},{7,6},{8,9},{9,8},{10,11... | collective-permute-start | bytes 196616 | tf_op jit(solution)/shard_map/ppermute | solution.py:91
  77.9 6.5 %collective-permute-start.30 = (bf16[256,512]{1,0:T(8,128)(2,1)S(1)}, bf16[256,512]{1,0:T(8,128)(2,1)S(1)}, u32[]{:S(2)}, u32[]{:S(2)}) collective-permute-start(bf16[256,512]{1,0:T(8,128)(2,1)S(1)} %collective-permute-done.17.refs_7_), channel_id=1, source_target_pairs={{0,1},{1,0},{2,3},{3,2},{4,5},{5,4},{6,7},{7,6},{8,9},{9,8},{10,11... | collective-permute-start | bytes 786440 | tf_op jit(solution)/shard_map/ppermute | solution.py:91
  78.4 6.0 %collective-permute-start.31 = (bf16[256,512]{1,0:T(8,128)(2,1)S(1)}, bf16[256,512]{1,0:T(8,128)(2,1)S(1)}, u32[]{:S(2)}, u32[]{:S(2)}) collective-permute-start(bf16[256,512]{1,0:T(8,128)(2,1)S(1)} %collective-permute-done.18.refs_8_), channel_id=1, source_target_pairs={{0,1},{1,0},{2,3},{3,2},{4,5},{5,4},{6,7},{7,6},{8,9},{9,8},{10,11... | collective-permute-start | bytes 786440 | tf_op jit(solution)/shard_map/ppermute | solution.py:91
  78.4 6.0 %collective-permute-start.32 = (bf16[256,512]{1,0:T(8,128)(2,1)S(1)}, bf16[256,512]{1,0:T(8,128)(2,1)S(1)}, u32[]{:S(2)}, u32[]{:S(2)}) collective-permute-start(bf16[256,512]{1,0:T(8,128)(2,1)S(1)} %collective-permute-done.19.refs_9_), channel_id=1, source_target_pairs={{0,1},{1,0},{2,3},{3,2},{4,5},{5,4},{6,7},{7,6},{8,9},{9,8},{10,11... | collective-permute-start | bytes 786440 | tf_op jit(solution)/shard_map/ppermute | solution.py:91
  78.9 5.5 %collective-permute-start.33 = (bf16[256,512]{1,0:T(8,128)(2,1)S(1)}, bf16[256,512]{1,0:T(8,128)(2,1)S(1)}, u32[]{:S(2)}, u32[]{:S(2)}) collective-permute-start(bf16[256,512]{1,0:T(8,128)(2,1)S(1)} %collective-permute-done.20.refs_10_), channel_id=1, source_target_pairs={{0,1},{1,0},{2,3},{3,2},{4,5},{5,4},{6,7},{7,6},{8,9},{9,8},{10,11... | collective-permute-start | bytes 786440 | tf_op jit(solution)/shard_map/ppermute | solution.py:91
  79.2 5.2 %collective-permute-start.34 = (bf16[256,512]{1,0:T(8,128)(2,1)S(1)}, bf16[256,512]{1,0:T(8,128)(2,1)S(1)}, u32[]{:S(2)}, u32[]{:S(2)}) collective-permute-start(bf16[256,512]{1,0:T(8,128)(2,1)S(1)} %collective-permute-done.21.refs_11_), channel_id=1, source_target_pairs={{0,1},{1,0},{2,3},{3,2},{4,5},{5,4},{6,7},{7,6},{8,9},{9,8},{10,11... | collective-permute-start | bytes 786440 | tf_op jit(solution)/shard_map/ppermute | solution.py:91

commit v2 on v1

v2 whole, which is shorter than its diff:
```python
import math

import jax
import jax.numpy as jnp
from jax import lax
from jax.experimental import pallas as pl
from jax.experimental.pallas import tpu as pltpu
from jax.sharding import PartitionSpec as P

BLOCK = 128
AXES = ("groups", "fsdp")

lowrank_scale = 0.5


def weight_transpose(left, right):
    return lax.dot_general(
        left, right, (((1,), (1,)), ((), ())), preferred_element_type=jnp.float32
    )


def leading(left, right):
    return lax.dot_general(
        left, right, (((0,), (0,)), ((), ())), preferred_element_type=jnp.float32
    )


def dequantize(quant_codes, block_scales):
    spread_scales = jnp.repeat(jnp.repeat(block_scales, BLOCK, axis=0), BLOCK, axis=1)
    return (quant_codes.astype(jnp.float32) * spread_scales).astype(jnp.bfloat16)


def per_device_general(
    activations, quant_codes, block_scales, lowrank_down_factor, lowrank_up_factor, cotangent
):
    value_weight = dequantize(quant_codes, block_scales)
    lowrank_hidden = jnp.dot(
        activations, lowrank_down_factor, preferred_element_type=jnp.float32
    ).astype(jnp.bfloat16)
    lowrank_update = lowrank_scale * jnp.dot(
        lowrank_hidden, lowrank_up_factor, preferred_element_type=jnp.float32
    )
    hidden_gradient = weight_transpose(cotangent, lowrank_up_factor).astype(jnp.bfloat16)
    gathered = lax.all_gather(value_weight, "fsdp", axis=0, tiled=True)
    projected = (
        lowrank_update + jnp.dot(activations, gathered, preferred_element_type=jnp.float32)
    ).astype(jnp.bfloat16)
    input_gradient = (
        weight_transpose(cotangent, gathered)
        + lowrank_scale * weight_transpose(hidden_gradient, lowrank_down_factor)
    ).astype(jnp.bfloat16)
    scaling_factor = lowrank_scale / math.sqrt(activations.shape[0] * lax.axis_size("fsdp"))
    grad_down = lax.psum_scatter(
        scaling_factor * leading(activations, hidden_gradient),
        "fsdp",
        scatter_dimension=0,
        tiled=True,
    )
    grad_up = lax.psum(scaling_factor * leading(lowrank_hidden, cotangent), "fsdp")
    return (projected, input_gradient, grad_down, grad_up)


NZ = 4
VMEM_LIMIT = 40 * 1024 * 1024


def pairs_of(move):
    found = []
    for g in range(2):
        for z in range(NZ):
            for y in range(2):
                for c in range(2):
                    to = move(g, z, y, c)
                    found.append((index_of(g, z, y, c), index_of(*to)))
    return found


def index_of(g, z, y, c):
    return ((g * NZ + z) * 2 + y) * 2 + c


OVER_CORE = pairs_of(lambda g, z, y, c: (g, z, y, 1 - c))
OVER_Y = pairs_of(lambda g, z, y, c: (g, z, 1 - y, c))
OVER_X = pairs_of(lambda g, z, y, c: (1 - g, z, y, c))
Z_UP = pairs_of(lambda g, z, y, c: (g, (z + 1) % NZ, y, c))
Z_DOWN = pairs_of(lambda g, z, y, c: (g, (z - 1) % NZ, y, c))
Z_FAR = pairs_of(lambda g, z, y, c: (g, (z + 2) % NZ, y, c))


def send(array, pairs):
    return lax.ppermute(array, AXES, pairs)


def whole():
    return pl.BlockSpec(memory_space=pltpu.VMEM)


def scalars():
    return pl.BlockSpec(memory_space=pltpu.SMEM)


def anywhere():
    return pl.BlockSpec(memory_space=pl.ANY)


def params():
    return pltpu.CompilerParams(vmem_limit_bytes=VMEM_LIMIT)


LITTLE = pl.CostEstimate(flops=1, bytes_accessed=1, transcendentals=0)


def dequantize_shard(place, quant_codes, block_scales):
    rows, columns = quant_codes.shape
    half = rows // 2

    def kernel(place_ref, codes_ref, scales_ref, own_ref, first_ref):
        g = place_ref[0]
        for i in range(rows // BLOCK):
            source = lax.rem(g * (half // BLOCK) + i, rows // BLOCK)
            start = pl.multiple_of(source * BLOCK, BLOCK)
            for j in range(columns // BLOCK):
                at = slice(j * BLOCK, (j + 1) * BLOCK)
                block = codes_ref[pl.ds(start, BLOCK), at].astype(jnp.float32)
                block = (block * scales_ref[source, j]).astype(jnp.bfloat16)
                own_ref[i * BLOCK : (i + 1) * BLOCK, at] = block
                if i < half // BLOCK:
                    first_ref[i * BLOCK : (i + 1) * BLOCK, at] = block

    return pl.pallas_call(
        kernel,
        out_shape=[
            jax.ShapeDtypeStruct((rows, columns), jnp.bfloat16),
            jax.ShapeDtypeStruct((half, columns), jnp.bfloat16),
        ],
        in_specs=[scalars(), whole(), scalars()],
        out_specs=[whole()] * 2,
        compiler_params=params(),
        cost_estimate=LITTLE,
        name="dequantize",
    )(place, quant_codes, block_scales)


def local_gradients(place, activations, down_t, up, cotangent):
    tokens, width = activations.shape
    rank, features = up.shape
    chips = NZ * 2
    chunk = width // chips
    part = chunk // 2
    up_part = features // 2
    packed = chips * part + up_part

    def kernel(
        place_ref, act_ref, down_ref, up_ref, cot_ref, latent_ref, lgrad_ref, own_ref, away_ref,
        total, lgrad_t,
    ):
        step = pl.program_id(0)
        y, c = place_ref[2], place_ref[3]

        @pl.when(step == 0)
        def _():
            total[...] = jnp.zeros_like(total)
            held = weight_transpose(cot_ref[...], up_ref[...]).astype(jnp.bfloat16)
            lgrad_ref[...] = held
            lgrad_t[...] = weight_transpose(up_ref[...], cot_ref[...]).astype(jnp.bfloat16)

        block = act_ref[...]
        total[...] += weight_transpose(block, down_ref[...])
        term = jnp.dot(lgrad_t[...], block, preferred_element_type=jnp.float32)
        z_of, y_of = step // 2, step % 2
        here = jnp.where(y_of == y, NZ, 0) + z_of
        at = pl.ds(pl.multiple_of(here * part, part), part)

        @pl.when(c == 0)
        def _():
            own_ref[:, at] = term[:, :part]
            away_ref[:, at] = term[:, part:]

        @pl.when(c == 1)
        def _():
            own_ref[:, at] = term[:, part:]
            away_ref[:, at] = term[:, :part]

        @pl.when(step == chips - 1)
        def _():
            latent = total[...].astype(jnp.bfloat16)
            latent_ref[...] = latent
            both = leading(latent, cot_ref[...])

            @pl.when(c == 0)
            def _():
                own_ref[:, chips * part :] = both[:, :up_part]
                away_ref[:, chips * part :] = both[:, up_part:]

            @pl.when(c == 1)
            def _():
                own_ref[:, chips * part :] = both[:, up_part:]
                away_ref[:, chips * part :] = both[:, :up_part]

    fixed = lambda shape: pl.BlockSpec(shape, lambda i: (0,) * len(shape))
    return pl.pallas_call(
        kernel,
        grid=(chips,),
        out_shape=[
            jax.ShapeDtypeStruct((tokens, rank), jnp.bfloat16),
            jax.ShapeDtypeStruct((tokens, rank), jnp.bfloat16),
            jax.ShapeDtypeStruct((rank, packed), jnp.float32),
            jax.ShapeDtypeStruct((rank, packed), jnp.float32),
        ],
        in_specs=[
            scalars(),
            pl.BlockSpec((tokens, chunk), lambda i: (0, i)),
            pl.BlockSpec((rank, chunk), lambda i: (0, i)),
            fixed((rank, features)),
            fixed((tokens, features)),
        ],
        out_specs=[
            fixed((tokens, rank)),
            fixed((tokens, rank)),
            fixed((rank, packed)),
            fixed((rank, packed)),
        ],
        scratch_shapes=[
            pltpu.VMEM((tokens, rank), jnp.float32),
            pltpu.VMEM((rank, tokens), jnp.bfloat16),
        ],
        compiler_params=params(),
        cost_estimate=LITTLE,
        name="local_gradients",
    )(place, activations, down_t, up, cotangent)


def fold(array):
    rank = array.shape[0]
    return jnp.concatenate([array[: rank // 2], array[rank // 2 :]], axis=1)


def add_cores(own, came, up_part):
    rank, packed = own.shape
    part = (packed - up_part) // (2 * NZ)
    half = NZ * part

    def kernel(own_ref, came_ref, message_ref, kept_ref):
        for z in range(NZ):
            at = slice(z * part, (z + 1) * part)
            message_ref[z * rank : (z + 1) * rank, :] = (
                own_ref[:, at] + came_ref[:, at]
            ).astype(jnp.bfloat16)
        kept_ref[...] = own_ref[:, half : 2 * half] + came_ref[:, half : 2 * half]
        message_ref[NZ * rank :, :] = fold(
            own_ref[:, 2 * half :] + came_ref[:, 2 * half :]
        ).astype(jnp.bfloat16)

    return pl.pallas_call(
        kernel,
        out_shape=[
            jax.ShapeDtypeStruct((NZ * rank + rank // 2, part), jnp.bfloat16),
            jax.ShapeDtypeStruct((rank, half), jnp.float32),
        ],
        in_specs=[whole()] * 2,
        out_specs=[whole()] * 2,
        compiler_params=params(),
        cost_estimate=LITTLE,
        name="add_cores",
    )(own, came)


def add_y(place, kept, sent, came, came_from):
    rank, half = kept.shape
    part = half // NZ
    rows = rank + rank // 2

    def kernel(place_ref, kept_ref, sent_ref, came_ref, own_ref, up_ref, far_ref, down_ref):
        z = place_ref[1]
        tail = sent_ref[NZ * rank :, :].astype(jnp.float32) + came_ref[
            came_from + NZ * rank :, :
        ].astype(jnp.float32)
        for shift, out_ref in ((0, own_ref), (1, up_ref), (2, far_ref), (3, down_ref)):
            to = lax.rem(z + shift, NZ)
            kept_at = pl.ds(pl.multiple_of(to * part, part), part)
            came_at = pl.ds(pl.multiple_of(came_from + to * rank, rank), rank)
            summed = kept_ref[:, kept_at] + came_ref[came_at, :].astype(jnp.float32)
            out_ref[:rank, :] = summed.astype(out_ref.dtype)
            out_ref[rank:, :] = tail.astype(jnp.bfloat16).astype(out_ref.dtype)

    return pl.pallas_call(
        kernel,
        out_shape=[jax.ShapeDtypeStruct((rows, part), jnp.float32)]
        + [jax.ShapeDtypeStruct((rows, part), jnp.bfloat16)] * 3,
        in_specs=[scalars()] + [whole()] * 3,
        out_specs=[whole()] * 4,
        compiler_params=params(),
        cost_estimate=LITTLE,
        name="add_y",
    )(place, kept, sent, came)


def add_z(own, from_down, from_far, from_up, up_from, factor):
    rows, part = own.shape
    rank = rows * 2 // 3

    def kernel(own_ref, a_ref, b_ref, c_ref, gd_ref, gu_ref):
        f32 = jnp.float32
        summed = (own_ref[...] + b_ref[...].astype(f32)) + (
            a_ref[...].astype(f32) + c_ref[up_from : up_from + rows, :].astype(f32)
        )
        summed = summed * factor
        gd_ref[...] = summed[:rank, :]
        gu_ref[...] = summed[rank:, :]

    return pl.pallas_call(
        kernel,
        out_shape=[
            jax.ShapeDtypeStruct((rank, part), jnp.float32),
            jax.ShapeDtypeStruct((rows - rank, part), jnp.float32),
        ],
        in_specs=[whole()] * 4,
        out_specs=[whole()] * 2,
        compiler_params=params(),
        cost_estimate=LITTLE,
        name="add_z",
    )(own, from_down, from_far, from_up)


def join_cores(place, own, came):
    half, folded = own.shape
    width = folded // 2

    def kernel(place_ref, own_ref, came_ref, out_ref):
        c = place_ref[3]
        for ref, core in ((own_ref, c), (came_ref, 1 - c)):
            at = pl.ds(pl.multiple_of(core * width, width), width)
            out_ref[:half, at] = ref[:, :width]
            out_ref[half:, at] = ref[:, width:]

    return pl.pallas_call(
        kernel,
        out_shape=jax.ShapeDtypeStruct((2 * half, folded), jnp.float32),
        in_specs=[scalars(), whole(), whole()],
        out_specs=whole(),
        compiler_params=params(),
        cost_estimate=LITTLE,
        name="join_cores",
    )(place, own, came)


def multiply(place, pieces, activations, down_t, cotangent, lgrad, total, gradient, finish=None):
    tokens, width = activations.shape
    features = cotangent.shape[1]
    arrays = []
    for array, _, _ in pieces:
        if not any(array is other for other in arrays):
            arrays.append(array)
    where = [next(i for i, a in enumerate(arrays) if a is array) for array, _, _ in pieces]
    count = len(pieces)
    started = total is not None
    rows = width // (NZ * 2 * 2 * 2)

    def kernel(*refs):
        refs = list(refs)
        place_ref, act_ref, down_ref, cot_ref, lgrad_ref = refs[:5]
        del refs[:5]
        if started:
            total_ref = refs.pop(0)
            refs.pop(0)
        if finish is not None:
            latent_ref, up_ref = refs.pop(0), refs.pop(0)
        array_refs = refs[: len(arrays)]
        del refs[: len(arrays)]
        out_ref, grad_ref, sums, grads, out_sems = refs
        g, z, y, c = (place_ref[i] for i in range(4))
        if finish is not None:
            sums[...] = total_ref[...] + lowrank_scale * jnp.dot(
                latent_ref[...], up_ref[...], preferred_element_type=jnp.float32
            )
        elif started:
            sums[...] = total_ref[...]
        else:
            sums[...] = jnp.zeros_like(sums)
        going = []
        for p, (_, first, (dz, dy, dc, dh)) in enumerate(pieces):
            chip = lax.rem(z + (NZ - dz), NZ) * 2 + (1 - y if dy else y)
            device = chip * 2 + (1 - c if dc else c)
            start = (device * 2 + (1 - g if dh else g)) * rows
            at = pl.ds(pl.multiple_of(start, rows), rows)
            weight = array_refs[where[p]][first : first + rows, :]
            sums[...] += jnp.dot(act_ref[:, at], weight, preferred_element_type=jnp.float32)
            grads[p] = (
                weight_transpose(cot_ref[...], weight)
                + lowrank_scale
                * jnp.dot(lgrad_ref[...], down_ref[:, at], preferred_element_type=jnp.float32)
            ).astype(jnp.bfloat16)
            copy = pltpu.make_async_copy(grads.at[p], grad_ref.at[:, at], out_sems.at[p])
            copy.start()
            going.append(copy)
        out_ref[...] = sums[...].astype(out_ref.dtype)
        for copy in going:
            copy.wait()

    operands = [place, activations, down_t, cotangent, lgrad]
    specs = [scalars()] + [whole()] * 4
    aliases = {}
    if started:
        operands += [total, gradient]
        specs += [whole(), anywhere()]
        aliases = {6: 1}
    if finish is not None:
        operands += list(finish)
        specs += [whole(), whole()]
    operands += arrays
    specs += [whole()] * len(arrays)
    out_type = jnp.float32 if finish is None else jnp.bfloat16
    return pl.pallas_call(
        kernel,
        out_shape=[
            jax.ShapeDtypeStruct((tokens, features), out_type),
            jax.ShapeDtypeStruct((tokens, width), jnp.bfloat16),
        ],
        in_specs=specs,
        out_specs=[whole(), anywhere()],
        scratch_shapes=[
            pltpu.VMEM((tokens, features), jnp.float32),
            pltpu.VMEM((count, tokens, rows), jnp.bfloat16),
            pltpu.SemaphoreType.DMA((count,)),
        ],
        input_output_aliases=aliases,
        compiler_params=params(),
        cost_estimate=LITTLE,
        name="multiply",
    )(*operands)


def per_device(
    activations, quant_codes, block_scales, lowrank_down_factor, lowrank_up_factor, cotangent
):
    g = lax.axis_index("groups")
    f = lax.axis_index("fsdp")
    place = jnp.stack([g, f >> 2, (f >> 1) & 1, f & 1]).astype(jnp.int32)
    half = quant_codes.shape[0] // 2
    up_part = lowrank_up_factor.shape[1] // 2
    down_t = lowrank_down_factor.T
    factor = lowrank_scale / math.sqrt(activations.shape[0] * lax.axis_size("fsdp"))
    barrier = lax.optimization_barrier
    join = lambda *arrays: jnp.concatenate(arrays, axis=0)

    def products(pieces, total, gradient, finish=None):
        return multiply(
            place, pieces, activations, down_t, cotangent, lgrad, total, gradient, finish
        )

    def listed(array, dc, *keys):
        return [(array, i * half, (dz, dy, dc, dh)) for i, (dz, dy, dh) in enumerate(keys)]

    own, first = dequantize_shard(place, quant_codes, block_scales)
    own, first, place = barrier((own, first, place))

    y1, up1, down1 = send(own, OVER_Y), send(first, Z_UP), send(first, Z_DOWN)
    swap1 = send(own, OVER_CORE)
    latent, lgrad, own_terms, away_terms = local_gradients(
        place, activations, down_t, lowrank_up_factor, cotangent
    )
    came = send(away_terms, OVER_CORE)
    own_keys = [(0, 0, 0), (0, 0, 1)]
    total, gradient = products(
        listed(own, 0, *own_keys) + listed(swap1, 1, *own_keys), None, None
    )
    terms_y, kept = add_cores(own_terms, came, up_part)
    y1, up1, down1, terms_y, kept, total, gradient = barrier(
        (y1, up1, down1, terms_y, kept, total, gradient)
    )

    y2, x2 = send(join(up1, terms_y), OVER_Y), send(join(up1, down1), OVER_X)
    up2, down2 = send(up1, Z_UP), send(y1[half:], Z_DOWN)
    swap2 = send(join(up1, down1, y1), OVER_CORE)
    keys = [(1, 0, 0), (3, 0, 0), (0, 1, 0), (0, 1, 1)]
    total, gradient = products(
        listed(up1, 0, keys[0])
        + listed(down1, 0, keys[1])
        + listed(y1, 0, *keys[2:])
        + listed(swap2, 1, *keys),
        total, gradient,
    )
    y2, x2, up2, down2, total, gradient = barrier((y2, x2, up2, down2, total, gradient))

    own_part, to_up, to_far, to_down = add_y(place, kept, terms_y, y2, half)
    y3, x3 = send(join(down1, up2), OVER_Y), send(join(up2, y2[:half]), OVER_X)
    down3, up3 = send(join(down2, to_down), Z_DOWN), send(to_up, Z_UP)
    swap3 = send(join(y2[:half], x2, up2, down2), OVER_CORE)
    swap3, to_far = barrier((swap3, to_far))
    far3 = send(to_far, Z_FAR)
    keys = [(1, 1, 0), (1, 0, 1), (3, 0, 1), (2, 0, 0), (3, 1, 1)]
    total, gradient = products(
        listed(y2, 0, keys[0])
        + listed(x2, 0, *keys[1:3])
        + listed(up2, 0, keys[3])
        + listed(down2, 0, keys[4])
        + listed(swap3, 1, *keys),
        total, gradient,
    )
    y3, x3, down3, up3, far3, total, gradient = barrier(
        (y3, x3, down3, up3, far3, total, gradient)
    )

    swap4 = send(join(y3, x3, down3[:half]), OVER_CORE)
    grad_down_t, up_own = add_z(own_part, up3, far3, down3, half, factor)
    up_came = send(up_own, OVER_CORE)
    keys = [(3, 1, 0), (2, 1, 0), (2, 0, 1), (1, 1, 1), (2, 1, 1)]
    total, gradient = products(
        listed(y3, 0, *keys[:2]) + listed(x3, 0, *keys[2:4]) + listed(down3, 0, keys[4]),
        total, gradient,
    )
    projected, gradient = products(
        listed(swap4, 1, *keys), total, gradient, finish=(latent, lowrank_up_factor)
    )
    grad_up = join_cores(place, up_own, up_came)
    return (projected, gradient, grad_down_t.T, grad_up)


def solution(mesh):
    in_specs = (
        P(("groups", "fsdp"), None),
        P("fsdp", None),
        P("fsdp", None),
        P("groups", None),
        P("groups", None),
        P(("groups", "fsdp"), None),
    )
    out_specs = (
        P(("groups", "fsdp"), None),
        P(("groups", "fsdp"), None),
        P(("groups", "fsdp"), None),
        P("groups", None),
    )
    small = mesh.shape["groups"] == 2 and mesh.shape["fsdp"] == NZ * 4
    return jax.shard_map(
        per_device if small else per_device_general,
        mesh=mesh,
        in_specs=in_specs,
        out_specs=out_specs,
        check_vma=False,
    )
```

time: 89.5 us -> 77 us (0.86)
  Pallas kernels: 30.7 us -> 21 us
  starting transfers between devices: 27 us -> 18.3 us
  waiting for transfers between devices: 25.3 us -> 29 us
  local copies, waits for them, and re-layouts: 5.22 us -> 6.98 us
    pallas_call x5, Pallas kernels: 23.2 us -> 13.5 us  [multiply(): pl.pallas_call(kernel, out_shape=[jax.ShapeDtypeStruct((tokens, features)...]
    ppermute x36 -> x18, starting transfers between devices: 27 us -> 18.3 us  [send(): return lax.ppermute(array, AXES, pairs)]
    ppermute x36 -> x18, waiting for transfers between devices: 25.3 us -> 29 us  [send(): return lax.ppermute(array, AXES, pairs)]
    unnamed x16 -> x18, local copies, waits for them, and re-layouts: 5.22 us -> 6.93 us
  transfers between devices with their start and end apart: 36 -> 18, of which waited for: 10 -> 6; matrix products, arithmetic and copies ran while one was open for 0% -> 0% of each run, Pallas kernels for 24% -> 17%
where the time goes in v2:
time: 77 us; the launch traced here: 76.6 us
  waiting for transfers between devices  29 us (38%)
  Pallas kernels  21 us (27%)
  starting transfers between devices  18.3 us (24%)
  local copies, waits for them, and re-layouts  6.98 us (9%)
  between operations  0.84 us (1%)
    ppermute x18, waiting for transfers between devices, send(): return lax.ppermute(array, AXES, pairs)  29 us
    ppermute x18, starting transfers between devices, send(): return lax.ppermute(array, AXES, pairs)  18.3 us
    pallas_call x5, Pallas kernels, multiply(): pl.pallas_call(kernel, out_shape=[jax.ShapeDtypeStruct((tokens, features)...  13.5 us
    unnamed x18, local copies, waits for them, and re-layouts  6.93 us
    pallas_call x1, Pallas kernels, local_gradients(): pl.pallas_call(kernel, grid=(chips,), out_shape=[jax.ShapeDtypeStruct((to...  4.19 us
  transfers between devices with their start and end apart: 18, of which 6 were waited for; matrix products, arithmetic and copies ran while one was open for 0% of the time, Pallas kernels for 17%

profile of v2, /device:TPU:0, one launch (start us, length us, event | category | flops | bytes accessed | tf_op | source)
XLA Modules:
  0.0 76.6 jit_solution(6797538646338835113)
XLA Ops:
  0.6 0.1 pad_add_fusion.place_ref.refs_0_
  0.7 1.0 %copy-done.5 = bf16[512,512]{1,0:T(8,128)(2,1)S(1)} copy-done((bf16[512,512]{1,0:T(8,128)(2,1)S(1)}, bf16[512,512]{1,0:T(8,128)(2,1)}, u32[]{:S(2)}) %copy-start.5) | copy-done | bytes 524312
  1.8 0.7 copy-done.8
  2.4 0.7 dequantize.1
  3.1 0.0 copy-start
  3.2 2.2 %copy-done = bf16[256,8192]{1,0:T(8,128)(2,1)S(1)} copy-done((bf16[256,8192]{1,0:T(8,128)(2,1)S(1)}, bf16[256,8192]{1,0:T(8,128)(2,1)}, u32[]{:S(2)}) %copy-start) | copy-done | bytes 4194328
  5.3 1.2 %copy-done.2 = bf16[8192,64]{0,1:T(8,128)(2,1)S(1)} copy-done((bf16[8192,64]{0,1:T(8,128)(2,1)S(1)}, bf16[8192,64]{0,1:T(8,128)(2,1)}, u32[]{:S(2)}) %copy-start.2) | copy-done | bytes 1048600
  6.6 0.9 %copy-done.3 = bf16[256,512]{1,0:T(8,128)(2,1)S(1)} copy-done((bf16[256,512]{1,0:T(8,128)(2,1)S(1)}, bf16[256,512]{1,0:T(8,128)(2,1)}, u32[]{:S(2)}) %copy-start.3) | copy-done | bytes 262168
  7.5 0.8 %copy-done.6 = bf16[64,512]{1,0:T(8,128)(2,1)S(1)} copy-done((bf16[64,512]{1,0:T(8,128)(2,1)S(1)}, bf16[64,512]{1,0:T(8,128)(2,1)}, u32[]{:S(2)}) %copy-start.6) | copy-done | bytes 65560
  8.4 4.2 %local_gradients.1 = (bf16[256,64]{1,0:T(8,128)(2,1)S(1)}, bf16[256,64]{1,0:T(8,128)(2,1)S(1)}, f32[64,4352]{1,0:T(8,128)S(1)}, f32[64,4352]{1,0:T(8,128)S(1)}) custom-call(s32[4]{0:T(128)S(1)} %pad_add_fusion.place_ref.refs_0_, bf16[256,8192]{1,0:T(8,128)(2,1)S(1)} %copy-done, bf16[64,8192]{1,0:T(8,128)(2,1)S(1)} %bitcast.6, bf16[64,512]{1,0:T(8,128)(2,1)S(1)} %copy-done.6, ...), custom_call_target="tpu_custom_call" | custom-call | flops 1 | bytes 1 | tf_op jit(solution)/shard_map/local_gradients/pallas_call | solution.py:201
  12.6 0.7 collective-permute-start.3
  13.2 0.1 collective-permute-start.4
  13.3 2.8 %collective-permute-start = (bf16[512,512]{1,0:T(8,128)(2,1)S(1)}, bf16[512,512]{1,0:T(8,128)(2,1)S(1)}, u32[]{:S(2)}, u32[]{:S(2)}) collective-permute-start(bf16[512,512]{1,0:T(8,128)(2,1)S(1)} %get-tuple-element.57.refs_5_), channel_id=1, source_target_pairs={{0,2},{1,3},{2,0},{3,1},{4,6},{5,7},{6,4},{7,5},{8,10},{9,11},{10,... | collective-permute-start | bytes 1572872 | tf_op jit(solution)/shard_map/ppermute | solution.py:91
  16.1 1.6 %collective-permute-start.1 = (bf16[256,512]{1,0:T(8,128)(2,1)S(1)}, bf16[256,512]{1,0:T(8,128)(2,1)S(1)}, u32[]{:S(2)}, u32[]{:S(2)}) collective-permute-start(bf16[256,512]{1,0:T(8,128)(2,1)S(1)} %get-tuple-element.58), channel_id=1, source_target_pairs={{0,4},{1,5},{2,6},{3,7},{4,8},{5,9},{6,10},{7,11},{8,12},{9,13},{1... | collective-permute-start | bytes 786440 | tf_op jit(solution)/shard_map/ppermute | solution.py:91
  17.7 2.3 %collective-permute-start.2 = (bf16[256,512]{1,0:T(8,128)(2,1)S(1)}, bf16[256,512]{1,0:T(8,128)(2,1)S(1)}, u32[]{:S(2)}, u32[]{:S(2)}) collective-permute-start(bf16[256,512]{1,0:T(8,128)(2,1)S(1)} %get-tuple-element.58), channel_id=1, source_target_pairs={{0,12},{1,13},{2,14},{3,15},{4,0},{5,1},{6,2},{7,3},{8,4},{9,5},{1... | collective-permute-start | bytes 786440 | tf_op jit(solution)/shard_map/ppermute | solution.py:91
  19.9 0.0 collective-permute-done.4.refs_6_
  19.9 2.1 %multiply.5 = (f32[256,512]{1,0:T(8,128)S(1)}, bf16[256,8192]{1,0:T(8,128)(2,1)}) custom-call(s32[4]{0:T(128)S(1)} %pad_add_fusion.place_ref.refs_0_, bf16[256,8192]{1,0:T(8,128)(2,1)S(1)} %copy-done, bf16[64,8192]{1,0:T(8,128)(2,1)S(1)} %bitcast.7, bf16[256,512]{1,0:T(8,128)(2,1)S(1)} %copy-done.4, bf16[256,64]{1,0:T(8,128)(2,1)S(1)} %get-tuple-element.56.refs_4_, ...), custom_call_target="tpu_custom_call" | custom-call | flops 1 | bytes 1 | tf_op jit(solution)/shard_map/multiply/pallas_call | solution.py:413
  22.0 0.0 collective-permute-done.3.came_ref
  22.1 0.1 add_cores.1
  22.2 5.0 %collective-permute-done.1.refs_7_ = bf16[256,512]{1,0:T(8,128)(2,1)S(1)} collective-permute-done((bf16[256,512]{1,0:T(8,128)(2,1)S(1)}, bf16[256,512]{1,0:T(8,128)(2,1)S(1)}, u32[]{:S(2)}, u32[]{:S(2)}) %collective-permute-start.1) | collective-permute-done | bytes 262176 | tf_op jit(solution)/shard_map/ppermute | solution.py:91
  27.1 3.9 %collective-permute-done.2.refs_8_ = bf16[256,512]{1,0:T(8,128)(2,1)S(1)} collective-permute-done((bf16[256,512]{1,0:T(8,128)(2,1)S(1)}, bf16[256,512]{1,0:T(8,128)(2,1)S(1)}, u32[]{:S(2)}, u32[]{:S(2)}) %collective-permute-start.2) | collective-permute-done | bytes 262176 | tf_op jit(solution)/shard_map/ppermute | solution.py:91
  31.0 0.1 pad_maximum_fusion.2
  31.1 0.1 collective-permute-start.9
  31.2 0.6 collective-permute-start.5
  31.8 1.6 %collective-permute-start.6 = (bf16[512,512]{1,0:T(8,128)(2,1)S(1)}, bf16[512,512]{1,0:T(8,128)(2,1)S(1)}, u32[]{:S(2)}, u32[]{:S(2)}) collective-permute-start(bf16[512,512]{1,0:T(8,128)(2,1)S(1)} %pad_maximum_fusion.4), channel_id=1, source_target_pairs={{0,16},{1,17},{2,18},{3,19},{4,20},{5,21},{6,22},{7,23},{8,24},{9,... | collective-permute-start | bytes 1572872 | tf_op jit(solution)/shard_map/ppermute | solution.py:91
  33.4 2.4 %collective-permute-start.8 = (bf16[256,512]{1,0:T(8,128)(2,1)S(1)}, bf16[256,512]{1,0:T(8,128)(2,1)S(1)}, u32[]{:S(2)}, u32[]{:S(2)}) collective-permute-start(bf16[256,512]{1,0:T(8,128)(2,1)S(1)} %slice.10), channel_id=1, source_target_pairs={{0,12},{1,13},{2,14},{3,15},{4,0},{5,1},{6,2},{7,3},{8,4},{9,5},{1... | collective-permute-start | bytes 786440 | tf_op jit(solution)/shard_map/ppermute | solution.py:91
  35.8 2.9 %multiply.6 = (f32[256,512]{1,0:T(8,128)S(1)}, bf16[256,8192]{1,0:T(8,128)(2,1)}) custom-call(s32[4]{0:T(128)S(1)} %pad_add_fusion.place_ref.refs_0_, bf16[256,8192]{1,0:T(8,128)(2,1)S(1)} %copy-done.1, bf16[64,8192]{1,0:T(8,128)(2,1)S(1)} %bitcast.8, bf16[256,512]{1,0:T(8,128)(2,1)S(1)} %copy-done.4, ...), custom_call_target="tpu_custom_call", output_to_operand_aliasing={{1}: (6, {})} | custom-call | flops 1 | bytes 1 | tf_op jit(solution)/shard_map/multiply/pallas_call | solution.py:413
  38.7 3.8 %collective-permute-done.8.refs_10_ = bf16[256,512]{1,0:T(8,128)(2,1)S(1)} collective-permute-done((bf16[256,512]{1,0:T(8,128)(2,1)S(1)}, bf16[256,512]{1,0:T(8,128)(2,1)S(1)}, u32[]{:S(2)}, u32[]{:S(2)}) %collective-permute-start.8) | collective-permute-done | bytes 262176 | tf_op jit(solution)/shard_map/ppermute | solution.py:91
  42.5 5.5 %collective-permute-done.7.refs_9_ = bf16[256,512]{1,0:T(8,128)(2,1)S(1)} collective-permute-done((bf16[256,512]{1,0:T(8,128)(2,1)S(1)}, bf16[256,512]{1,0:T(8,128)(2,1)S(1)}, u32[]{:S(2)}, u32[]{:S(2)}) %collective-permute-start.7) | collective-permute-done | bytes 262176 | tf_op jit(solution)/shard_map/ppermute | solution.py:91
  48.0 0.1 pad_maximum_fusion
  48.1 0.1 collective-permute-start.14
  48.2 0.1 pad_maximum_fusion.6
  48.2 1.6 %collective-permute-start.10 = (bf16[512,512]{1,0:T(8,128)(2,1)S(1)}, bf16[512,512]{1,0:T(8,128)(2,1)S(1)}, u32[]{:S(2)}, u32[]{:S(2)}) collective-permute-start(bf16[512,512]{1,0:T(8,128)(2,1)S(1)} %get-tuple-element.103), channel_id=1, source_target_pairs={{0,2},{1,3},{2,0},{3,1},{4,6},{5,7},{6,4},{7,5},{8,10},{9,11},{10,... | collective-permute-start | bytes 1572872 | tf_op jit(solution)/shard_map/ppermute | solution.py:91
  49.8 0.5 collective-permute-start.11
  50.4 0.6 add_y.1
  51.0 1.8 %collective-permute-start.12 = (bf16[352,512]{1,0:T(8,128)(2,1)S(1)}, bf16[352,512]{1,0:T(8,128)(2,1)S(1)}, u32[]{:S(2)}, u32[]{:S(2)}) collective-permute-start(bf16[352,512]{1,0:T(8,128)(2,1)S(1)} %pad_maximum_fusion.7), channel_id=1, source_target_pairs={{0,12},{1,13},{2,14},{3,15},{4,0},{5,1},{6,2},{7,3},{8,4},{9,5},{1... | collective-permute-start | bytes 1081352 | tf_op jit(solution)/shard_map/ppermute | solution.py:91
  52.8 0.3 collective-permute-start.13
  53.1 1.6 %collective-permute-start.15 = (bf16[96,512]{1,0:T(8,128)(2,1)S(1)}, bf16[96,512]{1,0:T(8,128)(2,1)S(1)}, u32[]{:S(2)}, u32[]{:S(2)}) collective-permute-start(bf16[96,512]{1,0:T(8,128)(2,1)S(1)} %get-tuple-element.81), channel_id=1, source_target_pairs={{0,8},{1,9},{2,10},{3,11},{4,12},{5,13},{6,14},{7,15},{8,0},{9,1},... | collective-permute-start | bytes 294920 | tf_op jit(solution)/shard_map/ppermute | solution.py:91
  54.7 3.2 %multiply.7 = (f32[256,512]{1,0:T(8,128)S(1)}, bf16[256,8192]{1,0:T(8,128)(2,1)}) custom-call(s32[4]{0:T(128)S(1)} %pad_add_fusion.place_ref.refs_0_, bf16[256,8192]{1,0:T(8,128)(2,1)S(1)} %copy-done.1, bf16[64,8192]{1,0:T(8,128)(2,1)S(1)} %bitcast.9, bf16[256,512]{1,0:T(8,128)(2,1)S(1)} %copy-done.4, ...), custom_call_target="tpu_custom_call", output_to_operand_aliasing={{1}: (6, {})} | custom-call | flops 1 | bytes 1 | tf_op jit(solution)/shard_map/multiply/pallas_call | solution.py:413
  57.9 7.7 %collective-permute-done.13.a_ref = bf16[96,512]{1,0:T(8,128)(2,1)S(1)} collective-permute-done((bf16[96,512]{1,0:T(8,128)(2,1)S(1)}, bf16[96,512]{1,0:T(8,128)(2,1)S(1)}, u32[]{:S(2)}, u32[]{:S(2)}) %collective-permute-start.13) | collective-permute-done | bytes 98336 | tf_op jit(solution)/shard_map/ppermute | solution.py:91
  65.6 3.1 %collective-permute-done.15.b_ref = bf16[96,512]{1,0:T(8,128)(2,1)S(1)} collective-permute-done((bf16[96,512]{1,0:T(8,128)(2,1)S(1)}, bf16[96,512]{1,0:T(8,128)(2,1)S(1)}, u32[]{:S(2)}, u32[]{:S(2)}) %collective-permute-start.15) | collective-permute-done | bytes 98336 | tf_op jit(solution)/shard_map/ppermute | solution.py:91
  68.7 0.1 pad_maximum_fusion.1
  68.8 0.1 collective-permute-start.16
  68.9 0.7 add_z.1
  69.6 0.5 collective-permute-start.17
  70.1 2.3 %multiply.8 = (f32[256,512]{1,0:T(8,128)S(1)}, bf16[256,8192]{1,0:T(8,128)(2,1)}) custom-call(s32[4]{0:T(128)S(1)} %pad_add_fusion.place_ref.refs_0_, bf16[256,8192]{1,0:T(8,128)(2,1)S(1)} %copy-done.1, bf16[64,8192]{1,0:T(8,128)(2,1)S(1)} %bitcast.10, bf16[256,512]{1,0:T(8,128)(2,1)S(1)} %copy-done.4, ...), custom_call_target="tpu_custom_call", output_to_operand_aliasing={{1}: (6, {})} | custom-call | flops 1 | bytes 1 | tf_op jit(solution)/shard_map/multiply/pallas_call | solution.py:413
  72.4 1.2 %join_cores.1 = f32[64,512]{1,0:T(8,128)} custom-call(s32[4]{0:T(128)S(1)} %pad_add_fusion.place_ref.refs_0_, f32[32,512]{1,0:T(8,128)S(1)} %get-tuple-element.101.own_ref, f32[32,512]{1,0:T(8,128)S(1)} %collective-permute-done.17.came_ref), custom_call_target="tpu_custom_call" | custom-call | flops 1 | bytes 1 | tf_op jit(solution)/shard_map/join_cores/pallas_call | solution.py:336
  73.6 3.0 %multiply.9 = (bf16[256,512]{1,0:T(8,128)(2,1)}, bf16[256,8192]{1,0:T(8,128)(2,1)}) custom-call(s32[4]{0:T(128)S(1)} %pad_add_fusion.place_ref.refs_0_, bf16[256,8192]{1,0:T(8,128)(2,1)S(1)} %copy-done.1, bf16[64,8192]{1,0:T(8,128)(2,1)S(1)} %bitcast.11, bf16[256,512]{1,0:T(8,128)(2,1)S(1)} %copy-done.4, ...), custom_call_target="tpu_custom_call", output_to_operand_aliasing={{1}: (6, {})} | custom-call | flops 1 | bytes 1 | tf_op jit(solution)/shard_map/multiply/pallas_call | solution.py:413
  (28 shorter events, 0.2 us)
Async XLA Ops:
  0.7 1.0 %copy-start.5 = (bf16[512,512]{1,0:T(8,128)(2,1)S(1)}, bf16[512,512]{1,0:T(8,128)(2,1)}, u32[]{:S(2)}) copy-start(bf16[512,512]{1,0:T(8,128)(2,1)} %codes_ref.1) | copy-start | bytes 1572868
  1.8 0.7 copy-start.8
  3.1 2.2 %copy-start = (bf16[256,8192]{1,0:T(8,128)(2,1)S(1)}, bf16[256,8192]{1,0:T(8,128)(2,1)}, u32[]{:S(2)}) copy-start(bf16[256,8192]{1,0:T(8,128)(2,1)} %refs_1_.9) | copy-start | bytes 12582916
  5.3 1.2 %copy-start.2 = (bf16[8192,64]{0,1:T(8,128)(2,1)S(1)}, bf16[8192,64]{0,1:T(8,128)(2,1)}, u32[]{:S(2)}) copy-start(bf16[8192,64]{0,1:T(8,128)(2,1)} %param.9) | copy-start | bytes 3145732
  6.6 0.9 %copy-start.3 = (bf16[256,512]{1,0:T(8,128)(2,1)S(1)}, bf16[256,512]{1,0:T(8,128)(2,1)}, u32[]{:S(2)}) copy-start(bf16[256,512]{1,0:T(8,128)(2,1)} %refs_3_.9) | copy-start | bytes 786436
  7.5 0.8 %copy-start.6 = (bf16[64,512]{1,0:T(8,128)(2,1)S(1)}, bf16[64,512]{1,0:T(8,128)(2,1)}, u32[]{:S(2)}) copy-start(bf16[64,512]{1,0:T(8,128)(2,1)} %refs_8_.1) | copy-start | bytes 196612
  8.4 11.6 %copy-start.4 = (bf16[256,512]{1,0:T(8,128)(2,1)S(1)}, bf16[256,512]{1,0:T(8,128)(2,1)}, u32[]{:S(2)}) copy-start(bf16[256,512]{1,0:T(8,128)(2,1)} %refs_3_.9) | copy-start | bytes 786436
  12.6 9.5 %collective-permute-start.3 = (f32[64,4352]{1,0:T(8,128)S(1)}, f32[64,4352]{1,0:T(8,128)S(1)}, u32[]{:S(2)}, u32[]{:S(2)}) collective-permute-start(f32[64,4352]{1,0:T(8,128)S(1)} %get-tuple-element.60), channel_id=1, source_target_pairs={{0,1},{1,0},{2,3},{3,2},{4,5},{5,4},{6,7},{7,6},{8,9},{9,8},{10,11... | collective-permute-start | bytes 3342344 | tf_op jit(solution)/shard_map/ppermute | solution.py:91
  13.2 6.7 %collective-permute-start.4 = (bf16[512,512]{1,0:T(8,128)(2,1)S(1)}, bf16[512,512]{1,0:T(8,128)(2,1)S(1)}, u32[]{:S(2)}, u32[]{:S(2)}) collective-permute-start(bf16[512,512]{1,0:T(8,128)(2,1)S(1)} %get-tuple-element.57.refs_5_), channel_id=1, source_target_pairs={{0,1},{1,0},{2,3},{3,2},{4,5},{5,4},{6,7},{7,6},{8,9},{9,8},{10,11... | collective-permute-start | bytes 1572872 | tf_op jit(solution)/shard_map/ppermute | solution.py:91
  13.3 17.7 %collective-permute-start = (bf16[512,512]{1,0:T(8,128)(2,1)S(1)}, bf16[512,512]{1,0:T(8,128)(2,1)S(1)}, u32[]{:S(2)}, u32[]{:S(2)}) collective-permute-start(bf16[512,512]{1,0:T(8,128)(2,1)S(1)} %get-tuple-element.57.refs_5_), channel_id=1, source_target_pairs={{0,2},{1,3},{2,0},{3,1},{4,6},{5,7},{6,4},{7,5},{8,10},{9,11},{10,... | collective-permute-start | bytes 1572872 | tf_op jit(solution)/shard_map/ppermute | solution.py:91
  16.1 11.0 %collective-permute-start.1 = (bf16[256,512]{1,0:T(8,128)(2,1)S(1)}, bf16[256,512]{1,0:T(8,128)(2,1)S(1)}, u32[]{:S(2)}, u32[]{:S(2)}) collective-permute-start(bf16[256,512]{1,0:T(8,128)(2,1)S(1)} %get-tuple-element.58), channel_id=1, source_target_pairs={{0,4},{1,5},{2,6},{3,7},{4,8},{5,9},{6,10},{7,11},{8,12},{9,13},{1... | collective-permute-start | bytes 786440 | tf_op jit(solution)/shard_map/ppermute | solution.py:91
  17.7 13.3 %collective-permute-start.2 = (bf16[256,512]{1,0:T(8,128)(2,1)S(1)}, bf16[256,512]{1,0:T(8,128)(2,1)S(1)}, u32[]{:S(2)}, u32[]{:S(2)}) collective-permute-start(bf16[256,512]{1,0:T(8,128)(2,1)S(1)} %get-tuple-element.58), channel_id=1, source_target_pairs={{0,12},{1,13},{2,14},{3,15},{4,0},{5,1},{6,2},{7,3},{8,4},{9,5},{1... | collective-permute-start | bytes 786440 | tf_op jit(solution)/shard_map/ppermute | solution.py:91
  31.0 4.8 %copy-start.1 = (bf16[256,8192]{1,0:T(8,128)(2,1)S(1)}, bf16[256,8192]{1,0:T(8,128)(2,1)}, u32[]{:S(2)}) copy-start(bf16[256,8192]{1,0:T(8,128)(2,1)} %refs_1_.9) | copy-start | bytes 12582916
  31.1 4.7 %collective-permute-start.9 = (bf16[1024,512]{1,0:T(8,128)(2,1)S(1)}, bf16[1024,512]{1,0:T(8,128)(2,1)S(1)}, u32[]{:S(2)}, u32[]{:S(2)}) collective-permute-start(bf16[1024,512]{1,0:T(8,128)(2,1)S(1)} %pad_maximum_fusion.2), channel_id=1, source_target_pairs={{0,1},{1,0},{2,3},{3,2},{4,5},{5,4},{6,7},{7,6},{8,9},{9,8},{10,11... | collective-permute-start | bytes 3145736 | tf_op jit(solution)/shard_map/ppermute | solution.py:91
  31.2 16.7 %collective-permute-start.5 = (bf16[544,512]{1,0:T(8,128)(2,1)S(1)}, bf16[544,512]{1,0:T(8,128)(2,1)S(1)}, u32[]{:S(2)}, u32[]{:S(2)}) collective-permute-start(bf16[544,512]{1,0:T(8,128)(2,1)S(1)} %pad_maximum_fusion.3), channel_id=1, source_target_pairs={{0,2},{1,3},{2,0},{3,1},{4,6},{5,7},{6,4},{7,5},{8,10},{9,11},{10,... | collective-permute-start | bytes 1671176 | tf_op jit(solution)/shard_map/ppermute | solution.py:91
  31.8 16.1 %collective-permute-start.6 = (bf16[512,512]{1,0:T(8,128)(2,1)S(1)}, bf16[512,512]{1,0:T(8,128)(2,1)S(1)}, u32[]{:S(2)}, u32[]{:S(2)}) collective-permute-start(bf16[512,512]{1,0:T(8,128)(2,1)S(1)} %pad_maximum_fusion.4), channel_id=1, source_target_pairs={{0,16},{1,17},{2,18},{3,19},{4,20},{5,21},{6,22},{7,23},{8,24},{9,... | collective-permute-start | bytes 1572872 | tf_op jit(solution)/shard_map/ppermute | solution.py:91
  33.4 9.1 %collective-permute-start.8 = (bf16[256,512]{1,0:T(8,128)(2,1)S(1)}, bf16[256,512]{1,0:T(8,128)(2,1)S(1)}, u32[]{:S(2)}, u32[]{:S(2)}) collective-permute-start(bf16[256,512]{1,0:T(8,128)(2,1)S(1)} %slice.10), channel_id=1, source_target_pairs={{0,12},{1,13},{2,14},{3,15},{4,0},{5,1},{6,2},{7,3},{8,4},{9,5},{1... | collective-permute-start | bytes 786440 | tf_op jit(solution)/shard_map/ppermute | solution.py:91
  35.8 12.2 %collective-permute-start.7 = (bf16[256,512]{1,0:T(8,128)(2,1)S(1)}, bf16[256,512]{1,0:T(8,128)(2,1)S(1)}, u32[]{:S(2)}, u32[]{:S(2)}) collective-permute-start(bf16[256,512]{1,0:T(8,128)(2,1)S(1)} %collective-permute-done.1.refs_7_), channel_id=1, source_target_pairs={{0,4},{1,5},{2,6},{3,7},{4,8},{5,9},{6,10},{7,11},{8,12},{9,13},{1... | collective-permute-start | bytes 786440 | tf_op jit(solution)/shard_map/ppermute | solution.py:91
  48.1 5.0 %collective-permute-start.14 = (bf16[1280,512]{1,0:T(8,128)(2,1)S(1)}, bf16[1280,512]{1,0:T(8,128)(2,1)S(1)}, u32[]{:S(2)}, u32[]{:S(2)}) collective-permute-start(bf16[1280,512]{1,0:T(8,128)(2,1)S(1)} %pad_maximum_fusion), channel_id=1, source_target_pairs={{0,1},{1,0},{2,3},{3,2},{4,5},{5,4},{6,7},{7,6},{8,9},{9,8},{10,11... | collective-permute-start | bytes 3932168 | tf_op jit(solution)/shard_map/ppermute | solution.py:91
  48.2 17.3 %collective-permute-start.10 = (bf16[512,512]{1,0:T(8,128)(2,1)S(1)}, bf16[512,512]{1,0:T(8,128)(2,1)S(1)}, u32[]{:S(2)}, u32[]{:S(2)}) collective-permute-start(bf16[512,512]{1,0:T(8,128)(2,1)S(1)} %get-tuple-element.103), channel_id=1, source_target_pairs={{0,2},{1,3},{2,0},{3,1},{4,6},{5,7},{6,4},{7,5},{8,10},{9,11},{10,... | collective-permute-start | bytes 1572872 | tf_op jit(solution)/shard_map/ppermute | solution.py:91
  49.8 15.7 %collective-permute-start.11 = (bf16[512,512]{1,0:T(8,128)(2,1)S(1)}, bf16[512,512]{1,0:T(8,128)(2,1)S(1)}, u32[]{:S(2)}, u32[]{:S(2)}) collective-permute-start(bf16[512,512]{1,0:T(8,128)(2,1)S(1)} %get-tuple-element.102), channel_id=1, source_target_pairs={{0,16},{1,17},{2,18},{3,19},{4,20},{5,21},{6,22},{7,23},{8,24},{9,... | collective-permute-start | bytes 1572872 | tf_op jit(solution)/shard_map/ppermute | solution.py:91
  51.0 14.6 %collective-permute-start.12 = (bf16[352,512]{1,0:T(8,128)(2,1)S(1)}, bf16[352,512]{1,0:T(8,128)(2,1)S(1)}, u32[]{:S(2)}, u32[]{:S(2)}) collective-permute-start(bf16[352,512]{1,0:T(8,128)(2,1)S(1)} %pad_maximum_fusion.7), channel_id=1, source_target_pairs={{0,12},{1,13},{2,14},{3,15},{4,0},{5,1},{6,2},{7,3},{8,4},{9,5},{1... | collective-permute-start | bytes 1081352 | tf_op jit(solution)/shard_map/ppermute | solution.py:91
  52.8 12.8 %collective-permute-start.13 = (bf16[96,512]{1,0:T(8,128)(2,1)S(1)}, bf16[96,512]{1,0:T(8,128)(2,1)S(1)}, u32[]{:S(2)}, u32[]{:S(2)}) collective-permute-start(bf16[96,512]{1,0:T(8,128)(2,1)S(1)} %get-tuple-element.78), channel_id=1, source_target_pairs={{0,4},{1,5},{2,6},{3,7},{4,8},{5,9},{6,10},{7,11},{8,12},{9,13},{1... | collective-permute-start | bytes 294920 | tf_op jit(solution)/shard_map/ppermute | solution.py:91
  53.1 15.6 %collective-permute-start.15 = (bf16[96,512]{1,0:T(8,128)(2,1)S(1)}, bf16[96,512]{1,0:T(8,128)(2,1)S(1)}, u32[]{:S(2)}, u32[]{:S(2)}) collective-permute-start(bf16[96,512]{1,0:T(8,128)(2,1)S(1)} %get-tuple-element.81), channel_id=1, source_target_pairs={{0,8},{1,9},{2,10},{3,11},{4,12},{5,13},{6,14},{7,15},{8,0},{9,1},... | collective-permute-start | bytes 294920 | tf_op jit(solution)/shard_map/ppermute | solution.py:91
  68.8 4.8 %collective-permute-start.16 = (bf16[1280,512]{1,0:T(8,128)(2,1)S(1)}, bf16[1280,512]{1,0:T(8,128)(2,1)S(1)}, u32[]{:S(2)}, u32[]{:S(2)}) collective-permute-start(bf16[1280,512]{1,0:T(8,128)(2,1)S(1)} %pad_maximum_fusion.1), channel_id=1, source_target_pairs={{0,1},{1,0},{2,3},{3,2},{4,5},{5,4},{6,7},{7,6},{8,9},{9,8},{10,11... | collective-permute-start | bytes 3932168 | tf_op jit(solution)/shard_map/ppermute | solution.py:91
  69.6 4.0 %copy-start.7 = (bf16[64,512]{1,0:T(8,128)(2,1)S(1)}, bf16[64,512]{1,0:T(8,128)(2,1)}, u32[]{:S(2)}) copy-start(bf16[64,512]{1,0:T(8,128)(2,1)} %refs_8_.1) | copy-start | bytes 196612
  69.6 2.8 %collective-permute-start.17 = (f32[32,512]{1,0:T(8,128)S(1)}, f32[32,512]{1,0:T(8,128)S(1)}, u32[]{:S(2)}, u32[]{:S(2)}) collective-permute-start(f32[32,512]{1,0:T(8,128)S(1)} %get-tuple-element.101.own_ref), channel_id=1, source_target_pairs={{0,1},{1,0},{2,3},{3,2},{4,5},{5,4},{6,7},{7,6},{8,9},{9,8},{10,11... | collective-permute-start | bytes 196616 | tf_op jit(solution)/shard_map/ppermute | solution.py:91

commit v3 on v2

--- a/solution.py
+++ b/solution.py
@@ -99,8 +99,8 @@
     return pl.BlockSpec(memory_space=pltpu.SMEM)
 
 
-def anywhere():
-    return pl.BlockSpec(memory_space=pl.ANY)
+def in_hbm():
+    return pl.BlockSpec(memory_space=pltpu.HBM)
 
 
 def params():
@@ -114,7 +114,15 @@
     rows, columns = quant_codes.shape
     half = rows // 2
 
-    def kernel(place_ref, codes_ref, scales_ref, own_ref, first_ref):
+    def kernel(place_ref, codes_hbm, scales_hbm, own_ref, first_ref, codes_ref, scales_ref, sems):
+        copies = [
+            pltpu.make_async_copy(scales_hbm, scales_ref, sems.at[0]),
+            pltpu.make_async_copy(codes_hbm, codes_ref, sems.at[1]),
+        ]
+        for copy in copies:
+            copy.start()
+        for copy in copies:
+            copy.wait()
         g = place_ref[0]
         for i in range(rows // BLOCK):
             source = lax.rem(g * (half // BLOCK) + i, rows // BLOCK)
@@ -133,8 +141,13 @@
             jax.ShapeDtypeStruct((rows, columns), jnp.bfloat16),
             jax.ShapeDtypeStruct((half, columns), jnp.bfloat16),
         ],
-        in_specs=[scalars(), whole(), scalars()],
+        in_specs=[scalars(), in_hbm(), in_hbm()],
         out_specs=[whole()] * 2,
+        scratch_shapes=[
+            pltpu.VMEM(quant_codes.shape, quant_codes.dtype),
+            pltpu.SMEM(block_scales.shape, block_scales.dtype),
+            pltpu.SemaphoreType.DMA((2,)),
+        ],
         compiler_params=params(),
         cost_estimate=LITTLE,
         name="dequantize",
@@ -322,29 +335,9 @@
     )(own, from_down, from_far, from_up)
 
 
-def join_cores(place, own, came):
-    half, folded = own.shape
-    width = folded // 2
-
-    def kernel(place_ref, own_ref, came_ref, out_ref):
-        c = place_ref[3]
-        for ref, core in ((own_ref, c), (came_ref, 1 - c)):
-            at = pl.ds(pl.multiple_of(core * width, width), width)
-            out_ref[:half, at] = ref[:, :width]
-            out_ref[half:, at] = ref[:, width:]
-
-    return pl.pallas_call(
-        kernel,
-        out_shape=jax.ShapeDtypeStruct((2 * half, folded), jnp.float32),
-        in_specs=[scalars(), whole(), whole()],
-        out_specs=whole(),
-        compiler_params=params(),
-        cost_estimate=LITTLE,
-        name="join_cores",
-    )(place, own, came)
-
-
-def multiply(place, pieces, activations, down_t, cotangent, lgrad, total, gradient, finish=None):
+def multiply(
+    place, pieces, activations, down_t, cotangent, lgrad, begin=None, so_far=None, end=None
+):
     tokens, width = activations.shape
     features = cotangent.shape[1]
     arrays = []
@@ -353,71 +346,84 @@
             arrays.append(array)
     where = [next(i for i, a in enumerate(arrays) if a is array) for array, _, _ in pieces]
     count = len(pieces)
-    started = total is not None
     rows = width // (NZ * 2 * 2 * 2)
 
     def kernel(*refs):
         refs = list(refs)
-        place_ref, act_ref, down_ref, cot_ref, lgrad_ref = refs[:5]
-        del refs[:5]
-        if started:
-            total_ref = refs.pop(0)
-            refs.pop(0)
-        if finish is not None:
-            latent_ref, up_ref = refs.pop(0), refs.pop(0)
+        place_ref, act_ref, down_ref, cot_ref, lgrad_ref, one_ref, two_ref = refs[:7]
+        del refs[:7]
+        if end is not None:
+            up_refs = refs[:2]
+            del refs[:2]
         array_refs = refs[: len(arrays)]
         del refs[: len(arrays)]
-        out_ref, grad_ref, sums, grads, out_sems = refs
+        out_ref, grad_ref = refs[:2]
+        sums, grads, out_sems = refs[-3:]
         g, z, y, c = (place_ref[i] for i in range(4))
-        if finish is not None:
-            sums[...] = total_ref[...] + lowrank_scale * jnp.dot(
-                latent_ref[...], up_ref[...], preferred_element_type=jnp.float32
-            )
-        elif started:
-            sums[...] = total_ref[...]
-        else:
-            sums[...] = jnp.zeros_like(sums)
-        going = []
+        columns, weights, going = [], [], []
         for p, (_, first, (dz, dy, dc, dh)) in enumerate(pieces):
             chip = lax.rem(z + (NZ - dz), NZ) * 2 + (1 - y if dy else y)
             device = chip * 2 + (1 - c if dc else c)
             start = (device * 2 + (1 - g if dh else g)) * rows
-            at = pl.ds(pl.multiple_of(start, rows), rows)
-            weight = array_refs[where[p]][first : first + rows, :]
-            sums[...] += jnp.dot(act_ref[:, at], weight, preferred_element_type=jnp.float32)
+            columns.append(pl.ds(pl.multiple_of(start, rows), rows))
+            weights.append(array_refs[where[p]].at[first : first + rows, :])
+        for p in range(count):
             grads[p] = (
-                weight_transpose(cot_ref[...], weight)
+                weight_transpose(cot_ref[...], weights[p][...])
                 + lowrank_scale
-                * jnp.dot(lgrad_ref[...], down_ref[:, at], preferred_element_type=jnp.float32)
+                * jnp.dot(
+                    lgrad_ref[...], down_ref[:, columns[p]], preferred_element_type=jnp.float32
+                )
             ).astype(jnp.bfloat16)
-            copy = pltpu.make_async_copy(grads.at[p], grad_ref.at[:, at], out_sems.at[p])
+            copy = pltpu.make_async_copy(grads.at[p], grad_ref.at[:, columns[p]], out_sems.at[p])
             copy.start()
             going.append(copy)
+        if begin is not None:
+            sums[...] = lowrank_scale * jnp.dot(
+                one_ref[...], two_ref[...], preferred_element_type=jnp.float32
+            )
+        else:
+            sums[...] = one_ref[...]
+        for p in range(count):
+            sums[...] += jnp.dot(
+                act_ref[:, columns[p]], weights[p][...], preferred_element_type=jnp.float32
+            )
         out_ref[...] = sums[...].astype(out_ref.dtype)
+        if end is not None:
+            up_part = features // 2
+            rank = down_ref.shape[0]
+            for ref, core in zip(up_refs, (c, 1 - c), strict=True):
+                at = pl.ds(pl.multiple_of(core * up_part, up_part), up_part)
+                refs[2][: rank // 2, at] = ref[:, :up_part]
+                refs[2][rank // 2 :, at] = ref[:, up_part:]
         for copy in going:
             copy.wait()
 
     operands = [place, activations, down_t, cotangent, lgrad]
     specs = [scalars()] + [whole()] * 4
+    out_shape = [
+        jax.ShapeDtypeStruct((tokens, features), jnp.float32 if end is None else jnp.bfloat16),
+        jax.ShapeDtypeStruct((tokens, width), jnp.bfloat16),
+    ]
+    out_specs = [whole(), in_hbm()]
     aliases = {}
-    if started:
-        operands += [total, gradient]
-        specs += [whole(), anywhere()]
+    if begin is not None:
+        operands += begin
+        specs += [whole()] * 2
+    else:
+        operands += so_far
+        specs += [whole(), in_hbm()]
         aliases = {6: 1}
-    if finish is not None:
-        operands += list(finish)
-        specs += [whole(), whole()]
-    operands += arrays
-    specs += [whole()] * len(arrays)
-    out_type = jnp.float32 if finish is None else jnp.bfloat16
+    if end is not None:
+        operands += end
+        specs += [whole()] * 2
+        out_shape.append(jax.ShapeDtypeStruct((down_t.shape[0], features), jnp.float32))
+        out_specs.append(whole())
     return pl.pallas_call(
         kernel,
-        out_shape=[
-            jax.ShapeDtypeStruct((tokens, features), out_type),
-            jax.ShapeDtypeStruct((tokens, width), jnp.bfloat16),
-        ],
-        in_specs=specs,
-        out_specs=[whole(), anywhere()],
+        out_shape=out_shape,
+        in_specs=specs + [whole()] * len(arrays),
+        out_specs=out_specs,
         scratch_shapes=[
             pltpu.VMEM((tokens, features), jnp.float32),
             pltpu.VMEM((count, tokens, rows), jnp.bfloat16),
@@ -427,7 +433,7 @@
         compiler_params=params(),
         cost_estimate=LITTLE,
         name="multiply",
-    )(*operands)
+    )(*operands, *arrays)
 
 
 def per_device(
@@ -443,44 +449,52 @@
     barrier = lax.optimization_barrier
     join = lambda *arrays: jnp.concatenate(arrays, axis=0)
 
-    def products(pieces, total, gradient, finish=None):
-        return multiply(
-            place, pieces, activations, down_t, cotangent, lgrad, total, gradient, finish
-        )
+    def products(pieces, **more):
+        return multiply(place, pieces, activations, down_t, cotangent, lgrad, **more)
 
     def listed(array, dc, *keys):
         return [(array, i * half, (dz, dy, dc, dh)) for i, (dz, dy, dh) in enumerate(keys)]
 
+    def block(body, *operands):
+        def never(*operands):
+            shapes = jax.eval_shape(body, *operands)
+            return jax.tree.map(lambda shape: jnp.zeros(shape.shape, shape.dtype), shapes)
+
+        return lax.cond(place[0] >= 0, body, never, *operands)
+
     own, first = dequantize_shard(place, quant_codes, block_scales)
     own, first, place = barrier((own, first, place))
 
     y1, up1, down1 = send(own, OVER_Y), send(first, Z_UP), send(first, Z_DOWN)
     swap1 = send(own, OVER_CORE)
-    latent, lgrad, own_terms, away_terms = local_gradients(
-        place, activations, down_t, lowrank_up_factor, cotangent
-    )
-    came = send(away_terms, OVER_CORE)
-    own_keys = [(0, 0, 0), (0, 0, 1)]
-    total, gradient = products(
-        listed(own, 0, *own_keys) + listed(swap1, 1, *own_keys), None, None
-    )
-    terms_y, kept = add_cores(own_terms, came, up_part)
-    y1, up1, down1, terms_y, kept, total, gradient = barrier(
-        (y1, up1, down1, terms_y, kept, total, gradient)
-    )
+
+    def lowrank(place):
+        latent, lgrad, own_terms, away_terms = local_gradients(
+            place, activations, down_t, lowrank_up_factor, cotangent
+        )
+        came = send(away_terms, OVER_CORE)
+        terms_y, kept = add_cores(own_terms, came, up_part)
+        return latent, lgrad, terms_y, kept
+
+    latent, lgrad, terms_y, kept = block(lowrank, place)
+    keys = [(0, 0, 0), (0, 0, 1)]
+    done = products(
+        listed(own, 0, *keys) + listed(swap1, 1, *keys), begin=[latent, lowrank_up_factor]
+    )
+    y1, up1, down1, terms_y, kept, done = barrier((y1, up1, down1, terms_y, kept, done))
 
     y2, x2 = send(join(up1, terms_y), OVER_Y), send(join(up1, down1), OVER_X)
     up2, down2 = send(up1, Z_UP), send(y1[half:], Z_DOWN)
     swap2 = send(join(up1, down1, y1), OVER_CORE)
     keys = [(1, 0, 0), (3, 0, 0), (0, 1, 0), (0, 1, 1)]
-    total, gradient = products(
+    done = products(
         listed(up1, 0, keys[0])
         + listed(down1, 0, keys[1])
         + listed(y1, 0, *keys[2:])
         + listed(swap2, 1, *keys),
-        total, gradient,
-    )
-    y2, x2, up2, down2, total, gradient = barrier((y2, x2, up2, down2, total, gradient))
+        so_far=done,
+    )
+    y2, x2, up2, down2, done = barrier((y2, x2, up2, down2, done))
 
     own_part, to_up, to_far, to_down = add_y(place, kept, terms_y, y2, half)
     y3, x3 = send(join(down1, up2), OVER_Y), send(join(up2, y2[:half]), OVER_X)
@@ -489,30 +503,27 @@
     swap3, to_far = barrier((swap3, to_far))
     far3 = send(to_far, Z_FAR)
     keys = [(1, 1, 0), (1, 0, 1), (3, 0, 1), (2, 0, 0), (3, 1, 1)]
-    total, gradient = products(
+    done = products(
         listed(y2, 0, keys[0])
         + listed(x2, 0, *keys[1:3])
         + listed(up2, 0, keys[3])
         + listed(down2, 0, keys[4])
         + listed(swap3, 1, *keys),
-        total, gradient,
-    )
-    y3, x3, down3, up3, far3, total, gradient = barrier(
-        (y3, x3, down3, up3, far3, total, gradient)
-    )
+        so_far=done,
+    )
+    y3, x3, down3, up3, far3, done = barrier((y3, x3, down3, up3, far3, done))
 
     swap4 = send(join(y3, x3, down3[:half]), OVER_CORE)
     grad_down_t, up_own = add_z(own_part, up3, far3, down3, half, factor)
     up_came = send(up_own, OVER_CORE)
     keys = [(3, 1, 0), (2, 1, 0), (2, 0, 1), (1, 1, 1), (2, 1, 1)]
-    total, gradient = products(
+    done = products(
         listed(y3, 0, *keys[:2]) + listed(x3, 0, *keys[2:4]) + listed(down3, 0, keys[4]),
-        total, gradient,
-    )
-    projected, gradient = products(
-        listed(swap4, 1, *keys), total, gradient, finish=(latent, lowrank_up_factor)
-    )
-    grad_up = join_cores(place, up_own, up_came)
+        so_far=done,
+    )
+    projected, gradient, grad_up = products(
+        listed(swap4, 1, *keys), so_far=done, end=[up_own, up_came]
+    )
     return (projected, gradient, grad_down_t.T, grad_up)
 
 

time: 77 us -> 68.8 us (0.89)
  waiting for transfers between devices: 29 us -> 22.9 us
  local copies, waits for them, and re-layouts: 6.98 us -> 1.8 us
  Pallas kernels: 21 us -> 24.8 us
  starting transfers between devices: 18.3 us -> 17.5 us
    ppermute x18, waiting for transfers between devices: 29 us -> 22.9 us  [send(): return lax.ppermute(array, AXES, pairs)]
    unnamed x18 -> x10, local copies, waits for them, and re-layouts: 6.93 us -> 1.74 us
    pallas_call x1, Pallas kernels: 4.19 us -> 6.81 us  [local_gradients(): pl.pallas_call(kernel, grid=(chips,), out_shape=[jax.ShapeDtypeStruct((to...]
    ppermute x18, starting transfers between devices: 18.3 us -> 17.5 us  [send(): return lax.ppermute(array, AXES, pairs)]
    pallas_call x6 -> x5, Pallas kernels: 14.7 us -> 15.3 us  [multiply(): pl.pallas_call(kernel, out_shape=out_shape, in_specs=specs + [whole()] *...]
  transfers between devices with their start and end apart: 18 -> 18, of which waited for: 6 -> 5; matrix products, arithmetic and copies ran while one was open for 0% -> 0% of each run, Pallas kernels for 17% -> 30%
where the time goes in v3:
time: 68.8 us; the launch traced here: 68.5 us
  Pallas kernels  24.8 us (36%)
  waiting for transfers between devices  22.9 us (33%)
  starting transfers between devices  17.5 us (25%)
  local copies, waits for them, and re-layouts  1.8 us (3%)
  between operations  0.91 us (1%)
    ppermute x18, waiting for transfers between devices, send(): return lax.ppermute(array, AXES, pairs)  22.9 us
    ppermute x18, starting transfers between devices, send(): return lax.ppermute(array, AXES, pairs)  17.5 us
    pallas_call x5, Pallas kernels, multiply(): pl.pallas_call(kernel, out_shape=out_shape, in_specs=specs + [whole()] *...  15.3 us
    pallas_call x1, Pallas kernels, local_gradients(): pl.pallas_call(kernel, grid=(chips,), out_shape=[jax.ShapeDtypeStruct((to...  6.81 us
    unnamed x10, local copies, waits for them, and re-layouts  1.74 us
  transfers between devices with their start and end apart: 18, of which 5 were waited for; matrix products, arithmetic and copies ran while one was open for 0% of the time, Pallas kernels for 30%

profile of v3, /device:TPU:0, one launch (start us, length us, event | category | flops | bytes accessed | tf_op | source)
XLA Modules:
  0.0 68.5 jit_solution(10222003387156462406)
XLA Ops:
  0.6 0.1 pad_add_fusion.place_ref.refs_0_
  0.7 1.0 %copy-done = bf16[512,512]{1,0:T(8,128)(2,1)S(1)} copy-done((bf16[512,512]{1,0:T(8,128)(2,1)S(1)}, bf16[512,512]{1,0:T(8,128)(2,1)}, u32[]{:S(2)}) %copy-start) | copy-done | bytes 524312
  1.8 0.7 copy-done.1
  2.4 1.2 %dequantize.1 = (bf16[512,512]{1,0:T(8,128)(2,1)S(1)}, bf16[256,512]{1,0:T(8,128)(2,1)S(1)}) custom-call(s32[4]{0:T(128)S(1)} %pad_add_fusion.place_ref.refs_0_, bf16[512,512]{1,0:T(8,128)(2,1)S(1)} %copy-done, f32[4,4]{1,0:T(4,128)S(1)} %copy-done.1), custom_call_target="tpu_custom_call" | custom-call | flops 1 | bytes 1 | tf_op jit(solution)/shard_map/dequantize/pallas_call | solution.py:138
  3.7 0.5 collective-permute-start.4
  4.2 2.6 %collective-permute-start.1 = (bf16[512,512]{1,0:T(8,128)(2,1)S(1)}, bf16[512,512]{1,0:T(8,128)(2,1)S(1)}, u32[]{:S(2)}, u32[]{:S(2)}) collective-permute-start(bf16[512,512]{1,0:T(8,128)(2,1)S(1)} %get-tuple-element.77.refs_7_), channel_id=1, source_target_pairs={{0,2},{1,3},{2,0},{3,1},{4,6},{5,7},{6,4},{7,5},{8,10},{9,11},{10,... | collective-permute-start | bytes 1572872 | tf_op jit(solution)/shard_map/ppermute | solution.py:91
  6.8 1.6 %collective-permute-start.2 = (bf16[256,512]{1,0:T(8,128)(2,1)S(1)}, bf16[256,512]{1,0:T(8,128)(2,1)S(1)}, u32[]{:S(2)}, u32[]{:S(2)}) collective-permute-start(bf16[256,512]{1,0:T(8,128)(2,1)S(1)} %get-tuple-element.78), channel_id=1, source_target_pairs={{0,4},{1,5},{2,6},{3,7},{4,8},{5,9},{6,10},{7,11},{8,12},{9,13},{1... | collective-permute-start | bytes 786440 | tf_op jit(solution)/shard_map/ppermute | solution.py:91
  8.4 2.2 %collective-permute-start.3 = (bf16[256,512]{1,0:T(8,128)(2,1)S(1)}, bf16[256,512]{1,0:T(8,128)(2,1)S(1)}, u32[]{:S(2)}, u32[]{:S(2)}) collective-permute-start(bf16[256,512]{1,0:T(8,128)(2,1)S(1)} %get-tuple-element.78), channel_id=1, source_target_pairs={{0,12},{1,13},{2,14},{3,15},{4,0},{5,1},{6,2},{7,3},{8,4},{9,5},{1... | collective-permute-start | bytes 786440 | tf_op jit(solution)/shard_map/ppermute | solution.py:91
  10.7 9.8 %conditional.1 = (bf16[256,64]{1,0:T(8,128)(2,1)S(1)}, bf16[256,64]{1,0:T(8,128)(2,1)S(1)}, bf16[288,512]{1,0:T(8,128)(2,1)S(1)}, f32[64,2048]{1,0:T(8,128)S(1)}) conditional(s32[]{:T(128)} %bitcast.5, () %tuple.22, (s32[4]{0:T(128)S(1)}, bf16[256,8192]{1,0:T(8,128)(2,1)}, bf16[64,8192]{1,0:T(8,128)(2,1)}, bf16[64,512]{1,0:T(8,128)(2,1)}, ...), branch_computations={%region_0.0_spmd, %region_1.0_spmd} | conditional | flops 2 | bytes 4456522 | solution.py:463
  10.7 6.8 %local_gradients.1 = (bf16[256,64]{1,0:T(8,128)(2,1)S(1)}, bf16[256,64]{1,0:T(8,128)(2,1)S(1)}, f32[64,4352]{1,0:T(8,128)S(1)}, f32[64,4352]{1,0:T(8,128)S(1)}) custom-call(s32[4]{0:T(128)S(1)} %get-tuple-element.10.place_ref, bf16[256,8192]{1,0:T(8,128)(2,1)} %get-tuple-element.11.act_ref, bf16[64,8192]{1,0:T(8,128)(2,1)} %get-tuple-element.12.down_ref, ...), custom_call_target="tpu_custom_call" | custom-call | flops 1 | bytes 1 | tf_op jit(solution)/shard_map/cond/branch_1_fun/local_gradients/pallas_call | solution.py:214
  17.5 0.1 collective-permute-start
  17.6 2.7 %collective-permute-done.came_ref = f32[64,4352]{1,0:T(8,128)S(1)} collective-permute-done((f32[64,4352]{1,0:T(8,128)S(1)}, f32[64,4352]{1,0:T(8,128)S(1)}, u32[]{:S(2)}, u32[]{:S(2)}) %collective-permute-start) | collective-permute-done | bytes 1114144 | tf_op jit(solution)/shard_map/cond/branch_1_fun/ppermute | solution.py:91
  20.3 0.1 add_cores.1
  20.4 0.0 collective-permute-done.4.refs_8_
  20.5 0.0 copy-start.3
  20.5 4.1 %multiply.5 = (f32[256,512]{1,0:T(8,128)S(1)}, bf16[256,8192]{1,0:T(8,128)(2,1)}) custom-call(s32[4]{0:T(128)S(1)} %pad_add_fusion.place_ref.refs_0_, bf16[256,8192]{1,0:T(8,128)(2,1)} %refs_1_.9, bf16[64,8192]{1,0:T(8,128)(2,1)} %bitcast.9, bf16[256,512]{1,0:T(8,128)(2,1)} %refs_3_.9, bf16[256,64]{1,0:T(8,128)(2,1)S(1)} %get-tuple-element.76.refs_4_, ...), custom_call_target="tpu_custom_call" | custom-call | flops 1 | bytes 1 | tf_op jit(solution)/shard_map/multiply/pallas_call | solution.py:422
  24.5 0.0 collective-permute-done.2.refs_7_
  24.6 0.0 collective-permute-done.3.refs_8_
  24.6 0.0 copy-start.2
  24.6 0.0 copy-start.4
  24.6 0.1 pad_maximum_fusion.2
  24.7 0.2 collective-permute-start.9
  24.9 0.4 collective-permute-start.5
  25.3 1.8 %collective-permute-start.6 = (bf16[512,512]{1,0:T(8,128)(2,1)S(1)}, bf16[512,512]{1,0:T(8,128)(2,1)S(1)}, u32[]{:S(2)}, u32[]{:S(2)}) collective-permute-start(bf16[512,512]{1,0:T(8,128)(2,1)S(1)} %pad_maximum_fusion.4), channel_id=1, source_target_pairs={{0,16},{1,17},{2,18},{3,19},{4,20},{5,21},{6,22},{7,23},{8,24},{9,... | collective-permute-start | bytes 1572872 | tf_op jit(solution)/shard_map/ppermute | solution.py:91
  27.1 1.8 %collective-permute-start.8 = (bf16[256,512]{1,0:T(8,128)(2,1)S(1)}, bf16[256,512]{1,0:T(8,128)(2,1)S(1)}, u32[]{:S(2)}, u32[]{:S(2)}) collective-permute-start(bf16[256,512]{1,0:T(8,128)(2,1)S(1)} %slice.14), channel_id=1, source_target_pairs={{0,12},{1,13},{2,14},{3,15},{4,0},{5,1},{6,2},{7,3},{8,4},{9,5},{1... | collective-permute-start | bytes 786440 | tf_op jit(solution)/shard_map/ppermute | solution.py:91
  29.0 0.2 collective-permute-start.7
  29.2 0.0 collective-permute-done.9.refs_10_
  29.2 2.8 %multiply.6 = (f32[256,512]{1,0:T(8,128)S(1)}, bf16[256,8192]{1,0:T(8,128)(2,1)}) custom-call(s32[4]{0:T(128)S(1)} %pad_add_fusion.place_ref.refs_0_, bf16[256,8192]{1,0:T(8,128)(2,1)S(1)} %copy-done.2, bf16[64,8192]{1,0:T(8,128)(2,1)S(1)} %bitcast.10, bf16[256,512]{1,0:T(8,128)(2,1)S(1)} %copy-done.4, ...), custom_call_target="tpu_custom_call", output_to_operand_aliasing={{1}: (6, {})} | custom-call | flops 1 | bytes 1 | tf_op jit(solution)/shard_map/multiply/pallas_call | solution.py:422
  32.0 4.1 %collective-permute-done.8.refs_10_ = bf16[256,512]{1,0:T(8,128)(2,1)S(1)} collective-permute-done((bf16[256,512]{1,0:T(8,128)(2,1)S(1)}, bf16[256,512]{1,0:T(8,128)(2,1)S(1)}, u32[]{:S(2)}, u32[]{:S(2)}) %collective-permute-start.8) | collective-permute-done | bytes 262176 | tf_op jit(solution)/shard_map/ppermute | solution.py:91
  36.2 4.9 %collective-permute-done.7.refs_9_ = bf16[256,512]{1,0:T(8,128)(2,1)S(1)} collective-permute-done((bf16[256,512]{1,0:T(8,128)(2,1)S(1)}, bf16[256,512]{1,0:T(8,128)(2,1)S(1)}, u32[]{:S(2)}, u32[]{:S(2)}) %collective-permute-start.7) | collective-permute-done | bytes 262176 | tf_op jit(solution)/shard_map/ppermute | solution.py:91
  41.1 0.1 pad_maximum_fusion
  41.1 0.1 collective-permute-start.14
  41.2 0.1 pad_maximum_fusion.6
  41.3 1.6 %collective-permute-start.10 = (bf16[512,512]{1,0:T(8,128)(2,1)S(1)}, bf16[512,512]{1,0:T(8,128)(2,1)S(1)}, u32[]{:S(2)}, u32[]{:S(2)}) collective-permute-start(bf16[512,512]{1,0:T(8,128)(2,1)S(1)} %get-tuple-element.122), channel_id=1, source_target_pairs={{0,2},{1,3},{2,0},{3,1},{4,6},{5,7},{6,4},{7,5},{8,10},{9,11},{10,... | collective-permute-start | bytes 1572872 | tf_op jit(solution)/shard_map/ppermute | solution.py:91
  42.9 0.5 collective-permute-start.11
  43.4 0.6 add_y.1
  44.1 1.8 %collective-permute-start.12 = (bf16[352,512]{1,0:T(8,128)(2,1)S(1)}, bf16[352,512]{1,0:T(8,128)(2,1)S(1)}, u32[]{:S(2)}, u32[]{:S(2)}) collective-permute-start(bf16[352,512]{1,0:T(8,128)(2,1)S(1)} %pad_maximum_fusion.7), channel_id=1, source_target_pairs={{0,12},{1,13},{2,14},{3,15},{4,0},{5,1},{6,2},{7,3},{8,4},{9,5},{1... | collective-permute-start | bytes 1081352 | tf_op jit(solution)/shard_map/ppermute | solution.py:91
  45.9 0.3 collective-permute-start.13
  46.2 1.3 %collective-permute-start.15 = (bf16[96,512]{1,0:T(8,128)(2,1)S(1)}, bf16[96,512]{1,0:T(8,128)(2,1)S(1)}, u32[]{:S(2)}, u32[]{:S(2)}) collective-permute-start(bf16[96,512]{1,0:T(8,128)(2,1)S(1)} %get-tuple-element.100), channel_id=1, source_target_pairs={{0,8},{1,9},{2,10},{3,11},{4,12},{5,13},{6,14},{7,15},{8,0},{9,1},... | collective-permute-start | bytes 294920 | tf_op jit(solution)/shard_map/ppermute | solution.py:91
  47.4 3.2 %multiply.7 = (f32[256,512]{1,0:T(8,128)S(1)}, bf16[256,8192]{1,0:T(8,128)(2,1)}) custom-call(s32[4]{0:T(128)S(1)} %pad_add_fusion.place_ref.refs_0_, bf16[256,8192]{1,0:T(8,128)(2,1)S(1)} %copy-done.2, bf16[64,8192]{1,0:T(8,128)(2,1)S(1)} %bitcast.11, bf16[256,512]{1,0:T(8,128)(2,1)S(1)} %copy-done.4, ...), custom_call_target="tpu_custom_call", output_to_operand_aliasing={{1}: (6, {})} | custom-call | flops 1 | bytes 1 | tf_op jit(solution)/shard_map/multiply/pallas_call | solution.py:422
  50.6 7.7 %collective-permute-done.13.a_ref = bf16[96,512]{1,0:T(8,128)(2,1)S(1)} collective-permute-done((bf16[96,512]{1,0:T(8,128)(2,1)S(1)}, bf16[96,512]{1,0:T(8,128)(2,1)S(1)}, u32[]{:S(2)}, u32[]{:S(2)}) %collective-permute-start.13) | collective-permute-done | bytes 98336 | tf_op jit(solution)/shard_map/ppermute | solution.py:91
  58.3 3.4 %collective-permute-done.15.b_ref = bf16[96,512]{1,0:T(8,128)(2,1)S(1)} collective-permute-done((bf16[96,512]{1,0:T(8,128)(2,1)S(1)}, bf16[96,512]{1,0:T(8,128)(2,1)S(1)}, u32[]{:S(2)}, u32[]{:S(2)}) %collective-permute-start.15) | collective-permute-done | bytes 98336 | tf_op jit(solution)/shard_map/ppermute | solution.py:91
  61.8 0.1 pad_maximum_fusion.1
  61.9 0.1 collective-permute-start.17
  62.0 0.7 %add_z.1 = (f32[64,512]{1,0:T(8,128)}, f32[32,512]{1,0:T(8,128)S(1)}) custom-call(f32[96,512]{1,0:T(8,128)S(1)} %get-tuple-element.113.own_ref, bf16[96,512]{1,0:T(8,128)(2,1)S(1)} %collective-permute-done.13.a_ref, bf16[96,512]{1,0:T(8,128)(2,1)S(1)} %collective-permute-done.15.b_ref, bf16[352,512]{1,0:T(8,128)(2,1)S(1)} %collective-permute-done.12.refs_9_.c_ref), custom_call_target="tpu_custom_call" | custom-call | flops 1 | bytes 1 | tf_op jit(solution)/shard_map/add_z/pallas_call | solution.py:324
  62.7 0.5 collective-permute-start.16
  63.1 2.3 %multiply.8 = (f32[256,512]{1,0:T(8,128)S(1)}, bf16[256,8192]{1,0:T(8,128)(2,1)}) custom-call(s32[4]{0:T(128)S(1)} %pad_add_fusion.place_ref.refs_0_, bf16[256,8192]{1,0:T(8,128)(2,1)S(1)} %copy-done.2, bf16[64,8192]{1,0:T(8,128)(2,1)S(1)} %bitcast.12, bf16[256,512]{1,0:T(8,128)(2,1)S(1)} %copy-done.4, ...), custom_call_target="tpu_custom_call", output_to_operand_aliasing={{1}: (6, {})} | custom-call | flops 1 | bytes 1 | tf_op jit(solution)/shard_map/multiply/pallas_call | solution.py:422
  65.4 3.0 %multiply.9 = (bf16[256,512]{1,0:T(8,128)(2,1)}, bf16[256,8192]{1,0:T(8,128)(2,1)}, f32[64,512]{1,0:T(8,128)}) custom-call(s32[4]{0:T(128)S(1)} %pad_add_fusion.place_ref.refs_0_, bf16[256,8192]{1,0:T(8,128)(2,1)S(1)} %copy-done.2, bf16[64,8192]{1,0:T(8,128)(2,1)S(1)} %bitcast.13, bf16[256,512]{1,0:T(8,128)(2,1)S(1)} %copy-done.4, ...), custom_call_target="tpu_custom_call", output_to_operand_aliasing={{1}: (6, {})} | custom-call | flops 1 | bytes 1 | tf_op jit(solution)/shard_map/multiply/pallas_call | solution.py:422
  (20 shorter events, 0.2 us)
Async XLA Ops:
  0.7 1.0 %copy-start = (bf16[512,512]{1,0:T(8,128)(2,1)S(1)}, bf16[512,512]{1,0:T(8,128)(2,1)}, u32[]{:S(2)}) copy-start(bf16[512,512]{1,0:T(8,128)(2,1)} %codes_hbm.1) | copy-start | bytes 1572868
  1.8 0.7 copy-start.1
  3.7 16.7 %collective-permute-start.4 = (bf16[512,512]{1,0:T(8,128)(2,1)S(1)}, bf16[512,512]{1,0:T(8,128)(2,1)S(1)}, u32[]{:S(2)}, u32[]{:S(2)}) collective-permute-start(bf16[512,512]{1,0:T(8,128)(2,1)S(1)} %get-tuple-element.77.refs_7_), channel_id=1, source_target_pairs={{0,1},{1,0},{2,3},{3,2},{4,5},{5,4},{6,7},{7,6},{8,9},{9,8},{10,11... | collective-permute-start | bytes 1572872 | tf_op jit(solution)/shard_map/ppermute | solution.py:91
  4.2 20.4 %collective-permute-start.1 = (bf16[512,512]{1,0:T(8,128)(2,1)S(1)}, bf16[512,512]{1,0:T(8,128)(2,1)S(1)}, u32[]{:S(2)}, u32[]{:S(2)}) collective-permute-start(bf16[512,512]{1,0:T(8,128)(2,1)S(1)} %get-tuple-element.77.refs_7_), channel_id=1, source_target_pairs={{0,2},{1,3},{2,0},{3,1},{4,6},{5,7},{6,4},{7,5},{8,10},{9,11},{10,... | collective-permute-start | bytes 1572872 | tf_op jit(solution)/shard_map/ppermute | solution.py:91
  6.8 17.7 %collective-permute-start.2 = (bf16[256,512]{1,0:T(8,128)(2,1)S(1)}, bf16[256,512]{1,0:T(8,128)(2,1)S(1)}, u32[]{:S(2)}, u32[]{:S(2)}) collective-permute-start(bf16[256,512]{1,0:T(8,128)(2,1)S(1)} %get-tuple-element.78), channel_id=1, source_target_pairs={{0,4},{1,5},{2,6},{3,7},{4,8},{5,9},{6,10},{7,11},{8,12},{9,13},{1... | collective-permute-start | bytes 786440 | tf_op jit(solution)/shard_map/ppermute | solution.py:91
  8.4 16.2 %collective-permute-start.3 = (bf16[256,512]{1,0:T(8,128)(2,1)S(1)}, bf16[256,512]{1,0:T(8,128)(2,1)S(1)}, u32[]{:S(2)}, u32[]{:S(2)}) collective-permute-start(bf16[256,512]{1,0:T(8,128)(2,1)S(1)} %get-tuple-element.78), channel_id=1, source_target_pairs={{0,12},{1,13},{2,14},{3,15},{4,0},{5,1},{6,2},{7,3},{8,4},{9,5},{1... | collective-permute-start | bytes 786440 | tf_op jit(solution)/shard_map/ppermute | solution.py:91
  17.5 2.8 %collective-permute-start = (f32[64,4352]{1,0:T(8,128)S(1)}, f32[64,4352]{1,0:T(8,128)S(1)}, u32[]{:S(2)}, u32[]{:S(2)}) collective-permute-start(f32[64,4352]{1,0:T(8,128)S(1)} %get-tuple-element.18), channel_id=1, source_target_pairs={{0,1},{1,0},{2,3},{3,2},{4,5},{5,4},{6,7},{7,6},{8,9},{9,8},{10,11... | collective-permute-start | bytes 3342344 | tf_op jit(solution)/shard_map/cond/branch_1_fun/ppermute | solution.py:91
  20.5 8.8 %copy-start.3 = (bf16[8192,64]{0,1:T(8,128)(2,1)S(1)}, bf16[8192,64]{0,1:T(8,128)(2,1)}, u32[]{:S(2)}) copy-start(bf16[8192,64]{0,1:T(8,128)(2,1)} %param.11) | copy-start | bytes 3145732
  24.6 4.6 %copy-start.2 = (bf16[256,8192]{1,0:T(8,128)(2,1)S(1)}, bf16[256,8192]{1,0:T(8,128)(2,1)}, u32[]{:S(2)}) copy-start(bf16[256,8192]{1,0:T(8,128)(2,1)} %refs_1_.9) | copy-start | bytes 12582916
  24.6 4.6 %copy-start.4 = (bf16[256,512]{1,0:T(8,128)(2,1)S(1)}, bf16[256,512]{1,0:T(8,128)(2,1)}, u32[]{:S(2)}) copy-start(bf16[256,512]{1,0:T(8,128)(2,1)} %refs_3_.9) | copy-start | bytes 786436
  24.7 4.5 %collective-permute-start.9 = (bf16[1024,512]{1,0:T(8,128)(2,1)S(1)}, bf16[1024,512]{1,0:T(8,128)(2,1)S(1)}, u32[]{:S(2)}, u32[]{:S(2)}) collective-permute-start(bf16[1024,512]{1,0:T(8,128)(2,1)S(1)} %pad_maximum_fusion.2), channel_id=1, source_target_pairs={{0,1},{1,0},{2,3},{3,2},{4,5},{5,4},{6,7},{7,6},{8,9},{9,8},{10,11... | collective-permute-start | bytes 3145736 | tf_op jit(solution)/shard_map/ppermute | solution.py:91
  24.9 16.1 %collective-permute-start.5 = (bf16[544,512]{1,0:T(8,128)(2,1)S(1)}, bf16[544,512]{1,0:T(8,128)(2,1)S(1)}, u32[]{:S(2)}, u32[]{:S(2)}) collective-permute-start(bf16[544,512]{1,0:T(8,128)(2,1)S(1)} %pad_maximum_fusion.3), channel_id=1, source_target_pairs={{0,2},{1,3},{2,0},{3,1},{4,6},{5,7},{6,4},{7,5},{8,10},{9,11},{10,... | collective-permute-start | bytes 1671176 | tf_op jit(solution)/shard_map/ppermute | solution.py:91
  25.3 15.7 %collective-permute-start.6 = (bf16[512,512]{1,0:T(8,128)(2,1)S(1)}, bf16[512,512]{1,0:T(8,128)(2,1)S(1)}, u32[]{:S(2)}, u32[]{:S(2)}) collective-permute-start(bf16[512,512]{1,0:T(8,128)(2,1)S(1)} %pad_maximum_fusion.4), channel_id=1, source_target_pairs={{0,16},{1,17},{2,18},{3,19},{4,20},{5,21},{6,22},{7,23},{8,24},{9,... | collective-permute-start | bytes 1572872 | tf_op jit(solution)/shard_map/ppermute | solution.py:91
  27.1 9.0 %collective-permute-start.8 = (bf16[256,512]{1,0:T(8,128)(2,1)S(1)}, bf16[256,512]{1,0:T(8,128)(2,1)S(1)}, u32[]{:S(2)}, u32[]{:S(2)}) collective-permute-start(bf16[256,512]{1,0:T(8,128)(2,1)S(1)} %slice.14), channel_id=1, source_target_pairs={{0,12},{1,13},{2,14},{3,15},{4,0},{5,1},{6,2},{7,3},{8,4},{9,5},{1... | collective-permute-start | bytes 786440 | tf_op jit(solution)/shard_map/ppermute | solution.py:91
  29.0 12.1 %collective-permute-start.7 = (bf16[256,512]{1,0:T(8,128)(2,1)S(1)}, bf16[256,512]{1,0:T(8,128)(2,1)S(1)}, u32[]{:S(2)}, u32[]{:S(2)}) collective-permute-start(bf16[256,512]{1,0:T(8,128)(2,1)S(1)} %collective-permute-done.2.refs_7_), channel_id=1, source_target_pairs={{0,4},{1,5},{2,6},{3,7},{4,8},{5,9},{6,10},{7,11},{8,12},{9,13},{1... | collective-permute-start | bytes 786440 | tf_op jit(solution)/shard_map/ppermute | solution.py:91
  41.1 5.0 %collective-permute-start.14 = (bf16[1280,512]{1,0:T(8,128)(2,1)S(1)}, bf16[1280,512]{1,0:T(8,128)(2,1)S(1)}, u32[]{:S(2)}, u32[]{:S(2)}) collective-permute-start(bf16[1280,512]{1,0:T(8,128)(2,1)S(1)} %pad_maximum_fusion), channel_id=1, source_target_pairs={{0,1},{1,0},{2,3},{3,2},{4,5},{5,4},{6,7},{7,6},{8,9},{9,8},{10,11... | collective-permute-start | bytes 3932168 | tf_op jit(solution)/shard_map/ppermute | solution.py:91
  41.3 17.0 %collective-permute-start.10 = (bf16[512,512]{1,0:T(8,128)(2,1)S(1)}, bf16[512,512]{1,0:T(8,128)(2,1)S(1)}, u32[]{:S(2)}, u32[]{:S(2)}) collective-permute-start(bf16[512,512]{1,0:T(8,128)(2,1)S(1)} %get-tuple-element.122), channel_id=1, source_target_pairs={{0,2},{1,3},{2,0},{3,1},{4,6},{5,7},{6,4},{7,5},{8,10},{9,11},{10,... | collective-permute-start | bytes 1572872 | tf_op jit(solution)/shard_map/ppermute | solution.py:91
  42.9 15.4 %collective-permute-start.11 = (bf16[512,512]{1,0:T(8,128)(2,1)S(1)}, bf16[512,512]{1,0:T(8,128)(2,1)S(1)}, u32[]{:S(2)}, u32[]{:S(2)}) collective-permute-start(bf16[512,512]{1,0:T(8,128)(2,1)S(1)} %get-tuple-element.121), channel_id=1, source_target_pairs={{0,16},{1,17},{2,18},{3,19},{4,20},{5,21},{6,22},{7,23},{8,24},{9,... | collective-permute-start | bytes 1572872 | tf_op jit(solution)/shard_map/ppermute | solution.py:91
  44.1 14.2 %collective-permute-start.12 = (bf16[352,512]{1,0:T(8,128)(2,1)S(1)}, bf16[352,512]{1,0:T(8,128)(2,1)S(1)}, u32[]{:S(2)}, u32[]{:S(2)}) collective-permute-start(bf16[352,512]{1,0:T(8,128)(2,1)S(1)} %pad_maximum_fusion.7), channel_id=1, source_target_pairs={{0,12},{1,13},{2,14},{3,15},{4,0},{5,1},{6,2},{7,3},{8,4},{9,5},{1... | collective-permute-start | bytes 1081352 | tf_op jit(solution)/shard_map/ppermute | solution.py:91
  45.9 12.4 %collective-permute-start.13 = (bf16[96,512]{1,0:T(8,128)(2,1)S(1)}, bf16[96,512]{1,0:T(8,128)(2,1)S(1)}, u32[]{:S(2)}, u32[]{:S(2)}) collective-permute-start(bf16[96,512]{1,0:T(8,128)(2,1)S(1)} %get-tuple-element.97), channel_id=1, source_target_pairs={{0,4},{1,5},{2,6},{3,7},{4,8},{5,9},{6,10},{7,11},{8,12},{9,13},{1... | collective-permute-start | bytes 294920 | tf_op jit(solution)/shard_map/ppermute | solution.py:91
  46.2 15.6 %collective-permute-start.15 = (bf16[96,512]{1,0:T(8,128)(2,1)S(1)}, bf16[96,512]{1,0:T(8,128)(2,1)S(1)}, u32[]{:S(2)}, u32[]{:S(2)}) collective-permute-start(bf16[96,512]{1,0:T(8,128)(2,1)S(1)} %get-tuple-element.100), channel_id=1, source_target_pairs={{0,8},{1,9},{2,10},{3,11},{4,12},{5,13},{6,14},{7,15},{8,0},{9,1},... | collective-permute-start | bytes 294920 | tf_op jit(solution)/shard_map/ppermute | solution.py:91
  61.9 3.5 %collective-permute-start.17 = (bf16[1280,512]{1,0:T(8,128)(2,1)S(1)}, bf16[1280,512]{1,0:T(8,128)(2,1)S(1)}, u32[]{:S(2)}, u32[]{:S(2)}) collective-permute-start(bf16[1280,512]{1,0:T(8,128)(2,1)S(1)} %pad_maximum_fusion.1), channel_id=1, source_target_pairs={{0,1},{1,0},{2,3},{3,2},{4,5},{5,4},{6,7},{7,6},{8,9},{9,8},{10,11... | collective-permute-start | bytes 3932168 | tf_op jit(solution)/shard_map/ppermute | solution.py:91
  62.7 2.8 %collective-permute-start.16 = (f32[32,512]{1,0:T(8,128)S(1)}, f32[32,512]{1,0:T(8,128)S(1)}, u32[]{:S(2)}, u32[]{:S(2)}) collective-permute-start(f32[32,512]{1,0:T(8,128)S(1)} %get-tuple-element.116.refs_7_), channel_id=1, source_target_pairs={{0,1},{1,0},{2,3},{3,2},{4,5},{5,4},{6,7},{7,6},{8,9},{9,8},{10,11... | collective-permute-start | bytes 196616 | tf_op jit(solution)/shard_map/ppermute | solution.py:91

commit v4 on v3

--- a/solution.py
+++ b/solution.py
@@ -114,15 +114,7 @@
     rows, columns = quant_codes.shape
     half = rows // 2
 
-    def kernel(place_ref, codes_hbm, scales_hbm, own_ref, first_ref, codes_ref, scales_ref, sems):
-        copies = [
-            pltpu.make_async_copy(scales_hbm, scales_ref, sems.at[0]),
-            pltpu.make_async_copy(codes_hbm, codes_ref, sems.at[1]),
-        ]
-        for copy in copies:
-            copy.start()
-        for copy in copies:
-            copy.wait()
+    def kernel(place_ref, codes_ref, scales_ref, own_ref, first_ref):
         g = place_ref[0]
         for i in range(rows // BLOCK):
             source = lax.rem(g * (half // BLOCK) + i, rows // BLOCK)
@@ -141,13 +133,8 @@
             jax.ShapeDtypeStruct((rows, columns), jnp.bfloat16),
             jax.ShapeDtypeStruct((half, columns), jnp.bfloat16),
         ],
-        in_specs=[scalars(), in_hbm(), in_hbm()],
+        in_specs=[scalars(), whole(), scalars()],
         out_specs=[whole()] * 2,
-        scratch_shapes=[
-            pltpu.VMEM(quant_codes.shape, quant_codes.dtype),
-            pltpu.SMEM(block_scales.shape, block_scales.dtype),
-            pltpu.SemaphoreType.DMA((2,)),
-        ],
         compiler_params=params(),
         cost_estimate=LITTLE,
         name="dequantize",
@@ -164,78 +151,48 @@
     packed = chips * part + up_part
 
     def kernel(
-        place_ref, act_ref, down_ref, up_ref, cot_ref, latent_ref, lgrad_ref, own_ref, away_ref,
-        total, lgrad_t,
+        place_ref, act_hbm, down_ref, up_ref, cot_ref, latent_ref, lgrad_ref, terms_ref,
+        act_ref, total, lgrad_t, sems,
     ):
-        step = pl.program_id(0)
         y, c = place_ref[2], place_ref[3]
-
-        @pl.when(step == 0)
-        def _():
-            total[...] = jnp.zeros_like(total)
-            held = weight_transpose(cot_ref[...], up_ref[...]).astype(jnp.bfloat16)
-            lgrad_ref[...] = held
-            lgrad_t[...] = weight_transpose(up_ref[...], cot_ref[...]).astype(jnp.bfloat16)
-
-        block = act_ref[...]
-        total[...] += weight_transpose(block, down_ref[...])
-        term = jnp.dot(lgrad_t[...], block, preferred_element_type=jnp.float32)
-        z_of, y_of = step // 2, step % 2
-        here = jnp.where(y_of == y, NZ, 0) + z_of
-        at = pl.ds(pl.multiple_of(here * part, part), part)
-
-        @pl.when(c == 0)
-        def _():
-            own_ref[:, at] = term[:, :part]
-            away_ref[:, at] = term[:, part:]
-
-        @pl.when(c == 1)
-        def _():
-            own_ref[:, at] = term[:, part:]
-            away_ref[:, at] = term[:, :part]
-
-        @pl.when(step == chips - 1)
-        def _():
-            latent = total[...].astype(jnp.bfloat16)
-            latent_ref[...] = latent
-            both = leading(latent, cot_ref[...])
-
-            @pl.when(c == 0)
-            def _():
-                own_ref[:, chips * part :] = both[:, :up_part]
-                away_ref[:, chips * part :] = both[:, up_part:]
-
-            @pl.when(c == 1)
-            def _():
-                own_ref[:, chips * part :] = both[:, up_part:]
-                away_ref[:, chips * part :] = both[:, :up_part]
-
-    fixed = lambda shape: pl.BlockSpec(shape, lambda i: (0,) * len(shape))
+        copies = []
+        for i in range(chips):
+            at = slice(i * chunk, (i + 1) * chunk)
+            copies.append(pltpu.make_async_copy(act_hbm.at[:, at], act_ref.at[i], sems.at[i]))
+            copies[-1].start()
+        lgrad_ref[...] = weight_transpose(cot_ref[...], up_ref[...]).astype(jnp.bfloat16)
+        lgrad_t[...] = weight_transpose(up_ref[...], cot_ref[...]).astype(jnp.bfloat16)
+        for i in range(chips):
+            copies[i].wait()
+            term = jnp.dot(lgrad_t[...], act_ref[i], preferred_element_type=jnp.float32)
+            here = jnp.where(i % 2 == y, NZ, 0) + i // 2
+            at = pl.ds(pl.multiple_of(here * part, part), part)
+            terms_ref[c, :, at] = term[:, :part]
+            terms_ref[1 - c, :, at] = term[:, part:]
+            latent = weight_transpose(act_ref[i], down_ref[:, i * chunk : (i + 1) * chunk])
+            if i == 0:
+                total[...] = latent
+            else:
+                total[...] += latent
+        latent_ref[...] = total[...].astype(jnp.bfloat16)
+        term = leading(latent_ref[...], cot_ref[...])
+        terms_ref[c, :, chips * part :] = term[:, :up_part]
+        terms_ref[1 - c, :, chips * part :] = term[:, up_part:]
+
     return pl.pallas_call(
         kernel,
-        grid=(chips,),
         out_shape=[
             jax.ShapeDtypeStruct((tokens, rank), jnp.bfloat16),
             jax.ShapeDtypeStruct((tokens, rank), jnp.bfloat16),
-            jax.ShapeDtypeStruct((rank, packed), jnp.float32),
-            jax.ShapeDtypeStruct((rank, packed), jnp.float32),
+            jax.ShapeDtypeStruct((2, rank, packed), jnp.float32),
         ],
-        in_specs=[
-            scalars(),
-            pl.BlockSpec((tokens, chunk), lambda i: (0, i)),
-            pl.BlockSpec((rank, chunk), lambda i: (0, i)),
-            fixed((rank, features)),
-            fixed((tokens, features)),
-        ],
-        out_specs=[
-            fixed((tokens, rank)),
-            fixed((tokens, rank)),
-            fixed((rank, packed)),
-            fixed((rank, packed)),
-        ],
+        in_specs=[scalars(), in_hbm()] + [whole()] * 3,
+        out_specs=[whole()] * 3,
         scratch_shapes=[
+            pltpu.VMEM((chips, tokens, chunk), jnp.bfloat16),
             pltpu.VMEM((tokens, rank), jnp.float32),
             pltpu.VMEM((rank, tokens), jnp.bfloat16),
+            pltpu.SemaphoreType.DMA((chips,)),
         ],
         compiler_params=params(),
         cost_estimate=LITTLE,
@@ -251,24 +208,22 @@
 def add_cores(own, came, up_part):
     rank, packed = own.shape
     part = (packed - up_part) // (2 * NZ)
-    half = NZ * part
 
     def kernel(own_ref, came_ref, message_ref, kept_ref):
         for z in range(NZ):
+            to = slice(z * rank, (z + 1) * rank)
             at = slice(z * part, (z + 1) * part)
-            message_ref[z * rank : (z + 1) * rank, :] = (
-                own_ref[:, at] + came_ref[:, at]
-            ).astype(jnp.bfloat16)
-        kept_ref[...] = own_ref[:, half : 2 * half] + came_ref[:, half : 2 * half]
-        message_ref[NZ * rank :, :] = fold(
-            own_ref[:, 2 * half :] + came_ref[:, 2 * half :]
-        ).astype(jnp.bfloat16)
+            message_ref[to, :] = (own_ref[:, at] + came_ref[:, at]).astype(jnp.bfloat16)
+            at = slice((NZ + z) * part, (NZ + z + 1) * part)
+            kept_ref[to, :] = own_ref[:, at] + came_ref[:, at]
+        at = slice(2 * NZ * part, None)
+        message_ref[NZ * rank :, :] = fold(own_ref[:, at] + came_ref[:, at]).astype(jnp.bfloat16)
 
     return pl.pallas_call(
         kernel,
         out_shape=[
             jax.ShapeDtypeStruct((NZ * rank + rank // 2, part), jnp.bfloat16),
-            jax.ShapeDtypeStruct((rank, half), jnp.float32),
+            jax.ShapeDtypeStruct((NZ * rank, part), jnp.float32),
         ],
         in_specs=[whole()] * 2,
         out_specs=[whole()] * 2,
@@ -276,63 +231,6 @@
         cost_estimate=LITTLE,
         name="add_cores",
     )(own, came)
-
-
-def add_y(place, kept, sent, came, came_from):
-    rank, half = kept.shape
-    part = half // NZ
-    rows = rank + rank // 2
-
-    def kernel(place_ref, kept_ref, sent_ref, came_ref, own_ref, up_ref, far_ref, down_ref):
-        z = place_ref[1]
-        tail = sent_ref[NZ * rank :, :].astype(jnp.float32) + came_ref[
-            came_from + NZ * rank :, :
-        ].astype(jnp.float32)
-        for shift, out_ref in ((0, own_ref), (1, up_ref), (2, far_ref), (3, down_ref)):
-            to = lax.rem(z + shift, NZ)
-            kept_at = pl.ds(pl.multiple_of(to * part, part), part)
-            came_at = pl.ds(pl.multiple_of(came_from + to * rank, rank), rank)
-            summed = kept_ref[:, kept_at] + came_ref[came_at, :].astype(jnp.float32)
-            out_ref[:rank, :] = summed.astype(out_ref.dtype)
-            out_ref[rank:, :] = tail.astype(jnp.bfloat16).astype(out_ref.dtype)
-
-    return pl.pallas_call(
-        kernel,
-        out_shape=[jax.ShapeDtypeStruct((rows, part), jnp.float32)]
-        + [jax.ShapeDtypeStruct((rows, part), jnp.bfloat16)] * 3,
-        in_specs=[scalars()] + [whole()] * 3,
-        out_specs=[whole()] * 4,
-        compiler_params=params(),
-        cost_estimate=LITTLE,
-        name="add_y",
-    )(place, kept, sent, came)
-
-
-def add_z(own, from_down, from_far, from_up, up_from, factor):
-    rows, part = own.shape
-    rank = rows * 2 // 3
-
-    def kernel(own_ref, a_ref, b_ref, c_ref, gd_ref, gu_ref):
-        f32 = jnp.float32
-        summed = (own_ref[...] + b_ref[...].astype(f32)) + (
-            a_ref[...].astype(f32) + c_ref[up_from : up_from + rows, :].astype(f32)
-        )
-        summed = summed * factor
-        gd_ref[...] = summed[:rank, :]
-        gu_ref[...] = summed[rank:, :]
-
-    return pl.pallas_call(
-        kernel,
-        out_shape=[
-            jax.ShapeDtypeStruct((rank, part), jnp.float32),
-            jax.ShapeDtypeStruct((rows - rank, part), jnp.float32),
-        ],
-        in_specs=[whole()] * 4,
-        out_specs=[whole()] * 2,
-        compiler_params=params(),
-        cost_estimate=LITTLE,
-        name="add_z",
-    )(own, from_down, from_far, from_up)
 
 
 def multiply(
@@ -465,57 +363,77 @@
     own, first = dequantize_shard(place, quant_codes, block_scales)
     own, first, place = barrier((own, first, place))
 
-    y1, up1, down1 = send(own, OVER_Y), send(first, Z_UP), send(first, Z_DOWN)
-    swap1 = send(own, OVER_CORE)
+    def swap(*arrays):
+        return block(lambda *parts: send(join(*parts), OVER_CORE), *arrays)
+
+    down1, up1, y1 = send(first, Z_DOWN), send(first, Z_UP), send(own[half:], OVER_Y)
 
     def lowrank(place):
-        latent, lgrad, own_terms, away_terms = local_gradients(
+        latent, lgrad, terms = local_gradients(
             place, activations, down_t, lowrank_up_factor, cotangent
         )
-        came = send(away_terms, OVER_CORE)
-        terms_y, kept = add_cores(own_terms, came, up_part)
+        terms_y, kept = add_cores(terms[0], send(terms[1], OVER_CORE), up_part)
         return latent, lgrad, terms_y, kept
 
     latent, lgrad, terms_y, kept = block(lowrank, place)
-    keys = [(0, 0, 0), (0, 0, 1)]
+    came_y = send(terms_y, OVER_Y)
+    down1, up1, y1, kept = barrier((down1, up1, y1, kept))
+
+    y2, x2 = send(join(up1, first), OVER_Y), send(join(up1, down1), OVER_X)
+    down2 = send(y1, Z_DOWN)
+    rank = down_t.shape[0]
+    z = place[1]
+    summed = kept + came_y[: NZ * rank].astype(jnp.float32)
+    summed_up = terms_y[NZ * rank :].astype(jnp.float32) + came_y[NZ * rank :].astype(jnp.float32)
+    summed_up = summed_up.astype(jnp.bfloat16)
+
+    def part_of(shift):
+        return lax.dynamic_slice_in_dim(summed, ((z + shift) & (NZ - 1)) * rank, rank)
+
+    own_part, next_part = part_of(0), part_of(1)
+    far_part = join(part_of(2).astype(jnp.bfloat16), summed_up)
+    last_part = join(part_of(3).astype(jnp.bfloat16), summed_up)
+    up2 = send(join(up1, far_part), Z_UP)
+    swap2 = swap(own, up1, down1, y1)
+    keys = [(0, 0, 0), (0, 0, 1), (1, 0, 0), (3, 0, 0), (0, 1, 1)]
     done = products(
-        listed(own, 0, *keys) + listed(swap1, 1, *keys), begin=[latent, lowrank_up_factor]
-    )
-    y1, up1, down1, terms_y, kept, done = barrier((y1, up1, down1, terms_y, kept, done))
-
-    y2, x2 = send(join(up1, terms_y), OVER_Y), send(join(up1, down1), OVER_X)
-    up2, down2 = send(up1, Z_UP), send(y1[half:], Z_DOWN)
-    swap2 = send(join(up1, down1, y1), OVER_CORE)
-    keys = [(1, 0, 0), (3, 0, 0), (0, 1, 0), (0, 1, 1)]
+        listed(own, 0, *keys[:2])
+        + listed(up1, 0, keys[2])
+        + listed(down1, 0, keys[3])
+        + listed(y1, 0, keys[4])
+        + listed(swap2, 1, *keys),
+        begin=[latent, lowrank_up_factor],
+    )
+    y2, x2, down2, up2, own_part, next_part, last_part, summed_up, done = barrier(
+        (y2, x2, down2, up2, own_part, next_part, last_part, summed_up, done)
+    )
+
+    y3, x3 = send(join(down1, up2[:half]), OVER_Y), send(join(up2[:half], y2[:half]), OVER_X)
+    down3 = send(join(down2, last_part), Z_DOWN)
+    came_up = up2[half:]
+    next_part = next_part + came_up[:rank].astype(jnp.float32)
+    up3 = send(join(next_part.astype(jnp.bfloat16), came_up[rank:]), Z_UP)
+    swap3 = swap(y2, x2, up2[:half], down2)
+    keys = [(1, 1, 0), (0, 1, 0), (1, 0, 1), (3, 0, 1), (2, 0, 0), (3, 1, 1)]
     done = products(
-        listed(up1, 0, keys[0])
-        + listed(down1, 0, keys[1])
-        + listed(y1, 0, *keys[2:])
-        + listed(swap2, 1, *keys),
-        so_far=done,
-    )
-    y2, x2, up2, down2, done = barrier((y2, x2, up2, down2, done))
-
-    own_part, to_up, to_far, to_down = add_y(place, kept, terms_y, y2, half)
-    y3, x3 = send(join(down1, up2), OVER_Y), send(join(up2, y2[:half]), OVER_X)
-    down3, up3 = send(join(down2, to_down), Z_DOWN), send(to_up, Z_UP)
-    swap3 = send(join(y2[:half], x2, up2, down2), OVER_CORE)
-    swap3, to_far = barrier((swap3, to_far))
-    far3 = send(to_far, Z_FAR)
-    keys = [(1, 1, 0), (1, 0, 1), (3, 0, 1), (2, 0, 0), (3, 1, 1)]
-    done = products(
-        listed(y2, 0, keys[0])
-        + listed(x2, 0, *keys[1:3])
-        + listed(up2, 0, keys[3])
-        + listed(down2, 0, keys[4])
+        listed(y2, 0, *keys[:2])
+        + listed(x2, 0, *keys[2:4])
+        + listed(up2, 0, keys[4])
+        + listed(down2, 0, keys[5])
         + listed(swap3, 1, *keys),
         so_far=done,
     )
-    y3, x3, down3, up3, far3, done = barrier((y3, x3, down3, up3, far3, done))
+    y3, x3, down3, up3, came_up, own_part, summed_up, done = barrier(
+        (y3, x3, down3, up3, came_up, own_part, summed_up, done)
+    )
 
     swap4 = send(join(y3, x3, down3[:half]), OVER_CORE)
-    grad_down_t, up_own = add_z(own_part, up3, far3, down3, half, factor)
+    wide = lambda array: array.astype(jnp.float32)
+    up_own = factor * (
+        (wide(summed_up) + wide(up3[rank:])) + (wide(came_up[rank:]) + wide(down3[half + rank :]))
+    )
     up_came = send(up_own, OVER_CORE)
+    grad_down_t = factor * (own_part + (wide(up3[:rank]) + wide(down3[half : half + rank])))
     keys = [(3, 1, 0), (2, 1, 0), (2, 0, 1), (1, 1, 1), (2, 1, 1)]
     done = products(
         listed(y3, 0, *keys[:2]) + listed(x3, 0, *keys[2:4]) + listed(down3, 0, keys[4]),

time: 68.8 us -> 77.4 us (1.13)
  other arithmetic: 0.5 us -> 10.5 us
  waiting for transfers between devices: 22.9 us -> 13.4 us
  between operations: 0.91 us -> 4.27 us
  local copies, waits for them, and re-layouts: 1.8 us -> 5.06 us
  starting transfers between devices: 17.5 us -> 20 us
  Pallas kernels: 24.8 us -> 23.6 us
    ppermute x18 -> x17, waiting for transfers between devices: 22.9 us -> 13.4 us  [send(): return lax.ppermute(array, AXES, pairs)]
    concatenate x7 -> x9, other arithmetic: 0.42 us -> 8.06 us  [per_device(): join = lambda *arrays: jnp.concatenate(arrays, axis=0)]
    ppermute x18 -> x17, starting transfers between devices: 17.5 us -> 20 us  [send(): return lax.ppermute(array, AXES, pairs)]
    pallas_call x3 -> x1, Pallas kernels: 8.09 us -> 5.82 us  [local_gradients(): pl.pallas_call(kernel, out_shape=[jax.ShapeDtypeStruct((tokens, rank), jn...]
    slice x1 -> x6, local copies, waits for them, and re-layouts: 0.02 us -> 1.88 us  [the longest x1 0.72 us: per_device(): own[half:]]
    pallas_call x5 -> x4, Pallas kernels: 15.3 us -> 17 us  [multiply(): pl.pallas_call(kernel, out_shape=out_shape, in_specs=specs + [whole()] *...]
    transpose x0 -> x1, other arithmetic: none -> 1.52 us  [per_device(): return (projected, gradient, grad_down_t.T, grad_up)]
    slice x1, local copies, waits for them, and re-layouts: 0.02 us -> 1.17 us  [per_device(): y2[:half]]
  transfers between devices with their start and end apart: 18 -> 17, of which waited for: 5 -> 4; matrix products, arithmetic and copies ran while one was open for 0% -> 14% of each run, Pallas kernels for 30% -> 26%
where the time goes in v4:
time: 77.4 us; the launch traced here: 76.9 us
  Pallas kernels  23.6 us (30%)
  starting transfers between devices  20 us (26%)
  waiting for transfers between devices  13.4 us (17%)
  other arithmetic  10.5 us (14%)
  local copies, waits for them, and re-layouts  5.06 us (7%)
  between operations  4.27 us (6%)
    ppermute x17, starting transfers between devices, send(): return lax.ppermute(array, AXES, pairs)  20 us
    pallas_call x4, Pallas kernels, multiply(): pl.pallas_call(kernel, out_shape=out_shape, in_specs=specs + [whole()] *...  17 us
    ppermute x17, waiting for transfers between devices, send(): return lax.ppermute(array, AXES, pairs)  13.4 us
    concatenate x9, other arithmetic, per_device(): join = lambda *arrays: jnp.concatenate(arrays, axis=0)  8.06 us
    pallas_call x1, Pallas kernels, local_gradients(): pl.pallas_call(kernel, out_shape=[jax.ShapeDtypeStruct((tokens, rank), jn...  5.82 us
    unnamed x30, local copies, waits for them, and re-layouts  1.79 us
  transfers between devices with their start and end apart: 17, of which 4 were waited for; matrix products, arithmetic and copies ran while one was open for 14% of the time, Pallas kernels for 26%

profile of v4, /device:TPU:0, one launch (start us, length us, event | category | flops | bytes accessed | tf_op | source)
XLA Modules:
  0.0 76.9 jit_solution(9180808791311142255)
XLA Ops:
  0.6 0.1 pad_add_fusion.place_ref.refs_0_
  0.7 1.0 %copy-done.1 = bf16[512,512]{1,0:T(8,128)(2,1)S(1)} copy-done((bf16[512,512]{1,0:T(8,128)(2,1)S(1)}, bf16[512,512]{1,0:T(8,128)(2,1)}, u32[]{:S(2)}) %copy-start.1) | copy-done | bytes 524312
  1.8 0.7 copy-done.2
  2.4 0.7 dequantize.1
  3.2 5.1 %collective-permute-start.3 = (bf16[256,512]{1,0:T(8,128)(2,1)S(1)}, bf16[256,512]{1,0:T(8,128)(2,1)S(1)}, u32[]{:S(2)}, u32[]{:S(2)}) collective-permute-start(bf16[256,512]{1,0:T(8,128)(2,1)S(1)} %get-tuple-element.99), channel_id=1, source_target_pairs={{0,12},{1,13},{2,14},{3,15},{4,0},{5,1},{6,2},{7,3},{8,4},{9,5},{1... | collective-permute-start | bytes 786440 | tf_op jit(solution)/shard_map/ppermute | solution.py:91
  8.3 0.7 slice.64
  9.0 1.5 %collective-permute-start.5 = (bf16[256,512]{1,0:T(8,128)(2,1)}, bf16[256,512]{1,0:T(8,128)(2,1)}, u32[]{:S(2)}, u32[]{:S(2)}) collective-permute-start(bf16[256,512]{1,0:T(8,128)(2,1)} %slice.64), channel_id=1, source_target_pairs={{0,2},{1,3},{2,0},{3,1},{4,6},{5,7},{6,4},{7,5},{8,10},{9,11},{10,... | collective-permute-start | bytes 786440 | tf_op jit(solution)/shard_map/ppermute | solution.py:91
  10.5 0.6 fusion
  11.7 8.9 %conditional.3 = (bf16[256,64]{1,0:T(8,128)(2,1)S(1)}, bf16[256,64]{1,0:T(8,128)(2,1)S(1)}, bf16[288,512]{1,0:T(8,128)(2,1)S(1)}, f32[256,512]{1,0:T(8,128)S(1)}) conditional(s32[]{:T(128)} %bitcast.7, () %tuple.33, (s32[4]{0:T(128)S(1)}, bf16[256,8192]{1,0:T(8,128)(2,1)}, bf16[64,8192]{1,0:T(8,128)(2,1)}, bf16[64,512]{1,0:T(8,128)(2,1)}, ...), branch_computations={%region_0.0_spmd, %region_1.0_spmd} | conditional | flops 2 | bytes 8912970 | solution.py:361
  11.8 5.8 %local_gradients.1 = (bf16[256,64]{1,0:T(8,128)(2,1)S(1)}, bf16[256,64]{1,0:T(8,128)(2,1)S(1)}, f32[2,64,4352]{2,1,0:T(8,128)S(1)}) custom-call(s32[4]{0:T(128)S(1)} %get-tuple-element.27.place_ref, bf16[256,8192]{1,0:T(8,128)(2,1)} %get-tuple-element.28.act_hbm, bf16[64,8192]{1,0:T(8,128)(2,1)} %get-tuple-element.34.down_ref, ...), custom_call_target="tpu_custom_call" | custom-call | flops 1 | bytes 1 | tf_op jit(solution)/shard_map/cond/branch_1_fun/local_gradients/pallas_call | solution.py:182
  17.6 0.1 slice_bitcast_fusion
  17.7 0.1 collective-permute-start
  17.8 2.7 %collective-permute-done.came_ref = f32[64,4352]{1,0:T(8,128)S(1)} collective-permute-done((f32[64,4352]{1,0:T(8,128)S(1)}, f32[64,4352]{1,0:T(8,128)S(1)}, u32[]{:S(2)}, u32[]{:S(2)}) %collective-permute-start) | collective-permute-done | bytes 1114144 | tf_op jit(solution)/shard_map/cond/branch_1_fun/ppermute | solution.py:91
  20.6 0.1 add_cores.1
  20.7 0.6 collective-permute-start.9
  22.6 1.1 %pad_maximum_fusion.3 = (bf16[512,512]{1,0:T(8,128)(2,1)}, bf16[512,512]{1,0:T(8,128)(2,1)}) fusion(bf16[256,512]{1,0:T(8,128)(2,1)S(1)} %collective-permute-done.4.refs_8_, bf16[256,512]{1,0:T(8,128)(2,1)S(1)} %collective-permute-done.3.refs_9_, bf16[256,512]{1,0:T(8,128)(2,1)S(1)} %get-tuple-element.99), kind=kLoop, calls=%fused_computation.5 | loop fusion | flops 1835008 | bytes 1835008 | tf_op jit(solution)/shard_map/concatenate | solution.py:348
  23.6 1.5 %collective-permute-start.6 = (bf16[512,512]{1,0:T(8,128)(2,1)}, bf16[512,512]{1,0:T(8,128)(2,1)}, u32[]{:S(2)}, u32[]{:S(2)}) collective-permute-start(bf16[512,512]{1,0:T(8,128)(2,1)} %get-tuple-element.145), channel_id=1, source_target_pairs={{0,2},{1,3},{2,0},{3,1},{4,6},{5,7},{6,4},{7,5},{8,10},{9,11},{10,... | collective-permute-start | bytes 1572872 | tf_op jit(solution)/shard_map/ppermute | solution.py:91
  25.2 1.5 %collective-permute-start.7 = (bf16[512,512]{1,0:T(8,128)(2,1)}, bf16[512,512]{1,0:T(8,128)(2,1)}, u32[]{:S(2)}, u32[]{:S(2)}) collective-permute-start(bf16[512,512]{1,0:T(8,128)(2,1)} %get-tuple-element.144), channel_id=1, source_target_pairs={{0,16},{1,17},{2,18},{3,19},{4,20},{5,21},{6,22},{7,23},{8,24},{9,... | collective-permute-start | bytes 1572872 | tf_op jit(solution)/shard_map/ppermute | solution.py:91
  26.7 3.9 %collective-permute-done.9 = bf16[288,512]{1,0:T(8,128)(2,1)S(1)} collective-permute-done((bf16[288,512]{1,0:T(8,128)(2,1)S(1)}, bf16[288,512]{1,0:T(8,128)(2,1)S(1)}, u32[]{:S(2)}, u32[]{:S(2)}) %collective-permute-start.9) | collective-permute-done | bytes 294944 | tf_op jit(solution)/shard_map/ppermute | solution.py:91
  30.6 0.1 convert_add_fusion
  30.7 0.8 %pad_maximum_fusion.7 = bf16[352,512]{1,0:T(8,128)(2,1)} fusion(bf16[32,512]{1,0:T(8,128)(2,1)S(1)} %add_convert_fusion.1, bf16[64,512]{1,0:T(8,128)(2,1)S(1)} %get-tuple-element.139, bf16[256,512]{1,0:T(8,128)(2,1)S(1)} %collective-permute-done.4.refs_8_), kind=kLoop, calls=%fused_computation.10 | loop fusion | flops 1081344 | bytes 720896 | tf_op jit(solution)/shard_map/concatenate | solution.py:348
  31.6 3.8 %collective-permute-start.8 = (bf16[256,512]{1,0:T(8,128)(2,1)}, bf16[256,512]{1,0:T(8,128)(2,1)S(1)}, u32[]{:S(2)}, u32[]{:S(2)}) collective-permute-start(bf16[256,512]{1,0:T(8,128)(2,1)} %collective-permute-done.5.refs_10_), channel_id=1, source_target_pairs={{0,12},{1,13},{2,14},{3,15},{4,0},{5,1},{6,2},{7,3},{8,4},{9,5},{1... | collective-permute-start | bytes 786440 | tf_op jit(solution)/shard_map/ppermute | solution.py:91
  36.7 0.0 copy-start.5
  36.8 4.4 %conditional.4 = (bf16[1280,512]{1,0:T(8,128)(2,1)}) conditional(s32[]{:T(128)} %bitcast.7, () %tuple.36, (bf16[512,512]{1,0:T(8,128)(2,1)S(1)}, bf16[256,512]{1,0:T(8,128)(2,1)S(1)}, bf16[256,512]{1,0:T(8,128)(2,1)S(1)}, bf16[256,512]{1,0:T(8,128)(2,1)}) %tuple.37), branch_computations={%region_2.0_spmd, %region_3.0_spmd} | conditional | flops 5242880 | bytes 7864368 | solution.py:361
  36.8 1.1 %pad_maximum_fusion = bf16[1280,512]{1,0:T(8,128)(2,1)S(1)} fusion(bf16[256,512]{1,0:T(8,128)(2,1)} %get-tuple-element.45, bf16[256,512]{1,0:T(8,128)(2,1)S(1)} %get-tuple-element.44, bf16[256,512]{1,0:T(8,128)(2,1)S(1)} %get-tuple-element.43, bf16[512,512]{1,0:T(8,128)(2,1)S(1)} %get-tuple-element.42), kind=kLoop, calls=%fused_computation.2 | loop fusion | flops 5242880 | bytes 2621440 | tf_op jit(solution)/shard_map/cond/branch_1_fun/concatenate | solution.py:348
  37.9 0.1 collective-permute-start.1
  38.0 3.2 %collective-permute-done.1 = bf16[1280,512]{1,0:T(8,128)(2,1)} collective-permute-done((bf16[1280,512]{1,0:T(8,128)(2,1)S(1)}, bf16[1280,512]{1,0:T(8,128)(2,1)}, u32[]{:S(2)}, u32[]{:S(2)}) %collective-permute-start.1) | collective-permute-done | bytes 1310752 | tf_op jit(solution)/shard_map/cond/branch_1_fun/ppermute | solution.py:91
  41.2 5.4 %multiply.4 = (f32[256,512]{1,0:T(8,128)S(1)}, bf16[256,8192]{1,0:T(8,128)(2,1)}) custom-call(s32[4]{0:T(128)S(1)} %pad_add_fusion.place_ref.refs_0_, bf16[256,8192]{1,0:T(8,128)(2,1)} %refs_1_.7, bf16[64,8192]{1,0:T(8,128)(2,1)S(1)} %bitcast.17, bf16[256,512]{1,0:T(8,128)(2,1)S(1)} %copy-done.5, bf16[256,64]{1,0:T(8,128)(2,1)S(1)} %get-tuple-element.98.refs_4_, ...), custom_call_target="tpu_custom_call" | custom-call | flops 1 | bytes 1 | tf_op jit(solution)/shard_map/multiply/pallas_call | solution.py:320
  46.8 1.2 %slice.70 = bf16[256,512]{1,0:T(8,128)(2,1)S(1)} slice(bf16[512,512]{1,0:T(8,128)(2,1)} %collective-permute-done.6.refs_7_), slice={[0:256], [0:512]} | slice | bytes 524288 | tf_op jit(solution)/shard_map/slice | solution.py:411
  48.0 1.1 %pad_maximum_fusion.6 = (bf16[512,512]{1,0:T(8,128)(2,1)}, bf16[512,512]{1,0:T(8,128)(2,1)}) fusion(bf16[256,512]{1,0:T(8,128)(2,1)S(1)} %slice.70, bf16[256,512]{1,0:T(8,128)(2,1)S(1)} %slice.69, bf16[256,512]{1,0:T(8,128)(2,1)S(1)} %collective-permute-done.3.refs_9_), kind=kLoop, calls=%fused_computation.8 | loop fusion | flops 2097152 | bytes 1835008 | tf_op jit(solution)/shard_map/concatenate | solution.py:348
  49.0 0.5 collective-permute-start.11
  49.5 1.5 %collective-permute-start.12 = (bf16[512,512]{1,0:T(8,128)(2,1)}, bf16[512,512]{1,0:T(8,128)(2,1)S(1)}, u32[]{:S(2)}, u32[]{:S(2)}) collective-permute-start(bf16[512,512]{1,0:T(8,128)(2,1)} %get-tuple-element.142), channel_id=1, source_target_pairs={{0,16},{1,17},{2,18},{3,19},{4,20},{5,21},{6,22},{7,23},{8,24},{9,... | collective-permute-start | bytes 1572872 | tf_op jit(solution)/shard_map/ppermute | solution.py:91
  51.0 1.7 %pad_maximum_fusion.8 = bf16[352,512]{1,0:T(8,128)(2,1)} fusion(bf16[96,512]{1,0:T(8,128)(2,1)S(1)} %pad_maximum_fusion.9, bf16[256,512]{1,0:T(8,128)(2,1)} %copy-done.9), kind=kLoop, calls=%fused_computation.11 | loop fusion | flops 720896 | bytes 720896 | tf_op jit(solution)/shard_map/concatenate | solution.py:348
  52.8 3.3 %collective-permute-start.13 = (bf16[352,512]{1,0:T(8,128)(2,1)}, bf16[352,512]{1,0:T(8,128)(2,1)S(1)}, u32[]{:S(2)}, u32[]{:S(2)}) collective-permute-start(bf16[352,512]{1,0:T(8,128)(2,1)} %pad_maximum_fusion.8), channel_id=1, source_target_pairs={{0,12},{1,13},{2,14},{3,15},{4,0},{5,1},{6,2},{7,3},{8,4},{9,5},{1... | collective-permute-start | bytes 1081352 | tf_op jit(solution)/shard_map/ppermute | solution.py:91
  56.1 0.6 pad_maximum_fusion.10
  56.8 5.1 %conditional.5 = (bf16[1536,512]{1,0:T(8,128)(2,1)}) conditional(s32[]{:T(128)} %bitcast.7, () %tuple.39, (bf16[512,512]{1,0:T(8,128)(2,1)}, bf16[512,512]{1,0:T(8,128)(2,1)}, bf16[256,512]{1,0:T(8,128)(2,1)}, bf16[256,512]{1,0:T(8,128)(2,1)}) %tuple.57), branch_computations={%region_4.0_spmd, %region_5.0_spmd} | conditional | flops 6291456 | bytes 9437232 | solution.py:361
  56.8 1.5 %pad_maximum_fusion.1 = bf16[1536,512]{1,0:T(8,128)(2,1)S(1)} fusion(bf16[256,512]{1,0:T(8,128)(2,1)} %get-tuple-element.49, bf16[256,512]{1,0:T(8,128)(2,1)} %get-tuple-element.48, bf16[512,512]{1,0:T(8,128)(2,1)} %get-tuple-element.47, bf16[512,512]{1,0:T(8,128)(2,1)} %get-tuple-element.46), kind=kLoop, calls=%fused_computation.3 | loop fusion | flops 6291456 | bytes 3145728 | tf_op jit(solution)/shard_map/cond/branch_1_fun/concatenate | solution.py:348
  58.2 0.1 collective-permute-start.2
  58.3 3.5 %collective-permute-done.2 = bf16[1536,512]{1,0:T(8,128)(2,1)} collective-permute-done((bf16[1536,512]{1,0:T(8,128)(2,1)S(1)}, bf16[1536,512]{1,0:T(8,128)(2,1)}, u32[]{:S(2)}, u32[]{:S(2)}) %collective-permute-start.2) | collective-permute-done | bytes 1572896 | tf_op jit(solution)/shard_map/cond/branch_1_fun/ppermute | solution.py:91
  61.8 6.3 %multiply.5 = (f32[256,512]{1,0:T(8,128)S(1)}, bf16[256,8192]{1,0:T(8,128)(2,1)}) custom-call(s32[4]{0:T(128)S(1)} %pad_add_fusion.place_ref.refs_0_, bf16[256,8192]{1,0:T(8,128)(2,1)} %refs_1_.7, bf16[64,8192]{1,0:T(8,128)(2,1)S(1)} %bitcast.18, bf16[256,512]{1,0:T(8,128)(2,1)} %refs_3_.7, ...), custom_call_target="tpu_custom_call", output_to_operand_aliasing={{1}: (6, {})} | custom-call | flops 1 | bytes 1 | tf_op jit(solution)/shard_map/multiply/pallas_call | solution.py:320
  68.2 0.1 pad_maximum_fusion.2
  68.3 0.2 collective-permute-start.16
  68.5 0.5 slice-done
  69.1 0.8 %add_multiply_fusion.refs_7_ = f32[32,512]{1,0:T(8,128)S(1)} fusion(bf16[32,512]{1,0:T(8,128)(2,1)S(1)} %copy-done.13, bf16[352,512]{1,0:T(8,128)(2,1)S(1)} %collective-permute-done.13.refs_9_, bf16[96,512]{1,0:T(8,128)(2,1)S(1)} %slice-done, bf16[96,512]{1,0:T(8,128)(2,1)} %collective-permute-done.14), kind=kLoop, calls=%fused_computation.18 | loop fusion | flops 131072 | bytes 196608 | tf_op jit(solution)/shard_map/mul | solution.py:432
  69.9 0.2 collective-permute-start.15
  70.1 1.5 %multiply_bitcast_fusion = f32[512,64]{0,1:T(8,128)} fusion(f32[64,512]{1,0:T(8,128)S(1)} %get-tuple-element.134, bf16[352,512]{1,0:T(8,128)(2,1)S(1)} %collective-permute-done.13.refs_9_, bf16[96,512]{1,0:T(8,128)(2,1)} %collective-permute-done.14), kind=kLoop, calls=%fused_computation.12 | loop fusion | flops 163840 | bytes 393216 | tf_op jit(solution)/shard_map/transpose | solution.py:445
  71.6 2.2 %multiply.6 = (f32[256,512]{1,0:T(8,128)S(1)}, bf16[256,8192]{1,0:T(8,128)(2,1)}) custom-call(s32[4]{0:T(128)S(1)} %pad_add_fusion.place_ref.refs_0_, bf16[256,8192]{1,0:T(8,128)(2,1)S(1)} %copy-done.3, bf16[64,8192]{1,0:T(8,128)(2,1)S(1)} %bitcast.19, bf16[256,512]{1,0:T(8,128)(2,1)S(1)} %copy-done.6, ...), custom_call_target="tpu_custom_call", output_to_operand_aliasing={{1}: (6, {})} | custom-call | flops 1 | bytes 1 | tf_op jit(solution)/shard_map/multiply/pallas_call | solution.py:320
  73.9 3.0 %multiply.7 = (bf16[256,512]{1,0:T(8,128)(2,1)}, bf16[256,8192]{1,0:T(8,128)(2,1)}, f32[64,512]{1,0:T(8,128)}) custom-call(s32[4]{0:T(128)S(1)} %pad_add_fusion.place_ref.refs_0_, bf16[256,8192]{1,0:T(8,128)(2,1)S(1)} %copy-done.3, bf16[64,8192]{1,0:T(8,128)(2,1)S(1)} %bitcast.20, bf16[256,512]{1,0:T(8,128)(2,1)S(1)} %copy-done.6, ...), custom_call_target="tpu_custom_call", output_to_operand_aliasing={{1}: (6, {})} | custom-call | flops 1 | bytes 1 | tf_op jit(solution)/shard_map/multiply/pallas_call | solution.py:320
  (52 shorter events, 0.2 us)
Async XLA Ops:
  0.7 1.0 %copy-start.1 = (bf16[512,512]{1,0:T(8,128)(2,1)S(1)}, bf16[512,512]{1,0:T(8,128)(2,1)}, u32[]{:S(2)}) copy-start(bf16[512,512]{1,0:T(8,128)(2,1)} %codes_ref.1) | copy-start | bytes 1572868
  1.8 0.7 copy-start.2
  3.1 33.6 %copy-start.7 = (bf16[512,512]{1,0:T(8,128)(2,1)}, bf16[512,512]{1,0:T(8,128)(2,1)S(1)}, u32[]{:S(2)}) copy-start(bf16[512,512]{1,0:T(8,128)(2,1)S(1)} %get-tuple-element.100.refs_7_) | copy-start | bytes 1572868
  3.2 19.4 %collective-permute-start.3 = (bf16[256,512]{1,0:T(8,128)(2,1)S(1)}, bf16[256,512]{1,0:T(8,128)(2,1)S(1)}, u32[]{:S(2)}, u32[]{:S(2)}) collective-permute-start(bf16[256,512]{1,0:T(8,128)(2,1)S(1)} %get-tuple-element.99), channel_id=1, source_target_pairs={{0,12},{1,13},{2,14},{3,15},{4,0},{5,1},{6,2},{7,3},{8,4},{9,5},{1... | collective-permute-start | bytes 786440 | tf_op jit(solution)/shard_map/ppermute | solution.py:91
  8.3 14.3 %collective-permute-start.4 = (bf16[256,512]{1,0:T(8,128)(2,1)S(1)}, bf16[256,512]{1,0:T(8,128)(2,1)S(1)}, u32[]{:S(2)}, u32[]{:S(2)}) collective-permute-start(bf16[256,512]{1,0:T(8,128)(2,1)S(1)} %get-tuple-element.99), channel_id=1, source_target_pairs={{0,4},{1,5},{2,6},{3,7},{4,8},{5,9},{6,10},{7,11},{8,12},{9,13},{1... | collective-permute-start | bytes 786440 | tf_op jit(solution)/shard_map/ppermute | solution.py:91
  9.0 13.6 %collective-permute-start.5 = (bf16[256,512]{1,0:T(8,128)(2,1)}, bf16[256,512]{1,0:T(8,128)(2,1)}, u32[]{:S(2)}, u32[]{:S(2)}) collective-permute-start(bf16[256,512]{1,0:T(8,128)(2,1)} %slice.64), channel_id=1, source_target_pairs={{0,2},{1,3},{2,0},{3,1},{4,6},{5,7},{6,4},{7,5},{8,10},{9,11},{10,... | collective-permute-start | bytes 786440 | tf_op jit(solution)/shard_map/ppermute | solution.py:91
  17.7 2.8 %collective-permute-start = (f32[64,4352]{1,0:T(8,128)S(1)}, f32[64,4352]{1,0:T(8,128)S(1)}, u32[]{:S(2)}, u32[]{:S(2)}) collective-permute-start(f32[64,4352]{1,0:T(8,128)S(1)} %get-tuple-element.136), channel_id=1, source_target_pairs={{0,1},{1,0},{2,3},{3,2},{4,5},{5,4},{6,7},{7,6},{8,9},{9,8},{10,11... | collective-permute-start | bytes 3342344 | tf_op jit(solution)/shard_map/cond/branch_1_fun/ppermute | solution.py:91
  20.7 9.9 %collective-permute-start.9 = (bf16[288,512]{1,0:T(8,128)(2,1)S(1)}, bf16[288,512]{1,0:T(8,128)(2,1)S(1)}, u32[]{:S(2)}, u32[]{:S(2)}) collective-permute-start(bf16[288,512]{1,0:T(8,128)(2,1)S(1)} %get-tuple-element.106), channel_id=1, source_target_pairs={{0,2},{1,3},{2,0},{3,1},{4,6},{5,7},{6,4},{7,5},{8,10},{9,11},{10,... | collective-permute-start | bytes 884744 | tf_op jit(solution)/shard_map/ppermute | solution.py:91
  23.6 23.1 %collective-permute-start.6 = (bf16[512,512]{1,0:T(8,128)(2,1)}, bf16[512,512]{1,0:T(8,128)(2,1)}, u32[]{:S(2)}, u32[]{:S(2)}) collective-permute-start(bf16[512,512]{1,0:T(8,128)(2,1)} %get-tuple-element.145), channel_id=1, source_target_pairs={{0,2},{1,3},{2,0},{3,1},{4,6},{5,7},{6,4},{7,5},{8,10},{9,11},{10,... | collective-permute-start | bytes 1572872 | tf_op jit(solution)/shard_map/ppermute | solution.py:91
  25.2 21.6 %collective-permute-start.7 = (bf16[512,512]{1,0:T(8,128)(2,1)}, bf16[512,512]{1,0:T(8,128)(2,1)}, u32[]{:S(2)}, u32[]{:S(2)}) collective-permute-start(bf16[512,512]{1,0:T(8,128)(2,1)} %get-tuple-element.144), channel_id=1, source_target_pairs={{0,16},{1,17},{2,18},{3,19},{4,20},{5,21},{6,22},{7,23},{8,24},{9,... | collective-permute-start | bytes 1572872 | tf_op jit(solution)/shard_map/ppermute | solution.py:91
  30.6 16.0 %copy-start.12 = (bf16[32,512]{1,0:T(8,128)(2,1)}, bf16[32,512]{1,0:T(8,128)(2,1)S(1)}, u32[]{:S(2)}) copy-start(bf16[32,512]{1,0:T(8,128)(2,1)S(1)} %add_convert_fusion.1) | copy-start | bytes 98308
  30.7 6.0 %copy-start.10 = (f32[256,512]{1,0:T(8,128)}, f32[256,512]{1,0:T(8,128)S(1)}, u32[]{:S(2)}) copy-start(f32[256,512]{1,0:T(8,128)S(1)} %convert_add_fusion) | copy-start | bytes 1572868
  31.6 15.1 %collective-permute-start.10 = (bf16[352,512]{1,0:T(8,128)(2,1)}, bf16[352,512]{1,0:T(8,128)(2,1)S(1)}, u32[]{:S(2)}, u32[]{:S(2)}) collective-permute-start(bf16[352,512]{1,0:T(8,128)(2,1)} %pad_maximum_fusion.7), channel_id=1, source_target_pairs={{0,4},{1,5},{2,6},{3,7},{4,8},{5,9},{6,10},{7,11},{8,12},{9,13},{1... | collective-permute-start | bytes 1081352 | tf_op jit(solution)/shard_map/ppermute | solution.py:91
  31.6 15.1 %collective-permute-start.8 = (bf16[256,512]{1,0:T(8,128)(2,1)}, bf16[256,512]{1,0:T(8,128)(2,1)S(1)}, u32[]{:S(2)}, u32[]{:S(2)}) collective-permute-start(bf16[256,512]{1,0:T(8,128)(2,1)} %collective-permute-done.5.refs_10_), channel_id=1, source_target_pairs={{0,12},{1,13},{2,14},{3,15},{4,0},{5,1},{6,2},{7,3},{8,4},{9,5},{1... | collective-permute-start | bytes 786440 | tf_op jit(solution)/shard_map/ppermute | solution.py:91
  36.7 4.4 %copy-start.4 = (bf16[8192,64]{0,1:T(8,128)(2,1)S(1)}, bf16[8192,64]{0,1:T(8,128)(2,1)}, u32[]{:S(2)}) copy-start(bf16[8192,64]{0,1:T(8,128)(2,1)} %param.15) | copy-start | bytes 3145732
  36.7 4.4 %copy-start.5 = (bf16[256,512]{1,0:T(8,128)(2,1)S(1)}, bf16[256,512]{1,0:T(8,128)(2,1)}, u32[]{:S(2)}) copy-start(bf16[256,512]{1,0:T(8,128)(2,1)} %refs_3_.7) | copy-start | bytes 786436
  36.7 4.4 %copy-start.14 = (bf16[64,512]{1,0:T(8,128)(2,1)S(1)}, bf16[64,512]{1,0:T(8,128)(2,1)}, u32[]{:S(2)}) copy-start(bf16[64,512]{1,0:T(8,128)(2,1)} %refs_6_.1) | copy-start | bytes 196612
  37.9 3.2 %collective-permute-start.1 = (bf16[1280,512]{1,0:T(8,128)(2,1)S(1)}, bf16[1280,512]{1,0:T(8,128)(2,1)}, u32[]{:S(2)}, u32[]{:S(2)}) collective-permute-start(bf16[1280,512]{1,0:T(8,128)(2,1)S(1)} %pad_maximum_fusion), channel_id=1, source_target_pairs={{0,1},{1,0},{2,3},{3,2},{4,5},{5,4},{6,7},{7,6},{8,9},{9,8},{10,11... | collective-permute-start | bytes 3932168 | tf_op jit(solution)/shard_map/cond/branch_1_fun/ppermute | solution.py:91
  41.2 5.5 %copy-start.11 = (f32[256,512]{1,0:T(8,128)S(1)}, f32[256,512]{1,0:T(8,128)}, u32[]{:S(2)}) copy-start(f32[256,512]{1,0:T(8,128)} %copy-done.10) | copy-start | bytes 1572868
  46.7 2.4 %copy-start.9 = (bf16[256,512]{1,0:T(8,128)(2,1)}, bf16[256,512]{1,0:T(8,128)(2,1)S(1)}, u32[]{:S(2)}) copy-start(bf16[256,512]{1,0:T(8,128)(2,1)S(1)} %collective-permute-done.8.refs_10_) | copy-start | bytes 786436
  46.7 21.4 %copy-start = (bf16[352,512]{1,0:T(8,128)(2,1)}, bf16[352,512]{1,0:T(8,128)(2,1)S(1)}, u32[]{:S(2)}) copy-start(bf16[352,512]{1,0:T(8,128)(2,1)S(1)} %collective-permute-done.10.refs_9_) | copy-start | bytes 1081348
  46.8 4.3 %copy-start.8 = (bf16[256,512]{1,0:T(8,128)(2,1)}, bf16[256,512]{1,0:T(8,128)(2,1)S(1)}, u32[]{:S(2)}) copy-start(bf16[256,512]{1,0:T(8,128)(2,1)S(1)} %slice.69) | copy-start | bytes 786436
  49.0 19.1 %collective-permute-start.11 = (bf16[512,512]{1,0:T(8,128)(2,1)}, bf16[512,512]{1,0:T(8,128)(2,1)S(1)}, u32[]{:S(2)}, u32[]{:S(2)}) collective-permute-start(bf16[512,512]{1,0:T(8,128)(2,1)} %get-tuple-element.143), channel_id=1, source_target_pairs={{0,2},{1,3},{2,0},{3,1},{4,6},{5,7},{6,4},{7,5},{8,10},{9,11},{10,... | collective-permute-start | bytes 1572872 | tf_op jit(solution)/shard_map/ppermute | solution.py:91
  49.5 18.6 %collective-permute-start.12 = (bf16[512,512]{1,0:T(8,128)(2,1)}, bf16[512,512]{1,0:T(8,128)(2,1)S(1)}, u32[]{:S(2)}, u32[]{:S(2)}) collective-permute-start(bf16[512,512]{1,0:T(8,128)(2,1)} %get-tuple-element.142), channel_id=1, source_target_pairs={{0,16},{1,17},{2,18},{3,19},{4,20},{5,21},{6,22},{7,23},{8,24},{9,... | collective-permute-start | bytes 1572872 | tf_op jit(solution)/shard_map/ppermute | solution.py:91
  52.8 15.4 %collective-permute-start.13 = (bf16[352,512]{1,0:T(8,128)(2,1)}, bf16[352,512]{1,0:T(8,128)(2,1)S(1)}, u32[]{:S(2)}, u32[]{:S(2)}) collective-permute-start(bf16[352,512]{1,0:T(8,128)(2,1)} %pad_maximum_fusion.8), channel_id=1, source_target_pairs={{0,12},{1,13},{2,14},{3,15},{4,0},{5,1},{6,2},{7,3},{8,4},{9,5},{1... | collective-permute-start | bytes 1081352 | tf_op jit(solution)/shard_map/ppermute | solution.py:91
  56.8 11.4 %collective-permute-start.14 = (bf16[96,512]{1,0:T(8,128)(2,1)}, bf16[96,512]{1,0:T(8,128)(2,1)}, u32[]{:S(2)}, u32[]{:S(2)}) collective-permute-start(bf16[96,512]{1,0:T(8,128)(2,1)} %pad_maximum_fusion.10), channel_id=1, source_target_pairs={{0,4},{1,5},{2,6},{3,7},{4,8},{5,9},{6,10},{7,11},{8,12},{9,13},{1... | collective-permute-start | bytes 294920 | tf_op jit(solution)/shard_map/ppermute | solution.py:91
  58.2 3.6 %collective-permute-start.2 = (bf16[1536,512]{1,0:T(8,128)(2,1)S(1)}, bf16[1536,512]{1,0:T(8,128)(2,1)}, u32[]{:S(2)}, u32[]{:S(2)}) collective-permute-start(bf16[1536,512]{1,0:T(8,128)(2,1)S(1)} %pad_maximum_fusion.1), channel_id=1, source_target_pairs={{0,1},{1,0},{2,3},{3,2},{4,5},{5,4},{6,7},{7,6},{8,9},{9,8},{10,11... | collective-permute-start | bytes 4718600 | tf_op jit(solution)/shard_map/cond/branch_1_fun/ppermute | solution.py:91
  61.8 9.8 %copy-start.3 = (bf16[256,8192]{1,0:T(8,128)(2,1)S(1)}, bf16[256,8192]{1,0:T(8,128)(2,1)}, u32[]{:S(2)}) copy-start(bf16[256,8192]{1,0:T(8,128)(2,1)} %refs_1_.7) | copy-start | bytes 12582916
  68.2 0.9 %slice-start = ((bf16[352,512]{1,0:T(8,128)(2,1)}), bf16[96,512]{1,0:T(8,128)(2,1)S(1)}, s32[]{:S(2)}) async-start(bf16[352,512]{1,0:T(8,128)(2,1)} %copy-done), calls=%async_computation | async-start | bytes 196608 | tf_op jit(solution)/shard_map/slice | solution.py:413
  68.2 0.9 %copy-start.13 = (bf16[32,512]{1,0:T(8,128)(2,1)S(1)}, bf16[32,512]{1,0:T(8,128)(2,1)}, u32[]{:S(2)}) copy-start(bf16[32,512]{1,0:T(8,128)(2,1)} %copy-done.12) | copy-start | bytes 98308
  68.2 3.4 %copy-start.6 = (bf16[256,512]{1,0:T(8,128)(2,1)S(1)}, bf16[256,512]{1,0:T(8,128)(2,1)}, u32[]{:S(2)}) copy-start(bf16[256,512]{1,0:T(8,128)(2,1)} %refs_3_.7) | copy-start | bytes 786436
  68.3 5.5 %collective-permute-start.16 = (bf16[1280,512]{1,0:T(8,128)(2,1)S(1)}, bf16[1280,512]{1,0:T(8,128)(2,1)S(1)}, u32[]{:S(2)}, u32[]{:S(2)}) collective-permute-start(bf16[1280,512]{1,0:T(8,128)(2,1)S(1)} %pad_maximum_fusion.2), channel_id=1, source_target_pairs={{0,1},{1,0},{2,3},{3,2},{4,5},{5,4},{6,7},{7,6},{8,9},{9,8},{10,11... | collective-permute-start | bytes 3932168 | tf_op jit(solution)/shard_map/ppermute | solution.py:91
  69.9 4.0 %collective-permute-start.15 = (f32[32,512]{1,0:T(8,128)S(1)}, f32[32,512]{1,0:T(8,128)S(1)}, u32[]{:S(2)}, u32[]{:S(2)}) collective-permute-start(f32[32,512]{1,0:T(8,128)S(1)} %add_multiply_fusion.refs_7_), channel_id=1, source_target_pairs={{0,1},{1,0},{2,3},{3,2},{4,5},{5,4},{6,7},{7,6},{8,9},{9,8},{10,11... | collective-permute-start | bytes 196616 | tf_op jit(solution)/shard_map/ppermute | solution.py:91

commit v5 on v4

v5 whole, which is shorter than its diff:
```python
import math

import jax
import jax.numpy as jnp
from jax import lax
from jax.experimental import pallas as pl
from jax.experimental.pallas import tpu as pltpu
from jax.sharding import PartitionSpec as P

BLOCK = 128
AXES = ("groups", "fsdp")

lowrank_scale = 0.5


def weight_transpose(left, right):
    return lax.dot_general(
        left, right, (((1,), (1,)), ((), ())), preferred_element_type=jnp.float32
    )


def leading(left, right):
    return lax.dot_general(
        left, right, (((0,), (0,)), ((), ())), preferred_element_type=jnp.float32
    )


def dequantize(quant_codes, block_scales):
    spread_scales = jnp.repeat(jnp.repeat(block_scales, BLOCK, axis=0), BLOCK, axis=1)
    return (quant_codes.astype(jnp.float32) * spread_scales).astype(jnp.bfloat16)


def per_device_general(
    activations, quant_codes, block_scales, lowrank_down_factor, lowrank_up_factor, cotangent
):
    value_weight = dequantize(quant_codes, block_scales)
    lowrank_hidden = jnp.dot(
        activations, lowrank_down_factor, preferred_element_type=jnp.float32
    ).astype(jnp.bfloat16)
    lowrank_update = lowrank_scale * jnp.dot(
        lowrank_hidden, lowrank_up_factor, preferred_element_type=jnp.float32
    )
    hidden_gradient = weight_transpose(cotangent, lowrank_up_factor).astype(jnp.bfloat16)
    gathered = lax.all_gather(value_weight, "fsdp", axis=0, tiled=True)
    projected = (
        lowrank_update + jnp.dot(activations, gathered, preferred_element_type=jnp.float32)
    ).astype(jnp.bfloat16)
    input_gradient = (
        weight_transpose(cotangent, gathered)
        + lowrank_scale * weight_transpose(hidden_gradient, lowrank_down_factor)
    ).astype(jnp.bfloat16)
    scaling_factor = lowrank_scale / math.sqrt(activations.shape[0] * lax.axis_size("fsdp"))
    grad_down = lax.psum_scatter(
        scaling_factor * leading(activations, hidden_gradient),
        "fsdp",
        scatter_dimension=0,
        tiled=True,
    )
    grad_up = lax.psum(scaling_factor * leading(lowrank_hidden, cotangent), "fsdp")
    return (projected, input_gradient, grad_down, grad_up)


NZ = 4
VMEM_LIMIT = 24 * 1024 * 1024


def pairs_of(move):
    found = []
    for g in range(2):
        for z in range(NZ):
            for y in range(2):
                for c in range(2):
                    to = move(g, z, y, c)
                    found.append((index_of(g, z, y, c), index_of(*to)))
    return found


def index_of(g, z, y, c):
    return ((g * NZ + z) * 2 + y) * 2 + c


OVER_CORE = pairs_of(lambda g, z, y, c: (g, z, y, 1 - c))
OVER_Y = pairs_of(lambda g, z, y, c: (g, z, 1 - y, c))
OVER_X = pairs_of(lambda g, z, y, c: (1 - g, z, y, c))
Z_UP = pairs_of(lambda g, z, y, c: (g, (z + 1) % NZ, y, c))
Z_DOWN = pairs_of(lambda g, z, y, c: (g, (z - 1) % NZ, y, c))
Z_FAR = pairs_of(lambda g, z, y, c: (g, (z + 2) % NZ, y, c))


def send(array, pairs):
    return lax.ppermute(array, AXES, pairs)


def whole():
    return pl.BlockSpec(memory_space=pltpu.VMEM)


def scalars():
    return pl.BlockSpec(memory_space=pltpu.SMEM)


def in_hbm():
    return pl.BlockSpec(memory_space=pltpu.HBM)


def params():
    return pltpu.CompilerParams(vmem_limit_bytes=VMEM_LIMIT)


LITTLE = pl.CostEstimate(flops=1, bytes_accessed=1, transcendentals=0)


def dequantize_shard(place, quant_codes, block_scales):
    rows, columns = quant_codes.shape
    half = rows // 2

    def kernel(place_ref, codes_ref, scales_ref, own_ref, first_ref):
        g = place_ref[0]
        for i in range(rows // BLOCK):
            source = lax.rem(g * (half // BLOCK) + i, rows // BLOCK)
            start = pl.multiple_of(source * BLOCK, BLOCK)
            for j in range(columns // BLOCK):
                at = slice(j * BLOCK, (j + 1) * BLOCK)
                block = codes_ref[pl.ds(start, BLOCK), at].astype(jnp.float32)
                block = (block * scales_ref[source, j]).astype(jnp.bfloat16)
                own_ref[i * BLOCK : (i + 1) * BLOCK, at] = block
                if i < half // BLOCK:
                    first_ref[i * BLOCK : (i + 1) * BLOCK, at] = block

    return pl.pallas_call(
        kernel,
        out_shape=[
            jax.ShapeDtypeStruct((rows, columns), jnp.bfloat16),
            jax.ShapeDtypeStruct((half, columns), jnp.bfloat16),
        ],
        in_specs=[scalars(), whole(), scalars()],
        out_specs=[whole()] * 2,
        compiler_params=params(),
        cost_estimate=LITTLE,
        name="dequantize",
    )(place, quant_codes, block_scales)


def local_gradients(place, activations, down_t, up, cotangent, other_act, other_cot):
    tokens, width = activations.shape
    rank, features = up.shape
    chips = NZ * 2
    chunk = width // chips
    part = chunk // 2

    def kernel(
        place_ref, act_hbm, down_hbm, up_hbm, cot_hbm, other_hbm, other_cot_hbm, latent_ref,
        lgrad_ref, message_ref, kept_ref, act_ref, down_ref, up_ref, cot_ref, other_ref,
        other_cot_ref, total, lgrad_t, other_t, sums, sems,
    ):
        y, c = place_ref[2], place_ref[3]
        copies = []

        def fetch(source, target):
            copies.append(pltpu.make_async_copy(source, target, sems.at[len(copies)]))
            copies[-1].start()

        for source, target in (
            (up_hbm, up_ref), (cot_hbm, cot_ref), (other_cot_hbm, other_cot_ref),
        ):
            fetch(source, target)
        for i in range(chips):
            at = slice(i * chunk, (i + 1) * chunk)
            mine = pl.ds(pl.multiple_of((2 * i + c) * part, part), part)
            fetch(act_hbm.at[:, at], act_ref.at[i])
            fetch(other_hbm.at[:, mine], other_ref.at[i])
            fetch(down_hbm.at[:, at], down_ref.at[i])
        for copy in copies[:3]:
            copy.wait()
        lgrad_ref[...] = weight_transpose(cot_ref[...], up_ref[...]).astype(jnp.bfloat16)
        lgrad_t[...] = weight_transpose(up_ref[...], cot_ref[...]).astype(jnp.bfloat16)
        other_t[...] = weight_transpose(up_ref[...], other_cot_ref[...]).astype(jnp.bfloat16)
        mine = pl.ds(pl.multiple_of(c * part, part), part)
        for i in range(chips):
            for copy in copies[3 * i + 3 : 3 * i + 6]:
                copy.wait()
            sums[i % 2, i // 2 * rank : (i // 2 + 1) * rank, :] = jnp.dot(
                lgrad_t[...], act_ref[i, :, mine], preferred_element_type=jnp.float32
            ) + jnp.dot(other_t[...], other_ref[i], preferred_element_type=jnp.float32)
            latent = weight_transpose(act_ref[i], down_ref[i])
            if i == 0:
                total[...] = latent
            else:
                total[...] += latent
        message_ref[: NZ * rank, :] = sums[1 - y].astype(jnp.bfloat16)
        kept_ref[...] = sums[y]
        latent_ref[...] = total[...].astype(jnp.bfloat16)
        message_ref[NZ * rank :, :] = leading(latent_ref[...], cot_ref[...]).astype(jnp.bfloat16)

    bf16 = jnp.bfloat16
    return pl.pallas_call(
        kernel,
        out_shape=[
            jax.ShapeDtypeStruct((tokens, rank), bf16),
            jax.ShapeDtypeStruct((tokens, rank), bf16),
            jax.ShapeDtypeStruct(((NZ + 1) * rank, part), bf16),
            jax.ShapeDtypeStruct((NZ * rank, part), jnp.float32),
        ],
        in_specs=[scalars()] + [in_hbm()] * 6,
        out_specs=[whole()] * 4,
        scratch_shapes=[
            pltpu.VMEM((chips, tokens, chunk), bf16),
            pltpu.VMEM((chips, rank, chunk), bf16),
            pltpu.VMEM((rank, features), bf16),
            pltpu.VMEM((tokens, features), bf16),
            pltpu.VMEM((chips, tokens, part), bf16),
            pltpu.VMEM((tokens, features), bf16),
            pltpu.VMEM((tokens, rank), jnp.float32),
            pltpu.VMEM((rank, tokens), bf16),
            pltpu.VMEM((rank, tokens), bf16),
            pltpu.VMEM((2, NZ * rank, part), jnp.float32),
            pltpu.SemaphoreType.DMA((3 * chips + 3,)),
        ],
        compiler_params=pltpu.CompilerParams(vmem_limit_bytes=50 * 1024 * 1024),
        cost_estimate=LITTLE,
        name="local_gradients",
    )(place, activations, down_t, up, cotangent, other_act, other_cot)


def add_y(place, kept, sent, came):
    rows, part = kept.shape
    rank = rows // NZ

    def kernel(place_ref, kept_ref, sent_ref, came_ref, own_ref, next_ref, far_ref, last_ref):
        z = place_ref[1]
        f32 = jnp.float32
        tail = sent_ref[rows:, :].astype(f32) + came_ref[rows:, :].astype(f32)
        for shift, out_ref in enumerate((own_ref, next_ref, far_ref, last_ref)):
            at = pl.ds(pl.multiple_of(lax.rem(z + shift, NZ) * rank, rank), rank)
            summed = kept_ref[at, :] + came_ref[at, :].astype(f32)
            out_ref[:rank, :] = summed.astype(out_ref.dtype)
            if shift >= 2:
                out_ref[rank:, :] = tail.astype(jnp.bfloat16)

    return pl.pallas_call(
        kernel,
        out_shape=[jax.ShapeDtypeStruct((rank, part), jnp.float32)] * 2
        + [jax.ShapeDtypeStruct((2 * rank, part), jnp.bfloat16)] * 2,
        in_specs=[scalars()] + [whole()] * 3,
        out_specs=[whole()] * 4,
        compiler_params=params(),
        cost_estimate=pl.CostEstimate(flops=20000000000, bytes_accessed=1, transcendentals=0),
        name="add_y",
    )(place, kept, sent, came)


def multiply(
    place, pieces, activations, down_t, cotangent, lgrad, factor, begin=None, so_far=None, end=None
):
    tokens, width = activations.shape
    features = cotangent.shape[1]
    arrays = []
    for array, _, _ in pieces:
        if not any(array is other for other in arrays):
            arrays.append(array)
    where = [next(i for i, a in enumerate(arrays) if a is array) for array, _, _ in pieces]
    count = len(pieces)
    rows = width // (NZ * 2 * 2 * 2)

    def kernel(*refs):
        refs = list(refs)
        place_ref, act_ref, down_ref, cot_ref, lgrad_ref, one_ref, two_ref = refs[:7]
        del refs[:7]
        if end is not None:
            terms = refs[:5]
            del refs[:5]
        array_refs = refs[: len(arrays)]
        del refs[: len(arrays)]
        out_ref, grad_ref = refs[:2]
        sums, grads, out_sems = refs[-3:]
        g, z, y, c = (place_ref[i] for i in range(4))
        columns, weights, going = [], [], []
        for p, (_, first, (dz, dy, dc, dh)) in enumerate(pieces):
            chip = lax.rem(z + (NZ - dz), NZ) * 2 + (1 - y if dy else y)
            device = chip * 2 + (1 - c if dc else c)
            start = (device * 2 + (1 - g if dh else g)) * rows
            columns.append(pl.ds(pl.multiple_of(start, rows), rows))
            weights.append(array_refs[where[p]].at[first : first + rows, :])

        def give(source, target):
            going.append(pltpu.make_async_copy(source, target, out_sems.at[len(going)]))
            going[-1].start()

        def backward():
            for p in range(count):
                grads[p] = (
                    weight_transpose(cot_ref[...], weights[p][...])
                    + lowrank_scale
                    * jnp.dot(
                        lgrad_ref[...], down_ref[:, columns[p]], preferred_element_type=jnp.float32
                    )
                ).astype(jnp.bfloat16)
                give(grads.at[p], grad_ref.at[:, columns[p]])

        def forward():
            if begin is not None:
                sums[...] = lowrank_scale * jnp.dot(
                    one_ref[...], two_ref[...], preferred_element_type=jnp.float32
                )
            else:
                sums[...] = one_ref[...]
            for p in range(count):
                sums[...] += jnp.dot(
                    act_ref[:, columns[p]], weights[p][...], preferred_element_type=jnp.float32
                )

        if end is None:
            backward()
            forward()
            out_ref[...] = sums[...]
        else:
            up_out, down_out, rounded, up_sum, down_sum = refs[2:7]
            up_sum[...] = terms[0][...] + terms[1][...]
            give(up_sum, up_out)
            rank = down_ref.shape[0]
            down_sum[...] = factor * (
                terms[2][...]
                + terms[3][:rank, :].astype(jnp.float32)
                + terms[4][rows : rows + rank, :].astype(jnp.float32)
            )
            give(down_sum, down_out)
            forward()
            rounded[...] = sums[...].astype(jnp.bfloat16)
            give(rounded, out_ref)
            backward()
        for copy in going:
            copy.wait()

    operands = [place, activations, down_t, cotangent, lgrad]
    specs = [scalars()] + [whole()] * 4
    out_shape = [
        jax.ShapeDtypeStruct((tokens, features), jnp.float32 if end is None else jnp.bfloat16),
        jax.ShapeDtypeStruct((tokens, width), jnp.bfloat16),
    ]
    out_specs = [whole() if end is None else in_hbm(), in_hbm()]
    scratch = [] if end is None else [pltpu.VMEM((tokens, features), jnp.bfloat16)]
    aliases = {}
    if begin is not None:
        operands += begin
        specs += [whole()] * 2
    else:
        operands += so_far
        specs += [whole(), in_hbm()]
        aliases = {6: 1}
    if end is not None:
        operands += end
        specs += [whole()] * 5
        for term in (end[0], end[2]):
            out_shape.append(jax.ShapeDtypeStruct(term.shape, jnp.float32))
            out_specs.append(in_hbm())
            scratch.append(pltpu.VMEM(term.shape, jnp.float32))
    return pl.pallas_call(
        kernel,
        out_shape=out_shape,
        in_specs=specs + [whole()] * len(arrays),
        out_specs=out_specs,
        scratch_shapes=scratch
        + [
            pltpu.VMEM((tokens, features), jnp.float32),
            pltpu.VMEM((count, tokens, rows), jnp.bfloat16),
            pltpu.SemaphoreType.DMA((count + 3,)),
        ],
        input_output_aliases=aliases,
        compiler_params=params(),
        cost_estimate=LITTLE,
        name="multiply",
    )(*operands, *arrays)


def per_device(
    activations, quant_codes, block_scales, lowrank_down_factor, lowrank_up_factor, cotangent
):
    g = lax.axis_index("groups")
    f = lax.axis_index("fsdp")
    place = jnp.stack([g, f >> 2, (f >> 1) & 1, f & 1]).astype(jnp.int32)
    half = quant_codes.shape[0] // 2
    down_t = lowrank_down_factor.T
    factor = lowrank_scale / math.sqrt(activations.shape[0] * lax.axis_size("fsdp"))
    barrier = lax.optimization_barrier
    join = lambda *arrays: jnp.concatenate(arrays, axis=0)

    def products(pieces, **more):
        return multiply(place, pieces, activations, down_t, cotangent, lgrad, factor, **more)

    def listed(array, dc, *keys):
        return [(array, i * half, (dz, dy, dc, dh)) for i, (dz, dy, dh) in enumerate(keys)]

    own, first = dequantize_shard(place, quant_codes, block_scales)
    own, first, place = barrier((own, first, place))

    def swap(*arrays):
        return send(join(*arrays), OVER_CORE)

    down1, up1, y1 = send(first, Z_DOWN), send(first, Z_UP), send(own[half:], OVER_Y)

    other_act, other_cot = send(activations, OVER_CORE), send(cotangent, OVER_CORE)
    latent, lgrad, terms_y, kept = local_gradients(
        place, activations, down_t, lowrank_up_factor, cotangent, other_act, other_cot
    )
    came_y = send(terms_y, OVER_Y)
    down1, up1, y1, kept = barrier((down1, up1, y1, kept))

    down2 = send(join(y1, down1), Z_DOWN)
    y2, x2 = send(join(up1, first), OVER_Y), send(join(up1, down1), OVER_X)
    rank = down_t.shape[0]
    own_part, next_part, far_part, last_part = add_y(place, kept, terms_y, came_y)
    came_up = send(far_part, Z_UP)
    swap2 = swap(up1, down1, y1)
    own_keys = [(0, 0, 0), (0, 0, 1)]
    keys = [(1, 0, 0), (3, 0, 0), (0, 1, 1)]
    done = products(
        listed(own, 0, *own_keys)
        + listed(up1, 0, keys[0])
        + listed(down1, 0, keys[1])
        + listed(y1, 0, keys[2])
        + listed(swap2, 1, *keys),
        begin=[latent, lowrank_up_factor],
    )
    y2, x2, down2, came_up, own_part, next_part, last_part, done = barrier(
        (y2, x2, down2, came_up, own_part, next_part, last_part, done)
    )

    two = down2[half:]
    down3 = send(join(down2[:half], last_part), Z_DOWN)
    y3, x3 = send(join(down1, two), OVER_Y), send(join(two, y2[:half]), OVER_X)
    next_part = next_part + came_up[:rank].astype(jnp.float32)
    up3 = send(join(next_part.astype(jnp.bfloat16), came_up[rank:]), Z_UP)
    swap3 = swap(y2, x2, down2, own)
    keys = [(1, 1, 0), (0, 1, 0), (1, 0, 1), (3, 0, 1), (3, 1, 1), (2, 0, 0)]
    done = products(
        listed(y2, 0, *keys[:2])
        + listed(x2, 0, *keys[2:4])
        + listed(down2, 0, *keys[4:])
        + listed(swap3, 1, *keys, *own_keys),
        so_far=done,
    )
    y3, x3, down3, up3, came_up, own_part, last_part, done = barrier(
        (y3, x3, down3, up3, came_up, own_part, last_part, done)
    )

    swap4 = send(join(y3, x3, down3[:half]), OVER_CORE)
    wide = lambda array: array.astype(jnp.float32)
    up_own = factor * (
        (wide(last_part[rank:]) + wide(up3[rank:])) + (wide(came_up[rank:]) + wide(down3[half + rank :]))
    )
    up_came = send(up_own, OVER_CORE)
    keys = [(3, 1, 0), (2, 1, 0), (2, 0, 1), (1, 1, 1), (2, 1, 1)]
    done = products(
        listed(y3, 0, *keys[:2]) + listed(x3, 0, *keys[2:4]) + listed(down3, 0, keys[4]),
        so_far=done,
    )
    projected, gradient, grad_up, grad_down_t = products(
        listed(swap4, 1, *keys), so_far=done, end=[up_own, up_came, own_part, up3, down3]
    )
    return (projected, gradient, grad_down_t.T, grad_up)


def solution(mesh):
    in_specs = (
        P(("groups", "fsdp"), None),
        P("fsdp", None),
        P("fsdp", None),
        P("groups", None),
        P("groups", None),
        P(("groups", "fsdp"), None),
    )
    out_specs = (
        P(("groups", "fsdp"), None),
        P(("groups", "fsdp"), None),
        P(("groups", "fsdp"), None),
        P("groups", None),
    )
    small = mesh.shape["groups"] == 2 and mesh.shape["fsdp"] == NZ * 4
    return jax.shard_map(
        per_device if small else per_device_general,
        mesh=mesh,
        in_specs=in_specs,
        out_specs=out_specs,
        check_vma=False,
    )
```

time: 77.4 us -> 65.9 us (0.85)
  other arithmetic: 10.5 us -> 0.65 us
  waiting for transfers between devices: 13.4 us -> 20.4 us
  Pallas kernels: 23.6 us -> 18.6 us
  between operations: 4.27 us -> 0.85 us
    concatenate x9 -> x7, other arithmetic: 8.06 us -> 0.52 us  [per_device(): join = lambda *arrays: jnp.concatenate(arrays, axis=0)]
    ppermute x17 -> x18, waiting for transfers between devices: 13.4 us -> 20.4 us  [send(): return lax.ppermute(array, AXES, pairs)]
    pallas_call x4, Pallas kernels: 17 us -> 11.5 us  [multiply(): pl.pallas_call(kernel, out_shape=out_shape, in_specs=specs + [whole()] *...]
    unnamed x30 -> x12, local copies, waits for them, and re-layouts: 1.79 us -> 5.12 us
    transpose x1 -> x0, other arithmetic: 1.52 us -> none  [per_device(): return (projected, gradient, grad_down_t.T, grad_up)]
    slice x1, local copies, waits for them, and re-layouts: 1.17 us -> 0.02 us  [per_device(): y2[:half]]
    slice x4 -> x1, local copies, waits for them, and re-layouts: 1.15 us -> 0.04 us  [per_device(): down3 = send(join(down2[:half], last_part), Z_DOWN)]
    ppermute x17 -> x18, starting transfers between devices: 20 us -> 19.9 us  [send(): return lax.ppermute(array, AXES, pairs)]
  transfers between devices with their start and end apart: 17 -> 18, of which waited for: 4 -> 5; matrix products, arithmetic and copies ran while one was open for 14% -> 1% of each run, Pallas kernels for 26% -> 25%
where the time goes in v5:
time: 65.9 us; the launch traced here: 65.6 us
  waiting for transfers between devices  20.4 us (31%)
  starting transfers between devices  19.9 us (30%)
  Pallas kernels  18.6 us (28%)
  local copies, waits for them, and re-layouts  5.21 us (8%)
  between operations  0.85 us (1%)
    ppermute x18, waiting for transfers between devices, send(): return lax.ppermute(array, AXES, pairs)  20.4 us
    ppermute x18, starting transfers between devices, send(): return lax.ppermute(array, AXES, pairs)  19.9 us
    pallas_call x4, Pallas kernels, multiply(): pl.pallas_call(kernel, out_shape=out_shape, in_specs=specs + [whole()] *...  11.5 us
    pallas_call x1, Pallas kernels, local_gradients(): pl.pallas_call(kernel, out_shape=[jax.ShapeDtypeStruct((tokens, rank), bf...  5.83 us
    unnamed x12, local copies, waits for them, and re-layouts  5.12 us
  transfers between devices with their start and end apart: 18, of which 5 were waited for; matrix products, arithmetic and copies ran while one was open for 1% of the time, Pallas kernels for 25%

profile of v5, /device:TPU:0, one launch (start us, length us, event | category | flops | bytes accessed | tf_op | source)
XLA Modules:
  0.0 65.6 jit_solution(2016803386281323245)
XLA Ops:
  0.6 0.5 collective-permute-start
  1.1 0.1 collective-permute-start.1
  1.2 0.1 pad_add_fusion.place_ref.refs_0_
  1.3 1.0 %copy-done.3 = bf16[512,512]{1,0:T(8,128)(2,1)S(1)} copy-done((bf16[512,512]{1,0:T(8,128)(2,1)S(1)}, bf16[512,512]{1,0:T(8,128)(2,1)}, u32[]{:S(2)}) %copy-start.3) | copy-done | bytes 524312
  2.4 0.7 %copy-done.5 = f32[4,4]{1,0:T(4,128)S(1)} copy-done((f32[4,4]{1,0:T(4,128)S(1)}, f32[4,4]{1,0:T(4,128)}, u32[]{:S(2)}) %copy-start.5) | copy-done | bytes 88
  3.0 0.7 %dequantize.1 = (bf16[512,512]{1,0:T(8,128)(2,1)S(1)}, bf16[256,512]{1,0:T(8,128)(2,1)S(1)}) custom-call(s32[4]{0:T(128)S(1)} %pad_add_fusion.place_ref.refs_0_, bf16[512,512]{1,0:T(8,128)(2,1)S(1)} %copy-done.3, f32[4,4]{1,0:T(4,128)S(1)} %copy-done.5), custom_call_target="tpu_custom_call" | custom-call | flops 1 | bytes 1 | tf_op jit(solution)/shard_map/dequantize/pallas_call | solution.py:130
  3.8 3.0 %collective-permute-start.4 = (bf16[256,512]{1,0:T(8,128)(2,1)S(1)}, bf16[256,512]{1,0:T(8,128)(2,1)S(1)}, u32[]{:S(2)}, u32[]{:S(2)}) collective-permute-start(bf16[256,512]{1,0:T(8,128)(2,1)S(1)} %slice.33), channel_id=1, source_target_pairs={{0,2},{1,3},{2,0},{3,1},{4,6},{5,7},{6,4},{7,5},{8,10},{9,11},{10,... | collective-permute-start | bytes 786440 | tf_op jit(solution)/shard_map/ppermute | solution.py:91
  6.8 3.6 %collective-permute-start.2 = (bf16[256,512]{1,0:T(8,128)(2,1)S(1)}, bf16[256,512]{1,0:T(8,128)(2,1)S(1)}, u32[]{:S(2)}, u32[]{:S(2)}) collective-permute-start(bf16[256,512]{1,0:T(8,128)(2,1)S(1)} %get-tuple-element.53), channel_id=1, source_target_pairs={{0,12},{1,13},{2,14},{3,15},{4,0},{5,1},{6,2},{7,3},{8,4},{9,5},{1... | collective-permute-start | bytes 786440 | tf_op jit(solution)/shard_map/ppermute | solution.py:91
  10.4 0.0 collective-permute-start.3
  10.4 0.0 collective-permute-done.1.other_cot_hbm
  10.4 0.0 copy-start.1
  10.4 1.2 %copy-done.1 = bf16[8192,64]{0,1:T(8,128)(2,1)S(1)} copy-done((bf16[8192,64]{0,1:T(8,128)(2,1)S(1)}, bf16[8192,64]{0,1:T(8,128)(2,1)}, u32[]{:S(2)}) %copy-start.1) | copy-done | bytes 1048600
  11.6 0.9 %copy-done.2 = bf16[256,512]{1,0:T(8,128)(2,1)S(1)} copy-done((bf16[256,512]{1,0:T(8,128)(2,1)S(1)}, bf16[256,512]{1,0:T(8,128)(2,1)}, u32[]{:S(2)}) %copy-start.2) | copy-done | bytes 262168
  12.6 0.8 %copy-done.4 = bf16[64,512]{1,0:T(8,128)(2,1)S(1)} copy-done((bf16[64,512]{1,0:T(8,128)(2,1)S(1)}, bf16[64,512]{1,0:T(8,128)(2,1)}, u32[]{:S(2)}) %copy-start.4) | copy-done | bytes 65560
  13.4 5.8 %local_gradients.1 = (bf16[256,64]{1,0:T(8,128)(2,1)S(1)}, bf16[256,64]{1,0:T(8,128)(2,1)S(1)}, bf16[320,512]{1,0:T(8,128)(2,1)S(1)}, f32[256,512]{1,0:T(8,128)S(1)}) custom-call(s32[4]{0:T(128)S(1)} %pad_add_fusion.place_ref.refs_0_, bf16[256,8192]{1,0:T(8,128)(2,1)} %refs_1_.7, bf16[64,8192]{1,0:T(8,128)(2,1)S(1)} %bitcast.6, ...), custom_call_target="tpu_custom_call" | custom-call | flops 1 | bytes 1 | tf_op jit(solution)/shard_map/local_gradients/pallas_call | solution.py:196
  19.2 1.2 %collective-permute-start.8 = (bf16[320,512]{1,0:T(8,128)(2,1)S(1)}, bf16[320,512]{1,0:T(8,128)(2,1)S(1)}, u32[]{:S(2)}, u32[]{:S(2)}) collective-permute-start(bf16[320,512]{1,0:T(8,128)(2,1)S(1)} %get-tuple-element.60.sent_ref), channel_id=1, source_target_pairs={{0,2},{1,3},{2,0},{3,1},{4,6},{5,7},{6,4},{7,5},{8,10},{9,11},{10,... | collective-permute-start | bytes 983048 | tf_op jit(solution)/shard_map/ppermute | solution.py:91
  20.5 2.0 %collective-permute-done.3.refs_8_ = bf16[256,512]{1,0:T(8,128)(2,1)S(1)} collective-permute-done((bf16[256,512]{1,0:T(8,128)(2,1)S(1)}, bf16[256,512]{1,0:T(8,128)(2,1)S(1)}, u32[]{:S(2)}, u32[]{:S(2)}) %collective-permute-start.3) | collective-permute-done | bytes 262176 | tf_op jit(solution)/shard_map/ppermute | solution.py:91
  22.4 0.1 pad_maximum_fusion.2
  22.5 0.1 collective-permute-start.10
  22.6 0.1 pad_maximum_fusion.5
  22.7 0.6 collective-permute-start.5
  23.3 1.5 %collective-permute-start.6 = (bf16[512,512]{1,0:T(8,128)(2,1)S(1)}, bf16[512,512]{1,0:T(8,128)(2,1)S(1)}, u32[]{:S(2)}, u32[]{:S(2)}) collective-permute-start(bf16[512,512]{1,0:T(8,128)(2,1)S(1)} %get-tuple-element.99), channel_id=1, source_target_pairs={{0,16},{1,17},{2,18},{3,19},{4,20},{5,21},{6,22},{7,23},{8,24},{9,... | collective-permute-start | bytes 1572872 | tf_op jit(solution)/shard_map/ppermute | solution.py:91
  24.8 2.2 %collective-permute-start.7 = (bf16[512,512]{1,0:T(8,128)(2,1)S(1)}, bf16[512,512]{1,0:T(8,128)(2,1)S(1)}, u32[]{:S(2)}, u32[]{:S(2)}) collective-permute-start(bf16[512,512]{1,0:T(8,128)(2,1)S(1)} %get-tuple-element.98), channel_id=1, source_target_pairs={{0,12},{1,13},{2,14},{3,15},{4,0},{5,1},{6,2},{7,3},{8,4},{9,5},{1... | collective-permute-start | bytes 1572872 | tf_op jit(solution)/shard_map/ppermute | solution.py:91
  27.0 3.0 %collective-permute-done.8.came_ref = bf16[320,512]{1,0:T(8,128)(2,1)S(1)} collective-permute-done((bf16[320,512]{1,0:T(8,128)(2,1)S(1)}, bf16[320,512]{1,0:T(8,128)(2,1)S(1)}, u32[]{:S(2)}, u32[]{:S(2)}) %collective-permute-start.8) | collective-permute-done | bytes 327712 | tf_op jit(solution)/shard_map/ppermute | solution.py:91
  29.9 0.6 add_y.1
  30.6 1.2 %collective-permute-start.9 = (bf16[128,512]{1,0:T(8,128)(2,1)S(1)}, bf16[128,512]{1,0:T(8,128)(2,1)S(1)}, u32[]{:S(2)}, u32[]{:S(2)}) collective-permute-start(bf16[128,512]{1,0:T(8,128)(2,1)S(1)} %get-tuple-element.61), channel_id=1, source_target_pairs={{0,4},{1,5},{2,6},{3,7},{4,8},{5,9},{6,10},{7,11},{8,12},{9,13},{1... | collective-permute-start | bytes 393224 | tf_op jit(solution)/shard_map/ppermute | solution.py:91
  31.8 0.4 copy-done
  32.1 2.8 %multiply.4 = (f32[256,512]{1,0:T(8,128)S(1)}, bf16[256,8192]{1,0:T(8,128)(2,1)}) custom-call(s32[4]{0:T(128)S(1)} %pad_add_fusion.place_ref.refs_0_, bf16[256,8192]{1,0:T(8,128)(2,1)S(1)} %copy-done, bf16[64,8192]{1,0:T(8,128)(2,1)S(1)} %bitcast.7, bf16[256,512]{1,0:T(8,128)(2,1)S(1)} %copy-done.2, bf16[256,64]{1,0:T(8,128)(2,1)S(1)} %get-tuple-element.52.refs_4_, ...), custom_call_target="tpu_custom_call" | custom-call | flops 1 | bytes 1 | tf_op jit(solution)/shard_map/multiply/pallas_call | solution.py:357
  34.9 7.0 %collective-permute-done.9 = bf16[128,512]{1,0:T(8,128)(2,1)S(1)} collective-permute-done((bf16[128,512]{1,0:T(8,128)(2,1)S(1)}, bf16[128,512]{1,0:T(8,128)(2,1)S(1)}, u32[]{:S(2)}, u32[]{:S(2)}) %collective-permute-start.9) | collective-permute-done | bytes 131104 | tf_op jit(solution)/shard_map/ppermute | solution.py:91
  41.9 0.0 collective-permute-done.5.refs_7_
  41.9 0.0 collective-permute-done.6.refs_8_
  41.9 0.1 pad_maximum_fusion
  42.1 0.1 collective-permute-start.15
  42.2 0.1 pad_maximum_fusion.7
  42.3 1.3 %collective-permute-start.11 = (bf16[512,512]{1,0:T(8,128)(2,1)S(1)}, bf16[512,512]{1,0:T(8,128)(2,1)S(1)}, u32[]{:S(2)}, u32[]{:S(2)}) collective-permute-start(bf16[512,512]{1,0:T(8,128)(2,1)S(1)} %get-tuple-element.97), channel_id=1, source_target_pairs={{0,2},{1,3},{2,0},{3,1},{4,6},{5,7},{6,4},{7,5},{8,10},{9,11},{10,... | collective-permute-start | bytes 1572872 | tf_op jit(solution)/shard_map/ppermute | solution.py:91
  43.6 0.5 collective-permute-start.12
  44.2 3.3 %collective-permute-start.13 = (bf16[384,512]{1,0:T(8,128)(2,1)S(1)}, bf16[384,512]{1,0:T(8,128)(2,1)S(1)}, u32[]{:S(2)}, u32[]{:S(2)}) collective-permute-start(bf16[384,512]{1,0:T(8,128)(2,1)S(1)} %pad_maximum_fusion.8), channel_id=1, source_target_pairs={{0,12},{1,13},{2,14},{3,15},{4,0},{5,1},{6,2},{7,3},{8,4},{9,5},{1... | collective-permute-start | bytes 1179656 | tf_op jit(solution)/shard_map/ppermute | solution.py:91
  47.5 0.1 collective-permute-start.14
  47.6 0.0 collective-permute-done.15.refs_10_
  47.6 4.0 %multiply.5 = (f32[256,512]{1,0:T(8,128)S(1)}, bf16[256,8192]{1,0:T(8,128)(2,1)}) custom-call(s32[4]{0:T(128)S(1)} %pad_add_fusion.place_ref.refs_0_, bf16[256,8192]{1,0:T(8,128)(2,1)S(1)} %copy-done, bf16[64,8192]{1,0:T(8,128)(2,1)S(1)} %bitcast.8, bf16[256,512]{1,0:T(8,128)(2,1)S(1)} %copy-done.2, ...), custom_call_target="tpu_custom_call", output_to_operand_aliasing={{1}: (6, {})} | custom-call | flops 1 | bytes 1 | tf_op jit(solution)/shard_map/multiply/pallas_call | solution.py:357
  51.6 8.1 %collective-permute-done.14.refs_10_ = bf16[128,512]{1,0:T(8,128)(2,1)S(1)} collective-permute-done((bf16[128,512]{1,0:T(8,128)(2,1)S(1)}, bf16[128,512]{1,0:T(8,128)(2,1)S(1)}, u32[]{:S(2)}, u32[]{:S(2)}) %collective-permute-start.14) | collective-permute-done | bytes 131104 | tf_op jit(solution)/shard_map/ppermute | solution.py:91
  59.8 0.1 pad_maximum_fusion.1
  59.9 0.1 collective-permute-start.17
  60.0 0.6 collective-permute-start.16
  60.6 2.3 %multiply.6 = (f32[256,512]{1,0:T(8,128)S(1)}, bf16[256,8192]{1,0:T(8,128)(2,1)}) custom-call(s32[4]{0:T(128)S(1)} %pad_add_fusion.place_ref.refs_0_, bf16[256,8192]{1,0:T(8,128)(2,1)S(1)} %copy-done, bf16[64,8192]{1,0:T(8,128)(2,1)S(1)} %bitcast.9, bf16[256,512]{1,0:T(8,128)(2,1)S(1)} %copy-done.2, ...), custom_call_target="tpu_custom_call", output_to_operand_aliasing={{1}: (6, {})} | custom-call | flops 1 | bytes 1 | tf_op jit(solution)/shard_map/multiply/pallas_call | solution.py:357
  62.9 0.3 collective-permute-done.16.refs_8_
  63.2 0.0 collective-permute-done.17.refs_12_
  63.2 2.4 %multiply.7 = (bf16[256,512]{1,0:T(8,128)(2,1)}, bf16[256,8192]{1,0:T(8,128)(2,1)}, f32[64,512]{1,0:T(8,128)}, f32[64,512]{1,0:T(8,128)}) custom-call(s32[4]{0:T(128)S(1)} %pad_add_fusion.place_ref.refs_0_, bf16[256,8192]{1,0:T(8,128)(2,1)S(1)} %copy-done, bf16[64,8192]{1,0:T(8,128)(2,1)S(1)} %bitcast.10, ...), custom_call_target="tpu_custom_call", output_to_operand_aliasing={{1}: (6, {})} | custom-call | flops 1 | bytes 1 | tf_op jit(solution)/shard_map/multiply/pallas_call | solution.py:357
  (22 shorter events, 0.2 us)
Async XLA Ops:
  0.6 9.8 %collective-permute-start = (bf16[256,8192]{1,0:T(8,128)(2,1)}, bf16[256,8192]{1,0:T(8,128)(2,1)}, u32[]{:S(2)}, u32[]{:S(2)}) collective-permute-start(bf16[256,8192]{1,0:T(8,128)(2,1)} %refs_1_.7), channel_id=1, source_target_pairs={{0,1},{1,0},{2,3},{3,2},{4,5},{5,4},{6,7},{7,6},{8,9},{9,8},{10,11... | collective-permute-start | bytes 12582920 | tf_op jit(solution)/shard_map/ppermute | solution.py:91
  1.1 9.2 %collective-permute-start.1 = (bf16[256,512]{1,0:T(8,128)(2,1)}, bf16[256,512]{1,0:T(8,128)(2,1)S(1)}, u32[]{:S(2)}, u32[]{:S(2)}) collective-permute-start(bf16[256,512]{1,0:T(8,128)(2,1)} %refs_3_.7), channel_id=1, source_target_pairs={{0,1},{1,0},{2,3},{3,2},{4,5},{5,4},{6,7},{7,6},{8,9},{9,8},{10,11... | collective-permute-start | bytes 786440 | tf_op jit(solution)/shard_map/ppermute | solution.py:91
  1.3 1.0 %copy-start.3 = (bf16[512,512]{1,0:T(8,128)(2,1)S(1)}, bf16[512,512]{1,0:T(8,128)(2,1)}, u32[]{:S(2)}) copy-start(bf16[512,512]{1,0:T(8,128)(2,1)} %codes_ref.1) | copy-start | bytes 1572868
  2.4 0.7 %copy-start.5 = (f32[4,4]{1,0:T(4,128)S(1)}, f32[4,4]{1,0:T(4,128)}, u32[]{:S(2)}) copy-start(f32[4,4]{1,0:T(4,128)} %scales_ref.1) | copy-start | bytes 196
  3.8 16.7 %collective-permute-start.4 = (bf16[256,512]{1,0:T(8,128)(2,1)S(1)}, bf16[256,512]{1,0:T(8,128)(2,1)S(1)}, u32[]{:S(2)}, u32[]{:S(2)}) collective-permute-start(bf16[256,512]{1,0:T(8,128)(2,1)S(1)} %slice.33), channel_id=1, source_target_pairs={{0,2},{1,3},{2,0},{3,1},{4,6},{5,7},{6,4},{7,5},{8,10},{9,11},{10,... | collective-permute-start | bytes 786440 | tf_op jit(solution)/shard_map/ppermute | solution.py:91
  6.8 13.7 %collective-permute-start.2 = (bf16[256,512]{1,0:T(8,128)(2,1)S(1)}, bf16[256,512]{1,0:T(8,128)(2,1)S(1)}, u32[]{:S(2)}, u32[]{:S(2)}) collective-permute-start(bf16[256,512]{1,0:T(8,128)(2,1)S(1)} %get-tuple-element.53), channel_id=1, source_target_pairs={{0,12},{1,13},{2,14},{3,15},{4,0},{5,1},{6,2},{7,3},{8,4},{9,5},{1... | collective-permute-start | bytes 786440 | tf_op jit(solution)/shard_map/ppermute | solution.py:91
  10.4 12.1 %collective-permute-start.3 = (bf16[256,512]{1,0:T(8,128)(2,1)S(1)}, bf16[256,512]{1,0:T(8,128)(2,1)S(1)}, u32[]{:S(2)}, u32[]{:S(2)}) collective-permute-start(bf16[256,512]{1,0:T(8,128)(2,1)S(1)} %get-tuple-element.53), channel_id=1, source_target_pairs={{0,4},{1,5},{2,6},{3,7},{4,8},{5,9},{6,10},{7,11},{8,12},{9,13},{1... | collective-permute-start | bytes 786440 | tf_op jit(solution)/shard_map/ppermute | solution.py:91
  10.4 1.2 %copy-start.1 = (bf16[8192,64]{0,1:T(8,128)(2,1)S(1)}, bf16[8192,64]{0,1:T(8,128)(2,1)}, u32[]{:S(2)}) copy-start(bf16[8192,64]{0,1:T(8,128)(2,1)} %param.9) | copy-start | bytes 3145732
  11.6 0.9 %copy-start.2 = (bf16[256,512]{1,0:T(8,128)(2,1)S(1)}, bf16[256,512]{1,0:T(8,128)(2,1)}, u32[]{:S(2)}) copy-start(bf16[256,512]{1,0:T(8,128)(2,1)} %refs_3_.7) | copy-start | bytes 786436
  12.6 0.8 %copy-start.4 = (bf16[64,512]{1,0:T(8,128)(2,1)S(1)}, bf16[64,512]{1,0:T(8,128)(2,1)}, u32[]{:S(2)}) copy-start(bf16[64,512]{1,0:T(8,128)(2,1)} %refs_6_.1) | copy-start | bytes 196612
  19.2 10.7 %collective-permute-start.8 = (bf16[320,512]{1,0:T(8,128)(2,1)S(1)}, bf16[320,512]{1,0:T(8,128)(2,1)S(1)}, u32[]{:S(2)}, u32[]{:S(2)}) collective-permute-start(bf16[320,512]{1,0:T(8,128)(2,1)S(1)} %get-tuple-element.60.sent_ref), channel_id=1, source_target_pairs={{0,2},{1,3},{2,0},{3,1},{4,6},{5,7},{6,4},{7,5},{8,10},{9,11},{10,... | collective-permute-start | bytes 983048 | tf_op jit(solution)/shard_map/ppermute | solution.py:91
  22.5 9.3 %collective-permute-start.10 = (bf16[768,512]{1,0:T(8,128)(2,1)S(1)}, bf16[768,512]{1,0:T(8,128)(2,1)S(1)}, u32[]{:S(2)}, u32[]{:S(2)}) collective-permute-start(bf16[768,512]{1,0:T(8,128)(2,1)S(1)} %pad_maximum_fusion.2), channel_id=1, source_target_pairs={{0,1},{1,0},{2,3},{3,2},{4,5},{5,4},{6,7},{7,6},{8,9},{9,8},{10,11... | collective-permute-start | bytes 2359304 | tf_op jit(solution)/shard_map/ppermute | solution.py:91
  22.7 19.2 %collective-permute-start.5 = (bf16[512,512]{1,0:T(8,128)(2,1)S(1)}, bf16[512,512]{1,0:T(8,128)(2,1)S(1)}, u32[]{:S(2)}, u32[]{:S(2)}) collective-permute-start(bf16[512,512]{1,0:T(8,128)(2,1)S(1)} %get-tuple-element.100), channel_id=1, source_target_pairs={{0,2},{1,3},{2,0},{3,1},{4,6},{5,7},{6,4},{7,5},{8,10},{9,11},{10,... | collective-permute-start | bytes 1572872 | tf_op jit(solution)/shard_map/ppermute | solution.py:91
  23.3 18.7 %collective-permute-start.6 = (bf16[512,512]{1,0:T(8,128)(2,1)S(1)}, bf16[512,512]{1,0:T(8,128)(2,1)S(1)}, u32[]{:S(2)}, u32[]{:S(2)}) collective-permute-start(bf16[512,512]{1,0:T(8,128)(2,1)S(1)} %get-tuple-element.99), channel_id=1, source_target_pairs={{0,16},{1,17},{2,18},{3,19},{4,20},{5,21},{6,22},{7,23},{8,24},{9,... | collective-permute-start | bytes 1572872 | tf_op jit(solution)/shard_map/ppermute | solution.py:91
  24.8 17.2 %collective-permute-start.7 = (bf16[512,512]{1,0:T(8,128)(2,1)S(1)}, bf16[512,512]{1,0:T(8,128)(2,1)S(1)}, u32[]{:S(2)}, u32[]{:S(2)}) collective-permute-start(bf16[512,512]{1,0:T(8,128)(2,1)S(1)} %get-tuple-element.98), channel_id=1, source_target_pairs={{0,12},{1,13},{2,14},{3,15},{4,0},{5,1},{6,2},{7,3},{8,4},{9,5},{1... | collective-permute-start | bytes 1572872 | tf_op jit(solution)/shard_map/ppermute | solution.py:91
  29.9 2.2 %copy-start = (bf16[256,8192]{1,0:T(8,128)(2,1)S(1)}, bf16[256,8192]{1,0:T(8,128)(2,1)}, u32[]{:S(2)}) copy-start(bf16[256,8192]{1,0:T(8,128)(2,1)} %refs_1_.7) | copy-start | bytes 12582916
  30.6 11.4 %collective-permute-start.9 = (bf16[128,512]{1,0:T(8,128)(2,1)S(1)}, bf16[128,512]{1,0:T(8,128)(2,1)S(1)}, u32[]{:S(2)}, u32[]{:S(2)}) collective-permute-start(bf16[128,512]{1,0:T(8,128)(2,1)S(1)} %get-tuple-element.61), channel_id=1, source_target_pairs={{0,4},{1,5},{2,6},{3,7},{4,8},{5,9},{6,10},{7,11},{8,12},{9,13},{1... | collective-permute-start | bytes 393224 | tf_op jit(solution)/shard_map/ppermute | solution.py:91
  42.1 5.5 %collective-permute-start.15 = (bf16[2048,512]{1,0:T(8,128)(2,1)S(1)}, bf16[2048,512]{1,0:T(8,128)(2,1)S(1)}, u32[]{:S(2)}, u32[]{:S(2)}) collective-permute-start(bf16[2048,512]{1,0:T(8,128)(2,1)S(1)} %pad_maximum_fusion), channel_id=1, source_target_pairs={{0,1},{1,0},{2,3},{3,2},{4,5},{5,4},{6,7},{7,6},{8,9},{9,8},{10,11... | collective-permute-start | bytes 6291464 | tf_op jit(solution)/shard_map/ppermute | solution.py:91
  42.3 17.5 %collective-permute-start.11 = (bf16[512,512]{1,0:T(8,128)(2,1)S(1)}, bf16[512,512]{1,0:T(8,128)(2,1)S(1)}, u32[]{:S(2)}, u32[]{:S(2)}) collective-permute-start(bf16[512,512]{1,0:T(8,128)(2,1)S(1)} %get-tuple-element.97), channel_id=1, source_target_pairs={{0,2},{1,3},{2,0},{3,1},{4,6},{5,7},{6,4},{7,5},{8,10},{9,11},{10,... | collective-permute-start | bytes 1572872 | tf_op jit(solution)/shard_map/ppermute | solution.py:91
  43.6 16.2 %collective-permute-start.12 = (bf16[512,512]{1,0:T(8,128)(2,1)S(1)}, bf16[512,512]{1,0:T(8,128)(2,1)S(1)}, u32[]{:S(2)}, u32[]{:S(2)}) collective-permute-start(bf16[512,512]{1,0:T(8,128)(2,1)S(1)} %get-tuple-element.96), channel_id=1, source_target_pairs={{0,16},{1,17},{2,18},{3,19},{4,20},{5,21},{6,22},{7,23},{8,24},{9,... | collective-permute-start | bytes 1572872 | tf_op jit(solution)/shard_map/ppermute | solution.py:91
  44.2 15.6 %collective-permute-start.13 = (bf16[384,512]{1,0:T(8,128)(2,1)S(1)}, bf16[384,512]{1,0:T(8,128)(2,1)S(1)}, u32[]{:S(2)}, u32[]{:S(2)}) collective-permute-start(bf16[384,512]{1,0:T(8,128)(2,1)S(1)} %pad_maximum_fusion.8), channel_id=1, source_target_pairs={{0,12},{1,13},{2,14},{3,15},{4,0},{5,1},{6,2},{7,3},{8,4},{9,5},{1... | collective-permute-start | bytes 1179656 | tf_op jit(solution)/shard_map/ppermute | solution.py:91
  47.5 12.3 %collective-permute-start.14 = (bf16[128,512]{1,0:T(8,128)(2,1)S(1)}, bf16[128,512]{1,0:T(8,128)(2,1)S(1)}, u32[]{:S(2)}, u32[]{:S(2)}) collective-permute-start(bf16[128,512]{1,0:T(8,128)(2,1)S(1)} %pad_maximum_fusion.9), channel_id=1, source_target_pairs={{0,4},{1,5},{2,6},{3,7},{4,8},{5,9},{6,10},{7,11},{8,12},{9,13},{1... | collective-permute-start | bytes 393224 | tf_op jit(solution)/shard_map/ppermute | solution.py:91
  59.9 3.3 %collective-permute-start.17 = (bf16[1280,512]{1,0:T(8,128)(2,1)S(1)}, bf16[1280,512]{1,0:T(8,128)(2,1)S(1)}, u32[]{:S(2)}, u32[]{:S(2)}) collective-permute-start(bf16[1280,512]{1,0:T(8,128)(2,1)S(1)} %pad_maximum_fusion.1), channel_id=1, source_target_pairs={{0,1},{1,0},{2,3},{3,2},{4,5},{5,4},{6,7},{7,6},{8,9},{9,8},{10,11... | collective-permute-start | bytes 3932168 | tf_op jit(solution)/shard_map/ppermute | solution.py:91
  60.0 3.2 %collective-permute-start.16 = (f32[64,512]{1,0:T(8,128)S(1)}, f32[64,512]{1,0:T(8,128)S(1)}, u32[]{:S(2)}, u32[]{:S(2)}) collective-permute-start(f32[64,512]{1,0:T(8,128)S(1)} %add_multiply_fusion.refs_7_), channel_id=1, source_target_pairs={{0,1},{1,0},{2,3},{3,2},{4,5},{5,4},{6,7},{7,6},{8,9},{9,8},{10,11... | collective-permute-start | bytes 393224 | tf_op jit(solution)/shard_map/ppermute | solution.py:91

commit v6 on v5

--- a/solution.py
+++ b/solution.py
@@ -225,26 +225,31 @@
 def add_y(place, kept, sent, came):
     rows, part = kept.shape
     rank = rows // NZ
-
-    def kernel(place_ref, kept_ref, sent_ref, came_ref, own_ref, next_ref, far_ref, last_ref):
-        z = place_ref[1]
+    fold = rank // 2
+    kinds = [jnp.float32, jnp.float32, jnp.bfloat16, jnp.bfloat16]
+
+    def kernel(place_ref, kept_ref, sent_ref, came_ref, *out_refs):
+        z, c = place_ref[1], place_ref[3]
         f32 = jnp.float32
-        tail = sent_ref[rows:, :].astype(f32) + came_ref[rows:, :].astype(f32)
-        for shift, out_ref in enumerate((own_ref, next_ref, far_ref, last_ref)):
+        for shift in range(NZ):
             at = pl.ds(pl.multiple_of(lax.rem(z + shift, NZ) * rank, rank), rank)
             summed = kept_ref[at, :] + came_ref[at, :].astype(f32)
-            out_ref[:rank, :] = summed.astype(out_ref.dtype)
-            if shift >= 2:
-                out_ref[rank:, :] = tail.astype(jnp.bfloat16)
+            out_refs[shift][...] = summed.astype(kinds[shift])
+        term = sent_ref[rows:, :].astype(f32) + came_ref[rows:, :].astype(f32)
+        low, high = term[:, : part // 2], term[:, part // 2 :]
+        for core, ref in enumerate(out_refs[NZ:]):
+            half = jnp.where(c == core, low, high)
+            ref[:, : part // 2] = half[:fold]
+            ref[:, part // 2 :] = half[fold:]
 
     return pl.pallas_call(
         kernel,
-        out_shape=[jax.ShapeDtypeStruct((rank, part), jnp.float32)] * 2
-        + [jax.ShapeDtypeStruct((2 * rank, part), jnp.bfloat16)] * 2,
+        out_shape=[jax.ShapeDtypeStruct((rank, part), kind) for kind in kinds]
+        + [jax.ShapeDtypeStruct((fold, part), jnp.float32)] * 2,
         in_specs=[scalars()] + [whole()] * 3,
-        out_specs=[whole()] * 4,
+        out_specs=[whole()] * (NZ + 2),
         compiler_params=params(),
-        cost_estimate=pl.CostEstimate(flops=20000000000, bytes_accessed=1, transcendentals=0),
+        cost_estimate=pl.CostEstimate(flops=10000000000, bytes_accessed=1, transcendentals=0),
         name="add_y",
     )(place, kept, sent, came)
 
@@ -255,10 +260,10 @@
     tokens, width = activations.shape
     features = cotangent.shape[1]
     arrays = []
-    for array, _, _ in pieces:
+    for array, *_ in pieces:
         if not any(array is other for other in arrays):
             arrays.append(array)
-    where = [next(i for i, a in enumerate(arrays) if a is array) for array, _, _ in pieces]
+    where = [next(i for i, a in enumerate(arrays) if a is array) for array, *_ in pieces]
     count = len(pieces)
     rows = width // (NZ * 2 * 2 * 2)
 
@@ -275,12 +280,12 @@
         sums, grads, out_sems = refs[-3:]
         g, z, y, c = (place_ref[i] for i in range(4))
         columns, weights, going = [], [], []
-        for p, (_, first, (dz, dy, dc, dh)) in enumerate(pieces):
+        for p, (_, first, size, offset, (dz, dy, dc, dh)) in enumerate(pieces):
             chip = lax.rem(z + (NZ - dz), NZ) * 2 + (1 - y if dy else y)
             device = chip * 2 + (1 - c if dc else c)
-            start = (device * 2 + (1 - g if dh else g)) * rows
-            columns.append(pl.ds(pl.multiple_of(start, rows), rows))
-            weights.append(array_refs[where[p]].at[first : first + rows, :])
+            start = (device * 2 + (1 - g if dh else g)) * rows + offset
+            columns.append(pl.ds(pl.multiple_of(start, BLOCK), size))
+            weights.append(array_refs[where[p]].at[first : first + size, :])
 
         def give(source, target):
             going.append(pltpu.make_async_copy(source, target, out_sems.at[len(going)]))
@@ -288,14 +293,15 @@
 
         def backward():
             for p in range(count):
-                grads[p] = (
+                held = grads.at[p, :, : pieces[p][2]]
+                held[...] = (
                     weight_transpose(cot_ref[...], weights[p][...])
                     + lowrank_scale
                     * jnp.dot(
                         lgrad_ref[...], down_ref[:, columns[p]], preferred_element_type=jnp.float32
                     )
                 ).astype(jnp.bfloat16)
-                give(grads.at[p], grad_ref.at[:, columns[p]])
+                give(held, grad_ref.at[:, columns[p]])
 
         def forward():
             if begin is not None:
@@ -315,9 +321,13 @@
             out_ref[...] = sums[...]
         else:
             up_out, down_out, rounded, up_sum, down_sum = refs[2:7]
-            up_sum[...] = terms[0][...] + terms[1][...]
+            rank = down_ref.shape[0]
+            part = features // 2
+            for ref, core in zip(terms[:2], (c, 1 - c), strict=True):
+                at = pl.ds(pl.multiple_of(core * part, part), part)
+                up_sum[: rank // 2, at] = ref[:, :part]
+                up_sum[rank // 2 :, at] = ref[:, part:]
             give(up_sum, up_out)
-            rank = down_ref.shape[0]
             down_sum[...] = factor * (
                 terms[2][...]
                 + terms[3][:rank, :].astype(jnp.float32)
@@ -350,10 +360,10 @@
     if end is not None:
         operands += end
         specs += [whole()] * 5
-        for term in (end[0], end[2]):
-            out_shape.append(jax.ShapeDtypeStruct(term.shape, jnp.float32))
+        for _ in range(2):
+            out_shape.append(jax.ShapeDtypeStruct((down_t.shape[0], features), jnp.float32))
             out_specs.append(in_hbm())
-            scratch.append(pltpu.VMEM(term.shape, jnp.float32))
+            scratch.append(pltpu.VMEM((down_t.shape[0], features), jnp.float32))
     return pl.pallas_call(
         kernel,
         out_shape=out_shape,
@@ -387,8 +397,11 @@
     def products(pieces, **more):
         return multiply(place, pieces, activations, down_t, cotangent, lgrad, factor, **more)
 
+    def piece(array, first, dc, key, size=half, offset=0):
+        return (array, first, size, offset, (key[0], key[1], dc, key[2]))
+
     def listed(array, dc, *keys):
-        return [(array, i * half, (dz, dy, dc, dh)) for i, (dz, dy, dh) in enumerate(keys)]
+        return [piece(array, i * half, dc, key) for i, key in enumerate(keys)]
 
     own, first = dequantize_shard(place, quant_codes, block_scales)
     own, first, place = barrier((own, first, place))
@@ -396,8 +409,7 @@
     def swap(*arrays):
         return send(join(*arrays), OVER_CORE)
 
-    down1, up1, y1 = send(first, Z_DOWN), send(first, Z_UP), send(own[half:], OVER_Y)
-
+    down1, up1, y1 = send(first, Z_DOWN), send(first, Z_UP), send(own, OVER_Y)
     other_act, other_cot = send(activations, OVER_CORE), send(cotangent, OVER_CORE)
     latent, lgrad, terms_y, kept = local_gradients(
         place, activations, down_t, lowrank_up_factor, cotangent, other_act, other_cot
@@ -405,19 +417,23 @@
     came_y = send(terms_y, OVER_Y)
     down1, up1, y1, kept = barrier((down1, up1, y1, kept))
 
-    down2 = send(join(y1, down1), Z_DOWN)
-    y2, x2 = send(join(up1, first), OVER_Y), send(join(up1, down1), OVER_X)
+    down2 = send(join(y1[half:], down1), Z_DOWN)
+    y2, x2 = send(up1, OVER_Y), send(join(up1, down1), OVER_X)
     rank = down_t.shape[0]
-    own_part, next_part, far_part, last_part = add_y(place, kept, terms_y, came_y)
-    came_up = send(far_part, Z_UP)
+    own_part, next_part, far_part, last_part, up_own, up_away = add_y(
+        place, kept, terms_y, came_y
+    )
+    summed_up = (up_own + send(up_away, OVER_CORE)).astype(jnp.bfloat16)
+    came_up = send(join(far_part, summed_up), Z_UP)
+    last_part = join(last_part, summed_up)
     swap2 = swap(up1, down1, y1)
     own_keys = [(0, 0, 0), (0, 0, 1)]
-    keys = [(1, 0, 0), (3, 0, 0), (0, 1, 1)]
+    keys = [(1, 0, 0), (3, 0, 0), (0, 1, 0), (0, 1, 1)]
     done = products(
         listed(own, 0, *own_keys)
         + listed(up1, 0, keys[0])
         + listed(down1, 0, keys[1])
-        + listed(y1, 0, keys[2])
+        + listed(y1, 0, *keys[2:])
         + listed(swap2, 1, *keys),
         begin=[latent, lowrank_up_factor],
     )
@@ -427,15 +443,15 @@
 
     two = down2[half:]
     down3 = send(join(down2[:half], last_part), Z_DOWN)
-    y3, x3 = send(join(down1, two), OVER_Y), send(join(two, y2[:half]), OVER_X)
+    y3, x3 = send(join(down1, two), OVER_Y), send(join(two, y2), OVER_X)
     next_part = next_part + came_up[:rank].astype(jnp.float32)
     up3 = send(join(next_part.astype(jnp.bfloat16), came_up[rank:]), Z_UP)
     swap3 = swap(y2, x2, down2, own)
-    keys = [(1, 1, 0), (0, 1, 0), (1, 0, 1), (3, 0, 1), (3, 1, 1), (2, 0, 0)]
+    keys = [(1, 1, 0), (1, 0, 1), (3, 0, 1), (3, 1, 1), (2, 0, 0)]
     done = products(
-        listed(y2, 0, *keys[:2])
-        + listed(x2, 0, *keys[2:4])
-        + listed(down2, 0, *keys[4:])
+        listed(y2, 0, keys[0])
+        + listed(x2, 0, *keys[1:3])
+        + listed(down2, 0, *keys[3:])
         + listed(swap3, 1, *keys, *own_keys),
         so_far=done,
     )
@@ -446,16 +462,20 @@
     swap4 = send(join(y3, x3, down3[:half]), OVER_CORE)
     wide = lambda array: array.astype(jnp.float32)
     up_own = factor * (
-        (wide(last_part[rank:]) + wide(up3[rank:])) + (wide(came_up[rank:]) + wide(down3[half + rank :]))
+        (wide(last_part[rank:]) + wide(up3[rank:]))
+        + (wide(came_up[rank:]) + wide(down3[half + rank :]))
     )
     up_came = send(up_own, OVER_CORE)
+
     keys = [(3, 1, 0), (2, 1, 0), (2, 0, 1), (1, 1, 1), (2, 1, 1)]
     done = products(
         listed(y3, 0, *keys[:2]) + listed(x3, 0, *keys[2:4]) + listed(down3, 0, keys[4]),
         so_far=done,
     )
     projected, gradient, grad_up, grad_down_t = products(
-        listed(swap4, 1, *keys), so_far=done, end=[up_own, up_came, own_part, up3, down3]
+        listed(swap4, 1, *keys),
+        so_far=done,
+        end=[up_own, up_came, own_part, up3, down3],
     )
     return (projected, gradient, grad_down_t.T, grad_up)
 

time: 65.9 us -> 62.6 us (0.950)
  waiting for transfers between devices: 20.4 us -> 17.3 us
    ppermute x18 -> x19, waiting for transfers between devices: 20.4 us -> 17.3 us  [send(): return lax.ppermute(array, AXES, pairs)]
    ppermute x18 -> x19, starting transfers between devices: 19.9 us -> 20.1 us  [send(): return lax.ppermute(array, AXES, pairs)]
  transfers between devices with their start and end apart: 18 -> 19, of which waited for: 5 -> 6; matrix products, arithmetic and copies ran while one was open for 1% -> 1% of each run, Pallas kernels for 25% -> 26%
where the time goes in v6:
time: 62.6 us; the launch traced here: 62.3 us
  starting transfers between devices  20.1 us (32%)
  Pallas kernels  18.6 us (30%)
  waiting for transfers between devices  17.3 us (28%)
  local copies, waits for them, and re-layouts  4.81 us (8%)
  between operations  0.86 us (1%)
    ppermute x19, starting transfers between devices, send(): return lax.ppermute(array, AXES, pairs)  20.1 us
    ppermute x19, waiting for transfers between devices, send(): return lax.ppermute(array, AXES, pairs)  17.3 us
    pallas_call x4, Pallas kernels, multiply(): pl.pallas_call(kernel, out_shape=out_shape, in_specs=specs + [whole()] *...  11.5 us
    pallas_call x1, Pallas kernels, local_gradients(): pl.pallas_call(kernel, out_shape=[jax.ShapeDtypeStruct((tokens, rank), bf...  5.83 us
    unnamed x12, local copies, waits for them, and re-layouts  4.74 us
  transfers between devices with their start and end apart: 19, of which 6 were waited for; matrix products, arithmetic and copies ran while one was open for 1% of the time, Pallas kernels for 26%

profile of v6, /device:TPU:0, one launch (start us, length us, event | category | flops | bytes accessed | tf_op | source)
XLA Modules:
  0.0 62.3 jit_solution(18000313173599760330)
XLA Ops:
  0.6 0.5 collective-permute-start
  1.1 0.1 pad_add_fusion.place_ref.refs_0_
  1.2 1.0 %copy-done.3 = bf16[512,512]{1,0:T(8,128)(2,1)S(1)} copy-done((bf16[512,512]{1,0:T(8,128)(2,1)S(1)}, bf16[512,512]{1,0:T(8,128)(2,1)}, u32[]{:S(2)}) %copy-start.3) | copy-done | bytes 524312
  2.3 0.7 %copy-done.5 = f32[4,4]{1,0:T(4,128)S(1)} copy-done((f32[4,4]{1,0:T(4,128)S(1)}, f32[4,4]{1,0:T(4,128)}, u32[]{:S(2)}) %copy-start.5) | copy-done | bytes 88
  3.0 0.7 %dequantize.1 = (bf16[512,512]{1,0:T(8,128)(2,1)S(1)}, bf16[256,512]{1,0:T(8,128)(2,1)S(1)}) custom-call(s32[4]{0:T(128)S(1)} %pad_add_fusion.place_ref.refs_0_, bf16[512,512]{1,0:T(8,128)(2,1)S(1)} %copy-done.3, f32[4,4]{1,0:T(4,128)S(1)} %copy-done.5), custom_call_target="tpu_custom_call" | custom-call | flops 1 | bytes 1 | tf_op jit(solution)/shard_map/dequantize/pallas_call | solution.py:130
  3.7 2.6 %collective-permute-start.4 = (bf16[512,512]{1,0:T(8,128)(2,1)S(1)}, bf16[512,512]{1,0:T(8,128)(2,1)S(1)}, u32[]{:S(2)}, u32[]{:S(2)}) collective-permute-start(bf16[512,512]{1,0:T(8,128)(2,1)S(1)} %get-tuple-element.56.refs_7_), channel_id=1, source_target_pairs={{0,2},{1,3},{2,0},{3,1},{4,6},{5,7},{6,4},{7,5},{8,10},{9,11},{10,... | collective-permute-start | bytes 1572872 | tf_op jit(solution)/shard_map/ppermute | solution.py:91
  6.3 0.2 collective-permute-start.1
  6.5 3.6 %collective-permute-start.2 = (bf16[256,512]{1,0:T(8,128)(2,1)S(1)}, bf16[256,512]{1,0:T(8,128)(2,1)S(1)}, u32[]{:S(2)}, u32[]{:S(2)}) collective-permute-start(bf16[256,512]{1,0:T(8,128)(2,1)S(1)} %get-tuple-element.55), channel_id=1, source_target_pairs={{0,12},{1,13},{2,14},{3,15},{4,0},{5,1},{6,2},{7,3},{8,4},{9,5},{1... | collective-permute-start | bytes 786440 | tf_op jit(solution)/shard_map/ppermute | solution.py:91
  10.1 0.0 collective-permute-done.other_hbm
  10.1 0.0 copy-start.1
  10.1 1.2 %copy-done.1 = bf16[8192,64]{0,1:T(8,128)(2,1)S(1)} copy-done((bf16[8192,64]{0,1:T(8,128)(2,1)S(1)}, bf16[8192,64]{0,1:T(8,128)(2,1)}, u32[]{:S(2)}) %copy-start.1) | copy-done | bytes 1048600
  11.3 0.9 %copy-done.2 = bf16[256,512]{1,0:T(8,128)(2,1)S(1)} copy-done((bf16[256,512]{1,0:T(8,128)(2,1)S(1)}, bf16[256,512]{1,0:T(8,128)(2,1)}, u32[]{:S(2)}) %copy-start.2) | copy-done | bytes 262168
  12.3 0.8 %copy-done.4 = bf16[64,512]{1,0:T(8,128)(2,1)S(1)} copy-done((bf16[64,512]{1,0:T(8,128)(2,1)S(1)}, bf16[64,512]{1,0:T(8,128)(2,1)}, u32[]{:S(2)}) %copy-start.4) | copy-done | bytes 65560
  13.1 5.8 %local_gradients.1 = (bf16[256,64]{1,0:T(8,128)(2,1)S(1)}, bf16[256,64]{1,0:T(8,128)(2,1)S(1)}, bf16[320,512]{1,0:T(8,128)(2,1)S(1)}, f32[256,512]{1,0:T(8,128)S(1)}) custom-call(s32[4]{0:T(128)S(1)} %pad_add_fusion.place_ref.refs_0_, bf16[256,8192]{1,0:T(8,128)(2,1)} %refs_1_.7, bf16[64,8192]{1,0:T(8,128)(2,1)S(1)} %bitcast.6, ...), custom_call_target="tpu_custom_call" | custom-call | flops 1 | bytes 1 | tf_op jit(solution)/shard_map/local_gradients/pallas_call | solution.py:196
  18.9 1.4 %collective-permute-start.8 = (bf16[320,512]{1,0:T(8,128)(2,1)S(1)}, bf16[320,512]{1,0:T(8,128)(2,1)S(1)}, u32[]{:S(2)}, u32[]{:S(2)}) collective-permute-start(bf16[320,512]{1,0:T(8,128)(2,1)S(1)} %get-tuple-element.62.sent_ref), channel_id=1, source_target_pairs={{0,2},{1,3},{2,0},{3,1},{4,6},{5,7},{6,4},{7,5},{8,10},{9,11},{10,... | collective-permute-start | bytes 983048 | tf_op jit(solution)/shard_map/ppermute | solution.py:91
  20.3 2.3 %collective-permute-done.3.refs_8_ = bf16[256,512]{1,0:T(8,128)(2,1)S(1)} collective-permute-done((bf16[256,512]{1,0:T(8,128)(2,1)S(1)}, bf16[256,512]{1,0:T(8,128)(2,1)S(1)}, u32[]{:S(2)}, u32[]{:S(2)}) %collective-permute-start.3) | collective-permute-done | bytes 262176 | tf_op jit(solution)/shard_map/ppermute | solution.py:91
  22.6 0.0 collective-permute-done.4.refs_10_
  22.6 0.1 pad_maximum_fusion.2
  22.7 0.1 collective-permute-start.11
  22.8 0.1 pad_maximum_fusion.3
  22.9 1.6 %collective-permute-start.6 = (bf16[512,512]{1,0:T(8,128)(2,1)S(1)}, bf16[512,512]{1,0:T(8,128)(2,1)S(1)}, u32[]{:S(2)}, u32[]{:S(2)}) collective-permute-start(bf16[512,512]{1,0:T(8,128)(2,1)S(1)} %get-tuple-element.103), channel_id=1, source_target_pairs={{0,16},{1,17},{2,18},{3,19},{4,20},{5,21},{6,22},{7,23},{8,24},{9,... | collective-permute-start | bytes 1572872 | tf_op jit(solution)/shard_map/ppermute | solution.py:91
  24.4 1.7 %collective-permute-start.7 = (bf16[512,512]{1,0:T(8,128)(2,1)S(1)}, bf16[512,512]{1,0:T(8,128)(2,1)S(1)}, u32[]{:S(2)}, u32[]{:S(2)}) collective-permute-start(bf16[512,512]{1,0:T(8,128)(2,1)S(1)} %get-tuple-element.102), channel_id=1, source_target_pairs={{0,12},{1,13},{2,14},{3,15},{4,0},{5,1},{6,2},{7,3},{8,4},{9,5},{1... | collective-permute-start | bytes 1572872 | tf_op jit(solution)/shard_map/ppermute | solution.py:91
  26.2 2.5 %collective-permute-done.8.came_ref = bf16[320,512]{1,0:T(8,128)(2,1)S(1)} collective-permute-done((bf16[320,512]{1,0:T(8,128)(2,1)S(1)}, bf16[320,512]{1,0:T(8,128)(2,1)S(1)}, u32[]{:S(2)}, u32[]{:S(2)}) %collective-permute-start.8) | collective-permute-done | bytes 327712 | tf_op jit(solution)/shard_map/ppermute | solution.py:91
  28.7 0.6 add_y.1
  29.3 0.1 collective-permute-start.9
  29.4 1.5 %collective-permute-start.5 = (bf16[256,512]{1,0:T(8,128)(2,1)S(1)}, bf16[256,512]{1,0:T(8,128)(2,1)S(1)}, u32[]{:S(2)}, u32[]{:S(2)}) collective-permute-start(bf16[256,512]{1,0:T(8,128)(2,1)S(1)} %collective-permute-done.3.refs_8_), channel_id=1, source_target_pairs={{0,2},{1,3},{2,0},{3,1},{4,6},{5,7},{6,4},{7,5},{8,10},{9,11},{10,... | collective-permute-start | bytes 786440 | tf_op jit(solution)/shard_map/ppermute | solution.py:91
  30.9 0.0 collective-permute-done.9
  30.9 1.6 %collective-permute-start.10 = (bf16[96,512]{1,0:T(8,128)(2,1)S(1)}, bf16[96,512]{1,0:T(8,128)(2,1)S(1)}, u32[]{:S(2)}, u32[]{:S(2)}) collective-permute-start(bf16[96,512]{1,0:T(8,128)(2,1)S(1)} %get-tuple-element.105), channel_id=1, source_target_pairs={{0,4},{1,5},{2,6},{3,7},{4,8},{5,9},{6,10},{7,11},{8,12},{9,13},{1... | collective-permute-start | bytes 294920 | tf_op jit(solution)/shard_map/ppermute | solution.py:91
  32.5 3.2 %multiply.4 = (f32[256,512]{1,0:T(8,128)S(1)}, bf16[256,8192]{1,0:T(8,128)(2,1)}) custom-call(s32[4]{0:T(128)S(1)} %pad_add_fusion.place_ref.refs_0_, bf16[256,8192]{1,0:T(8,128)(2,1)S(1)} %copy-done, bf16[64,8192]{1,0:T(8,128)(2,1)S(1)} %bitcast.7, bf16[256,512]{1,0:T(8,128)(2,1)S(1)} %copy-done.2, bf16[256,64]{1,0:T(8,128)(2,1)S(1)} %get-tuple-element.54.refs_4_, ...), custom_call_target="tpu_custom_call" | custom-call | flops 1 | bytes 1 | tf_op jit(solution)/shard_map/multiply/pallas_call | solution.py:367
  35.7 2.4 %collective-permute-done.5.refs_7_ = bf16[256,512]{1,0:T(8,128)(2,1)S(1)} collective-permute-done((bf16[256,512]{1,0:T(8,128)(2,1)S(1)}, bf16[256,512]{1,0:T(8,128)(2,1)S(1)}, u32[]{:S(2)}, u32[]{:S(2)}) %collective-permute-start.5) | collective-permute-done | bytes 262176 | tf_op jit(solution)/shard_map/ppermute | solution.py:91
  38.1 2.8 %collective-permute-done.10 = bf16[96,512]{1,0:T(8,128)(2,1)S(1)} collective-permute-done((bf16[96,512]{1,0:T(8,128)(2,1)S(1)}, bf16[96,512]{1,0:T(8,128)(2,1)S(1)}, u32[]{:S(2)}, u32[]{:S(2)}) %collective-permute-start.10) | collective-permute-done | bytes 98336 | tf_op jit(solution)/shard_map/ppermute | solution.py:91
  40.9 0.1 pad_maximum_fusion
  41.0 0.1 collective-permute-start.16
  41.1 0.1 pad_maximum_fusion.6
  41.2 0.6 collective-permute-start.12
  41.8 0.5 collective-permute-start.13
  42.4 3.3 %collective-permute-start.14 = (bf16[352,512]{1,0:T(8,128)(2,1)S(1)}, bf16[352,512]{1,0:T(8,128)(2,1)S(1)}, u32[]{:S(2)}, u32[]{:S(2)}) collective-permute-start(bf16[352,512]{1,0:T(8,128)(2,1)S(1)} %pad_maximum_fusion.7), channel_id=1, source_target_pairs={{0,12},{1,13},{2,14},{3,15},{4,0},{5,1},{6,2},{7,3},{8,4},{9,5},{1... | collective-permute-start | bytes 1081352 | tf_op jit(solution)/shard_map/ppermute | solution.py:91
  45.7 0.1 collective-permute-start.15
  45.8 3.6 %multiply.5 = (f32[256,512]{1,0:T(8,128)S(1)}, bf16[256,8192]{1,0:T(8,128)(2,1)}) custom-call(s32[4]{0:T(128)S(1)} %pad_add_fusion.place_ref.refs_0_, bf16[256,8192]{1,0:T(8,128)(2,1)S(1)} %copy-done, bf16[64,8192]{1,0:T(8,128)(2,1)S(1)} %bitcast.8, bf16[256,512]{1,0:T(8,128)(2,1)S(1)} %copy-done.2, ...), custom_call_target="tpu_custom_call", output_to_operand_aliasing={{1}: (6, {})} | custom-call | flops 1 | bytes 1 | tf_op jit(solution)/shard_map/multiply/pallas_call | solution.py:367
  49.5 7.1 %collective-permute-done.15.refs_10_ = bf16[96,512]{1,0:T(8,128)(2,1)S(1)} collective-permute-done((bf16[96,512]{1,0:T(8,128)(2,1)S(1)}, bf16[96,512]{1,0:T(8,128)(2,1)S(1)}, u32[]{:S(2)}, u32[]{:S(2)}) %collective-permute-start.15) | collective-permute-done | bytes 98336 | tf_op jit(solution)/shard_map/ppermute | solution.py:91
  56.6 0.0 collective-permute-done.13.refs_8_
  56.6 0.1 pad_maximum_fusion.1
  56.7 0.1 collective-permute-start.18
  56.8 0.6 collective-permute-start.17
  57.4 2.3 %multiply.6 = (f32[256,512]{1,0:T(8,128)S(1)}, bf16[256,8192]{1,0:T(8,128)(2,1)}) custom-call(s32[4]{0:T(128)S(1)} %pad_add_fusion.place_ref.refs_0_, bf16[256,8192]{1,0:T(8,128)(2,1)S(1)} %copy-done, bf16[64,8192]{1,0:T(8,128)(2,1)S(1)} %bitcast.9, bf16[256,512]{1,0:T(8,128)(2,1)S(1)} %copy-done.2, ...), custom_call_target="tpu_custom_call", output_to_operand_aliasing={{1}: (6, {})} | custom-call | flops 1 | bytes 1 | tf_op jit(solution)/shard_map/multiply/pallas_call | solution.py:367
  59.7 0.2 collective-permute-done.17.refs_8_
  59.9 0.0 collective-permute-done.18.refs_12_
  59.9 2.4 %multiply.7 = (bf16[256,512]{1,0:T(8,128)(2,1)}, bf16[256,8192]{1,0:T(8,128)(2,1)}, f32[64,512]{1,0:T(8,128)}, f32[64,512]{1,0:T(8,128)}) custom-call(s32[4]{0:T(128)S(1)} %pad_add_fusion.place_ref.refs_0_, bf16[256,8192]{1,0:T(8,128)(2,1)S(1)} %copy-done, bf16[64,8192]{1,0:T(8,128)(2,1)S(1)} %bitcast.10, ...), custom_call_target="tpu_custom_call", output_to_operand_aliasing={{1}: (6, {})} | custom-call | flops 1 | bytes 1 | tf_op jit(solution)/shard_map/multiply/pallas_call | solution.py:367
  (25 shorter events, 0.2 us)
Async XLA Ops:
  0.6 9.4 %collective-permute-start = (bf16[256,8192]{1,0:T(8,128)(2,1)}, bf16[256,8192]{1,0:T(8,128)(2,1)}, u32[]{:S(2)}, u32[]{:S(2)}) collective-permute-start(bf16[256,8192]{1,0:T(8,128)(2,1)} %refs_1_.7), channel_id=1, source_target_pairs={{0,1},{1,0},{2,3},{3,2},{4,5},{5,4},{6,7},{7,6},{8,9},{9,8},{10,11... | collective-permute-start | bytes 12582920 | tf_op jit(solution)/shard_map/ppermute | solution.py:91
  1.2 1.0 %copy-start.3 = (bf16[512,512]{1,0:T(8,128)(2,1)S(1)}, bf16[512,512]{1,0:T(8,128)(2,1)}, u32[]{:S(2)}) copy-start(bf16[512,512]{1,0:T(8,128)(2,1)} %codes_ref.1) | copy-start | bytes 1572868
  2.3 0.7 %copy-start.5 = (f32[4,4]{1,0:T(4,128)S(1)}, f32[4,4]{1,0:T(4,128)}, u32[]{:S(2)}) copy-start(f32[4,4]{1,0:T(4,128)} %scales_ref.1) | copy-start | bytes 196
  3.7 19.0 %collective-permute-start.4 = (bf16[512,512]{1,0:T(8,128)(2,1)S(1)}, bf16[512,512]{1,0:T(8,128)(2,1)S(1)}, u32[]{:S(2)}, u32[]{:S(2)}) collective-permute-start(bf16[512,512]{1,0:T(8,128)(2,1)S(1)} %get-tuple-element.56.refs_7_), channel_id=1, source_target_pairs={{0,2},{1,3},{2,0},{3,1},{4,6},{5,7},{6,4},{7,5},{8,10},{9,11},{10,... | collective-permute-start | bytes 1572872 | tf_op jit(solution)/shard_map/ppermute | solution.py:91
  6.3 3.8 %collective-permute-start.1 = (bf16[256,512]{1,0:T(8,128)(2,1)}, bf16[256,512]{1,0:T(8,128)(2,1)S(1)}, u32[]{:S(2)}, u32[]{:S(2)}) collective-permute-start(bf16[256,512]{1,0:T(8,128)(2,1)} %refs_3_.7), channel_id=1, source_target_pairs={{0,1},{1,0},{2,3},{3,2},{4,5},{5,4},{6,7},{7,6},{8,9},{9,8},{10,11... | collective-permute-start | bytes 786440 | tf_op jit(solution)/shard_map/ppermute | solution.py:91
  6.5 13.9 %collective-permute-start.2 = (bf16[256,512]{1,0:T(8,128)(2,1)S(1)}, bf16[256,512]{1,0:T(8,128)(2,1)S(1)}, u32[]{:S(2)}, u32[]{:S(2)}) collective-permute-start(bf16[256,512]{1,0:T(8,128)(2,1)S(1)} %get-tuple-element.55), channel_id=1, source_target_pairs={{0,12},{1,13},{2,14},{3,15},{4,0},{5,1},{6,2},{7,3},{8,4},{9,5},{1... | collective-permute-start | bytes 786440 | tf_op jit(solution)/shard_map/ppermute | solution.py:91
  10.1 12.6 %collective-permute-start.3 = (bf16[256,512]{1,0:T(8,128)(2,1)S(1)}, bf16[256,512]{1,0:T(8,128)(2,1)S(1)}, u32[]{:S(2)}, u32[]{:S(2)}) collective-permute-start(bf16[256,512]{1,0:T(8,128)(2,1)S(1)} %get-tuple-element.55), channel_id=1, source_target_pairs={{0,4},{1,5},{2,6},{3,7},{4,8},{5,9},{6,10},{7,11},{8,12},{9,13},{1... | collective-permute-start | bytes 786440 | tf_op jit(solution)/shard_map/ppermute | solution.py:91
  10.1 1.2 %copy-start.1 = (bf16[8192,64]{0,1:T(8,128)(2,1)S(1)}, bf16[8192,64]{0,1:T(8,128)(2,1)}, u32[]{:S(2)}) copy-start(bf16[8192,64]{0,1:T(8,128)(2,1)} %param.9) | copy-start | bytes 3145732
  11.3 0.9 %copy-start.2 = (bf16[256,512]{1,0:T(8,128)(2,1)S(1)}, bf16[256,512]{1,0:T(8,128)(2,1)}, u32[]{:S(2)}) copy-start(bf16[256,512]{1,0:T(8,128)(2,1)} %refs_3_.7) | copy-start | bytes 786436
  12.3 0.8 %copy-start.4 = (bf16[64,512]{1,0:T(8,128)(2,1)S(1)}, bf16[64,512]{1,0:T(8,128)(2,1)}, u32[]{:S(2)}) copy-start(bf16[64,512]{1,0:T(8,128)(2,1)} %refs_6_.1) | copy-start | bytes 196612
  18.9 9.7 %collective-permute-start.8 = (bf16[320,512]{1,0:T(8,128)(2,1)S(1)}, bf16[320,512]{1,0:T(8,128)(2,1)S(1)}, u32[]{:S(2)}, u32[]{:S(2)}) collective-permute-start(bf16[320,512]{1,0:T(8,128)(2,1)S(1)} %get-tuple-element.62.sent_ref), channel_id=1, source_target_pairs={{0,2},{1,3},{2,0},{3,1},{4,6},{5,7},{6,4},{7,5},{8,10},{9,11},{10,... | collective-permute-start | bytes 983048 | tf_op jit(solution)/shard_map/ppermute | solution.py:91
  22.7 9.8 %collective-permute-start.11 = (bf16[1024,512]{1,0:T(8,128)(2,1)S(1)}, bf16[1024,512]{1,0:T(8,128)(2,1)S(1)}, u32[]{:S(2)}, u32[]{:S(2)}) collective-permute-start(bf16[1024,512]{1,0:T(8,128)(2,1)S(1)} %pad_maximum_fusion.2), channel_id=1, source_target_pairs={{0,1},{1,0},{2,3},{3,2},{4,5},{5,4},{6,7},{7,6},{8,9},{9,8},{10,11... | collective-permute-start | bytes 3145736 | tf_op jit(solution)/shard_map/ppermute | solution.py:91
  22.9 18.0 %collective-permute-start.6 = (bf16[512,512]{1,0:T(8,128)(2,1)S(1)}, bf16[512,512]{1,0:T(8,128)(2,1)S(1)}, u32[]{:S(2)}, u32[]{:S(2)}) collective-permute-start(bf16[512,512]{1,0:T(8,128)(2,1)S(1)} %get-tuple-element.103), channel_id=1, source_target_pairs={{0,16},{1,17},{2,18},{3,19},{4,20},{5,21},{6,22},{7,23},{8,24},{9,... | collective-permute-start | bytes 1572872 | tf_op jit(solution)/shard_map/ppermute | solution.py:91
  24.4 16.4 %collective-permute-start.7 = (bf16[512,512]{1,0:T(8,128)(2,1)S(1)}, bf16[512,512]{1,0:T(8,128)(2,1)S(1)}, u32[]{:S(2)}, u32[]{:S(2)}) collective-permute-start(bf16[512,512]{1,0:T(8,128)(2,1)S(1)} %get-tuple-element.102), channel_id=1, source_target_pairs={{0,12},{1,13},{2,14},{3,15},{4,0},{5,1},{6,2},{7,3},{8,4},{9,5},{1... | collective-permute-start | bytes 1572872 | tf_op jit(solution)/shard_map/ppermute | solution.py:91
  28.6 3.9 %copy-start = (bf16[256,8192]{1,0:T(8,128)(2,1)S(1)}, bf16[256,8192]{1,0:T(8,128)(2,1)}, u32[]{:S(2)}) copy-start(bf16[256,8192]{1,0:T(8,128)(2,1)} %refs_1_.7) | copy-start | bytes 12582916
  29.3 1.6 %collective-permute-start.9 = (f32[32,512]{1,0:T(8,128)S(1)}, f32[32,512]{1,0:T(8,128)S(1)}, u32[]{:S(2)}, u32[]{:S(2)}) collective-permute-start(f32[32,512]{1,0:T(8,128)S(1)} %get-tuple-element.65), channel_id=1, source_target_pairs={{0,1},{1,0},{2,3},{3,2},{4,5},{5,4},{6,7},{7,6},{8,9},{9,8},{10,11... | collective-permute-start | bytes 196616 | tf_op jit(solution)/shard_map/ppermute | solution.py:91
  29.4 8.7 %collective-permute-start.5 = (bf16[256,512]{1,0:T(8,128)(2,1)S(1)}, bf16[256,512]{1,0:T(8,128)(2,1)S(1)}, u32[]{:S(2)}, u32[]{:S(2)}) collective-permute-start(bf16[256,512]{1,0:T(8,128)(2,1)S(1)} %collective-permute-done.3.refs_8_), channel_id=1, source_target_pairs={{0,2},{1,3},{2,0},{3,1},{4,6},{5,7},{6,4},{7,5},{8,10},{9,11},{10,... | collective-permute-start | bytes 786440 | tf_op jit(solution)/shard_map/ppermute | solution.py:91
  30.9 10.0 %collective-permute-start.10 = (bf16[96,512]{1,0:T(8,128)(2,1)S(1)}, bf16[96,512]{1,0:T(8,128)(2,1)S(1)}, u32[]{:S(2)}, u32[]{:S(2)}) collective-permute-start(bf16[96,512]{1,0:T(8,128)(2,1)S(1)} %get-tuple-element.105), channel_id=1, source_target_pairs={{0,4},{1,5},{2,6},{3,7},{4,8},{5,9},{6,10},{7,11},{8,12},{9,13},{1... | collective-permute-start | bytes 294920 | tf_op jit(solution)/shard_map/ppermute | solution.py:91
  41.0 4.8 %collective-permute-start.16 = (bf16[1792,512]{1,0:T(8,128)(2,1)S(1)}, bf16[1792,512]{1,0:T(8,128)(2,1)S(1)}, u32[]{:S(2)}, u32[]{:S(2)}) collective-permute-start(bf16[1792,512]{1,0:T(8,128)(2,1)S(1)} %pad_maximum_fusion), channel_id=1, source_target_pairs={{0,1},{1,0},{2,3},{3,2},{4,5},{5,4},{6,7},{7,6},{8,9},{9,8},{10,11... | collective-permute-start | bytes 5505032 | tf_op jit(solution)/shard_map/ppermute | solution.py:91
  41.2 15.3 %collective-permute-start.12 = (bf16[512,512]{1,0:T(8,128)(2,1)S(1)}, bf16[512,512]{1,0:T(8,128)(2,1)S(1)}, u32[]{:S(2)}, u32[]{:S(2)}) collective-permute-start(bf16[512,512]{1,0:T(8,128)(2,1)S(1)} %get-tuple-element.101), channel_id=1, source_target_pairs={{0,2},{1,3},{2,0},{3,1},{4,6},{5,7},{6,4},{7,5},{8,10},{9,11},{10,... | collective-permute-start | bytes 1572872 | tf_op jit(solution)/shard_map/ppermute | solution.py:91
  41.8 14.8 %collective-permute-start.13 = (bf16[512,512]{1,0:T(8,128)(2,1)S(1)}, bf16[512,512]{1,0:T(8,128)(2,1)S(1)}, u32[]{:S(2)}, u32[]{:S(2)}) collective-permute-start(bf16[512,512]{1,0:T(8,128)(2,1)S(1)} %get-tuple-element.100), channel_id=1, source_target_pairs={{0,16},{1,17},{2,18},{3,19},{4,20},{5,21},{6,22},{7,23},{8,24},{9,... | collective-permute-start | bytes 1572872 | tf_op jit(solution)/shard_map/ppermute | solution.py:91
  42.4 14.2 %collective-permute-start.14 = (bf16[352,512]{1,0:T(8,128)(2,1)S(1)}, bf16[352,512]{1,0:T(8,128)(2,1)S(1)}, u32[]{:S(2)}, u32[]{:S(2)}) collective-permute-start(bf16[352,512]{1,0:T(8,128)(2,1)S(1)} %pad_maximum_fusion.7), channel_id=1, source_target_pairs={{0,12},{1,13},{2,14},{3,15},{4,0},{5,1},{6,2},{7,3},{8,4},{9,5},{1... | collective-permute-start | bytes 1081352 | tf_op jit(solution)/shard_map/ppermute | solution.py:91
  45.7 10.8 %collective-permute-start.15 = (bf16[96,512]{1,0:T(8,128)(2,1)S(1)}, bf16[96,512]{1,0:T(8,128)(2,1)S(1)}, u32[]{:S(2)}, u32[]{:S(2)}) collective-permute-start(bf16[96,512]{1,0:T(8,128)(2,1)S(1)} %pad_maximum_fusion.10), channel_id=1, source_target_pairs={{0,4},{1,5},{2,6},{3,7},{4,8},{5,9},{6,10},{7,11},{8,12},{9,13},{1... | collective-permute-start | bytes 294920 | tf_op jit(solution)/shard_map/ppermute | solution.py:91
  56.7 3.2 %collective-permute-start.18 = (bf16[1280,512]{1,0:T(8,128)(2,1)S(1)}, bf16[1280,512]{1,0:T(8,128)(2,1)S(1)}, u32[]{:S(2)}, u32[]{:S(2)}) collective-permute-start(bf16[1280,512]{1,0:T(8,128)(2,1)S(1)} %pad_maximum_fusion.1), channel_id=1, source_target_pairs={{0,1},{1,0},{2,3},{3,2},{4,5},{5,4},{6,7},{7,6},{8,9},{9,8},{10,11... | collective-permute-start | bytes 3932168 | tf_op jit(solution)/shard_map/ppermute | solution.py:91
  56.8 3.1 %collective-permute-start.17 = (f32[32,512]{1,0:T(8,128)S(1)}, f32[32,512]{1,0:T(8,128)S(1)}, u32[]{:S(2)}, u32[]{:S(2)}) collective-permute-start(f32[32,512]{1,0:T(8,128)S(1)} %add_multiply_fusion.refs_7_), channel_id=1, source_target_pairs={{0,1},{1,0},{2,3},{3,2},{4,5},{5,4},{6,7},{7,6},{8,9},{9,8},{10,11... | collective-permute-start | bytes 196616 | tf_op jit(solution)/shard_map/ppermute | solution.py:91

commit v7 on v6

--- a/solution.py
+++ b/solution.py
@@ -87,6 +87,11 @@
 Z_FAR = pairs_of(lambda g, z, y, c: (g, (z + 2) % NZ, y, c))
 
 
+def position():
+    f = lax.axis_index("fsdp")
+    return lax.axis_index("groups"), f >> 2, (f >> 1) & 1, f & 1
+
+
 def send(array, pairs):
     return lax.ppermute(array, AXES, pairs)
 
@@ -110,12 +115,12 @@
 LITTLE = pl.CostEstimate(flops=1, bytes_accessed=1, transcendentals=0)
 
 
-def dequantize_shard(place, quant_codes, block_scales):
+def dequantize_shard(quant_codes, block_scales):
     rows, columns = quant_codes.shape
     half = rows // 2
 
-    def kernel(place_ref, codes_ref, scales_ref, own_ref, first_ref):
-        g = place_ref[0]
+    def kernel(codes_ref, scales_ref, own_ref, first_ref):
+        g = position()[0]
         for i in range(rows // BLOCK):
             source = lax.rem(g * (half // BLOCK) + i, rows // BLOCK)
             start = pl.multiple_of(source * BLOCK, BLOCK)
@@ -133,15 +138,15 @@
             jax.ShapeDtypeStruct((rows, columns), jnp.bfloat16),
             jax.ShapeDtypeStruct((half, columns), jnp.bfloat16),
         ],
-        in_specs=[scalars(), whole(), scalars()],
+        in_specs=[whole(), scalars()],
         out_specs=[whole()] * 2,
         compiler_params=params(),
         cost_estimate=LITTLE,
         name="dequantize",
-    )(place, quant_codes, block_scales)
-
-
-def local_gradients(place, activations, down_t, up, cotangent, other_act, other_cot):
+    )(quant_codes, block_scales)
+
+
+def local_gradients(activations, down_t, up, cotangent, other_act, other_cot):
     tokens, width = activations.shape
     rank, features = up.shape
     chips = NZ * 2
@@ -149,11 +154,11 @@
     part = chunk // 2
 
     def kernel(
-        place_ref, act_hbm, down_hbm, up_hbm, cot_hbm, other_hbm, other_cot_hbm, latent_ref,
+        act_hbm, down_hbm, up_hbm, cot_hbm, other_hbm, other_cot_hbm, latent_ref,
         lgrad_ref, message_ref, kept_ref, act_ref, down_ref, up_ref, cot_ref, other_ref,
         other_cot_ref, total, lgrad_t, other_t, sums, sems,
     ):
-        y, c = place_ref[2], place_ref[3]
+        _, _, y, c = position()
         copies = []
 
         def fetch(source, target):
@@ -201,7 +206,7 @@
             jax.ShapeDtypeStruct(((NZ + 1) * rank, part), bf16),
             jax.ShapeDtypeStruct((NZ * rank, part), jnp.float32),
         ],
-        in_specs=[scalars()] + [in_hbm()] * 6,
+        in_specs=[in_hbm()] * 6,
         out_specs=[whole()] * 4,
         scratch_shapes=[
             pltpu.VMEM((chips, tokens, chunk), bf16),
@@ -216,20 +221,20 @@
             pltpu.VMEM((2, NZ * rank, part), jnp.float32),
             pltpu.SemaphoreType.DMA((3 * chips + 3,)),
         ],
-        compiler_params=pltpu.CompilerParams(vmem_limit_bytes=50 * 1024 * 1024),
+        compiler_params=pltpu.CompilerParams(vmem_limit_bytes=54 * 1024 * 1024),
         cost_estimate=LITTLE,
         name="local_gradients",
-    )(place, activations, down_t, up, cotangent, other_act, other_cot)
-
-
-def add_y(place, kept, sent, came):
+    )(activations, down_t, up, cotangent, other_act, other_cot)
+
+
+def add_y(kept, sent, came):
     rows, part = kept.shape
     rank = rows // NZ
     fold = rank // 2
     kinds = [jnp.float32, jnp.float32, jnp.bfloat16, jnp.bfloat16]
 
-    def kernel(place_ref, kept_ref, sent_ref, came_ref, *out_refs):
-        z, c = place_ref[1], place_ref[3]
+    def kernel(kept_ref, sent_ref, came_ref, *out_refs):
+        _, z, _, c = position()
         f32 = jnp.float32
         for shift in range(NZ):
             at = pl.ds(pl.multiple_of(lax.rem(z + shift, NZ) * rank, rank), rank)
@@ -246,16 +251,16 @@
         kernel,
         out_shape=[jax.ShapeDtypeStruct((rank, part), kind) for kind in kinds]
         + [jax.ShapeDtypeStruct((fold, part), jnp.float32)] * 2,
-        in_specs=[scalars()] + [whole()] * 3,
+        in_specs=[whole()] * 3,
         out_specs=[whole()] * (NZ + 2),
         compiler_params=params(),
         cost_estimate=pl.CostEstimate(flops=10000000000, bytes_accessed=1, transcendentals=0),
         name="add_y",
-    )(place, kept, sent, came)
+    )(kept, sent, came)
 
 
 def multiply(
-    place, pieces, activations, down_t, cotangent, lgrad, factor, begin=None, so_far=None, end=None
+    pieces, activations, down_t, cotangent, lgrad, factor, begin=None, so_far=None, end=None
 ):
     tokens, width = activations.shape
     features = cotangent.shape[1]
@@ -269,8 +274,8 @@
 
     def kernel(*refs):
         refs = list(refs)
-        place_ref, act_ref, down_ref, cot_ref, lgrad_ref, one_ref, two_ref = refs[:7]
-        del refs[:7]
+        act_ref, down_ref, cot_ref, lgrad_ref, one_ref, two_ref = refs[:6]
+        del refs[:6]
         if end is not None:
             terms = refs[:5]
             del refs[:5]
@@ -278,7 +283,7 @@
         del refs[: len(arrays)]
         out_ref, grad_ref = refs[:2]
         sums, grads, out_sems = refs[-3:]
-        g, z, y, c = (place_ref[i] for i in range(4))
+        g, z, y, c = position()
         columns, weights, going = [], [], []
         for p, (_, first, size, offset, (dz, dy, dc, dh)) in enumerate(pieces):
             chip = lax.rem(z + (NZ - dz), NZ) * 2 + (1 - y if dy else y)
@@ -341,8 +346,8 @@
         for copy in going:
             copy.wait()
 
-    operands = [place, activations, down_t, cotangent, lgrad]
-    specs = [scalars()] + [whole()] * 4
+    operands = [activations, down_t, cotangent, lgrad]
+    specs = [whole()] * 4
     out_shape = [
         jax.ShapeDtypeStruct((tokens, features), jnp.float32 if end is None else jnp.bfloat16),
         jax.ShapeDtypeStruct((tokens, width), jnp.bfloat16),
@@ -356,7 +361,7 @@
     else:
         operands += so_far
         specs += [whole(), in_hbm()]
-        aliases = {6: 1}
+        aliases = {5: 1}
     if end is not None:
         operands += end
         specs += [whole()] * 5
@@ -385,9 +390,6 @@
 def per_device(
     activations, quant_codes, block_scales, lowrank_down_factor, lowrank_up_factor, cotangent
 ):
-    g = lax.axis_index("groups")
-    f = lax.axis_index("fsdp")
-    place = jnp.stack([g, f >> 2, (f >> 1) & 1, f & 1]).astype(jnp.int32)
     half = quant_codes.shape[0] // 2
     down_t = lowrank_down_factor.T
     factor = lowrank_scale / math.sqrt(activations.shape[0] * lax.axis_size("fsdp"))
@@ -395,7 +397,7 @@
     join = lambda *arrays: jnp.concatenate(arrays, axis=0)
 
     def products(pieces, **more):
-        return multiply(place, pieces, activations, down_t, cotangent, lgrad, factor, **more)
+        return multiply(pieces, activations, down_t, cotangent, lgrad, factor, **more)
 
     def piece(array, first, dc, key, size=half, offset=0):
         return (array, first, size, offset, (key[0], key[1], dc, key[2]))
@@ -403,8 +405,7 @@
     def listed(array, dc, *keys):
         return [piece(array, i * half, dc, key) for i, key in enumerate(keys)]
 
-    own, first = dequantize_shard(place, quant_codes, block_scales)
-    own, first, place = barrier((own, first, place))
+    own, first = dequantize_shard(quant_codes, block_scales)
 
     def swap(*arrays):
         return send(join(*arrays), OVER_CORE)
@@ -412,21 +413,20 @@
     down1, up1, y1 = send(first, Z_DOWN), send(first, Z_UP), send(own, OVER_Y)
     other_act, other_cot = send(activations, OVER_CORE), send(cotangent, OVER_CORE)
     latent, lgrad, terms_y, kept = local_gradients(
-        place, activations, down_t, lowrank_up_factor, cotangent, other_act, other_cot
+        activations, down_t, lowrank_up_factor, cotangent, other_act, other_cot
     )
     came_y = send(terms_y, OVER_Y)
     down1, up1, y1, kept = barrier((down1, up1, y1, kept))
 
     down2 = send(join(y1[half:], down1), Z_DOWN)
-    y2, x2 = send(up1, OVER_Y), send(join(up1, down1), OVER_X)
+    x2 = send(join(up1, down1), OVER_X)
+    y2 = send(join(down1, up1), OVER_Y)
     rank = down_t.shape[0]
-    own_part, next_part, far_part, last_part, up_own, up_away = add_y(
-        place, kept, terms_y, came_y
-    )
+    own_part, next_part, far_part, last_part, up_own, up_away = add_y(kept, terms_y, came_y)
     summed_up = (up_own + send(up_away, OVER_CORE)).astype(jnp.bfloat16)
     came_up = send(join(far_part, summed_up), Z_UP)
     last_part = join(last_part, summed_up)
-    swap2 = swap(up1, down1, y1)
+    swap2 = swap(up1, down1, y1[half:])
     own_keys = [(0, 0, 0), (0, 0, 1)]
     keys = [(1, 0, 0), (3, 0, 0), (0, 1, 0), (0, 1, 1)]
     done = products(
@@ -434,46 +434,54 @@
         + listed(up1, 0, keys[0])
         + listed(down1, 0, keys[1])
         + listed(y1, 0, *keys[2:])
-        + listed(swap2, 1, *keys),
+        + listed(swap2, 1, *keys[:2], keys[3]),
         begin=[latent, lowrank_up_factor],
     )
-    y2, x2, down2, came_up, own_part, next_part, last_part, done = barrier(
-        (y2, x2, down2, came_up, own_part, next_part, last_part, done)
+    down2, x2, y2, came_up, own_part, next_part, last_part, done = barrier(
+        (down2, x2, y2, came_up, own_part, next_part, last_part, done)
     )
 
     two = down2[half:]
+    quarter = half // 2
     down3 = send(join(down2[:half], last_part), Z_DOWN)
-    y3, x3 = send(join(down1, two), OVER_Y), send(join(two, y2), OVER_X)
+    y3 = send(join(two, x2[:quarter]), OVER_Y)
+    x3 = send(join(two, y2[half + quarter :]), OVER_X)
     next_part = next_part + came_up[:rank].astype(jnp.float32)
     up3 = send(join(next_part.astype(jnp.bfloat16), came_up[rank:]), Z_UP)
-    swap3 = swap(y2, x2, down2, own)
-    keys = [(1, 1, 0), (1, 0, 1), (3, 0, 1), (3, 1, 1), (2, 0, 0)]
+    swap3 = swap(y2, x2, down2, own, y1[:half])
+    keys = [(3, 1, 0), (1, 1, 0), (1, 0, 1), (3, 0, 1), (3, 1, 1), (2, 0, 0)]
     done = products(
-        listed(y2, 0, keys[0])
-        + listed(x2, 0, *keys[1:3])
-        + listed(down2, 0, *keys[3:])
-        + listed(swap3, 1, *keys, *own_keys),
+        listed(y2, 0, *keys[:2])
+        + listed(x2, 0, *keys[2:4])
+        + listed(down2, 0, *keys[4:])
+        + listed(swap3, 1, *keys, *own_keys, (0, 1, 0)),
         so_far=done,
     )
-    y3, x3, down3, up3, came_up, own_part, last_part, done = barrier(
-        (y3, x3, down3, up3, came_up, own_part, last_part, done)
-    )
-
-    swap4 = send(join(y3, x3, down3[:half]), OVER_CORE)
+    x3, y3, down3, up3, came_up, own_part, last_part, done = barrier(
+        (x3, y3, down3, up3, came_up, own_part, last_part, done)
+    )
+
+    swap4 = swap(y3, x3, down3[:half])
     wide = lambda array: array.astype(jnp.float32)
+    tail = slice(half + rank, None)
     up_own = factor * (
-        (wide(last_part[rank:]) + wide(up3[rank:]))
-        + (wide(came_up[rank:]) + wide(down3[half + rank :]))
+        (wide(last_part[rank:]) + wide(up3[rank:])) + (wide(came_up[rank:]) + wide(down3[tail]))
     )
     up_came = send(up_own, OVER_CORE)
 
-    keys = [(3, 1, 0), (2, 1, 0), (2, 0, 1), (1, 1, 1), (2, 1, 1)]
-    done = products(
-        listed(y3, 0, *keys[:2]) + listed(x3, 0, *keys[2:4]) + listed(down3, 0, keys[4]),
-        so_far=done,
-    )
+    def last(dc, y3, x3, down3, x3_from, down3_from):
+        return [
+            piece(y3, 0, dc, (2, 1, 0)),
+            piece(x3, x3_from, dc, (2, 0, 1)),
+            piece(down3, down3_from, dc, (2, 1, 1)),
+            piece(y3, half, dc, (1, 1, 1), quarter),
+            piece(x3, x3_from + half, dc, (1, 1, 1), quarter, quarter),
+        ]
+
+    done = products(last(0, y3, x3, down3, 0, 0), so_far=done)
+    x3_from = half + quarter
     projected, gradient, grad_up, grad_down_t = products(
-        listed(swap4, 1, *keys),
+        last(1, swap4, swap4, swap4, x3_from, 2 * x3_from),
         so_far=done,
         end=[up_own, up_came, own_part, up3, down3],
     )

time: 62.6 us -> 61.1 us (0.976)
  Pallas kernels: 18.6 us -> 16.5 us
  starting transfers between devices: 20.1 us -> 22 us
  local copies, waits for them, and re-layouts: 4.81 us -> 4.09 us
    pallas_call x4, Pallas kernels: 11.5 us -> 9.37 us  [multiply(): pl.pallas_call(kernel, out_shape=out_shape, in_specs=specs + [whole()] *...]
    ppermute x19, starting transfers between devices: 20.1 us -> 22 us  [send(): return lax.ppermute(array, AXES, pairs)]
    unnamed x12 -> x28, local copies, waits for them, and re-layouts: 4.74 us -> 3.98 us
  transfers between devices with their start and end apart: 19 -> 19, of which waited for: 6 -> 8; matrix products, arithmetic and copies ran while one was open for 1% -> 1% of each run, Pallas kernels for 26% -> 24%
where the time goes in v7:
time: 61.1 us; the launch traced here: 60.9 us
  starting transfers between devices  22 us (36%)
  waiting for transfers between devices  17 us (28%)
  Pallas kernels  16.5 us (27%)
  local copies, waits for them, and re-layouts  4.09 us (7%)
  between operations  0.97 us (2%)
    ppermute x19, starting transfers between devices, send(): return lax.ppermute(array, AXES, pairs)  22 us
    ppermute x19, waiting for transfers between devices, send(): return lax.ppermute(array, AXES, pairs)  17 us
    pallas_call x4, Pallas kernels, multiply(): pl.pallas_call(kernel, out_shape=out_shape, in_specs=specs + [whole()] *...  9.37 us
    pallas_call x1, Pallas kernels, local_gradients(): pl.pallas_call(kernel, out_shape=[jax.ShapeDtypeStruct((tokens, rank), bf...  6.38 us
    unnamed x28, local copies, waits for them, and re-layouts  3.98 us
  transfers between devices with their start and end apart: 19, of which 8 were waited for; matrix products, arithmetic and copies ran while one was open for 1% of the time, Pallas kernels for 24%

profile of v7, /device:TPU:0, one launch (start us, length us, event | category | flops | bytes accessed | tf_op | source)
XLA Modules:
  0.0 60.9 jit_solution(4611442643107792740)
XLA Ops:
  0.6 0.5 collective-permute-start
  1.2 1.0 %copy-done.4 = bf16[512,512]{1,0:T(8,128)(2,1)S(1)} copy-done((bf16[512,512]{1,0:T(8,128)(2,1)S(1)}, bf16[512,512]{1,0:T(8,128)(2,1)}, u32[]{:S(2)}) %copy-start.4) | copy-done | bytes 524312
  2.2 0.7 %copy-done.7 = f32[4,4]{1,0:T(4,128)S(1)} copy-done((f32[4,4]{1,0:T(4,128)S(1)}, f32[4,4]{1,0:T(4,128)}, u32[]{:S(2)}) %copy-start.7) | copy-done | bytes 88
  2.9 0.7 %dequantize.1 = (bf16[512,512]{1,0:T(8,128)(2,1)S(1)}, bf16[256,512]{1,0:T(8,128)(2,1)S(1)}) custom-call(bf16[512,512]{1,0:T(8,128)(2,1)S(1)} %copy-done.4, f32[4,4]{1,0:T(4,128)S(1)} %copy-done.7), custom_call_target="tpu_custom_call" | custom-call | flops 1 | bytes 1 | tf_op jit(solution)/shard_map/dequantize/pallas_call | solution.py:135
  3.6 2.6 %collective-permute-start.4 = (bf16[512,512]{1,0:T(8,128)(2,1)S(1)}, bf16[512,512]{1,0:T(8,128)(2,1)S(1)}, u32[]{:S(2)}, u32[]{:S(2)}) collective-permute-start(bf16[512,512]{1,0:T(8,128)(2,1)S(1)} %get-tuple-element.50.refs_6_), channel_id=1, source_target_pairs={{0,2},{1,3},{2,0},{3,1},{4,6},{5,7},{6,4},{7,5},{8,10},{9,11},{10,... | collective-permute-start | bytes 1572872 | tf_op jit(solution)/shard_map/ppermute | solution.py:96
  6.2 0.2 collective-permute-start.1
  6.4 3.6 %collective-permute-start.2 = (bf16[256,512]{1,0:T(8,128)(2,1)S(1)}, bf16[256,512]{1,0:T(8,128)(2,1)S(1)}, u32[]{:S(2)}, u32[]{:S(2)}) collective-permute-start(bf16[256,512]{1,0:T(8,128)(2,1)S(1)} %get-tuple-element.49), channel_id=1, source_target_pairs={{0,12},{1,13},{2,14},{3,15},{4,0},{5,1},{6,2},{7,3},{8,4},{9,5},{1... | collective-permute-start | bytes 786440 | tf_op jit(solution)/shard_map/ppermute | solution.py:96
  10.0 0.0 collective-permute-done.1.other_cot_hbm
  10.0 0.0 collective-permute-done.other_hbm
  10.0 0.0 copy-start.10
  10.0 0.7 %copy-done.11 = bf16[256,512]{1,0:T(8,128)(2,1)} copy-done((bf16[256,512]{1,0:T(8,128)(2,1)}, bf16[256,512]{1,0:T(8,128)(2,1)S(1)}, u32[]{:S(2)}) %copy-start.11) | copy-done | bytes 262168
  10.7 1.4 %copy-done.10 = bf16[256,8192]{1,0:T(8,128)(2,1)} copy-done((bf16[256,8192]{1,0:T(8,128)(2,1)}, bf16[256,8192]{1,0:T(8,128)(2,1)S(1)}, u32[]{:S(2)}) %copy-start.10) | copy-done | bytes 4194328
  12.1 6.4 %local_gradients.1 = (bf16[256,64]{1,0:T(8,128)(2,1)}, bf16[256,64]{1,0:T(8,128)(2,1)}, bf16[320,512]{1,0:T(8,128)(2,1)}, f32[256,512]{1,0:T(8,128)}) custom-call(bf16[256,8192]{1,0:T(8,128)(2,1)} %refs_0_.7, bf16[64,8192]{1,0:T(8,128)(2,1)} %bitcast.2, bf16[64,512]{1,0:T(8,128)(2,1)} %refs_5_.1, bf16[256,512]{1,0:T(8,128)(2,1)} %refs_2_.7, ...), custom_call_target="tpu_custom_call" | custom-call | flops 1 | bytes 1 | tf_op jit(solution)/shard_map/local_gradients/pallas_call | solution.py:201
  18.5 1.5 %collective-permute-start.8 = (bf16[320,512]{1,0:T(8,128)(2,1)}, bf16[320,512]{1,0:T(8,128)(2,1)S(1)}, u32[]{:S(2)}, u32[]{:S(2)}) collective-permute-start(bf16[320,512]{1,0:T(8,128)(2,1)} %get-tuple-element.56.sent_ref), channel_id=1, source_target_pairs={{0,2},{1,3},{2,0},{3,1},{4,6},{5,7},{6,4},{7,5},{8,10},{9,11},{10,... | collective-permute-start | bytes 983048 | tf_op jit(solution)/shard_map/ppermute | solution.py:96
  20.0 2.6 %collective-permute-done.3.refs_7_ = bf16[256,512]{1,0:T(8,128)(2,1)S(1)} collective-permute-done((bf16[256,512]{1,0:T(8,128)(2,1)S(1)}, bf16[256,512]{1,0:T(8,128)(2,1)S(1)}, u32[]{:S(2)}, u32[]{:S(2)}) %collective-permute-start.3) | collective-permute-done | bytes 262176 | tf_op jit(solution)/shard_map/ppermute | solution.py:96
  22.5 0.0 collective-permute-done.4.refs_9_
  22.6 0.1 pad_maximum_fusion.1
  22.6 0.1 collective-permute-start.11
  22.7 0.1 pad_maximum_fusion.4
  22.9 1.8 %collective-permute-start.5 = (bf16[512,512]{1,0:T(8,128)(2,1)S(1)}, bf16[512,512]{1,0:T(8,128)(2,1)S(1)}, u32[]{:S(2)}, u32[]{:S(2)}) collective-permute-start(bf16[512,512]{1,0:T(8,128)(2,1)S(1)} %get-tuple-element.98), channel_id=1, source_target_pairs={{0,12},{1,13},{2,14},{3,15},{4,0},{5,1},{6,2},{7,3},{8,4},{9,5},{1... | collective-permute-start | bytes 1572872 | tf_op jit(solution)/shard_map/ppermute | solution.py:96
  24.6 1.5 %collective-permute-start.6 = (bf16[512,512]{1,0:T(8,128)(2,1)S(1)}, bf16[512,512]{1,0:T(8,128)(2,1)S(1)}, u32[]{:S(2)}, u32[]{:S(2)}) collective-permute-start(bf16[512,512]{1,0:T(8,128)(2,1)S(1)} %get-tuple-element.95), channel_id=1, source_target_pairs={{0,16},{1,17},{2,18},{3,19},{4,20},{5,21},{6,22},{7,23},{8,24},{9,... | collective-permute-start | bytes 1572872 | tf_op jit(solution)/shard_map/ppermute | solution.py:96
  26.2 0.0 copy-start.6
  26.2 0.6 collective-permute-start.7
  26.7 1.7 %collective-permute-done.8.came_ref = bf16[320,512]{1,0:T(8,128)(2,1)S(1)} collective-permute-done((bf16[320,512]{1,0:T(8,128)(2,1)}, bf16[320,512]{1,0:T(8,128)(2,1)S(1)}, u32[]{:S(2)}, u32[]{:S(2)}) %collective-permute-start.8) | collective-permute-done | bytes 327712 | tf_op jit(solution)/shard_map/ppermute | solution.py:96
  28.4 0.1 add_y.1
  28.5 0.1 collective-permute-start.9
  28.6 1.2 %collective-permute-done.9 = f32[32,512]{1,0:T(8,128)S(1)} collective-permute-done((f32[32,512]{1,0:T(8,128)S(1)}, f32[32,512]{1,0:T(8,128)S(1)}, u32[]{:S(2)}, u32[]{:S(2)}) %collective-permute-start.9) | collective-permute-done | bytes 65568 | tf_op jit(solution)/shard_map/ppermute | solution.py:96
  29.9 2.4 %collective-permute-start.10 = (bf16[96,512]{1,0:T(8,128)(2,1)S(1)}, bf16[96,512]{1,0:T(8,128)(2,1)S(1)}, u32[]{:S(2)}, u32[]{:S(2)}) collective-permute-start(bf16[96,512]{1,0:T(8,128)(2,1)S(1)} %get-tuple-element.100), channel_id=1, source_target_pairs={{0,4},{1,5},{2,6},{3,7},{4,8},{5,9},{6,10},{7,11},{8,12},{9,13},{1... | collective-permute-start | bytes 294920 | tf_op jit(solution)/shard_map/ppermute | solution.py:96
  32.3 0.0 collective-permute-done.11.refs_10_
  32.3 2.4 %multiply.4 = (f32[256,512]{1,0:T(8,128)S(1)}, bf16[256,8192]{1,0:T(8,128)(2,1)}) custom-call(bf16[256,8192]{1,0:T(8,128)(2,1)S(1)} %copy-done, bf16[64,8192]{1,0:T(8,128)(2,1)S(1)} %bitcast.3, bf16[256,512]{1,0:T(8,128)(2,1)S(1)} %copy-done.2, bf16[256,64]{1,0:T(8,128)(2,1)S(1)} %copy-done.3, bf16[256,64]{1,0:T(8,128)(2,1)S(1)} %copy-done.6, ...), custom_call_target="tpu_custom_call" | custom-call | flops 1 | bytes 1 | tf_op jit(solution)/shard_map/multiply/pallas_call | solution.py:372
  34.7 4.9 %collective-permute-done.10 = bf16[96,512]{1,0:T(8,128)(2,1)S(1)} collective-permute-done((bf16[96,512]{1,0:T(8,128)(2,1)S(1)}, bf16[96,512]{1,0:T(8,128)(2,1)S(1)}, u32[]{:S(2)}, u32[]{:S(2)}) %collective-permute-start.10) | collective-permute-done | bytes 98336 | tf_op jit(solution)/shard_map/ppermute | solution.py:96
  39.6 0.4 collective-permute-done.7.refs_6_
  40.2 0.1 collective-permute-start.16
  40.4 3.3 %collective-permute-start.14 = (bf16[352,512]{1,0:T(8,128)(2,1)S(1)}, bf16[352,512]{1,0:T(8,128)(2,1)S(1)}, u32[]{:S(2)}, u32[]{:S(2)}) collective-permute-start(bf16[352,512]{1,0:T(8,128)(2,1)S(1)} %pad_maximum_fusion.7), channel_id=1, source_target_pairs={{0,12},{1,13},{2,14},{3,15},{4,0},{5,1},{6,2},{7,3},{8,4},{9,5},{1... | collective-permute-start | bytes 1081352 | tf_op jit(solution)/shard_map/ppermute | solution.py:96
  43.7 0.1 pad_maximum_fusion.5
  43.8 1.6 %collective-permute-start.12 = (bf16[384,512]{1,0:T(8,128)(2,1)S(1)}, bf16[384,512]{1,0:T(8,128)(2,1)S(1)}, u32[]{:S(2)}, u32[]{:S(2)}) collective-permute-start(bf16[384,512]{1,0:T(8,128)(2,1)S(1)} %get-tuple-element.97), channel_id=1, source_target_pairs={{0,16},{1,17},{2,18},{3,19},{4,20},{5,21},{6,22},{7,23},{8,24},{9,... | collective-permute-start | bytes 1179656 | tf_op jit(solution)/shard_map/ppermute | solution.py:96
  45.3 1.5 %collective-permute-start.13 = (bf16[384,512]{1,0:T(8,128)(2,1)S(1)}, bf16[384,512]{1,0:T(8,128)(2,1)S(1)}, u32[]{:S(2)}, u32[]{:S(2)}) collective-permute-start(bf16[384,512]{1,0:T(8,128)(2,1)S(1)} %get-tuple-element.96), channel_id=1, source_target_pairs={{0,2},{1,3},{2,0},{3,1},{4,6},{5,7},{6,4},{7,5},{8,10},{9,11},{10,... | collective-permute-start | bytes 1179656 | tf_op jit(solution)/shard_map/ppermute | solution.py:96
  46.9 0.1 collective-permute-start.15
  47.0 3.6 %multiply.5 = (f32[256,512]{1,0:T(8,128)S(1)}, bf16[256,8192]{1,0:T(8,128)(2,1)}) custom-call(bf16[256,8192]{1,0:T(8,128)(2,1)S(1)} %copy-done, bf16[64,8192]{1,0:T(8,128)(2,1)S(1)} %bitcast.4, bf16[256,512]{1,0:T(8,128)(2,1)S(1)} %copy-done.2, bf16[256,64]{1,0:T(8,128)(2,1)S(1)} %copy-done.3, ...), custom_call_target="tpu_custom_call", output_to_operand_aliasing={{1}: (5, {})} | custom-call | flops 1 | bytes 1 | tf_op jit(solution)/shard_map/multiply/pallas_call | solution.py:372
  50.6 4.5 %collective-permute-done.15.refs_9_ = bf16[96,512]{1,0:T(8,128)(2,1)S(1)} collective-permute-done((bf16[96,512]{1,0:T(8,128)(2,1)S(1)}, bf16[96,512]{1,0:T(8,128)(2,1)S(1)}, u32[]{:S(2)}, u32[]{:S(2)}) %collective-permute-start.15) | collective-permute-done | bytes 98336 | tf_op jit(solution)/shard_map/ppermute | solution.py:96
  55.1 0.0 collective-permute-done.12.refs_7_
  55.1 1.2 %collective-permute-done.13.refs_6_ = bf16[384,512]{1,0:T(8,128)(2,1)S(1)} collective-permute-done((bf16[384,512]{1,0:T(8,128)(2,1)S(1)}, bf16[384,512]{1,0:T(8,128)(2,1)S(1)}, u32[]{:S(2)}, u32[]{:S(2)}) %collective-permute-start.13) | collective-permute-done | bytes 393248 | tf_op jit(solution)/shard_map/ppermute | solution.py:96
  56.3 0.1 pad_maximum_fusion
  56.4 0.1 collective-permute-start.18
  56.5 0.6 collective-permute-start.17
  57.1 1.7 %multiply.6 = (f32[256,512]{1,0:T(8,128)S(1)}, bf16[256,8192]{1,0:T(8,128)(2,1)}) custom-call(bf16[256,8192]{1,0:T(8,128)(2,1)S(1)} %copy-done, bf16[64,8192]{1,0:T(8,128)(2,1)S(1)} %bitcast.5, bf16[256,512]{1,0:T(8,128)(2,1)S(1)} %copy-done.2, bf16[256,64]{1,0:T(8,128)(2,1)S(1)} %copy-done.3, ...), custom_call_target="tpu_custom_call", output_to_operand_aliasing={{1}: (5, {})} | custom-call | flops 1 | bytes 1 | tf_op jit(solution)/shard_map/multiply/pallas_call | solution.py:372
  58.8 0.5 collective-permute-done.17.refs_7_
  59.2 1.7 %multiply.7 = (bf16[256,512]{1,0:T(8,128)(2,1)}, bf16[256,8192]{1,0:T(8,128)(2,1)}, f32[64,512]{1,0:T(8,128)}, f32[64,512]{1,0:T(8,128)}) custom-call(bf16[256,8192]{1,0:T(8,128)(2,1)S(1)} %copy-done, bf16[64,8192]{1,0:T(8,128)(2,1)S(1)} %bitcast.6, bf16[256,512]{1,0:T(8,128)(2,1)S(1)} %copy-done.2, ...), custom_call_target="tpu_custom_call", output_to_operand_aliasing={{1}: (5, {})} | custom-call | flops 1 | bytes 1 | tf_op jit(solution)/shard_map/multiply/pallas_call | solution.py:372
  (42 shorter events, 0.4 us)
Async XLA Ops:
  0.6 9.4 %collective-permute-start = (bf16[256,8192]{1,0:T(8,128)(2,1)}, bf16[256,8192]{1,0:T(8,128)(2,1)S(1)}, u32[]{:S(2)}, u32[]{:S(2)}) collective-permute-start(bf16[256,8192]{1,0:T(8,128)(2,1)} %refs_0_.7), channel_id=1, source_target_pairs={{0,1},{1,0},{2,3},{3,2},{4,5},{5,4},{6,7},{7,6},{8,9},{9,8},{10,11... | collective-permute-start | bytes 12582920 | tf_op jit(solution)/shard_map/ppermute | solution.py:96
  1.1 1.0 %copy-start.4 = (bf16[512,512]{1,0:T(8,128)(2,1)S(1)}, bf16[512,512]{1,0:T(8,128)(2,1)}, u32[]{:S(2)}) copy-start(bf16[512,512]{1,0:T(8,128)(2,1)} %codes_ref.1) | copy-start | bytes 1572868
  2.2 0.7 %copy-start.7 = (f32[4,4]{1,0:T(4,128)S(1)}, f32[4,4]{1,0:T(4,128)}, u32[]{:S(2)}) copy-start(f32[4,4]{1,0:T(4,128)} %scales_ref.1) | copy-start | bytes 196
  3.6 19.0 %collective-permute-start.4 = (bf16[512,512]{1,0:T(8,128)(2,1)S(1)}, bf16[512,512]{1,0:T(8,128)(2,1)S(1)}, u32[]{:S(2)}, u32[]{:S(2)}) collective-permute-start(bf16[512,512]{1,0:T(8,128)(2,1)S(1)} %get-tuple-element.50.refs_6_), channel_id=1, source_target_pairs={{0,2},{1,3},{2,0},{3,1},{4,6},{5,7},{6,4},{7,5},{8,10},{9,11},{10,... | collective-permute-start | bytes 1572872 | tf_op jit(solution)/shard_map/ppermute | solution.py:96
  6.2 3.8 %collective-permute-start.1 = (bf16[256,512]{1,0:T(8,128)(2,1)}, bf16[256,512]{1,0:T(8,128)(2,1)S(1)}, u32[]{:S(2)}, u32[]{:S(2)}) collective-permute-start(bf16[256,512]{1,0:T(8,128)(2,1)} %refs_2_.7), channel_id=1, source_target_pairs={{0,1},{1,0},{2,3},{3,2},{4,5},{5,4},{6,7},{7,6},{8,9},{9,8},{10,11... | collective-permute-start | bytes 786440 | tf_op jit(solution)/shard_map/ppermute | solution.py:96
  6.4 13.6 %collective-permute-start.2 = (bf16[256,512]{1,0:T(8,128)(2,1)S(1)}, bf16[256,512]{1,0:T(8,128)(2,1)S(1)}, u32[]{:S(2)}, u32[]{:S(2)}) collective-permute-start(bf16[256,512]{1,0:T(8,128)(2,1)S(1)} %get-tuple-element.49), channel_id=1, source_target_pairs={{0,12},{1,13},{2,14},{3,15},{4,0},{5,1},{6,2},{7,3},{8,4},{9,5},{1... | collective-permute-start | bytes 786440 | tf_op jit(solution)/shard_map/ppermute | solution.py:96
  10.0 12.5 %collective-permute-start.3 = (bf16[256,512]{1,0:T(8,128)(2,1)S(1)}, bf16[256,512]{1,0:T(8,128)(2,1)S(1)}, u32[]{:S(2)}, u32[]{:S(2)}) collective-permute-start(bf16[256,512]{1,0:T(8,128)(2,1)S(1)} %get-tuple-element.49), channel_id=1, source_target_pairs={{0,4},{1,5},{2,6},{3,7},{4,8},{5,9},{6,10},{7,11},{8,12},{9,13},{1... | collective-permute-start | bytes 786440 | tf_op jit(solution)/shard_map/ppermute | solution.py:96
  10.0 0.7 %copy-start.11 = (bf16[256,512]{1,0:T(8,128)(2,1)}, bf16[256,512]{1,0:T(8,128)(2,1)S(1)}, u32[]{:S(2)}) copy-start(bf16[256,512]{1,0:T(8,128)(2,1)S(1)} %collective-permute-done.1.other_cot_hbm) | copy-start | bytes 786436
  10.0 2.1 %copy-start.10 = (bf16[256,8192]{1,0:T(8,128)(2,1)}, bf16[256,8192]{1,0:T(8,128)(2,1)S(1)}, u32[]{:S(2)}) copy-start(bf16[256,8192]{1,0:T(8,128)(2,1)S(1)} %collective-permute-done.other_hbm) | copy-start | bytes 12582916
  18.5 9.9 %copy-start.8 = (f32[256,512]{1,0:T(8,128)S(1)}, f32[256,512]{1,0:T(8,128)}, u32[]{:S(2)}) copy-start(f32[256,512]{1,0:T(8,128)} %get-tuple-element.55.kept_ref) | copy-start | bytes 1572868
  18.5 9.9 %copy-start.9 = (bf16[320,512]{1,0:T(8,128)(2,1)S(1)}, bf16[320,512]{1,0:T(8,128)(2,1)}, u32[]{:S(2)}) copy-start(bf16[320,512]{1,0:T(8,128)(2,1)} %get-tuple-element.56.sent_ref) | copy-start | bytes 983044
  18.5 9.9 %collective-permute-start.8 = (bf16[320,512]{1,0:T(8,128)(2,1)}, bf16[320,512]{1,0:T(8,128)(2,1)S(1)}, u32[]{:S(2)}, u32[]{:S(2)}) collective-permute-start(bf16[320,512]{1,0:T(8,128)(2,1)} %get-tuple-element.56.sent_ref), channel_id=1, source_target_pairs={{0,2},{1,3},{2,0},{3,1},{4,6},{5,7},{6,4},{7,5},{8,10},{9,11},{10,... | collective-permute-start | bytes 983048 | tf_op jit(solution)/shard_map/ppermute | solution.py:96
  22.6 9.7 %collective-permute-start.11 = (bf16[768,512]{1,0:T(8,128)(2,1)S(1)}, bf16[768,512]{1,0:T(8,128)(2,1)S(1)}, u32[]{:S(2)}, u32[]{:S(2)}) collective-permute-start(bf16[768,512]{1,0:T(8,128)(2,1)S(1)} %pad_maximum_fusion.1), channel_id=1, source_target_pairs={{0,1},{1,0},{2,3},{3,2},{4,5},{5,4},{6,7},{7,6},{8,9},{9,8},{10,11... | collective-permute-start | bytes 2359304 | tf_op jit(solution)/shard_map/ppermute | solution.py:96
  22.9 16.8 %collective-permute-start.5 = (bf16[512,512]{1,0:T(8,128)(2,1)S(1)}, bf16[512,512]{1,0:T(8,128)(2,1)S(1)}, u32[]{:S(2)}, u32[]{:S(2)}) collective-permute-start(bf16[512,512]{1,0:T(8,128)(2,1)S(1)} %get-tuple-element.98), channel_id=1, source_target_pairs={{0,12},{1,13},{2,14},{3,15},{4,0},{5,1},{6,2},{7,3},{8,4},{9,5},{1... | collective-permute-start | bytes 1572872 | tf_op jit(solution)/shard_map/ppermute | solution.py:96
  24.6 15.0 %collective-permute-start.6 = (bf16[512,512]{1,0:T(8,128)(2,1)S(1)}, bf16[512,512]{1,0:T(8,128)(2,1)S(1)}, u32[]{:S(2)}, u32[]{:S(2)}) collective-permute-start(bf16[512,512]{1,0:T(8,128)(2,1)S(1)} %get-tuple-element.95), channel_id=1, source_target_pairs={{0,16},{1,17},{2,18},{3,19},{4,20},{5,21},{6,22},{7,23},{8,24},{9,... | collective-permute-start | bytes 1572872 | tf_op jit(solution)/shard_map/ppermute | solution.py:96
  26.1 6.2 %copy-start.1 = (bf16[8192,64]{0,1:T(8,128)(2,1)S(1)}, bf16[8192,64]{0,1:T(8,128)(2,1)}, u32[]{:S(2)}) copy-start(bf16[8192,64]{0,1:T(8,128)(2,1)} %param.9) | copy-start | bytes 3145732
  26.1 6.2 %copy-start.2 = (bf16[256,512]{1,0:T(8,128)(2,1)S(1)}, bf16[256,512]{1,0:T(8,128)(2,1)}, u32[]{:S(2)}) copy-start(bf16[256,512]{1,0:T(8,128)(2,1)} %refs_2_.7) | copy-start | bytes 786436
  26.1 6.2 %copy-start.3 = (bf16[256,64]{1,0:T(8,128)(2,1)S(1)}, bf16[256,64]{1,0:T(8,128)(2,1)}, u32[]{:S(2)}) copy-start(bf16[256,64]{1,0:T(8,128)(2,1)} %get-tuple-element.48.refs_3_) | copy-start | bytes 98308
  26.1 6.2 %copy-start.5 = (bf16[64,512]{1,0:T(8,128)(2,1)S(1)}, bf16[64,512]{1,0:T(8,128)(2,1)}, u32[]{:S(2)}) copy-start(bf16[64,512]{1,0:T(8,128)(2,1)} %refs_5_.1) | copy-start | bytes 196612
  26.2 6.2 %copy-start.6 = (bf16[256,64]{1,0:T(8,128)(2,1)S(1)}, bf16[256,64]{1,0:T(8,128)(2,1)}, u32[]{:S(2)}) copy-start(bf16[256,64]{1,0:T(8,128)(2,1)} %get-tuple-element.63.refs_4_) | copy-start | bytes 98308
  26.2 13.8 %collective-permute-start.7 = (bf16[512,512]{1,0:T(8,128)(2,1)S(1)}, bf16[512,512]{1,0:T(8,128)(2,1)S(1)}, u32[]{:S(2)}, u32[]{:S(2)}) collective-permute-start(bf16[512,512]{1,0:T(8,128)(2,1)S(1)} %get-tuple-element.94), channel_id=1, source_target_pairs={{0,2},{1,3},{2,0},{3,1},{4,6},{5,7},{6,4},{7,5},{8,10},{9,11},{10,... | collective-permute-start | bytes 1572872 | tf_op jit(solution)/shard_map/ppermute | solution.py:96
  28.4 3.9 %copy-start = (bf16[256,8192]{1,0:T(8,128)(2,1)S(1)}, bf16[256,8192]{1,0:T(8,128)(2,1)}, u32[]{:S(2)}) copy-start(bf16[256,8192]{1,0:T(8,128)(2,1)} %refs_0_.7) | copy-start | bytes 12582916
  28.5 1.3 %collective-permute-start.9 = (f32[32,512]{1,0:T(8,128)S(1)}, f32[32,512]{1,0:T(8,128)S(1)}, u32[]{:S(2)}, u32[]{:S(2)}) collective-permute-start(f32[32,512]{1,0:T(8,128)S(1)} %get-tuple-element.59), channel_id=1, source_target_pairs={{0,1},{1,0},{2,3},{3,2},{4,5},{5,4},{6,7},{7,6},{8,9},{9,8},{10,11... | collective-permute-start | bytes 196616 | tf_op jit(solution)/shard_map/ppermute | solution.py:96
  29.9 9.7 %collective-permute-start.10 = (bf16[96,512]{1,0:T(8,128)(2,1)S(1)}, bf16[96,512]{1,0:T(8,128)(2,1)S(1)}, u32[]{:S(2)}, u32[]{:S(2)}) collective-permute-start(bf16[96,512]{1,0:T(8,128)(2,1)S(1)} %get-tuple-element.100), channel_id=1, source_target_pairs={{0,4},{1,5},{2,6},{3,7},{4,8},{5,9},{6,10},{7,11},{8,12},{9,13},{1... | collective-permute-start | bytes 294920 | tf_op jit(solution)/shard_map/ppermute | solution.py:96
  40.2 6.8 %collective-permute-start.16 = (bf16[2304,512]{1,0:T(8,128)(2,1)S(1)}, bf16[2304,512]{1,0:T(8,128)(2,1)S(1)}, u32[]{:S(2)}, u32[]{:S(2)}) collective-permute-start(bf16[2304,512]{1,0:T(8,128)(2,1)S(1)} %slice_dynamic-update-slice_fusion), channel_id=1, source_target_pairs={{0,1},{1,0},{2,3},{3,2},{4,5},{5,4},{6,7},{7,6},{8,9},{9,8},{10,11... | collective-permute-start | bytes 7077896 | tf_op jit(solution)/shard_map/ppermute | solution.py:96
  40.4 14.7 %collective-permute-start.14 = (bf16[352,512]{1,0:T(8,128)(2,1)S(1)}, bf16[352,512]{1,0:T(8,128)(2,1)S(1)}, u32[]{:S(2)}, u32[]{:S(2)}) collective-permute-start(bf16[352,512]{1,0:T(8,128)(2,1)S(1)} %pad_maximum_fusion.7), channel_id=1, source_target_pairs={{0,12},{1,13},{2,14},{3,15},{4,0},{5,1},{6,2},{7,3},{8,4},{9,5},{1... | collective-permute-start | bytes 1081352 | tf_op jit(solution)/shard_map/ppermute | solution.py:96
  43.8 11.3 %collective-permute-start.12 = (bf16[384,512]{1,0:T(8,128)(2,1)S(1)}, bf16[384,512]{1,0:T(8,128)(2,1)S(1)}, u32[]{:S(2)}, u32[]{:S(2)}) collective-permute-start(bf16[384,512]{1,0:T(8,128)(2,1)S(1)} %get-tuple-element.97), channel_id=1, source_target_pairs={{0,16},{1,17},{2,18},{3,19},{4,20},{5,21},{6,22},{7,23},{8,24},{9,... | collective-permute-start | bytes 1179656 | tf_op jit(solution)/shard_map/ppermute | solution.py:96
  45.3 11.0 %collective-permute-start.13 = (bf16[384,512]{1,0:T(8,128)(2,1)S(1)}, bf16[384,512]{1,0:T(8,128)(2,1)S(1)}, u32[]{:S(2)}, u32[]{:S(2)}) collective-permute-start(bf16[384,512]{1,0:T(8,128)(2,1)S(1)} %get-tuple-element.96), channel_id=1, source_target_pairs={{0,2},{1,3},{2,0},{3,1},{4,6},{5,7},{6,4},{7,5},{8,10},{9,11},{10,... | collective-permute-start | bytes 1179656 | tf_op jit(solution)/shard_map/ppermute | solution.py:96
  46.9 8.2 %collective-permute-start.15 = (bf16[96,512]{1,0:T(8,128)(2,1)S(1)}, bf16[96,512]{1,0:T(8,128)(2,1)S(1)}, u32[]{:S(2)}, u32[]{:S(2)}) collective-permute-start(bf16[96,512]{1,0:T(8,128)(2,1)S(1)} %pad_maximum_fusion.10), channel_id=1, source_target_pairs={{0,4},{1,5},{2,6},{3,7},{4,8},{5,9},{6,10},{7,11},{8,12},{9,13},{1... | collective-permute-start | bytes 294920 | tf_op jit(solution)/shard_map/ppermute | solution.py:96
  56.4 2.8 %collective-permute-start.18 = (bf16[1024,512]{1,0:T(8,128)(2,1)S(1)}, bf16[1024,512]{1,0:T(8,128)(2,1)S(1)}, u32[]{:S(2)}, u32[]{:S(2)}) collective-permute-start(bf16[1024,512]{1,0:T(8,128)(2,1)S(1)} %pad_maximum_fusion), channel_id=1, source_target_pairs={{0,1},{1,0},{2,3},{3,2},{4,5},{5,4},{6,7},{7,6},{8,9},{9,8},{10,11... | collective-permute-start | bytes 3145736 | tf_op jit(solution)/shard_map/ppermute | solution.py:96
  56.5 2.7 %collective-permute-start.17 = (f32[32,512]{1,0:T(8,128)S(1)}, f32[32,512]{1,0:T(8,128)S(1)}, u32[]{:S(2)}, u32[]{:S(2)}) collective-permute-start(f32[32,512]{1,0:T(8,128)S(1)} %add_multiply_fusion.refs_6_), channel_id=1, source_target_pairs={{0,1},{1,0},{2,3},{3,2},{4,5},{5,4},{6,7},{7,6},{8,9},{9,8},{10,11... | collective-permute-start | bytes 196616 | tf_op jit(solution)/shard_map/ppermute | solution.py:96

commit v8 on v7

--- a/solution.py
+++ b/solution.py
@@ -119,18 +119,30 @@
     rows, columns = quant_codes.shape
     half = rows // 2
 
-    def kernel(codes_ref, scales_ref, own_ref, first_ref):
+    def kernel(codes_hbm, scales_hbm, own_ref, first_ref, codes_ref, scales_ref, sems):
         g = position()[0]
-        for i in range(rows // BLOCK):
-            source = lax.rem(g * (half // BLOCK) + i, rows // BLOCK)
-            start = pl.multiple_of(source * BLOCK, BLOCK)
-            for j in range(columns // BLOCK):
-                at = slice(j * BLOCK, (j + 1) * BLOCK)
-                block = codes_ref[pl.ds(start, BLOCK), at].astype(jnp.float32)
-                block = (block * scales_ref[source, j]).astype(jnp.bfloat16)
-                own_ref[i * BLOCK : (i + 1) * BLOCK, at] = block
-                if i < half // BLOCK:
-                    first_ref[i * BLOCK : (i + 1) * BLOCK, at] = block
+        scales = pltpu.make_async_copy(scales_hbm, scales_ref, sems.at[0])
+        scales.start()
+        parts = []
+        for i in range(2):
+            source = pl.ds(pl.multiple_of(((g + i) & 1) * half, half), half)
+            parts.append(
+                pltpu.make_async_copy(codes_hbm.at[source, :], codes_ref.at[i], sems.at[i + 1])
+            )
+            parts[-1].start()
+        scales.wait()
+        for i in range(2):
+            parts[i].wait()
+            for k in range(half // BLOCK):
+                row = ((g + i) & 1) * (half // BLOCK) + k
+                rows_of = slice(k * BLOCK, (k + 1) * BLOCK)
+                for j in range(columns // BLOCK):
+                    at = slice(j * BLOCK, (j + 1) * BLOCK)
+                    block = codes_ref[i, rows_of, at].astype(jnp.float32)
+                    block = (block * scales_ref[row, j]).astype(jnp.bfloat16)
+                    own_ref[i * half + k * BLOCK : i * half + (k + 1) * BLOCK, at] = block
+                    if i == 0:
+                        first_ref[rows_of, at] = block
 
     return pl.pallas_call(
         kernel,
@@ -138,10 +150,15 @@
             jax.ShapeDtypeStruct((rows, columns), jnp.bfloat16),
             jax.ShapeDtypeStruct((half, columns), jnp.bfloat16),
         ],
-        in_specs=[whole(), scalars()],
+        in_specs=[in_hbm(), in_hbm()],
         out_specs=[whole()] * 2,
-        compiler_params=params(),
-        cost_estimate=LITTLE,
+        scratch_shapes=[
+            pltpu.VMEM((2, half, columns), quant_codes.dtype),
+            pltpu.SMEM(block_scales.shape, block_scales.dtype),
+            pltpu.SemaphoreType.DMA((3,)),
+        ],
+        compiler_params=pltpu.CompilerParams(vmem_limit_bytes=53 * 1024 * 1024),
+        cost_estimate=pl.CostEstimate(flops=20000000000, bytes_accessed=1, transcendentals=0),
         name="dequantize",
     )(quant_codes, block_scales)
 
@@ -221,7 +238,7 @@
             pltpu.VMEM((2, NZ * rank, part), jnp.float32),
             pltpu.SemaphoreType.DMA((3 * chips + 3,)),
         ],
-        compiler_params=pltpu.CompilerParams(vmem_limit_bytes=54 * 1024 * 1024),
+        compiler_params=pltpu.CompilerParams(vmem_limit_bytes=24 * 1024 * 1024),
         cost_estimate=LITTLE,
         name="local_gradients",
     )(activations, down_t, up, cotangent, other_act, other_cot)

time: 61.1 us -> 60.6 us (level)
  waiting for transfers between devices: 17 us -> 22.2 us
  local copies, waits for them, and re-layouts: 4.09 us -> 0.96 us
  starting transfers between devices: 22 us -> 19.6 us
    ppermute x19, waiting for transfers between devices: 17 us -> 22.2 us  [send(): return lax.ppermute(array, AXES, pairs)]
    unnamed x28 -> x14, local copies, waits for them, and re-layouts: 3.98 us -> 0.84 us
    ppermute x19, starting transfers between devices: 22 us -> 19.6 us  [send(): return lax.ppermute(array, AXES, pairs)]
    pallas_call x1, Pallas kernels: 6.38 us -> 5.31 us  [local_gradients(): pl.pallas_call(kernel, out_shape=[jax.ShapeDtypeStruct((tokens, rank), bf...]
  transfers between devices with their start and end apart: 19 -> 19, of which waited for: 8 -> 7; matrix products, arithmetic and copies ran while one was open for 1% -> 1% of each run, Pallas kernels for 24% -> 24%
where the time goes in v8:
time: 60.6 us; the launch traced here: 60.4 us
  waiting for transfers between devices  22.2 us (37%)
  starting transfers between devices  19.6 us (32%)
  Pallas kernels  16.2 us (27%)
  between operations  1.09 us (2%)
  local copies, waits for them, and re-layouts  0.96 us (2%)
    ppermute x19, waiting for transfers between devices, send(): return lax.ppermute(array, AXES, pairs)  22.2 us
    ppermute x19, starting transfers between devices, send(): return lax.ppermute(array, AXES, pairs)  19.6 us
    pallas_call x4, Pallas kernels, multiply(): pl.pallas_call(kernel, out_shape=out_shape, in_specs=specs + [whole()] *...  9.54 us
    pallas_call x1, Pallas kernels, local_gradients(): pl.pallas_call(kernel, out_shape=[jax.ShapeDtypeStruct((tokens, rank), bf...  5.31 us
    pallas_call x1, Pallas kernels, dequantize_shard(): pl.pallas_call(kernel, out_shape=[jax.ShapeDtypeStruct((rows, columns), j...  1.26 us
  transfers between devices with their start and end apart: 19, of which 7 were waited for; matrix products, arithmetic and copies ran while one was open for 1% of the time, Pallas kernels for 24%

profile of v8, /device:TPU:0, one launch (start us, length us, event | category | flops | bytes accessed | tf_op | source)
XLA Modules:
  0.0 60.4 jit_solution(4758774784306535152)
XLA Ops:
  0.7 0.5 collective-permute-start
  1.2 0.7 %copy-done.4 = f32[4,4]{1,0:T(4,128)S(1)} copy-done((f32[4,4]{1,0:T(4,128)S(1)}, f32[4,4]{1,0:T(4,128)}, u32[]{:S(2)}) %copy-start.4) | copy-done | bytes 88
  1.9 1.3 %dequantize.1 = (bf16[512,512]{1,0:T(8,128)(2,1)S(1)}, bf16[256,512]{1,0:T(8,128)(2,1)S(1)}) custom-call(bf16[512,512]{1,0:T(8,128)(2,1)} %codes_hbm.1, f32[4,4]{1,0:T(4,128)S(1)} %copy-done.4), custom_call_target="tpu_custom_call" | custom-call | flops 20000000000 | bytes 1 | tf_op jit(solution)/shard_map/dequantize/pallas_call | solution.py:147
  3.1 2.7 %collective-permute-start.4 = (bf16[512,512]{1,0:T(8,128)(2,1)S(1)}, bf16[512,512]{1,0:T(8,128)(2,1)S(1)}, u32[]{:S(2)}, u32[]{:S(2)}) collective-permute-start(bf16[512,512]{1,0:T(8,128)(2,1)S(1)} %get-tuple-element.50.refs_6_), channel_id=1, source_target_pairs={{0,2},{1,3},{2,0},{3,1},{4,6},{5,7},{6,4},{7,5},{8,10},{9,11},{10,... | collective-permute-start | bytes 1572872 | tf_op jit(solution)/shard_map/ppermute | solution.py:96
  5.8 0.1 collective-permute-start.1
  6.0 3.6 %collective-permute-start.2 = (bf16[256,512]{1,0:T(8,128)(2,1)S(1)}, bf16[256,512]{1,0:T(8,128)(2,1)S(1)}, u32[]{:S(2)}, u32[]{:S(2)}) collective-permute-start(bf16[256,512]{1,0:T(8,128)(2,1)S(1)} %get-tuple-element.49), channel_id=1, source_target_pairs={{0,12},{1,13},{2,14},{3,15},{4,0},{5,1},{6,2},{7,3},{8,4},{9,5},{1... | collective-permute-start | bytes 786440 | tf_op jit(solution)/shard_map/ppermute | solution.py:96
  9.6 0.0 collective-permute-start.3
  9.6 0.0 collective-permute-done.1.other_cot_hbm
  9.6 0.0 collective-permute-done.other_hbm
  9.6 5.3 %local_gradients.1 = (bf16[256,64]{1,0:T(8,128)(2,1)S(1)}, bf16[256,64]{1,0:T(8,128)(2,1)S(1)}, bf16[320,512]{1,0:T(8,128)(2,1)S(1)}, f32[256,512]{1,0:T(8,128)S(1)}) custom-call(bf16[256,8192]{1,0:T(8,128)(2,1)S(1)} %copy-done, bf16[64,8192]{1,0:T(8,128)(2,1)S(1)} %bitcast.2, bf16[64,512]{1,0:T(8,128)(2,1)S(1)} %copy-done.3, ...), custom_call_target="tpu_custom_call" | custom-call | flops 1 | bytes 1 | tf_op jit(solution)/shard_map/local_gradients/pallas_call | solution.py:218
  14.9 1.7 %collective-permute-start.8 = (bf16[320,512]{1,0:T(8,128)(2,1)S(1)}, bf16[320,512]{1,0:T(8,128)(2,1)S(1)}, u32[]{:S(2)}, u32[]{:S(2)}) collective-permute-start(bf16[320,512]{1,0:T(8,128)(2,1)S(1)} %get-tuple-element.56.sent_ref), channel_id=1, source_target_pairs={{0,2},{1,3},{2,0},{3,1},{4,6},{5,7},{6,4},{7,5},{8,10},{9,11},{10,... | collective-permute-start | bytes 983048 | tf_op jit(solution)/shard_map/ppermute | solution.py:96
  16.6 0.0 collective-permute-done.2.refs_8_
  16.6 5.5 %collective-permute-done.3.refs_7_ = bf16[256,512]{1,0:T(8,128)(2,1)S(1)} collective-permute-done((bf16[256,512]{1,0:T(8,128)(2,1)S(1)}, bf16[256,512]{1,0:T(8,128)(2,1)S(1)}, u32[]{:S(2)}, u32[]{:S(2)}) %collective-permute-start.3) | collective-permute-done | bytes 262176 | tf_op jit(solution)/shard_map/ppermute | solution.py:96
  22.2 0.0 collective-permute-done.4.refs_9_
  22.2 0.1 pad_maximum_fusion.1
  22.3 0.1 collective-permute-start.11
  22.3 0.1 pad_maximum_fusion.4
  22.5 1.8 %collective-permute-start.5 = (bf16[512,512]{1,0:T(8,128)(2,1)S(1)}, bf16[512,512]{1,0:T(8,128)(2,1)S(1)}, u32[]{:S(2)}, u32[]{:S(2)}) collective-permute-start(bf16[512,512]{1,0:T(8,128)(2,1)S(1)} %get-tuple-element.98), channel_id=1, source_target_pairs={{0,12},{1,13},{2,14},{3,15},{4,0},{5,1},{6,2},{7,3},{8,4},{9,5},{1... | collective-permute-start | bytes 1572872 | tf_op jit(solution)/shard_map/ppermute | solution.py:96
  24.3 1.5 %collective-permute-start.6 = (bf16[512,512]{1,0:T(8,128)(2,1)S(1)}, bf16[512,512]{1,0:T(8,128)(2,1)S(1)}, u32[]{:S(2)}, u32[]{:S(2)}) collective-permute-start(bf16[512,512]{1,0:T(8,128)(2,1)S(1)} %get-tuple-element.95), channel_id=1, source_target_pairs={{0,16},{1,17},{2,18},{3,19},{4,20},{5,21},{6,22},{7,23},{8,24},{9,... | collective-permute-start | bytes 1572872 | tf_op jit(solution)/shard_map/ppermute | solution.py:96
  25.8 0.5 collective-permute-start.7
  26.3 0.1 add_y.1
  26.4 0.1 collective-permute-start.9
  26.4 1.2 %collective-permute-done.9 = f32[32,512]{1,0:T(8,128)S(1)} collective-permute-done((f32[32,512]{1,0:T(8,128)S(1)}, f32[32,512]{1,0:T(8,128)S(1)}, u32[]{:S(2)}, u32[]{:S(2)}) %collective-permute-start.9) | collective-permute-done | bytes 65568 | tf_op jit(solution)/shard_map/ppermute | solution.py:96
  27.7 0.9 %collective-permute-start.10 = (bf16[96,512]{1,0:T(8,128)(2,1)S(1)}, bf16[96,512]{1,0:T(8,128)(2,1)S(1)}, u32[]{:S(2)}, u32[]{:S(2)}) collective-permute-start(bf16[96,512]{1,0:T(8,128)(2,1)S(1)} %get-tuple-element.100), channel_id=1, source_target_pairs={{0,4},{1,5},{2,6},{3,7},{4,8},{5,9},{6,10},{7,11},{8,12},{9,13},{1... | collective-permute-start | bytes 294920 | tf_op jit(solution)/shard_map/ppermute | solution.py:96
  28.6 0.0 collective-permute-done.11.refs_10_
  28.6 2.4 %multiply.4 = (f32[256,512]{1,0:T(8,128)S(1)}, bf16[256,8192]{1,0:T(8,128)(2,1)}) custom-call(bf16[256,8192]{1,0:T(8,128)(2,1)S(1)} %copy-done, bf16[64,8192]{1,0:T(8,128)(2,1)S(1)} %bitcast.3, bf16[256,512]{1,0:T(8,128)(2,1)S(1)} %copy-done.2, bf16[256,64]{1,0:T(8,128)(2,1)S(1)} %get-tuple-element.48.refs_3_, ...), custom_call_target="tpu_custom_call" | custom-call | flops 1 | bytes 1 | tf_op jit(solution)/shard_map/multiply/pallas_call | solution.py:389
  31.1 8.2 %collective-permute-done.10 = bf16[96,512]{1,0:T(8,128)(2,1)S(1)} collective-permute-done((bf16[96,512]{1,0:T(8,128)(2,1)S(1)}, bf16[96,512]{1,0:T(8,128)(2,1)S(1)}, u32[]{:S(2)}, u32[]{:S(2)}) %collective-permute-start.10) | collective-permute-done | bytes 98336 | tf_op jit(solution)/shard_map/ppermute | solution.py:96
  39.2 0.0 collective-permute-done.5.refs_8_
  39.3 0.0 collective-permute-done.6.refs_7_
  39.3 0.3 collective-permute-done.7.refs_6_
  39.7 0.1 collective-permute-start.16
  39.9 3.1 %collective-permute-start.14 = (bf16[352,512]{1,0:T(8,128)(2,1)S(1)}, bf16[352,512]{1,0:T(8,128)(2,1)S(1)}, u32[]{:S(2)}, u32[]{:S(2)}) collective-permute-start(bf16[352,512]{1,0:T(8,128)(2,1)S(1)} %pad_maximum_fusion.7), channel_id=1, source_target_pairs={{0,12},{1,13},{2,14},{3,15},{4,0},{5,1},{6,2},{7,3},{8,4},{9,5},{1... | collective-permute-start | bytes 1081352 | tf_op jit(solution)/shard_map/ppermute | solution.py:96
  43.0 0.1 pad_maximum_fusion.5
  43.1 1.6 %collective-permute-start.12 = (bf16[384,512]{1,0:T(8,128)(2,1)S(1)}, bf16[384,512]{1,0:T(8,128)(2,1)S(1)}, u32[]{:S(2)}, u32[]{:S(2)}) collective-permute-start(bf16[384,512]{1,0:T(8,128)(2,1)S(1)} %get-tuple-element.97), channel_id=1, source_target_pairs={{0,16},{1,17},{2,18},{3,19},{4,20},{5,21},{6,22},{7,23},{8,24},{9,... | collective-permute-start | bytes 1179656 | tf_op jit(solution)/shard_map/ppermute | solution.py:96
  44.7 0.4 collective-permute-start.13
  45.2 0.2 collective-permute-start.15
  45.4 0.0 collective-permute-done.16.refs_9_
  45.4 3.7 %multiply.5 = (f32[256,512]{1,0:T(8,128)S(1)}, bf16[256,8192]{1,0:T(8,128)(2,1)}) custom-call(bf16[256,8192]{1,0:T(8,128)(2,1)S(1)} %copy-done, bf16[64,8192]{1,0:T(8,128)(2,1)S(1)} %bitcast.4, bf16[256,512]{1,0:T(8,128)(2,1)S(1)} %copy-done.2, bf16[256,64]{1,0:T(8,128)(2,1)S(1)} %get-tuple-element.48.refs_3_, ...), custom_call_target="tpu_custom_call", output_to_operand_aliasing={{1}: (5, {})} | custom-call | flops 1 | bytes 1 | tf_op jit(solution)/shard_map/multiply/pallas_call | solution.py:389
  49.1 5.4 %collective-permute-done.15.refs_9_ = bf16[96,512]{1,0:T(8,128)(2,1)S(1)} collective-permute-done((bf16[96,512]{1,0:T(8,128)(2,1)S(1)}, bf16[96,512]{1,0:T(8,128)(2,1)S(1)}, u32[]{:S(2)}, u32[]{:S(2)}) %collective-permute-start.15) | collective-permute-done | bytes 98336 | tf_op jit(solution)/shard_map/ppermute | solution.py:96
  54.4 0.0 collective-permute-done.14.refs_8_.refs_10_
  54.4 1.2 %collective-permute-done.13.refs_6_ = bf16[384,512]{1,0:T(8,128)(2,1)S(1)} collective-permute-done((bf16[384,512]{1,0:T(8,128)(2,1)S(1)}, bf16[384,512]{1,0:T(8,128)(2,1)S(1)}, u32[]{:S(2)}, u32[]{:S(2)}) %collective-permute-start.13) | collective-permute-done | bytes 393248 | tf_op jit(solution)/shard_map/ppermute | solution.py:96
  55.6 0.1 pad_maximum_fusion
  55.7 0.1 collective-permute-start.18
  55.8 0.6 collective-permute-start.17
  56.4 1.7 %multiply.6 = (f32[256,512]{1,0:T(8,128)S(1)}, bf16[256,8192]{1,0:T(8,128)(2,1)}) custom-call(bf16[256,8192]{1,0:T(8,128)(2,1)S(1)} %copy-done, bf16[64,8192]{1,0:T(8,128)(2,1)S(1)} %bitcast.5, bf16[256,512]{1,0:T(8,128)(2,1)S(1)} %copy-done.2, bf16[256,64]{1,0:T(8,128)(2,1)S(1)} %get-tuple-element.48.refs_3_, ...), custom_call_target="tpu_custom_call", output_to_operand_aliasing={{1}: (5, {})} | custom-call | flops 1 | bytes 1 | tf_op jit(solution)/shard_map/multiply/pallas_call | solution.py:389
  58.1 0.5 collective-permute-done.17.refs_7_
  58.5 0.0 collective-permute-done.18.refs_11_
  58.5 1.7 %multiply.7 = (bf16[256,512]{1,0:T(8,128)(2,1)}, bf16[256,8192]{1,0:T(8,128)(2,1)}, f32[64,512]{1,0:T(8,128)}, f32[64,512]{1,0:T(8,128)}) custom-call(bf16[256,8192]{1,0:T(8,128)(2,1)S(1)} %copy-done, bf16[64,8192]{1,0:T(8,128)(2,1)S(1)} %bitcast.6, bf16[256,512]{1,0:T(8,128)(2,1)S(1)} %copy-done.2, ...), custom_call_target="tpu_custom_call", output_to_operand_aliasing={{1}: (5, {})} | custom-call | flops 1 | bytes 1 | tf_op jit(solution)/shard_map/multiply/pallas_call | solution.py:389
  (28 shorter events, 0.4 us)
Async XLA Ops:
  0.6 5.2 %copy-start.2 = (bf16[256,512]{1,0:T(8,128)(2,1)S(1)}, bf16[256,512]{1,0:T(8,128)(2,1)}, u32[]{:S(2)}) copy-start(bf16[256,512]{1,0:T(8,128)(2,1)} %refs_2_.7) | copy-start | bytes 786436
  0.6 9.0 %copy-start.1 = (bf16[8192,64]{0,1:T(8,128)(2,1)S(1)}, bf16[8192,64]{0,1:T(8,128)(2,1)}, u32[]{:S(2)}) copy-start(bf16[8192,64]{0,1:T(8,128)(2,1)} %param.9) | copy-start | bytes 3145732
  0.7 9.0 %copy-start.3 = (bf16[64,512]{1,0:T(8,128)(2,1)S(1)}, bf16[64,512]{1,0:T(8,128)(2,1)}, u32[]{:S(2)}) copy-start(bf16[64,512]{1,0:T(8,128)(2,1)} %refs_5_.1) | copy-start | bytes 196612
  0.7 8.9 %collective-permute-start = (bf16[256,8192]{1,0:T(8,128)(2,1)}, bf16[256,8192]{1,0:T(8,128)(2,1)S(1)}, u32[]{:S(2)}, u32[]{:S(2)}) collective-permute-start(bf16[256,8192]{1,0:T(8,128)(2,1)} %refs_0_.7), channel_id=1, source_target_pairs={{0,1},{1,0},{2,3},{3,2},{4,5},{5,4},{6,7},{7,6},{8,9},{9,8},{10,11... | collective-permute-start | bytes 12582920 | tf_op jit(solution)/shard_map/ppermute | solution.py:96
  1.2 0.7 %copy-start.4 = (f32[4,4]{1,0:T(4,128)S(1)}, f32[4,4]{1,0:T(4,128)}, u32[]{:S(2)}) copy-start(f32[4,4]{1,0:T(4,128)} %scales_hbm.1) | copy-start | bytes 196
  1.9 7.8 %copy-start = (bf16[256,8192]{1,0:T(8,128)(2,1)S(1)}, bf16[256,8192]{1,0:T(8,128)(2,1)}, u32[]{:S(2)}) copy-start(bf16[256,8192]{1,0:T(8,128)(2,1)} %refs_0_.7) | copy-start | bytes 12582916
  3.1 19.1 %collective-permute-start.4 = (bf16[512,512]{1,0:T(8,128)(2,1)S(1)}, bf16[512,512]{1,0:T(8,128)(2,1)S(1)}, u32[]{:S(2)}, u32[]{:S(2)}) collective-permute-start(bf16[512,512]{1,0:T(8,128)(2,1)S(1)} %get-tuple-element.50.refs_6_), channel_id=1, source_target_pairs={{0,2},{1,3},{2,0},{3,1},{4,6},{5,7},{6,4},{7,5},{8,10},{9,11},{10,... | collective-permute-start | bytes 1572872 | tf_op jit(solution)/shard_map/ppermute | solution.py:96
  5.8 3.8 %collective-permute-start.1 = (bf16[256,512]{1,0:T(8,128)(2,1)S(1)}, bf16[256,512]{1,0:T(8,128)(2,1)S(1)}, u32[]{:S(2)}, u32[]{:S(2)}) collective-permute-start(bf16[256,512]{1,0:T(8,128)(2,1)S(1)} %copy-done.2), channel_id=1, source_target_pairs={{0,1},{1,0},{2,3},{3,2},{4,5},{5,4},{6,7},{7,6},{8,9},{9,8},{10,11... | collective-permute-start | bytes 786440 | tf_op jit(solution)/shard_map/ppermute | solution.py:96
  6.0 10.7 %collective-permute-start.2 = (bf16[256,512]{1,0:T(8,128)(2,1)S(1)}, bf16[256,512]{1,0:T(8,128)(2,1)S(1)}, u32[]{:S(2)}, u32[]{:S(2)}) collective-permute-start(bf16[256,512]{1,0:T(8,128)(2,1)S(1)} %get-tuple-element.49), channel_id=1, source_target_pairs={{0,12},{1,13},{2,14},{3,15},{4,0},{5,1},{6,2},{7,3},{8,4},{9,5},{1... | collective-permute-start | bytes 786440 | tf_op jit(solution)/shard_map/ppermute | solution.py:96
  9.6 12.6 %collective-permute-start.3 = (bf16[256,512]{1,0:T(8,128)(2,1)S(1)}, bf16[256,512]{1,0:T(8,128)(2,1)S(1)}, u32[]{:S(2)}, u32[]{:S(2)}) collective-permute-start(bf16[256,512]{1,0:T(8,128)(2,1)S(1)} %get-tuple-element.49), channel_id=1, source_target_pairs={{0,4},{1,5},{2,6},{3,7},{4,8},{5,9},{6,10},{7,11},{8,12},{9,13},{1... | collective-permute-start | bytes 786440 | tf_op jit(solution)/shard_map/ppermute | solution.py:96
  14.9 11.3 %collective-permute-start.8 = (bf16[320,512]{1,0:T(8,128)(2,1)S(1)}, bf16[320,512]{1,0:T(8,128)(2,1)S(1)}, u32[]{:S(2)}, u32[]{:S(2)}) collective-permute-start(bf16[320,512]{1,0:T(8,128)(2,1)S(1)} %get-tuple-element.56.sent_ref), channel_id=1, source_target_pairs={{0,2},{1,3},{2,0},{3,1},{4,6},{5,7},{6,4},{7,5},{8,10},{9,11},{10,... | collective-permute-start | bytes 983048 | tf_op jit(solution)/shard_map/ppermute | solution.py:96
  22.3 6.4 %collective-permute-start.11 = (bf16[768,512]{1,0:T(8,128)(2,1)S(1)}, bf16[768,512]{1,0:T(8,128)(2,1)S(1)}, u32[]{:S(2)}, u32[]{:S(2)}) collective-permute-start(bf16[768,512]{1,0:T(8,128)(2,1)S(1)} %pad_maximum_fusion.1), channel_id=1, source_target_pairs={{0,1},{1,0},{2,3},{3,2},{4,5},{5,4},{6,7},{7,6},{8,9},{9,8},{10,11... | collective-permute-start | bytes 2359304 | tf_op jit(solution)/shard_map/ppermute | solution.py:96
  22.5 16.8 %collective-permute-start.5 = (bf16[512,512]{1,0:T(8,128)(2,1)S(1)}, bf16[512,512]{1,0:T(8,128)(2,1)S(1)}, u32[]{:S(2)}, u32[]{:S(2)}) collective-permute-start(bf16[512,512]{1,0:T(8,128)(2,1)S(1)} %get-tuple-element.98), channel_id=1, source_target_pairs={{0,12},{1,13},{2,14},{3,15},{4,0},{5,1},{6,2},{7,3},{8,4},{9,5},{1... | collective-permute-start | bytes 1572872 | tf_op jit(solution)/shard_map/ppermute | solution.py:96
  24.3 15.0 %collective-permute-start.6 = (bf16[512,512]{1,0:T(8,128)(2,1)S(1)}, bf16[512,512]{1,0:T(8,128)(2,1)S(1)}, u32[]{:S(2)}, u32[]{:S(2)}) collective-permute-start(bf16[512,512]{1,0:T(8,128)(2,1)S(1)} %get-tuple-element.95), channel_id=1, source_target_pairs={{0,16},{1,17},{2,18},{3,19},{4,20},{5,21},{6,22},{7,23},{8,24},{9,... | collective-permute-start | bytes 1572872 | tf_op jit(solution)/shard_map/ppermute | solution.py:96
  25.8 13.8 %collective-permute-start.7 = (bf16[512,512]{1,0:T(8,128)(2,1)S(1)}, bf16[512,512]{1,0:T(8,128)(2,1)S(1)}, u32[]{:S(2)}, u32[]{:S(2)}) collective-permute-start(bf16[512,512]{1,0:T(8,128)(2,1)S(1)} %get-tuple-element.94), channel_id=1, source_target_pairs={{0,2},{1,3},{2,0},{3,1},{4,6},{5,7},{6,4},{7,5},{8,10},{9,11},{10,... | collective-permute-start | bytes 1572872 | tf_op jit(solution)/shard_map/ppermute | solution.py:96
  26.4 1.3 %collective-permute-start.9 = (f32[32,512]{1,0:T(8,128)S(1)}, f32[32,512]{1,0:T(8,128)S(1)}, u32[]{:S(2)}, u32[]{:S(2)}) collective-permute-start(f32[32,512]{1,0:T(8,128)S(1)} %get-tuple-element.59), channel_id=1, source_target_pairs={{0,1},{1,0},{2,3},{3,2},{4,5},{5,4},{6,7},{7,6},{8,9},{9,8},{10,11... | collective-permute-start | bytes 196616 | tf_op jit(solution)/shard_map/ppermute | solution.py:96
  27.7 11.5 %collective-permute-start.10 = (bf16[96,512]{1,0:T(8,128)(2,1)S(1)}, bf16[96,512]{1,0:T(8,128)(2,1)S(1)}, u32[]{:S(2)}, u32[]{:S(2)}) collective-permute-start(bf16[96,512]{1,0:T(8,128)(2,1)S(1)} %get-tuple-element.100), channel_id=1, source_target_pairs={{0,4},{1,5},{2,6},{3,7},{4,8},{5,9},{6,10},{7,11},{8,12},{9,13},{1... | collective-permute-start | bytes 294920 | tf_op jit(solution)/shard_map/ppermute | solution.py:96
  39.7 5.7 %collective-permute-start.16 = (bf16[2304,512]{1,0:T(8,128)(2,1)S(1)}, bf16[2304,512]{1,0:T(8,128)(2,1)S(1)}, u32[]{:S(2)}, u32[]{:S(2)}) collective-permute-start(bf16[2304,512]{1,0:T(8,128)(2,1)S(1)} %slice_dynamic-update-slice_fusion), channel_id=1, source_target_pairs={{0,1},{1,0},{2,3},{3,2},{4,5},{5,4},{6,7},{7,6},{8,9},{9,8},{10,11... | collective-permute-start | bytes 7077896 | tf_op jit(solution)/shard_map/ppermute | solution.py:96
  39.9 14.5 %collective-permute-start.14 = (bf16[352,512]{1,0:T(8,128)(2,1)S(1)}, bf16[352,512]{1,0:T(8,128)(2,1)S(1)}, u32[]{:S(2)}, u32[]{:S(2)}) collective-permute-start(bf16[352,512]{1,0:T(8,128)(2,1)S(1)} %pad_maximum_fusion.7), channel_id=1, source_target_pairs={{0,12},{1,13},{2,14},{3,15},{4,0},{5,1},{6,2},{7,3},{8,4},{9,5},{1... | collective-permute-start | bytes 1081352 | tf_op jit(solution)/shard_map/ppermute | solution.py:96
  43.1 11.3 %collective-permute-start.12 = (bf16[384,512]{1,0:T(8,128)(2,1)S(1)}, bf16[384,512]{1,0:T(8,128)(2,1)S(1)}, u32[]{:S(2)}, u32[]{:S(2)}) collective-permute-start(bf16[384,512]{1,0:T(8,128)(2,1)S(1)} %get-tuple-element.97), channel_id=1, source_target_pairs={{0,16},{1,17},{2,18},{3,19},{4,20},{5,21},{6,22},{7,23},{8,24},{9,... | collective-permute-start | bytes 1179656 | tf_op jit(solution)/shard_map/ppermute | solution.py:96
  44.7 10.9 %collective-permute-start.13 = (bf16[384,512]{1,0:T(8,128)(2,1)S(1)}, bf16[384,512]{1,0:T(8,128)(2,1)S(1)}, u32[]{:S(2)}, u32[]{:S(2)}) collective-permute-start(bf16[384,512]{1,0:T(8,128)(2,1)S(1)} %get-tuple-element.96), channel_id=1, source_target_pairs={{0,2},{1,3},{2,0},{3,1},{4,6},{5,7},{6,4},{7,5},{8,10},{9,11},{10,... | collective-permute-start | bytes 1179656 | tf_op jit(solution)/shard_map/ppermute | solution.py:96
  45.2 9.3 %collective-permute-start.15 = (bf16[96,512]{1,0:T(8,128)(2,1)S(1)}, bf16[96,512]{1,0:T(8,128)(2,1)S(1)}, u32[]{:S(2)}, u32[]{:S(2)}) collective-permute-start(bf16[96,512]{1,0:T(8,128)(2,1)S(1)} %pad_maximum_fusion.10), channel_id=1, source_target_pairs={{0,4},{1,5},{2,6},{3,7},{4,8},{5,9},{6,10},{7,11},{8,12},{9,13},{1... | collective-permute-start | bytes 294920 | tf_op jit(solution)/shard_map/ppermute | solution.py:96
  55.7 2.8 %collective-permute-start.18 = (bf16[1024,512]{1,0:T(8,128)(2,1)S(1)}, bf16[1024,512]{1,0:T(8,128)(2,1)S(1)}, u32[]{:S(2)}, u32[]{:S(2)}) collective-permute-start(bf16[1024,512]{1,0:T(8,128)(2,1)S(1)} %pad_maximum_fusion), channel_id=1, source_target_pairs={{0,1},{1,0},{2,3},{3,2},{4,5},{5,4},{6,7},{7,6},{8,9},{9,8},{10,11... | collective-permute-start | bytes 3145736 | tf_op jit(solution)/shard_map/ppermute | solution.py:96
  55.8 2.7 %collective-permute-start.17 = (f32[32,512]{1,0:T(8,128)S(1)}, f32[32,512]{1,0:T(8,128)S(1)}, u32[]{:S(2)}, u32[]{:S(2)}) collective-permute-start(f32[32,512]{1,0:T(8,128)S(1)} %add_multiply_fusion.refs_6_), channel_id=1, source_target_pairs={{0,1},{1,0},{2,3},{3,2},{4,5},{5,4},{6,7},{7,6},{8,9},{9,8},{10,11... | collective-permute-start | bytes 196616 | tf_op jit(solution)/shard_map/ppermute | solution.py:96
